TPU v7x, 32 devices: a whole 2x2x4 slice. The times are simulated.
32 devices in a mesh: wide: 8 (over y, x, core), narrow: 4 (over z).
Axes of the slice: x: 2, y: 2, z: 4, core: 2. Of those that a mesh axis runs over, the one named last changes fastest.
Arguments:
- patches: bfloat16 [64, 512, 768], P(('wide', 'narrow')), may hold values from -6 to 6
- lengths: int32 [64, 6], P(('wide', 'narrow')), may hold values from 1 to 196, 512 in all within a row
- w_qkv: bfloat16 [768, 2304], P('wide', 'narrow'), may hold values from -0.3125 to 0.3125
- w_out: bfloat16 [768, 768], P('wide', 'narrow'), may hold values from -0.625 to 0.625
- w_up: bfloat16 [768, 3072], P('wide', 'narrow'), may hold values from -0.21875 to 0.21875
- w_down: bfloat16 [3072, 768], P('wide', 'narrow'), may hold values from -0.109375 to 0.109375
- ln1_gain: bfloat16 [768], P(('wide', 'narrow')), may hold values from 0.25 to 1.75
- ln1_bias: bfloat16 [768], P(('wide', 'narrow')), may hold values from -3 to 3
- q_bias: bfloat16 [768], P(('wide', 'narrow')), may hold values from -3 to 3
- v_bias: bfloat16 [768], P(('wide', 'narrow')), may hold values from -3 to 3
- out_bias: bfloat16 [768], P(('wide', 'narrow')), may hold values from -3 to 3
- attn_scale: bfloat16 [768], P(('wide', 'narrow')), may hold values from 0.5 to 1.5
- ln2_gain: bfloat16 [768], P(('wide', 'narrow')), may hold values from 0.25 to 1.75
- ln2_bias: bfloat16 [768], P(('wide', 'narrow')), may hold values from -3 to 3
- up_bias: bfloat16 [3072], P(('wide', 'narrow')), may hold values from -3 to 3
- down_bias: bfloat16 [768], P(('wide', 'narrow')), may hold values from -3 to 3
- mlp_scale: bfloat16 [768], P(('wide', 'narrow')), may hold values from 0.5 to 1.5
- cotangent: bfloat16 [64, 512, 768], P(('wide', 'narrow')), may hold values from -6 to 6
Outputs:
- result_rows: bfloat16 [64, 512, 768], P(('wide', 'narrow'))
- grad_patches: float32 [64, 512, 768], P(('wide', 'narrow'))
- grad_w_qkv: float32 [768, 2304], P('wide', 'narrow')
- grad_w_out: float32 [768, 768], P('wide', 'narrow')
- grad_w_up: float32 [768, 3072], P('wide', 'narrow')
- grad_w_down: float32 [3072, 768], P('wide', 'narrow')
- grad_ln1_gain: float32 [768], P(('wide', 'narrow'))
- grad_ln1_bias: float32 [768], P(('wide', 'narrow'))
- grad_q_bias: float32 [768], P(('wide', 'narrow'))
- grad_v_bias: float32 [768], P(('wide', 'narrow'))
- grad_out_bias: float32 [768], P(('wide', 'narrow'))
- grad_attn_scale: float32 [768], P(('wide', 'narrow'))
- grad_ln2_gain: float32 [768], P(('wide', 'narrow'))
- grad_ln2_bias: float32 [768], P(('wide', 'narrow'))
- grad_up_bias: float32 [3072], P(('wide', 'narrow'))
- grad_down_bias: float32 [768], P(('wide', 'narrow'))
- grad_mlp_scale: float32 [768], P(('wide', 'narrow'))
Inputs may be any that keep to these rules, and one draw needn't show every extreme that they name: `lengths`: in each pack the first 5 entries count the visible patches of its images, in order, and the last counts pad rows at its end; they sum to 512, and some entry equals 196 in every pack.
All inputs are finite; a program needn't handle non-finite values.
Results may differ from a plain program's by a relative error of at most 0.012.
The roundings to bfloat16 on the way count: a program that leaves them out, or rounds other values in their place, can miss the bound.
Values may be sent and summed in bfloat16 or wider, within the bound.
No kernel may reach another device: no remote copies, remote signals or barrier semaphores. Data moves between devices by JAX's collectives and lax.ppermute only.
A program may use at most 192 MiB of HBM per device.

v0:
```python
import jax
import jax.numpy as jnp
from jax import lax
from jax.sharding import PartitionSpec as P

HD = 64


LN_EPSILON = 1e-06
MASKED = -1e30


def layer_norm(values, scale_vec, shift_vec):
    row_mean = jnp.mean(values, axis=-1, keepdims=True)
    centred = values - row_mean
    row_var = jnp.mean(centred * centred, axis=-1, keepdims=True)
    return centred * lax.rsqrt(row_var + LN_EPSILON) * scale_vec + shift_vec


def gelu_exact(values):
    return jax.nn.gelu(values, approximate=False)


def segment_ids(lengths, row_count):
    slot_count = lengths.shape[1]
    boundary = jnp.cumsum(lengths, axis=1)
    position = jnp.arange(row_count, dtype=jnp.int32)
    segment = jnp.sum((position[None, :, None] >= boundary[:, None, :]).astype(jnp.int32), axis=2)
    live_rows = position[None, :] < boundary[:, slot_count - 2][:, None]
    segment = jnp.where(live_rows, segment, slot_count + position[None, :])
    return (segment, live_rows)


def reorder(vector, leading, trailing):
    piece_len = vector.shape[0] // (leading * trailing)
    return vector.reshape(leading, trailing, piece_len).transpose(1, 0, 2).reshape(-1)


def collect(
    w_qkv,
    w_out,
    w_up,
    w_down,
    ln1_gain,
    ln1_bias,
    q_bias,
    v_bias,
    out_bias,
    attn_scale,
    ln2_gain,
    ln2_bias,
    up_bias,
    down_bias,
    mlp_scale,
):
    wide_size = lax.axis_size("wide")
    narrow_size = lax.axis_size("narrow")
    section_one = (
        lax.all_gather(w_qkv, "wide", axis=0, tiled=True),
        lax.all_gather(w_out, "wide", axis=0, tiled=True),
        lax.all_gather(w_up, "wide", axis=0, tiled=True),
        lax.all_gather(w_down, "wide", axis=0, tiled=True),
        lax.all_gather(ln1_gain, "wide", axis=0, tiled=True),
        lax.all_gather(ln1_bias, "wide", axis=0, tiled=True),
        lax.all_gather(q_bias, "wide", axis=0, tiled=True),
        lax.all_gather(v_bias, "wide", axis=0, tiled=True),
        lax.all_gather(out_bias, "wide", axis=0, tiled=True),
        lax.all_gather(attn_scale, "wide", axis=0, tiled=True),
        lax.all_gather(ln2_gain, "wide", axis=0, tiled=True),
        lax.all_gather(ln2_bias, "wide", axis=0, tiled=True),
        lax.all_gather(up_bias, "wide", axis=0, tiled=True),
        lax.all_gather(down_bias, "wide", axis=0, tiled=True),
        lax.all_gather(mlp_scale, "wide", axis=0, tiled=True),
    )
    section_two = (
        lax.all_gather(section_one[0], "narrow", axis=1, tiled=True),
        lax.all_gather(section_one[1], "narrow", axis=1, tiled=True),
        lax.all_gather(section_one[2], "narrow", axis=1, tiled=True),
        lax.all_gather(section_one[3], "narrow", axis=1, tiled=True),
        lax.all_gather(section_one[4], "narrow", axis=0, tiled=True),
        lax.all_gather(section_one[5], "narrow", axis=0, tiled=True),
        lax.all_gather(section_one[6], "narrow", axis=0, tiled=True),
        lax.all_gather(section_one[7], "narrow", axis=0, tiled=True),
        lax.all_gather(section_one[8], "narrow", axis=0, tiled=True),
        lax.all_gather(section_one[9], "narrow", axis=0, tiled=True),
        lax.all_gather(section_one[10], "narrow", axis=0, tiled=True),
        lax.all_gather(section_one[11], "narrow", axis=0, tiled=True),
        lax.all_gather(section_one[12], "narrow", axis=0, tiled=True),
        lax.all_gather(section_one[13], "narrow", axis=0, tiled=True),
        lax.all_gather(section_one[14], "narrow", axis=0, tiled=True),
    )
    result_set = tuple(section_two[:4]) + tuple(
        (reorder(vector_piece, narrow_size, wide_size) for vector_piece in section_two[4:])
    )
    return result_set


def reduce_grads(grad_set):
    wide_size = lax.axis_size("wide")
    narrow_size = lax.axis_size("narrow")
    moved = tuple(grad_set[:4]) + tuple(
        (reorder(vector_piece, wide_size, narrow_size) for vector_piece in grad_set[4:])
    )
    section_one = (
        lax.psum_scatter(moved[0], "narrow", scatter_dimension=1, tiled=True),
        lax.psum_scatter(moved[1], "narrow", scatter_dimension=1, tiled=True),
        lax.psum_scatter(moved[2], "narrow", scatter_dimension=1, tiled=True),
        lax.psum_scatter(moved[3], "narrow", scatter_dimension=1, tiled=True),
        lax.psum_scatter(moved[4], "narrow", scatter_dimension=0, tiled=True),
        lax.psum_scatter(moved[5], "narrow", scatter_dimension=0, tiled=True),
        lax.psum_scatter(moved[6], "narrow", scatter_dimension=0, tiled=True),
        lax.psum_scatter(moved[7], "narrow", scatter_dimension=0, tiled=True),
        lax.psum_scatter(moved[8], "narrow", scatter_dimension=0, tiled=True),
        lax.psum_scatter(moved[9], "narrow", scatter_dimension=0, tiled=True),
        lax.psum_scatter(moved[10], "narrow", scatter_dimension=0, tiled=True),
        lax.psum_scatter(moved[11], "narrow", scatter_dimension=0, tiled=True),
        lax.psum_scatter(moved[12], "narrow", scatter_dimension=0, tiled=True),
        lax.psum_scatter(moved[13], "narrow", scatter_dimension=0, tiled=True),
        lax.psum_scatter(moved[14], "narrow", scatter_dimension=0, tiled=True),
    )
    section_two = (
        lax.psum_scatter(section_one[0], "wide", scatter_dimension=0, tiled=True),
        lax.psum_scatter(section_one[1], "wide", scatter_dimension=0, tiled=True),
        lax.psum_scatter(section_one[2], "wide", scatter_dimension=0, tiled=True),
        lax.psum_scatter(section_one[3], "wide", scatter_dimension=0, tiled=True),
        lax.psum_scatter(section_one[4], "wide", scatter_dimension=0, tiled=True),
        lax.psum_scatter(section_one[5], "wide", scatter_dimension=0, tiled=True),
        lax.psum_scatter(section_one[6], "wide", scatter_dimension=0, tiled=True),
        lax.psum_scatter(section_one[7], "wide", scatter_dimension=0, tiled=True),
        lax.psum_scatter(section_one[8], "wide", scatter_dimension=0, tiled=True),
        lax.psum_scatter(section_one[9], "wide", scatter_dimension=0, tiled=True),
        lax.psum_scatter(section_one[10], "wide", scatter_dimension=0, tiled=True),
        lax.psum_scatter(section_one[11], "wide", scatter_dimension=0, tiled=True),
        lax.psum_scatter(section_one[12], "wide", scatter_dimension=0, tiled=True),
        lax.psum_scatter(section_one[13], "wide", scatter_dimension=0, tiled=True),
        lax.psum_scatter(section_one[14], "wide", scatter_dimension=0, tiled=True),
    )
    return tuple(section_two)


def pack_scores(query_pack, key_pack, segment_pack):
    row_count = query_pack.shape[0]
    query_heads = query_pack.reshape(row_count, -1, HD)
    key_heads = key_pack.reshape(row_count, -1, HD)
    scores = jnp.einsum("qhe,khe->hqk", query_heads, key_heads, preferred_element_type=jnp.float32)
    allowed = segment_pack[:, None] == segment_pack[None, :]
    return jnp.where(allowed[None], scores, MASKED)


def attend(pieces):
    query_pack, key_pack, value_pack, segment_pack = pieces
    row_count, model_width = query_pack.shape
    scores = pack_scores(query_pack, key_pack, segment_pack)
    row_top = jnp.max(scores, axis=-1, keepdims=True)
    exp_scores = jnp.exp(scores - row_top)
    row_total = jnp.sum(exp_scores, axis=-1, keepdims=True)
    soft_probs = (exp_scores / row_total).astype(jnp.bfloat16)
    value_heads = value_pack.reshape(row_count, -1, HD)
    mixed_heads = jnp.einsum(
        "hqk,khe->qhe", soft_probs, value_heads, preferred_element_type=jnp.float32
    )
    log_total = row_top[..., 0] + jnp.log(row_total[..., 0])
    return (mixed_heads.reshape(row_count, model_width).astype(jnp.bfloat16), log_total)


def attend_back(pieces):
    query_pack, key_pack, value_pack, segment_pack, log_pack, grad_pack = pieces
    row_count, model_width = query_pack.shape
    scores = pack_scores(query_pack, key_pack, segment_pack)
    soft_probs = jnp.exp(scores - log_pack[..., None])
    weights = soft_probs.astype(jnp.bfloat16)
    query_heads = query_pack.reshape(row_count, -1, HD)
    key_heads = key_pack.reshape(row_count, -1, HD)
    value_heads = value_pack.reshape(row_count, -1, HD)
    grad_heads = grad_pack.reshape(row_count, -1, HD)
    grad_value = jnp.einsum("hqk,qhe->khe", weights, grad_heads, preferred_element_type=jnp.float32)
    grad_probs = jnp.einsum(
        "qhe,khe->hqk", grad_heads, value_heads, preferred_element_type=jnp.float32
    )
    centre = jnp.sum(grad_probs * soft_probs, axis=-1, keepdims=True)
    grad_scores = (soft_probs * (grad_probs - centre)).astype(jnp.bfloat16)
    grad_query = jnp.einsum(
        "hqk,khe->qhe", grad_scores, key_heads, preferred_element_type=jnp.float32
    )
    grad_key = jnp.einsum(
        "hqk,qhe->khe", grad_scores, query_heads, preferred_element_type=jnp.float32
    )
    grad_query = grad_query.reshape(row_count, model_width).astype(jnp.bfloat16) * 0.125
    grad_key = grad_key.reshape(row_count, model_width).astype(jnp.bfloat16)
    grad_value = grad_value.reshape(row_count, model_width).astype(jnp.bfloat16)
    return jnp.concatenate([grad_query, grad_key, grad_value], axis=-1)


def shards(
    patches,
    lengths,
    w_qkv,
    w_out,
    w_up,
    w_down,
    ln1_gain,
    ln1_bias,
    q_bias,
    v_bias,
    out_bias,
    attn_scale,
    ln2_gain,
    ln2_bias,
    up_bias,
    down_bias,
    mlp_scale,
    cotangent,
):
    gathered = collect(
        w_qkv,
        w_out,
        w_up,
        w_down,
        ln1_gain,
        ln1_bias,
        q_bias,
        v_bias,
        out_bias,
        attn_scale,
        ln2_gain,
        ln2_bias,
        up_bias,
        down_bias,
        mlp_scale,
    )
    qkv_full, out_full, up_full, down_full = gathered[:4]
    (
        gain_first,
        shift_first,
        query_bias,
        value_bias,
        branch_bias,
        attn_layer,
        gain_second,
        shift_second,
        hidden_bias,
        output_bias,
        mlp_layer,
    ) = tuple((vector_piece.astype(jnp.float32) for vector_piece in gathered[4:]))
    pack_count, row_count, model_width = patches.shape
    segment, live_rows = segment_ids(lengths, row_count)
    live_mask = live_rows[..., None]
    inputs = patches.astype(jnp.float32)
    normed_full, ln1_pull = jax.vjp(layer_norm, inputs, gain_first, shift_first)
    normed = normed_full.astype(jnp.bfloat16)
    projected = jnp.einsum("prd,df->prf", normed, qkv_full, preferred_element_type=jnp.float32)
    query_rows = ((projected[..., :model_width] + query_bias) * 0.125).astype(jnp.bfloat16)
    key_rows = projected[..., model_width : 2 * model_width].astype(jnp.bfloat16)
    value_rows = (projected[..., 2 * model_width :] + value_bias).astype(jnp.bfloat16)
    attended, log_total = lax.map(attend, (query_rows, key_rows, value_rows, segment))
    branch = (
        jnp.einsum("prd,df->prf", attended, out_full, preferred_element_type=jnp.float32)
        + branch_bias
    )
    middle = inputs + attn_layer * branch
    normed_two_full, ln2_pull = jax.vjp(layer_norm, middle, gain_second, shift_second)
    normed_two = normed_two_full.astype(jnp.bfloat16)
    up_pre = (
        jnp.einsum("prd,df->prf", normed_two, up_full, preferred_element_type=jnp.float32)
        + hidden_bias
    )
    activated_full, gelu_pull = jax.vjp(gelu_exact, up_pre)
    activated = activated_full.astype(jnp.bfloat16)
    down_out = (
        jnp.einsum("prf,fd->prd", activated, down_full, preferred_element_type=jnp.float32)
        + output_bias
    )
    result_rows = jnp.where(live_mask, middle + mlp_layer * down_out, 0.0).astype(jnp.bfloat16)
    regathered = collect(
        w_qkv,
        w_out,
        w_up,
        w_down,
        ln1_gain,
        ln1_bias,
        q_bias,
        v_bias,
        out_bias,
        attn_scale,
        ln2_gain,
        ln2_bias,
        up_bias,
        down_bias,
        mlp_scale,
    )
    qkv_back, out_back, up_back, down_back = regathered[:4]
    grad_out = jnp.where(live_mask, cotangent.astype(jnp.float32), 0.0)
    grad_mlp_layer = jnp.sum(grad_out * down_out, axis=(0, 1))
    grad_down = (grad_out * mlp_layer).astype(jnp.bfloat16)
    grad_output_bias = jnp.sum(grad_down.astype(jnp.float32), axis=(0, 1))
    grad_w_down = jnp.einsum(
        "prf,prd->fd", activated, grad_down, preferred_element_type=jnp.float32
    )
    grad_activated = jnp.einsum(
        "prd,fd->prf", grad_down, down_back, preferred_element_type=jnp.float32
    )
    grad_up = gelu_pull(grad_activated)[0].astype(jnp.bfloat16)
    grad_hidden_bias = jnp.sum(grad_up.astype(jnp.float32), axis=(0, 1))
    grad_w_up = jnp.einsum("prd,prf->df", normed_two, grad_up, preferred_element_type=jnp.float32)
    grad_normed_two = jnp.einsum(
        "prf,df->prd", grad_up, up_back, preferred_element_type=jnp.float32
    )
    grad_middle_norm, grad_gain_second, grad_shift_second = ln2_pull(grad_normed_two)
    grad_middle = grad_out + grad_middle_norm
    grad_attn_layer = jnp.sum(grad_middle * branch, axis=(0, 1))
    grad_branch = (grad_middle * attn_layer).astype(jnp.bfloat16)
    grad_branch_bias = jnp.sum(grad_branch.astype(jnp.float32), axis=(0, 1))
    grad_w_out = jnp.einsum(
        "prd,prf->df", attended, grad_branch, preferred_element_type=jnp.float32
    )
    grad_attended = jnp.einsum(
        "prf,df->prd", grad_branch, out_back, preferred_element_type=jnp.float32
    ).astype(jnp.bfloat16)
    grad_projected = lax.map(
        attend_back, (query_rows, key_rows, value_rows, segment, log_total, grad_attended)
    )
    grad_w_qkv = jnp.einsum(
        "prd,prf->df", normed, grad_projected, preferred_element_type=jnp.float32
    )
    grad_query_bias = jnp.sum(grad_projected[..., :model_width].astype(jnp.float32), axis=(0, 1))
    grad_value_bias = jnp.sum(
        grad_projected[..., 2 * model_width :].astype(jnp.float32), axis=(0, 1)
    )
    grad_normed = jnp.einsum(
        "prf,df->prd", grad_projected, qkv_back, preferred_element_type=jnp.float32
    )
    grad_input_norm, grad_gain_first, grad_shift_first = ln1_pull(grad_normed)
    grad_inputs = grad_middle + grad_input_norm
    reduced = reduce_grads(
        (
            grad_w_qkv,
            grad_w_out,
            grad_w_up,
            grad_w_down,
            grad_gain_first,
            grad_shift_first,
            grad_query_bias,
            grad_value_bias,
            grad_branch_bias,
            grad_attn_layer,
            grad_gain_second,
            grad_shift_second,
            grad_hidden_bias,
            grad_output_bias,
            grad_mlp_layer,
        )
    )
    return (
        result_rows,
        grad_inputs,
        reduced[0],
        reduced[1],
        reduced[2],
        reduced[3],
        reduced[4],
        reduced[5],
        reduced[6],
        reduced[7],
        reduced[8],
        reduced[9],
        reduced[10],
        reduced[11],
        reduced[12],
        reduced[13],
        reduced[14],
    )


def solution(mesh):
    return jax.shard_map(
        shards,
        mesh=mesh,
        in_specs=(
            P(("wide", "narrow"), None, None),
            P(("wide", "narrow"), None),
            P("wide", "narrow"),
            P("wide", "narrow"),
            P("wide", "narrow"),
            P("wide", "narrow"),
            P(("wide", "narrow")),
            P(("wide", "narrow")),
            P(("wide", "narrow")),
            P(("wide", "narrow")),
            P(("wide", "narrow")),
            P(("wide", "narrow")),
            P(("wide", "narrow")),
            P(("wide", "narrow")),
            P(("wide", "narrow")),
            P(("wide", "narrow")),
            P(("wide", "narrow")),
            P(("wide", "narrow"), None, None),
        ),
        out_specs=(
            P(("wide", "narrow"), None, None),
            P(("wide", "narrow"), None, None),
            P("wide", "narrow"),
            P("wide", "narrow"),
            P("wide", "narrow"),
            P("wide", "narrow"),
            P(("wide", "narrow")),
            P(("wide", "narrow")),
            P(("wide", "narrow")),
            P(("wide", "narrow")),
            P(("wide", "narrow")),
            P(("wide", "narrow")),
            P(("wide", "narrow")),
            P(("wide", "narrow")),
            P(("wide", "narrow")),
            P(("wide", "narrow")),
            P(("wide", "narrow")),
        ),
        check_vma=False,
    )
```

profile of v0, /device:TPU:0, one launch (start us, length us, event | category | flops | bytes accessed | tf_op | source)
XLA Modules:
  0.0 1083.6 jit_solution(2440033192655232563)
XLA Ops:
  8.9 12.8 %all_gather.104 = bf16[768,576]{1,0:T(8,128)(2,1)S(1)} all-gather(bf16[96,576]{1,0:T(8,128)(2,1)} %param.24), channel_id=1, replica_groups=mesh['wide'=8,'narrow'=4] {'wide'}, dimensions={0}, use_global_device_ids=true | all-gather | bytes 995328 | tf_op jit(solution)/shard_map/all_gather | solution.py:59
  23.0 9.2 all_gather.110
  33.1 3.6 all-gather.12.cloned.1.call-done
  41.7 13.5 %all-reduce.45 = (bf16[192]{0:T(256)(128)(2,1)S(1)}, bf16[192]{0:T(256)(128)(2,1)S(1)}, bf16[192]{0:T(256)(128)(2,1)S(1)}, bf16[192]{0:T(256)(128)(2,1)S(1)}, bf...) all-reduce(bf16[192]{0:T(256)(128)(2,1)S(1)} %dynamic-update-slice,, ...), channel_id=1, replica_groups=mesh['wide'=8,'narrow'=4] {'wide'}, use_global_device_ids=true, to_apply=%add | all-reduce | flops 2688 | bytes 10752
  55.2 13.1 %all-gather = bf16[4,1,768]{2,1,0:T(2,128)(2,1)S(1)} all-gather(bf16[1,1,768]{2,1,0:T(2,128)(2,1)S(1)} %reshape.553), channel_id=1, replica_groups=mesh['wide'=8,'narrow'=4] {'narrow'}, dimensions={0}, use_global_device_ids=true | all-gather | bytes 7680 | tf_op jit(solution)/shard_map/all_gather | solution.py:88
  71.3 20.7 %all-reduce.46 = (bf16[768]{0:T(1024)(128)(2,1)S(1)}, bf16[768]{0:T(1024)(128)(2,1)S(1)}, bf16[768]{0:T(1024)(128)(2,1)S(1)}, bf16[768]{0:T(1024)(128)(2,1)S(1)}...) all-reduce(bf16[768]{0:T(1024)(128)(2,1)S(1)} %dynamic-update-slice, ...), channel_id=1, replica_groups=mesh['wide'=8,'narrow'=4] {'narrow'}, use_global_device_ids=true, to_apply=%add.1 | all-reduce | flops 7680 | bytes 30720
  96.6 39.1 %all-gather.8.cloned.1.call-done = bf16[768,2304]{0,1:T(8,128)(2,1)} async-done(((bf16[768,576]{0,1:T(8,128)(2,1)}), bf16[768,2304]{0,1:T(8,128)(2,1)}) %all-gather.8.cloned.1.call-update) | async-done | bytes 3538960 | tf_op jit(solution)/shard_map/all_gather | solution.py:76
  135.7 6.2 fusion.37
  141.9 3.6 copy-done.5
  148.6 5.1 fusion.45
  153.6 2.6 copy.175
  156.2 2.6 copy.174
  158.8 27.2 %while.22 = (s32[]{:T(128)}, bf16[2,512,768]{1,2,0:T(8,128)(2,1)}, f32[2,12,512]{2,1,0:T(8,128)S(1)}, bf16[2,512,768]{1,2,0:T(8,128)(2,1)}, s32[2,512]{1,0:T(2,1...) while((s32[]{:T(128)}, bf16[2,512,768]{1,2,0:T(8,128)(2,1)}, ...), condition=%wide.region_7.8_spmd, body=%wide.region_4.7_spmd.sunk | while | flops 834267136 | bytes 61044904 | solution.py:255
  166.5 4.5 fusion.112
  180.1 4.5 fusion.112
  186.1 6.0 fusion.63
  194.6 62.1 %all-gather.14.cloned.1.call-done = bf16[768,3072]{1,0:T(8,128)(2,1)} async-done(((bf16[768,768]{1,0:T(8,128)(2,1)}), bf16[768,3072]{1,0:T(8,128)(2,1)}) %all-gather.14.cloned.1.call-update) | async-done | bytes 4718608 | tf_op jit(solution)/shard_map/all_gather | solution.py:78
  256.7 14.0 %fusion.48 = (u8[512,3072]{1,0:T(8,128)(4,1)}, u8[512,3072]{1,0:T(8,128)(4,1)}, f32[2,512,3072]{2,1,0:T(8,128)S(1)}) fusion(f32[3072]{0:T(1024)S(1)} %reshape.477, bf16[768,3072]{1,0:T(8,128)(2,1)} %all-gather.14.cloned.1.call-done, f32[2,512,768]{2,1,0:T(8,128)} %get-tuple-element.354, f32[768]{0:T(1024)S(1)} %reshape.476, f32[768]{0:T(1024)S(1)} %reshape.475, ...), kind=kOutput, calls=%fused_computation.111 | convolution fusion | flops 4876664832 | bytes 23619584 | tf_op jit(solution)/shard_map/prd,df->prf/dot_general | solution.py:264
  270.7 4.5 copy-done.2
  275.1 32.2 %multiply_convert_fusion.1 = (bf16[2,512,3072]{2,1,0:T(8,128)(2,1)}, f32[2,512,3072]{2,1,0:T(8,128)}) fusion(f32[2,512,3072]{2,1,0:T(8,128)S(1)} %get-tuple-element.372, f32[3072]{0:T(1024)S(1)} %reshape.477, u8[512,3072]{1,0:T(8,128)(4,1)} %get-tuple-element.261, u8[512,3072]{1,0:T(8,128)(4,1)} %get-tuple-element.260), kind=kLoop, calls=%fused_computation.45 | loop fusion | flops 223346688 | bytes 34615296 | tf_op jit(solution)/shard_map/convert_element_type | solution.py:268
  307.4 38.6 %all-gather.18.cloned.1.call-done = bf16[3072,768]{0,1:T(8,128)(2,1)} async-done(((bf16[3072,192]{0,1:T(8,128)(2,1)}), bf16[3072,768]{0,1:T(8,128)(2,1)}) %all-gather.18.cloned.1.call-update) | async-done | bytes 4718608 | tf_op jit(solution)/shard_map/all_gather | solution.py:79
  346.0 16.2 %convert_reduce_fusion = (f32[3072]{0:T(1024)}, bf16[2,512,3072]{2,1,0:T(8,128)(2,1)S(1)}) fusion(f32[2,512,3072]{2,1,0:T(8,128)} %get-tuple-element.352, bf16[3072,768]{0,1:T(8,128)(2,1)} %all-gather.18.cloned.1.call-done, bf16[2,512,768]{2,1,0:T(8,128)(2,1)} %param.39, f32[768]{0:T(1024)S(1)} %copy-done.38, pred[2,512]{1,0:T(4,128)(4,1)S(1)} %copy-done.36, ...), kind=kOutput, calls=%fused_computation.43 | convolution fusion | flops 4888458240 | bytes 37777408 | tf_op jit(solution)/shard_map/prd,fd->prf/dot_general | solution.py:299
  362.2 11.9 %multiply_reduce_fusion.2 = (f32[768]{0:T(1024)}, f32[2,512]{1,0:T(2,128)S(1)}, f32[768]{0:T(1024)}, f32[2,512,768]{2,1,0:T(8,128)S(1)}) fusion(f32[2,512,768]{2,1,0:T(8,128)} %get-tuple-element.354, f32[2,512]{1,0:T(2,128)S(1)} %fusion.57, f32[2,512]{1,0:T(2,128)S(1)} %broadcast_multiply_fusion, f32[768]{0:T(1024)S(1)} %reshape.475, ...), kind=kOutput, calls=%fused_computation.96 | convolution fusion | flops 4838126592 | bytes 17323008 | tf_op jit(solution)/shard_map/prf,df->prd/dot_general | solution.py:305
  374.1 2.7 fusion.61
  379.4 2.9 convolution_bitcast_fusion.3
  382.4 3.8 convolution_convert_fusion.2
  386.2 53.0 %while.23 = (s32[]{:T(128)}, bf16[2,512,2304]{1,2,0:T(8,128)(2,1)}, bf16[2,512,768]{1,2,0:T(8,128)(2,1)S(1)}, s32[2,512]{1,0:T(2,128)S(1)}, bf16[2,512,768]{1,2,...) while((s32[]{:T(128)}, bf16[2,512,2304]{1,2,0:T(8,128)(2,1)}, ...), condition=%wide.region_14.15_spmd, body=%wide.region_12.14_spmd.sunk | while | flops 2059921408 | bytes 116045952 | solution.py:319
  391.5 2.9 fusion.124
  394.3 6.6 multiply_reduce_fusion.7
  401.0 7.0 multiply_convert_fusion.8
  417.7 2.9 fusion.124
  420.6 6.6 multiply_reduce_fusion.7
  427.2 7.0 multiply_convert_fusion.8
  439.2 9.8 convolution_bitcast_fusion.2
  449.7 11.0 %convolution_bitcast_fusion.1 = f32[768,3072]{1,0:T(8,128)} fusion(bf16[2,512,3072]{2,1,0:T(8,128)(2,1)} %copy-done.6, f32[2,512,768]{2,1,0:T(8,128)} %get-tuple-element.354, f32[768]{0:T(1024)S(1)} %copy-done.16, f32[768]{0:T(1024)S(1)} %copy-done.14, f32[2,512]{1,0:T(2,128)S(1)} %copy-done.20, f32[2,512]{1,0:T(2,128)S(1)} %copy-done.18), kind=kOutput, calls=%fused_computation.59 | convolution fusion | flops 4835770368 | bytes 18888704 | tf_op jit(solution)/shard_map/prd,prf->df/dot_general | solution.py:304
  462.1 10.5 convolution_bitcast_fusion
  475.1 96.2 %reduce-scatter.13.cloned.1.call-done = f32[768,576]{0,1:T(8,128)} async-done(((f32[768,2304]{0,1:T(8,128)}), f32[768,576]{0,1:T(8,128)}) %reduce-scatter.13.cloned.1.call-update) | async-done | bytes 1769488 | tf_op jit(solution)/shard_map/reduce_scatter | solution.py:105
  571.2 2.8 copy.217
  574.1 161.3 %reduce-scatter.17.cloned.1.call-done = f32[768,768]{1,0:T(8,128)} async-done(((f32[768,3072]{1,0:T(8,128)}), f32[768,768]{1,0:T(8,128)}) %reduce-scatter.17.cloned.1.call-update) | async-done | bytes 2359312 | tf_op jit(solution)/shard_map/reduce_scatter | solution.py:107
  739.2 2.4 convert_reduce_fusion.4
  741.8 158.1 %reduce-scatter.21.cloned.1.call-done = f32[3072,192]{0,1:T(8,128)} async-done(((f32[3072,768]{0,1:T(8,128)}), f32[3072,192]{0,1:T(8,128)}) %reduce-scatter.21.cloned.1.call-update) | async-done | bytes 2359312 | tf_op jit(solution)/shard_map/reduce_scatter | solution.py:108
  899.9 7.6 fusion.60
  909.4 11.7 %multiply_reduce_fusion.1 = (f32[768]{0:T(1024)S(1)}, f32[768]{0:T(1024)S(1)}, f32[768]{0:T(1024)S(1)}, f32[2,512,768]{2,1,0:T(8,128)}, bf16[2,512,768]{2,1,0:T(8,128)(2,1)}) fusion(bf16[2,512,768]{2,1,0:T(8,128)(2,1)S(1)} %copy-done.12, f32[768]{0:T(1024)S(1)} %reshape.478, pred[2,512]{1,0:T(4,128)(4,1)S(1)} %copy-done.37, ...), kind=kOutput, calls=%fused_computation.94 | convolution fusion | flops 4853068800 | bytes 31500288 | tf_op jit(solution)/shard_map/prf,fd->prd/dot_general | solution.py:270
  922.2 19.2 %all-reduce.44 = (f32[768]{0:T(1024)S(1)}, f32[768]{0:T(1024)S(1)}, f32[768]{0:T(1024)S(1)}, f32[768]{0:T(1024)S(1)}, f32[768]{0:T(1024)S(1)}, /*index=5*/f32[76...) all-reduce(f32[768]{0:T(1024)S(1)} %reshape.447, ...), channel_id=10, replica_groups=mesh['wide'=8,'narrow'=4] {'narrow'}, use_global_device_ids=true, to_apply=%region_26.27.clone | all-reduce | flops 10752 | bytes 86016
  942.3 22.4 %all-reduce.43 = (f32[192]{0:T(256)S(1)}, f32[192]{0:T(256)S(1)}, f32[192]{0:T(256)S(1)}, f32[192]{0:T(256)S(1)}, f32[192]{0:T(256)S(1)}, /*index=5*/f32[192]{0:...) all-reduce(f32[192]{0:T(256)S(1)} %dynamic-slice.22, ...), channel_id=11, replica_groups=mesh['wide'=8,'narrow'=4] {'wide'}, use_global_device_ids=true, to_apply=%region_27.28.clone | all-reduce | flops 2688 | bytes 21504
  971.1 12.5 %reduce-scatter.25.cloned.1.call-done = f32[96,576]{1,0:T(8,128)} async-done(((f32[768,576]{1,0:T(8,128)}), f32[96,576]{1,0:T(8,128)}) %reduce-scatter.25.cloned.1.call-update) | async-done | bytes 221200
  983.6 46.8 %reduce-scatter.19.cloned.1.call-done = f32[96,768]{1,0:T(8,128)} async-done(((f32[768,768]{1,0:T(8,128)}), f32[96,768]{1,0:T(8,128)}) %reduce-scatter.19.cloned.1.call-update) | async-done | bytes 294928 | tf_op jit(solution)/shard_map/reduce_scatter | solution.py:124
  1030.4 46.3 %reduce-scatter.23.cloned.1.call-done = f32[384,192]{0,1:T(8,128)} async-done(((f32[3072,192]{0,1:T(8,128)}), f32[384,192]{0,1:T(8,128)}) %reduce-scatter.23.cloned.1.call-update) | async-done | bytes 294928 | tf_op jit(solution)/shard_map/reduce_scatter | solution.py:125
  (351 shorter events, 75.4 us)
Async XLA Ops:
  7.2 29.5 %all-gather.12.cloned.1.call-start = ((), (), s32[]{:S(2)}) async-start(), calls=%async_computation.10 | async-start | bytes 1327104 | tf_op jit(solution)/shard_map/all_gather | solution.py:61
  7.9 88.4 %all-gather.16.cloned.1.call-start = ((), (), s32[]{:S(2)}) async-start(), calls=%async_computation.12 | async-start | bytes 1327104 | tf_op jit(solution)/shard_map/all_gather | solution.py:62
  8.7 30.2 %copy-start.48 = (bf16[24]{0:T(256)(128)(2,1)S(1)}, bf16[24]{0:T(256)(128)(2,1)}, u32[]{:S(2)}) copy-start(bf16[24]{0:T(256)(128)(2,1)} %param.37) | copy-start | bytes 148
  8.7 30.5 %copy-start.49 = (bf16[24]{0:T(256)(128)(2,1)S(1)}, bf16[24]{0:T(256)(128)(2,1)}, u32[]{:S(2)}) copy-start(bf16[24]{0:T(256)(128)(2,1)} %param.35) | copy-start | bytes 148
  8.7 30.7 %copy-start.50 = (bf16[24]{0:T(256)(128)(2,1)S(1)}, bf16[24]{0:T(256)(128)(2,1)}, u32[]{:S(2)}) copy-start(bf16[24]{0:T(256)(128)(2,1)} %param.34) | copy-start | bytes 148
  8.8 30.9 %copy-start.51 = (bf16[24]{0:T(256)(128)(2,1)S(1)}, bf16[24]{0:T(256)(128)(2,1)}, u32[]{:S(2)}) copy-start(bf16[24]{0:T(256)(128)(2,1)} %param.38) | copy-start | bytes 148
  8.8 31.2 %copy-start.52 = (bf16[24]{0:T(256)(128)(2,1)S(1)}, bf16[24]{0:T(256)(128)(2,1)}, u32[]{:S(2)}) copy-start(bf16[24]{0:T(256)(128)(2,1)} %param.32) | copy-start | bytes 148
  8.8 31.4 %copy-start.53 = (bf16[24]{0:T(256)(128)(2,1)S(1)}, bf16[24]{0:T(256)(128)(2,1)}, u32[]{:S(2)}) copy-start(bf16[24]{0:T(256)(128)(2,1)} %param.30) | copy-start | bytes 148
  8.8 31.7 %copy-start.54 = (bf16[24]{0:T(256)(128)(2,1)S(1)}, bf16[24]{0:T(256)(128)(2,1)}, u32[]{:S(2)}) copy-start(bf16[24]{0:T(256)(128)(2,1)} %param.31) | copy-start | bytes 148
  8.8 31.9 %copy-start.55 = (bf16[24]{0:T(256)(128)(2,1)S(1)}, bf16[24]{0:T(256)(128)(2,1)}, u32[]{:S(2)}) copy-start(bf16[24]{0:T(256)(128)(2,1)} %param.29) | copy-start | bytes 148
  8.8 32.1 %copy-start.56 = (bf16[24]{0:T(256)(128)(2,1)S(1)}, bf16[24]{0:T(256)(128)(2,1)}, u32[]{:S(2)}) copy-start(bf16[24]{0:T(256)(128)(2,1)} %param.28) | copy-start | bytes 148
  8.8 32.4 %copy-start.57 = (bf16[24]{0:T(256)(128)(2,1)S(1)}, bf16[24]{0:T(256)(128)(2,1)}, u32[]{:S(2)}) copy-start(bf16[24]{0:T(256)(128)(2,1)} %param.33) | copy-start | bytes 148
  8.8 32.6 %copy-start.58 = (bf16[96]{0:T(256)(128)(2,1)S(1)}, bf16[96]{0:T(256)(128)(2,1)}, u32[]{:S(2)}) copy-start(bf16[96]{0:T(256)(128)(2,1)} %param.36) | copy-start | bytes 580
  8.8 126.9 %all-gather.8.cloned.1.call-start = ((), (), s32[]{:S(2)}) async-start(), calls=%async_computation.8 | async-start | bytes 4423680 | tf_op jit(solution)/shard_map/all_gather | solution.py:76
  21.6 73.0 %copy-start = (bf16[2,512,768]{2,1,0:T(8,128)(2,1)S(1)}, bf16[2,512,768]{2,1,0:T(8,128)(2,1)}, u32[]{:S(2)}) copy-start(bf16[2,512,768]{2,1,0:T(8,128)(2,1)} %param.22) | copy-start | bytes 4718596
  22.9 163.2 %all-gather.10.cloned.1.call-start = ((), (), s32[]{:S(2)}) async-start(), calls=%async_computation.9 | async-start | bytes 1474560 | tf_op jit(solution)/shard_map/all_gather | solution.py:77
  33.1 223.6 %all-gather.14.cloned.1.call-start = ((), (), s32[]{:S(2)}) async-start(), calls=%async_computation.11 | async-start | bytes 5898240 | tf_op jit(solution)/shard_map/all_gather | solution.py:78
  36.7 309.2 %all-gather.18.cloned.1.call-start = ((), (), s32[]{:S(2)}) async-start(), calls=%async_computation.13 | async-start | bytes 5898240 | tf_op jit(solution)/shard_map/all_gather | solution.py:79
  92.4 49.5 %copy-start.28 = (f32[768]{0:T(1024)}, f32[768]{0:T(1024)S(1)}, u32[]{:S(2)}) copy-start(f32[768]{0:T(1024)S(1)} %reshape.469) | copy-start | bytes 9220
  92.6 49.3 %copy-start.40 = (f32[768]{0:T(1024)}, f32[768]{0:T(1024)S(1)}, u32[]{:S(2)}) copy-start(f32[768]{0:T(1024)S(1)} %reshape.470) | copy-start | bytes 9220
  93.2 92.9 %copy-start.22 = (f32[768]{0:T(1024)}, f32[768]{0:T(1024)S(1)}, u32[]{:S(2)}) copy-start(f32[768]{0:T(1024)S(1)} %reshape.473) | copy-start | bytes 9220
  94.2 279.9 %copy-start.13 = (f32[768]{0:T(1024)}, f32[768]{0:T(1024)S(1)}, u32[]{:S(2)}) copy-start(f32[768]{0:T(1024)S(1)} %reshape.475) | copy-start | bytes 9220
  94.4 162.3 %copy-start.15 = (f32[768]{0:T(1024)}, f32[768]{0:T(1024)S(1)}, u32[]{:S(2)}) copy-start(f32[768]{0:T(1024)S(1)} %reshape.476) | copy-start | bytes 9220
  95.6 46.2 %copy-start.24 = (f32[2,512]{1,0:T(2,128)}, f32[2,512]{1,0:T(2,128)S(1)}, u32[]{:S(2)}) copy-start(f32[2,512]{1,0:T(2,128)S(1)} %broadcast_multiply_fusion.1) | copy-start | bytes 12292
  96.2 45.6 %copy-start.26 = (f32[2,512]{1,0:T(2,128)}, f32[2,512]{1,0:T(2,128)S(1)}, u32[]{:S(2)}) copy-start(f32[2,512]{1,0:T(2,128)S(1)} %fusion.42) | copy-start | bytes 12292
  96.3 45.6 %copy-start.31 = (f32[2,512]{1,0:T(2,128)}, f32[2,512]{1,0:T(2,128)S(1)}, u32[]{:S(2)}) copy-start(f32[2,512]{1,0:T(2,128)S(1)} %fusion.56) | copy-start | bytes 12292
  96.4 376.3 %reduce-scatter.15.cloned.1.call-start = ((), (), s32[]{:S(2)}) async-start(), calls=%async_computation.15 | async-start | bytes 2949120 | tf_op jit(solution)/shard_map/reduce_scatter | solution.py:106
  192.2 181.9 %copy-start.17 = (f32[2,512]{1,0:T(2,128)}, f32[2,512]{1,0:T(2,128)S(1)}, u32[]{:S(2)}) copy-start(f32[2,512]{1,0:T(2,128)S(1)} %broadcast_multiply_fusion) | copy-start | bytes 12292
  194.5 179.5 %copy-start.19 = (f32[2,512]{1,0:T(2,128)}, f32[2,512]{1,0:T(2,128)S(1)}, u32[]{:S(2)}) copy-start(f32[2,512]{1,0:T(2,128)S(1)} %fusion.57) | copy-start | bytes 12292
  275.1 70.9 %copy-start.36 = (pred[2,512]{1,0:T(4,128)(4,1)S(1)}, pred[2,512]{1,0:T(4,128)(4,1)}, u32[]{:S(2)}) copy-start(pred[2,512]{1,0:T(4,128)(4,1)} %iota_compare_fusion) | copy-start | bytes 3076
  275.1 70.9 %copy-start.38 = (f32[768]{0:T(1024)S(1)}, f32[768]{0:T(1024)}, u32[]{:S(2)}) copy-start(f32[768]{0:T(1024)} %reshape.474) | copy-start | bytes 9220
  382.3 188.9 %reduce-scatter.13.cloned.1.call-start = ((), (), s32[]{:S(2)}) async-start(), calls=%async_computation.14 | async-start | bytes 8847360 | tf_op jit(solution)/shard_map/reduce_scatter | solution.py:105
  386.2 53.0 %copy-start.25 = (f32[2,512]{1,0:T(2,128)S(1)}, f32[2,512]{1,0:T(2,128)}, u32[]{:S(2)}) copy-start(f32[2,512]{1,0:T(2,128)} %copy-done.24) | copy-start | bytes 12292
  386.2 53.0 %copy-start.29 = (f32[768]{0:T(1024)S(1)}, f32[768]{0:T(1024)}, u32[]{:S(2)}) copy-start(f32[768]{0:T(1024)} %copy-done.28) | copy-start | bytes 9220
  386.2 53.0 %copy-start.32 = (f32[2,512]{1,0:T(2,128)S(1)}, f32[2,512]{1,0:T(2,128)}, u32[]{:S(2)}) copy-start(f32[2,512]{1,0:T(2,128)} %copy-done.31) | copy-start | bytes 12292
  386.2 53.0 %copy-start.41 = (f32[768]{0:T(1024)S(1)}, f32[768]{0:T(1024)}, u32[]{:S(2)}) copy-start(f32[768]{0:T(1024)} %copy-done.40) | copy-start | bytes 9220
  449.0 286.4 %reduce-scatter.17.cloned.1.call-start = ((), (), s32[]{:S(2)}) async-start(), calls=%async_computation.16 | async-start | bytes 11796480 | tf_op jit(solution)/shard_map/reduce_scatter | solution.py:107
  460.7 439.1 %reduce-scatter.21.cloned.1.call-start = ((), (), s32[]{:S(2)}) async-start(), calls=%async_computation.18 | async-start | bytes 11796480 | tf_op jit(solution)/shard_map/reduce_scatter | solution.py:108
  472.6 498.5 %reduce-scatter.27.cloned.1.call-start = ((), (), s32[]{:S(2)}) async-start(), calls=%async_computation.21 | async-start | bytes 884736
  475.0 263.2 %copy-start.44 = (bf16[768]{0:T(1024)(128)(2,1)S(1)}, bf16[768]{0:T(1024)(128)(2,1)}, u32[]{:S(2)}) copy-start(bf16[768]{0:T(1024)(128)(2,1)} %get-tuple-element.346) | copy-start | bytes 4612
  475.0 508.6 %reduce-scatter.25.cloned.1.call-start = ((), (), s32[]{:S(2)}) async-start(), calls=%async_computation.20 | async-start | bytes 2211840
  574.0 164.4 %copy-start.35 = (f32[3072]{0:T(1024)S(1)}, f32[3072]{0:T(1024)}, u32[]{:S(2)}) copy-start(f32[3072]{0:T(1024)} %get-tuple-element.375) | copy-start | bytes 36868
  574.1 164.6 %copy-start.43 = (f32[768]{0:T(1024)S(1)}, f32[768]{0:T(1024)}, u32[]{:S(2)}) copy-start(f32[768]{0:T(1024)} %get-tuple-element.262) | copy-start | bytes 9220
  574.1 164.8 %copy-start.42 = (f32[768]{0:T(1024)S(1)}, f32[768]{0:T(1024)}, u32[]{:S(2)}) copy-start(f32[768]{0:T(1024)} %get-tuple-element.268) | copy-start | bytes 9220
  574.1 165.0 %copy-start.30 = (f32[768]{0:T(1024)S(1)}, f32[768]{0:T(1024)}, u32[]{:S(2)}) copy-start(f32[768]{0:T(1024)} %get-tuple-element.347) | copy-start | bytes 9220
  574.1 456.3 %reduce-scatter.19.cloned.1.call-start = ((), (), s32[]{:S(2)}) async-start(), calls=%async_computation.17 | async-start | bytes 2654208 | tf_op jit(solution)/shard_map/reduce_scatter | solution.py:124
  735.5 164.4 %copy-start.1 = (bf16[2,512,768]{2,1,0:T(8,128)(2,1)S(1)}, bf16[2,512,768]{2,1,0:T(8,128)(2,1)}, u32[]{:S(2)}) copy-start(bf16[2,512,768]{2,1,0:T(8,128)(2,1)} %param.22) | copy-start | bytes 4718596
  735.5 341.2 %reduce-scatter.23.cloned.1.call-start = ((), (), s32[]{:S(2)}) async-start(), calls=%async_computation.19 | async-start | bytes 2654208 | tf_op jit(solution)/shard_map/reduce_scatter | solution.py:125
  (27 other events, 170.0 us)
Sparse Core Ops, SparseCore 0:
  9.9 26.7 all-gather.11
  38.6 24.2 all-gather.15
  65.0 70.6 all-gather.7
  137.7 28.9 all-gather.9
  168.1 88.5 all-gather.13
  258.1 87.8 all-gather.17
  382.4 46.4 reduce-scatter.14
  449.1 122.0 reduce-scatter.12
  573.6 161.8 reduce-scatter.16
  737.7 162.1 reduce-scatter.20
  903.6 35.8 reduce-scatter.26
  943.3 40.2 reduce-scatter.24
  987.9 42.4 reduce-scatter.18
  1034.1 42.4 reduce-scatter.22
where the time goes:
time: 1090 us; the launch traced here: 1080 us
  waiting for transfers between devices  666 us (61%)
  matrix products  153 us (14%)
  blocking collectives  111 us (10%)
  other arithmetic  72.1 us (7%)
  local copies, waits for them, and re-layouts  59.6 us (5%)
  between operations  20.2 us (2%)
    reduce_scatter x1, waiting for transfers between devices, reduce_grads(): lax.psum_scatter(moved[2], 'narrow', scatter_dimension=1, tiled=True)  161 us
    reduce_scatter x1, waiting for transfers between devices, reduce_grads(): lax.psum_scatter(moved[3], 'narrow', scatter_dimension=1, tiled=True)  158 us
    reduce_scatter x1, waiting for transfers between devices, reduce_grads(): lax.psum_scatter(moved[0], 'narrow', scatter_dimension=1, tiled=True)  96.2 us
    unnamed x4, blocking collectives  75.8 us
    all_gather x1, waiting for transfers between devices, collect(): lax.all_gather(section_one[2], 'narrow', axis=1, tiled=True)  62.1 us
    reduce_scatter x1, waiting for transfers between devices, reduce_grads(): lax.psum_scatter(section_one[2], 'wide', scatter_dimension=0, tiled=True)  46.8 us
    reduce_scatter x1, waiting for transfers between devices, reduce_grads(): lax.psum_scatter(section_one[3], 'wide', scatter_dimension=0, tiled=True)  46.3 us
    all_gather x1, waiting for transfers between devices, collect(): lax.all_gather(section_one[0], 'narrow', axis=1, tiled=True)  39.1 us
  transfers between devices with their start and end apart: 14, of which 10 were waited for; matrix products, arithmetic and copies ran while one was open for 22% of the time, Pallas kernels for 0%

commit v1 on v0

--- a/solution.py
+++ b/solution.py
@@ -31,111 +31,192 @@
     return (segment, live_rows)
 
 
-def reorder(vector, leading, trailing):
-    piece_len = vector.shape[0] // (leading * trailing)
-    return vector.reshape(leading, trailing, piece_len).transpose(1, 0, 2).reshape(-1)
-
-
-def collect(
-    w_qkv,
-    w_out,
-    w_up,
-    w_down,
-    ln1_gain,
-    ln1_bias,
-    q_bias,
-    v_bias,
-    out_bias,
-    attn_scale,
-    ln2_gain,
-    ln2_bias,
-    up_bias,
-    down_bias,
-    mlp_scale,
-):
+def exchange(value, axis_name, partner):
+    size = lax.axis_size(axis_name)
+    return lax.ppermute(value, axis_name, [(i, partner(i) % size) for i in range(size)])
+
+
+def cross(value, bit):
+    return exchange(value, "wide", lambda i: i ^ (1 << bit))
+
+
+def shift(value, step):
+    return exchange(value, "narrow", lambda i: i + step)
+
+
+def wide_bits():
+    return lax.axis_size("wide").bit_length() - 1
+
+
+def by_origin(pieces):
+    size = len(pieces)
+    backward = jnp.stack(pieces[::-1])
+    twice = jnp.concatenate([backward, backward])
+    return lax.dynamic_slice_in_dim(twice, size - 1 - lax.axis_index("narrow"), size)
+
+
+def flip_own(stacked):
+    here = lax.axis_index("wide")
+    size = stacked.shape[0]
+    for bit in range(size.bit_length() - 1):
+        halves = stacked.reshape((size >> (bit + 1), 2, 1 << bit) + stacked.shape[1:])
+        halves = jnp.where((here >> bit) & 1, halves[:, ::-1], halves)
+        stacked = halves.reshape(stacked.shape)
+    return stacked
+
+
+def spread_wide(block):
+    rows = block.shape[0]
+    half = rows // 32 * 16
+    held = block[None]
+    for bit in range(3, wide_bits()):
+        held = jnp.concatenate([held, cross(held, bit)])
+    near = cross(held, 1)
+    far = cross(held, 2)
+    corner_one = cross(near[:, :half], 2)
+    corner_two = cross(far[:, half:], 1)
+    mine = [held, near, far, corner_one, corner_two]
+    theirs = [cross(piece, 0) for piece in mine]
+    quads = []
+    for at in range(3):
+        quads.append(jnp.stack([mine[at], theirs[at]], axis=1))
+    quads.append(
+        jnp.stack(
+            [
+                jnp.concatenate([mine[3], mine[4]], axis=1),
+                jnp.concatenate([theirs[3], theirs[4]], axis=1),
+            ],
+            axis=1,
+        )
+    )
+    stacked = jnp.stack(quads, axis=1).reshape((-1,) + block.shape)
+    return flip_own(stacked)
+
+
+def gather_narrow(shard):
+    size = lax.axis_size("narrow")
+    return by_origin([shard] + [shift(shard, step) for step in range(1, size)])
+
+
+def side_by_side(stacked):
+    return jnp.concatenate([stacked[i] for i in range(stacked.shape[0])], axis=1)
+
+
+VECTORS = 11
+
+
+def collect(w_qkv, w_out, w_up, w_down, *vectors):
+    narrow_size = lax.axis_size("narrow")
     wide_size = lax.axis_size("wide")
-    narrow_size = lax.axis_size("narrow")
-    section_one = (
-        lax.all_gather(w_qkv, "wide", axis=0, tiled=True),
-        lax.all_gather(w_out, "wide", axis=0, tiled=True),
-        lax.all_gather(w_up, "wide", axis=0, tiled=True),
-        lax.all_gather(w_down, "wide", axis=0, tiled=True),
-        lax.all_gather(ln1_gain, "wide", axis=0, tiled=True),
-        lax.all_gather(ln1_bias, "wide", axis=0, tiled=True),
-        lax.all_gather(q_bias, "wide", axis=0, tiled=True),
-        lax.all_gather(v_bias, "wide", axis=0, tiled=True),
-        lax.all_gather(out_bias, "wide", axis=0, tiled=True),
-        lax.all_gather(attn_scale, "wide", axis=0, tiled=True),
-        lax.all_gather(ln2_gain, "wide", axis=0, tiled=True),
-        lax.all_gather(ln2_bias, "wide", axis=0, tiled=True),
-        lax.all_gather(up_bias, "wide", axis=0, tiled=True),
-        lax.all_gather(down_bias, "wide", axis=0, tiled=True),
-        lax.all_gather(mlp_scale, "wide", axis=0, tiled=True),
-    )
-    section_two = (
-        lax.all_gather(section_one[0], "narrow", axis=1, tiled=True),
-        lax.all_gather(section_one[1], "narrow", axis=1, tiled=True),
-        lax.all_gather(section_one[2], "narrow", axis=1, tiled=True),
-        lax.all_gather(section_one[3], "narrow", axis=1, tiled=True),
-        lax.all_gather(section_one[4], "narrow", axis=0, tiled=True),
-        lax.all_gather(section_one[5], "narrow", axis=0, tiled=True),
-        lax.all_gather(section_one[6], "narrow", axis=0, tiled=True),
-        lax.all_gather(section_one[7], "narrow", axis=0, tiled=True),
-        lax.all_gather(section_one[8], "narrow", axis=0, tiled=True),
-        lax.all_gather(section_one[9], "narrow", axis=0, tiled=True),
-        lax.all_gather(section_one[10], "narrow", axis=0, tiled=True),
-        lax.all_gather(section_one[11], "narrow", axis=0, tiled=True),
-        lax.all_gather(section_one[12], "narrow", axis=0, tiled=True),
-        lax.all_gather(section_one[13], "narrow", axis=0, tiled=True),
-        lax.all_gather(section_one[14], "narrow", axis=0, tiled=True),
-    )
-    result_set = tuple(section_two[:4]) + tuple(
-        (reorder(vector_piece, narrow_size, wide_size) for vector_piece in section_two[4:])
-    )
-    return result_set
+    width = w_up.shape[1]
+    short = w_up.shape[0]
+    packed = jnp.concatenate(vectors)
+    row = jnp.pad(packed[None], ((0, 15), (0, width - packed.shape[0])))
+    one = jnp.concatenate([jnp.concatenate([w_qkv, w_out], axis=1), row])
+    down = jnp.concatenate(jnp.split(w_down, narrow_size, axis=0), axis=1)
+    one = gather_narrow(one)
+    two = gather_narrow(w_up)
+    three = gather_narrow(down)
+    qkv = side_by_side(one[:, :short, : w_qkv.shape[1]])
+    out = side_by_side(one[:, :short, w_qkv.shape[1] :])
+    rows = jnp.pad(one[:, short], ((0, 16 - narrow_size), (0, 0)))
+    one = jnp.concatenate([*jnp.split(qkv, 3, axis=1), out, rows])
+    two = two.reshape(-1, width)
+    quarter = w_down.shape[1]
+    three = jnp.concatenate(
+        [side_by_side(three[:, :, i * quarter : (i + 1) * quarter]) for i in range(narrow_size)]
+    )
+    one = spread_wide(one)
+    two = spread_wide(two)
+    three = spread_wide(three)
+    square = one[:, : 4 * short].reshape(wide_size, 4, short, width)
+    q, k, v, out = (square[:, i].reshape(-1, width) for i in range(4))
+    qkv_full = jnp.concatenate([q, k, v], axis=1)
+    up = two.reshape(wide_size, narrow_size, short, width).transpose(0, 2, 1, 3)
+    up_full = up.reshape(-1, narrow_size * width)
+    down_full = three.reshape(-1, width)
+    rows = one[:, 4 * short : 4 * short + narrow_size, : packed.shape[0]]
+    full, at = [], 0
+    for vector in vectors:
+        full.append(rows[:, :, at : at + vector.shape[0]].reshape(-1))
+        at += vector.shape[0]
+    return (qkv_full, out, up_full, down_full, *full)
+
+
+def add_low(left, right):
+    return (left.astype(jnp.float32) + right.astype(jnp.float32)).astype(left.dtype)
+
+
+def meet_wide(stacked):
+    stacked = flip_own(stacked)
+    rows = stacked.shape[1]
+    half = rows // 32 * 16
+    pieces = stacked.reshape((-1, 4, 2) + stacked.shape[1:])
+    held = add_low(pieces[:, :, 0], cross(pieces[:, :, 1], 0))
+    own, near, far, corner = (held[:, i] for i in range(4))
+    corner_one = cross(corner[:, :half], 1)
+    corner_two = cross(corner[:, half:], 2)
+    far = jnp.concatenate([add_low(far[:, :half], corner_one), far[:, half:]], axis=1)
+    near = jnp.concatenate([near[:, :half], add_low(near[:, half:], corner_two)], axis=1)
+    near = cross(near, 1).astype(jnp.float32)
+    far = cross(far, 2).astype(jnp.float32)
+    held = (own.astype(jnp.float32) + near + far).astype(stacked.dtype)
+    for bit in reversed(range(3, wide_bits())):
+        count = held.shape[0] // 2
+        held = add_low(held[:count], cross(held[count:], bit))
+    return held[0]
+
+
+def meet_narrow(stacked):
+    size = stacked.shape[0]
+    here = lax.axis_index("narrow")
+    total = lax.dynamic_index_in_dim(stacked, here, keepdims=False).astype(jnp.float32)
+    for step in range(1, size):
+        block = lax.dynamic_index_in_dim(stacked, lax.rem(here + step, size), keepdims=False)
+        total = total + shift(block, step).astype(jnp.float32)
+    return total
 
 
 def reduce_grads(grad_set):
     wide_size = lax.axis_size("wide")
     narrow_size = lax.axis_size("narrow")
-    moved = tuple(grad_set[:4]) + tuple(
-        (reorder(vector_piece, wide_size, narrow_size) for vector_piece in grad_set[4:])
-    )
-    section_one = (
-        lax.psum_scatter(moved[0], "narrow", scatter_dimension=1, tiled=True),
-        lax.psum_scatter(moved[1], "narrow", scatter_dimension=1, tiled=True),
-        lax.psum_scatter(moved[2], "narrow", scatter_dimension=1, tiled=True),
-        lax.psum_scatter(moved[3], "narrow", scatter_dimension=1, tiled=True),
-        lax.psum_scatter(moved[4], "narrow", scatter_dimension=0, tiled=True),
-        lax.psum_scatter(moved[5], "narrow", scatter_dimension=0, tiled=True),
-        lax.psum_scatter(moved[6], "narrow", scatter_dimension=0, tiled=True),
-        lax.psum_scatter(moved[7], "narrow", scatter_dimension=0, tiled=True),
-        lax.psum_scatter(moved[8], "narrow", scatter_dimension=0, tiled=True),
-        lax.psum_scatter(moved[9], "narrow", scatter_dimension=0, tiled=True),
-        lax.psum_scatter(moved[10], "narrow", scatter_dimension=0, tiled=True),
-        lax.psum_scatter(moved[11], "narrow", scatter_dimension=0, tiled=True),
-        lax.psum_scatter(moved[12], "narrow", scatter_dimension=0, tiled=True),
-        lax.psum_scatter(moved[13], "narrow", scatter_dimension=0, tiled=True),
-        lax.psum_scatter(moved[14], "narrow", scatter_dimension=0, tiled=True),
-    )
-    section_two = (
-        lax.psum_scatter(section_one[0], "wide", scatter_dimension=0, tiled=True),
-        lax.psum_scatter(section_one[1], "wide", scatter_dimension=0, tiled=True),
-        lax.psum_scatter(section_one[2], "wide", scatter_dimension=0, tiled=True),
-        lax.psum_scatter(section_one[3], "wide", scatter_dimension=0, tiled=True),
-        lax.psum_scatter(section_one[4], "wide", scatter_dimension=0, tiled=True),
-        lax.psum_scatter(section_one[5], "wide", scatter_dimension=0, tiled=True),
-        lax.psum_scatter(section_one[6], "wide", scatter_dimension=0, tiled=True),
-        lax.psum_scatter(section_one[7], "wide", scatter_dimension=0, tiled=True),
-        lax.psum_scatter(section_one[8], "wide", scatter_dimension=0, tiled=True),
-        lax.psum_scatter(section_one[9], "wide", scatter_dimension=0, tiled=True),
-        lax.psum_scatter(section_one[10], "wide", scatter_dimension=0, tiled=True),
-        lax.psum_scatter(section_one[11], "wide", scatter_dimension=0, tiled=True),
-        lax.psum_scatter(section_one[12], "wide", scatter_dimension=0, tiled=True),
-        lax.psum_scatter(section_one[13], "wide", scatter_dimension=0, tiled=True),
-        lax.psum_scatter(section_one[14], "wide", scatter_dimension=0, tiled=True),
-    )
-    return tuple(section_two)
+    qkv, out, up, down = (grad.astype(jnp.bfloat16) for grad in grad_set[:4])
+    width = out.shape[0]
+    short = width // wide_size
+    three = meet_wide(down.reshape(wide_size, -1, width))
+    three = meet_narrow(three.reshape(-1, narrow_size, width // narrow_size).transpose(1, 0, 2))
+    up = up.reshape(wide_size, short, narrow_size, width).transpose(0, 2, 1, 3)
+    two = meet_wide(up.reshape(wide_size, -1, width))
+    two = meet_narrow(two.reshape(narrow_size, short, width))
+    one = jnp.concatenate(
+        [
+            piece.reshape(wide_size, short, width)
+            for piece in (*jnp.split(qkv, 3, axis=1), out)
+        ],
+        axis=1,
+    )
+    one = meet_wide(one)
+    one_qkv = jnp.concatenate([one[i * short : (i + 1) * short] for i in range(3)], axis=1)
+    one_out = one[3 * short :]
+    one = jnp.concatenate(
+        [
+            one_qkv.reshape(short, narrow_size, -1).transpose(1, 0, 2),
+            one_out.reshape(short, narrow_size, -1).transpose(1, 0, 2),
+        ],
+        axis=2,
+    )
+    one = meet_narrow(one)
+    part = qkv.shape[1] // narrow_size
+    sums = jnp.concatenate(
+        [vector.reshape(wide_size, narrow_size, -1) for vector in grad_set[4:]], axis=2
+    )
+    sums = meet_narrow(meet_wide(sums).reshape(narrow_size, 1, -1))[0]
+    vectors, at = [], 0
+    for vector in grad_set[4:]:
+        count = vector.shape[0] // (wide_size * narrow_size)
+        vectors.append(sums[at : at + count])
+        at += count
+    return (one[:, :part], one[:, part:], two, three, *vectors)
 
 
 def pack_scores(query_pack, key_pack, segment_pack):
@@ -271,24 +352,7 @@
         + output_bias
     )
     result_rows = jnp.where(live_mask, middle + mlp_layer * down_out, 0.0).astype(jnp.bfloat16)
-    regathered = collect(
-        w_qkv,
-        w_out,
-        w_up,
-        w_down,
-        ln1_gain,
-        ln1_bias,
-        q_bias,
-        v_bias,
-        out_bias,
-        attn_scale,
-        ln2_gain,
-        ln2_bias,
-        up_bias,
-        down_bias,
-        mlp_scale,
-    )
-    qkv_back, out_back, up_back, down_back = regathered[:4]
+    qkv_back, out_back, up_back, down_back = gathered[:4]
     grad_out = jnp.where(live_mask, cotangent.astype(jnp.float32), 0.0)
     grad_mlp_layer = jnp.sum(grad_out * down_out, axis=(0, 1))
     grad_down = (grad_out * mlp_layer).astype(jnp.bfloat16)

time: 1090 us -> 564 us (0.52)
  waiting for transfers between devices: 666 us -> 113 us
  blocking collectives: 111 us -> 0 us
  starting transfers between devices: 0.74 us -> 68 us
  other arithmetic: 72.1 us -> 131 us
  local copies, waits for them, and re-layouts: 59.6 us -> 95.6 us
  between operations: 20.2 us -> 3.12 us
    reduce_scatter x6 -> x0, waiting for transfers between devices: 509 us -> none  [the longest x1 161 us: reduce_grads(): lax.psum_scatter(moved[2], 'narrow', scatter_dimension=1, tiled=True)]
    all_gather x6 -> x0, waiting for transfers between devices: 143 us -> none  [the longest x1 62.1 us: collect(): lax.all_gather(section_one[2], 'narrow', axis=1, tiled=True)]
    ppermute x0 -> x67, waiting for transfers between devices: none -> 113 us  [exchange(): lax.ppermute(value, axis_name, [(i, partner(i) % size) for i in range(siz...]
    unnamed x4 -> x0, blocking collectives: 75.8 us -> none
    ppermute x0 -> x67, starting transfers between devices: none -> 68 us  [exchange(): lax.ppermute(value, axis_name, [(i, partner(i) % size) for i in range(siz...]
    all_gather x3 -> x0, blocking collectives: 35 us -> none  [the longest x1 13.1 us: collect(): lax.all_gather(section_one[12], 'narrow', axis=0, tiled=True)]
    select_n x0 -> x21, other arithmetic: none -> 25.7 us  [flip_own(): halves = jnp.where(here >> bit & 1, halves[:, ::-1], halves)]
    reshape x22 -> x5, local copies, waits for them, and re-layouts: 1.84 us -> 25.6 us  [the longest x2 13 us: reduce_grads(): up = up.reshape(wide_size, short, narrow_size, width).transpose(0, 2, 1, 3)]
  transfers between devices with their start and end apart: 14 -> 67, of which waited for: 10 -> 20; matrix products, arithmetic and copies ran while one was open for 22% -> 16% of each run, Pallas kernels for 0% -> 0%
where the time goes in v1:
time: 564 us; the launch traced here: 557 us
  matrix products  145 us (26%)
  other arithmetic  131 us (23%)
  waiting for transfers between devices  113 us (20%)
  local copies, waits for them, and re-layouts  95.6 us (17%)
  starting transfers between devices  68 us (12%)
    ppermute x67, waiting for transfers between devices, exchange(): lax.ppermute(value, axis_name, [(i, partner(i) % size) for i in range(siz...  113 us
    ppermute x67, starting transfers between devices, exchange(): lax.ppermute(value, axis_name, [(i, partner(i) % size) for i in range(siz...  68 us
    convert_element_type x1, other arithmetic, shards(): activated = activated_full.astype(jnp.bfloat16)  32.1 us
    select_n x21, other arithmetic, flip_own(): halves = jnp.where(here >> bit & 1, halves[:, ::-1], halves)  25.7 us
    dot_general x1, matrix products, shards(): jnp.einsum('prd,fd->prf', grad_down, down_back, preferred_element_type=jn...  17.2 us
    convert_element_type x2, other arithmetic, attend_back(): grad_scores = (soft_probs * (grad_probs - centre)).astype(jnp.bfloat16)  13.9 us
    dot_general x1, matrix products, shards(): jnp.einsum('prd,df->prf', normed_two, up_full, preferred_element_type=jnp...  13.5 us
    dot_general x1, matrix products, shards(): jnp.einsum('prf,fd->prd', activated, down_full, preferred_element_type=jn...  13 us
  transfers between devices with their start and end apart: 67, of which 20 were waited for; matrix products, arithmetic and copies ran while one was open for 16% of the time, Pallas kernels for 0%

profile of v1, /device:TPU:0, one launch (start us, length us, event | category | flops | bytes accessed | tf_op | source)
XLA Modules:
  0.0 556.8 jit_solution(5031113343981230006)
XLA Ops:
  0.7 4.1 collective-permute-start.13
  6.8 7.4 %concatenate.142 = bf16[336]{0:T(512)(128)(2,1)S(1)} concatenate(bf16[24]{0:T(256)(128)(2,1)} %param.28, bf16[24]{0:T(256)(128)(2,1)} %param.29, bf16[24]{0:T(256)(128)(2,1)} %param.30, bf16[24]{0:T(256)(128)(2,1)} %param.31, bf16[24]{0:T(256)(128)(2,1)} %param.32, bf16[24]{0:T(256)(128)(2,1)} %param.33, bf16[24]{0:T(256)(128)(2,1)} %param.34, bf16[24]{0:T(256)(128)(2,1)} %param.35, ...), dimensions={0} | concatenate | bytes 1344 | tf_op jit(solution)/shard_map/concatenate | solution.py:113
  29.7 10.1 %collective-permute-done.24 = bf16[96,768]{1,0:T(8,128)(2,1)S(1)} collective-permute-done((bf16[96,768]{1,0:T(8,128)(2,1)S(1)}, bf16[96,768]{1,0:T(8,128)(2,1)S(1)}, u32[]{:S(2)}, u32[]{:S(2)}) %collective-permute-start.24) | collective-permute-done | bytes 147488 | tf_op jit(solution)/shard_map/ppermute | solution.py:36
  39.9 9.8 %collective-permute-done.25 = bf16[96,768]{1,0:T(8,128)(2,1)S(1)} collective-permute-done((bf16[96,768]{1,0:T(8,128)(2,1)S(1)}, bf16[96,768]{1,0:T(8,128)(2,1)S(1)}, u32[]{:S(2)}, u32[]{:S(2)}) %collective-permute-start.25) | collective-permute-done | bytes 147488 | tf_op jit(solution)/shard_map/ppermute | solution.py:36
  56.5 9.4 %collective-permute-done.18 = bf16[1,384,768]{2,1,0:T(8,128)(2,1)} collective-permute-done((bf16[1,384,768]{2,1,0:T(8,128)(2,1)S(1)}, bf16[1,384,768]{2,1,0:T(8,128)(2,1)}, u32[]{:S(2)}, u32[]{:S(2)}) %collective-permute-start.18) | collective-permute-done | bytes 589856 | tf_op jit(solution)/shard_map/ppermute | solution.py:36
  69.7 8.9 %collective-permute-done.30 = bf16[1,384,768]{2,1,0:T(8,128)(2,1)} collective-permute-done((bf16[1,384,768]{2,1,0:T(8,128)(2,1)}, bf16[1,384,768]{2,1,0:T(8,128)(2,1)}, u32[]{:S(2)}, u32[]{:S(2)}) %collective-permute-start.30) | collective-permute-done | bytes 589856 | tf_op jit(solution)/shard_map/ppermute | solution.py:36
  83.8 7.9 %collective-permute-done.6 = bf16[1,400,768]{2,1,0:T(8,128)(2,1)} collective-permute-done((bf16[1,400,768]{2,1,0:T(8,128)(2,1)S(1)}, bf16[1,400,768]{2,1,0:T(8,128)(2,1)}, u32[]{:S(2)}, u32[]{:S(2)}) %collective-permute-start.6) | collective-permute-done | bytes 614432 | tf_op jit(solution)/shard_map/ppermute | solution.py:36
  101.1 4.9 collective-permute-done.33
  108.7 4.0 collective-permute-done.8
  119.7 5.8 %copy.142 = bf16[8,96,4,768]{3,2,1,0:T(4,128)(2,1)} copy(bf16[8,96,4,768]{3,1,2,0:T(8,128)(2,1)S(1)} %bitcast.517) | data formatting | bytes 9437184 | tf_op jit(solution)/shard_map/transpose | solution.py:135
  125.6 9.3 %reshape.562 = bf16[768,3072,1]{1,0,2:T(8,128)(2,1)} reshape(bf16[8,96,4,768]{3,2,1,0:T(4,128)(2,1)} %copy.142) | data formatting | bytes 9437184 | tf_op jit(solution)/shard_map/reshape | solution.py:136
  154.7 4.3 fusion.91
  159.8 5.8 %fusion.42 = f32[2,512,2304]{2,1,0:T(8,128)S(1)} fusion(bf16[768,768]{1,0:T(8,128)(2,1)S(1)} %bitcast.547, bf16[768,768]{1,0:T(8,128)(2,1)} %bitcast.549, bf16[768,768]{1,0:T(8,128)(2,1)} %bitcast.551, bf16[2,512,768]{2,1,0:T(8,128)(2,1)S(1)} %copy-done.3, f32[768]{0:T(1024)S(1)} %reshape.542, f32[768]{0:T(1024)S(1)} %reshape.541, ...), kind=kOutput, calls=%fused_computation.138 | convolution fusion | flops 3639214080 | bytes 14563328 | tf_op jit(solution)/shard_map/prd,df->prf/dot_general | solution.py:332
  165.7 3.7 copy-done.6
  172.4 5.0 fusion.37
  182.6 27.1 %while.22 = (s32[]{:T(128)}, bf16[2,512,768]{1,2,0:T(8,128)(2,1)}, f32[2,12,512]{2,1,0:T(8,128)S(1)}, bf16[2,512,768]{1,2,0:T(8,128)(2,1)}, s32[2,512]{1,0:T(2,1...) while((s32[]{:T(128)}, bf16[2,512,768]{1,2,0:T(8,128)(2,1)}, ...), condition=%wide.region_7.8_spmd, body=%wide.region_4.7_spmd.sunk | while | flops 834267136 | bytes 61044904 | solution.py:336
  190.5 4.5 fusion.151
  203.9 4.5 fusion.151
  209.7 5.2 fusion.90
  215.4 13.5 %fusion.40 = (u8[512,3072]{1,0:T(8,128)(4,1)S(1)}, u8[512,3072]{1,0:T(8,128)(4,1)S(1)}, f32[2,512,3072]{2,1,0:T(8,128)}) fusion(f32[3072]{0:T(1024)S(1)} %reshape.549, bf16[768,3072,1]{1,0,2:T(8,128)(2,1)S(1)} %bitcast.534, f32[2,512,768]{2,1,0:T(8,128)S(1)} %get-tuple-element.211, f32[768]{0:T(1024)S(1)} %reshape.548, f32[768]{0:T(1024)S(1)} %reshape.547, ...), kind=kOutput, calls=%fused_computation.129 | convolution fusion | flops 4876664832 | bytes 23619584 | tf_op jit(solution)/shard_map/prd,df->prf/dot_general | solution.py:345
  229.0 32.1 %multiply_convert_fusion.1 = (bf16[2,512,3072]{2,1,0:T(8,128)(2,1)}, f32[2,512,3072]{2,1,0:T(8,128)}) fusion(f32[2,512,3072]{2,1,0:T(8,128)} %get-tuple-element.314, f32[3072]{0:T(1024)S(1)} %reshape.549, u8[512,3072]{1,0:T(8,128)(4,1)S(1)} %get-tuple-element.161, u8[512,3072]{1,0:T(8,128)(4,1)S(1)} %get-tuple-element.160), kind=kLoop, calls=%fused_computation.45 | loop fusion | flops 223346688 | bytes 34615296 | tf_op jit(solution)/shard_map/convert_element_type | solution.py:349
  261.1 17.2 %convert_reduce_fusion = (f32[3072]{0:T(1024)}, bf16[2,512,3072]{2,1,0:T(8,128)(2,1)}) fusion(f32[2,512,3072]{2,1,0:T(8,128)} %get-tuple-element.209, bf16[3072,768,1]{1,0,2:T(8,128)(2,1)} %bitcast.531, bf16[2,512,768]{2,1,0:T(8,128)(2,1)S(1)} %copy-done.14, f32[768]{0:T(1024)S(1)} %copy-done.57, pred[2,512]{1,0:T(4,128)(4,1)S(1)} %copy-done.55, ...), kind=kOutput, calls=%fused_computation.43 | convolution fusion | flops 4888458240 | bytes 37777408 | tf_op jit(solution)/shard_map/prd,fd->prf/dot_general | solution.py:363
  278.3 10.4 %multiply_reduce_fusion.2 = (f32[768]{0:T(1024)}, f32[2,512]{1,0:T(2,128)S(1)}, f32[768]{0:T(1024)}, f32[2,512,768]{2,1,0:T(8,128)S(1)}) fusion(f32[2,512,768]{2,1,0:T(8,128)} %copy-done, f32[2,512]{1,0:T(2,128)S(1)} %fusion.75, f32[2,512]{1,0:T(2,128)S(1)} %broadcast_multiply_fusion, f32[768]{0:T(1024)S(1)} %reshape.547, ...), kind=kOutput, calls=%fused_computation.114 | convolution fusion | flops 4838126592 | bytes 17323008 | tf_op jit(solution)/shard_map/prf,df->prd/dot_general | solution.py:369
  288.7 8.3 %bitcast_convert_fusion.1 = bf16[768,3072]{1,0:T(8,128)(2,1)} fusion(bf16[2,512,3072]{2,1,0:T(8,128)(2,1)S(1)} %copy-done.63, f32[2,512,768]{2,1,0:T(8,128)S(1)} %copy-done.1, f32[768]{0:T(1024)S(1)} %reshape.548, f32[768]{0:T(1024)S(1)} %reshape.547, f32[2,512]{1,0:T(2,128)S(1)} %fusion.75, f32[2,512]{1,0:T(2,128)S(1)} %broadcast_multiply_fusion), kind=kOutput, calls=%fused_computation.59 | convolution fusion | flops 4838129664 | bytes 14170112 | tf_op jit(solution)/shard_map/prd,prf->df/dot_general | solution.py:368
  305.9 52.9 %while.23 = (s32[]{:T(128)}, bf16[2,512,2304]{1,2,0:T(8,128)(2,1)}, bf16[2,512,768]{1,2,0:T(8,128)(2,1)S(1)}, s32[2,512]{1,0:T(2,128)S(1)}, bf16[2,512,768]{1,2,...) while((s32[]{:T(128)}, bf16[2,512,2304]{1,2,0:T(8,128)(2,1)}, ...), condition=%wide.region_14.15_spmd, body=%wide.region_12.14_spmd.sunk | while | flops 2059921408 | bytes 116045952 | solution.py:383
  314.3 6.5 %multiply_reduce_fusion.7 = (f32[12,512]{1,0:T(8,128)S(1)}, f32[12,512,512]{1,2,0:T(8,128)}) fusion(f32[12,512,512]{1,2,0:T(8,128)S(1)} %fusion.162, f32[12,512]{1,0:T(8,128)S(1)} %dynamic-slice_bitcast_fusion.32, pred[512,512]{0,1:T(8,128)(4,1)S(1)} %broadcast_compare_fusion.5, bf16[512,12,64]{0,2,1:T(8,128)(2,1)S(1)} %bitcast.488, ...), kind=kOutput, calls=%fused_computation.15.clone.1 | convolution fusion | flops 415229952 | bytes 27049984 | tf_op jit(solution)/shard_map/while/body/eval_jaxpr/qhe,khe->hqk/dot_general | solution.py:258
  320.8 7.0 %multiply_convert_fusion.8 = bf16[12,512,512]{1,2,0:T(8,128)(2,1)S(1)} fusion(f32[12,512,512]{1,2,0:T(8,128)} %get-tuple-element.429, f32[12,512,512]{1,2,0:T(8,128)S(1)} %fusion.162, f32[12,512]{1,0:T(8,128)S(1)} %get-tuple-element.430, f32[12,512]{1,0:T(8,128)S(1)} %dynamic-slice_bitcast_fusion.32, pred[512,512]{0,1:T(8,128)(4,1)S(1)} %broadcast_compare_fusion.5), kind=kLoop, calls=%fused_computation.14.clone.1 | loop fusion | flops 15728640 | bytes 31768576 | tf_op jit(solution)/shard_map/while/body/eval_jaxpr/convert_element_type | solution.py:262
  340.4 6.5 %multiply_reduce_fusion.7 = (f32[12,512]{1,0:T(8,128)S(1)}, f32[12,512,512]{1,2,0:T(8,128)}) fusion(f32[12,512,512]{1,2,0:T(8,128)S(1)} %fusion.162, f32[12,512]{1,0:T(8,128)S(1)} %dynamic-slice_bitcast_fusion.32, pred[512,512]{0,1:T(8,128)(4,1)S(1)} %broadcast_compare_fusion.5, bf16[512,12,64]{0,2,1:T(8,128)(2,1)S(1)} %bitcast.488, ...), kind=kOutput, calls=%fused_computation.15.clone.1 | convolution fusion | flops 415229952 | bytes 27049984 | tf_op jit(solution)/shard_map/while/body/eval_jaxpr/qhe,khe->hqk/dot_general | solution.py:258
  346.9 7.0 %multiply_convert_fusion.8 = bf16[12,512,512]{1,2,0:T(8,128)(2,1)S(1)} fusion(f32[12,512,512]{1,2,0:T(8,128)} %get-tuple-element.429, f32[12,512,512]{1,2,0:T(8,128)S(1)} %fusion.162, f32[12,512]{1,0:T(8,128)S(1)} %get-tuple-element.430, f32[12,512]{1,0:T(8,128)S(1)} %dynamic-slice_bitcast_fusion.32, pred[512,512]{0,1:T(8,128)(4,1)S(1)} %broadcast_compare_fusion.5), kind=kLoop, calls=%fused_computation.14.clone.1 | loop fusion | flops 15728640 | bytes 31768576 | tf_op jit(solution)/shard_map/while/body/eval_jaxpr/convert_element_type | solution.py:262
  358.8 10.1 %fusion.87 = (f32[768]{0:T(1024)S(1)}, f32[2,512]{1,0:T(2,128)S(1)}, f32[2,512,768]{2,1,0:T(8,128)}) fusion(f32[768]{0:T(1024)S(1)} %copy-done.48, f32[2,512]{1,0:T(2,128)S(1)} %copy-done.44, bf16[2,512,768]{2,1,0:T(8,128)(2,1)} %param.22, bf16[2,512,2304]{1,2,0:T(8,128)(2,1)} %get-tuple-element.99, bf16[768,768]{1,0:T(8,128)(2,1)} %bitcast.548, ...), kind=kOutput, calls=%fused_computation.358 | convolution fusion | flops 3639212288 | bytes 12990464 | tf_op jit(solution)/shard_map/prf,df->prd/dot_general | solution.py:393
  370.3 6.1 %bitcast_convert_fusion.2 = bf16[768,2304]{1,0:T(8,128)(2,1)} fusion(bf16[2,512,2304]{1,2,0:T(8,128)(2,1)S(1)} %copy-done.10, bf16[2,512,768]{2,1,0:T(8,128)(2,1)S(1)} %copy-done.4, f32[768]{0:T(1024)S(1)} %copy-done.60, f32[768]{0:T(1024)S(1)} %copy-done.48, f32[2,512]{1,0:T(2,128)S(1)} %copy-done.51, f32[2,512]{1,0:T(2,128)S(1)} %copy-done.44), kind=kOutput, calls=%fused_computation.63 | convolution fusion | flops 3630366720 | bytes 9844736 | tf_op jit(solution)/shard_map/prd,prf->df/dot_general | solution.py:386
  376.5 9.7 %reshape.539 = bf16[8,96,4,768]{3,2,1,0:T(4,128)(2,1)} reshape(bf16[768,3072]{1,0:T(8,128)(2,1)} %bitcast_convert_fusion.1) | data formatting | bytes 9437184 | tf_op jit(solution)/shard_map/reshape | solution.py:188
  386.3 3.2 copy.157
  391.5 3.1 reverse_select_fusion.6
  395.0 3.2 fusion.33
  398.3 9.0 %bitcast_convert_fusion = bf16[3072,768]{1,0:T(8,128)(2,1)S(1)} fusion(bf16[2,512,3072]{2,1,0:T(8,128)(2,1)} %get-tuple-element.208, bf16[2,512,768]{2,1,0:T(8,128)(2,1)S(1)} %copy-done.15, f32[768]{0:T(1024)S(1)} %copy-done.58, pred[2,512]{1,0:T(4,128)(4,1)S(1)} %copy-done.56), kind=kOutput, calls=%fused_computation.58 | convolution fusion | flops 4837343232 | bytes 12587008 | tf_op jit(solution)/shard_map/prf,prd->fd/dot_general | solution.py:360
  414.9 3.1 reverse_select_fusion.10
  418.2 13.0 %multiply_reduce_fusion.1 = (f32[768]{0:T(1024)S(1)}, f32[768]{0:T(1024)S(1)}, f32[768]{0:T(1024)S(1)}, f32[2,512,768]{2,1,0:T(8,128)}, bf16[2,512,768]{2,1,0:T(8,128)(2,1)}) fusion(bf16[2,512,768]{2,1,0:T(8,128)(2,1)} %param.39, f32[768]{0:T(1024)S(1)} %reshape.550, pred[2,512]{1,0:T(4,128)(4,1)S(1)} %copy-done.56, ...), kind=kOutput, calls=%fused_computation.112 | convolution fusion | flops 4853068800 | bytes 31500288 | tf_op jit(solution)/shard_map/prf,fd->prd/dot_general | solution.py:351
  442.6 3.8 collective-permute-start.66
  459.5 4.0 collective-permute-done.47
  472.3 3.8 collective-permute-done.39
  481.0 7.3 %collective-permute-done.48 = bf16[1,384,768]{2,1,0:T(8,128)(2,1)S(1)} collective-permute-done((bf16[1,384,768]{2,1,0:T(8,128)(2,1)S(1)}, bf16[1,384,768]{2,1,0:T(8,128)(2,1)S(1)}, u32[]{:S(2)}, u32[]{:S(2)}) %collective-permute-start.48) | collective-permute-done | bytes 589856 | tf_op jit(solution)/shard_map/ppermute | solution.py:36
  490.8 19.3 %collective-permute-done.40 = bf16[1,384,768]{2,1,0:T(8,128)(2,1)S(1)} collective-permute-done((bf16[1,384,768]{2,1,0:T(8,128)(2,1)S(1)}, bf16[1,384,768]{2,1,0:T(8,128)(2,1)S(1)}, u32[]{:S(2)}, u32[]{:S(2)}) %collective-permute-start.40) | collective-permute-done | bytes 589856 | tf_op jit(solution)/shard_map/ppermute | solution.py:36
  516.0 4.5 fusion.55
  530.0 6.5 %collective-permute-start.50 = (bf16[96,768]{1,0:T(8,128)(2,1)}, bf16[96,768]{1,0:T(8,128)(2,1)S(1)}, u32[]{:S(2)}, u32[]{:S(2)}) collective-permute-start(bf16[96,768]{1,0:T(8,128)(2,1)} %get-tuple-element.285), channel_id=1, source_target_pairs={{0,2},{1,3},{2,0},{3,1},{4,6},{5,7},{6,4},{7,5},{8,10},{9,11},{10,... | collective-permute-start | bytes 442376 | tf_op jit(solution)/shard_map/ppermute | solution.py:36
  536.4 3.5 collective-permute-done.42
  540.0 3.8 collective-permute-start.59
  550.7 4.8 collective-permute-done.58
  (513 shorter events, 207.6 us)
Async XLA Ops:
  0.7 24.9 %collective-permute-start.13 = (bf16[96,768]{1,0:T(8,128)(2,1)}, bf16[96,768]{1,0:T(8,128)(2,1)S(1)}, u32[]{:S(2)}, u32[]{:S(2)}) collective-permute-start(bf16[96,768]{1,0:T(8,128)(2,1)} %param.26), channel_id=1, source_target_pairs={{0,2},{1,3},{2,0},{3,1},{4,6},{5,7},{6,4},{7,5},{8,10},{9,11},{10,... | collective-permute-start | bytes 442376 | tf_op jit(solution)/shard_map/ppermute | solution.py:36
  4.8 20.4 %collective-permute-start.12 = (bf16[96,768]{1,0:T(8,128)(2,1)}, bf16[96,768]{1,0:T(8,128)(2,1)S(1)}, u32[]{:S(2)}, u32[]{:S(2)}) collective-permute-start(bf16[96,768]{1,0:T(8,128)(2,1)} %param.26), channel_id=1, source_target_pairs={{0,3},{1,0},{2,1},{3,2},{4,7},{5,4},{6,5},{7,6},{8,11},{9,8},{10,9... | collective-permute-start | bytes 442376 | tf_op jit(solution)/shard_map/ppermute | solution.py:36
  6.1 21.3 %collective-permute-start.14 = (bf16[96,768]{1,0:T(8,128)(2,1)}, bf16[96,768]{1,0:T(8,128)(2,1)S(1)}, u32[]{:S(2)}, u32[]{:S(2)}) collective-permute-start(bf16[96,768]{1,0:T(8,128)(2,1)} %param.26), channel_id=1, source_target_pairs={{0,1},{1,2},{2,3},{3,0},{4,5},{5,6},{6,7},{7,4},{8,9},{9,10},{10,1... | collective-permute-start | bytes 442376 | tf_op jit(solution)/shard_map/ppermute | solution.py:36
  15.3 37.9 %collective-permute-start.2 = (bf16[112,768]{1,0:T(8,128)(2,1)S(1)}, bf16[112,768]{1,0:T(8,128)(2,1)S(1)}, u32[]{:S(2)}, u32[]{:S(2)}) collective-permute-start(bf16[112,768]{1,0:T(8,128)(2,1)S(1)} %fusion.64), channel_id=1, source_target_pairs={{0,1},{1,2},{2,3},{3,0},{4,5},{5,6},{6,7},{7,4},{8,9},{9,10},{10,1... | collective-permute-start | bytes 516104 | tf_op jit(solution)/shard_map/ppermute | solution.py:36
  16.9 36.2 %collective-permute-start.1 = (bf16[112,768]{1,0:T(8,128)(2,1)S(1)}, bf16[112,768]{1,0:T(8,128)(2,1)S(1)}, u32[]{:S(2)}, u32[]{:S(2)}) collective-permute-start(bf16[112,768]{1,0:T(8,128)(2,1)S(1)} %fusion.64), channel_id=1, source_target_pairs={{0,2},{1,3},{2,0},{3,1},{4,6},{5,7},{6,4},{7,5},{8,10},{9,11},{10,... | collective-permute-start | bytes 516104 | tf_op jit(solution)/shard_map/ppermute | solution.py:36
  25.2 27.8 %collective-permute-start = (bf16[112,768]{1,0:T(8,128)(2,1)S(1)}, bf16[112,768]{1,0:T(8,128)(2,1)S(1)}, u32[]{:S(2)}, u32[]{:S(2)}) collective-permute-start(bf16[112,768]{1,0:T(8,128)(2,1)S(1)} %fusion.64), channel_id=1, source_target_pairs={{0,3},{1,0},{2,1},{3,2},{4,7},{5,4},{6,5},{7,6},{8,11},{9,8},{10,9... | collective-permute-start | bytes 516104 | tf_op jit(solution)/shard_map/ppermute | solution.py:36
  25.6 25.5 %collective-permute-start.26 = (bf16[96,768]{1,0:T(8,128)(2,1)S(1)}, bf16[96,768]{1,0:T(8,128)(2,1)S(1)}, u32[]{:S(2)}, u32[]{:S(2)}) collective-permute-start(bf16[96,768]{1,0:T(8,128)(2,1)S(1)} %pad_maximum_fusion.11), channel_id=1, source_target_pairs={{0,1},{1,2},{2,3},{3,0},{4,5},{5,6},{6,7},{7,4},{8,9},{9,10},{10,1... | collective-permute-start | bytes 442376 | tf_op jit(solution)/shard_map/ppermute | solution.py:36
  27.4 12.4 %collective-permute-start.24 = (bf16[96,768]{1,0:T(8,128)(2,1)S(1)}, bf16[96,768]{1,0:T(8,128)(2,1)S(1)}, u32[]{:S(2)}, u32[]{:S(2)}) collective-permute-start(bf16[96,768]{1,0:T(8,128)(2,1)S(1)} %pad_maximum_fusion.11), channel_id=1, source_target_pairs={{0,3},{1,0},{2,1},{3,2},{4,7},{5,4},{6,5},{7,6},{8,11},{9,8},{10,9... | collective-permute-start | bytes 442376 | tf_op jit(solution)/shard_map/ppermute | solution.py:36
  49.6 16.3 %collective-permute-start.18 = (bf16[1,384,768]{2,1,0:T(8,128)(2,1)S(1)}, bf16[1,384,768]{2,1,0:T(8,128)(2,1)}, u32[]{:S(2)}, u32[]{:S(2)}) collective-permute-start(bf16[1,384,768]{2,1,0:T(8,128)(2,1)S(1)} %bitcast.538), channel_id=1, source_target_pairs={{0,16},{4,20},{8,24},{12,28},{16,0},{20,4},{24,8},{28,12},{1,17},{... | collective-permute-start | bytes 1769480 | tf_op jit(solution)/shard_map/ppermute | solution.py:36
  51.1 16.3 %collective-permute-start.16 = (bf16[1,384,768]{2,1,0:T(8,128)(2,1)S(1)}, bf16[1,384,768]{2,1,0:T(8,128)(2,1)S(1)}, u32[]{:S(2)}, u32[]{:S(2)}) collective-permute-start(bf16[1,384,768]{2,1,0:T(8,128)(2,1)S(1)} %bitcast.539), channel_id=1, source_target_pairs={{0,8},{4,12},{8,0},{12,4},{16,24},{20,28},{24,16},{28,20},{1,9},{5... | collective-permute-start | bytes 1769480 | tf_op jit(solution)/shard_map/ppermute | solution.py:36
  53.0 15.1 %collective-permute-start.15 = (bf16[1,384,768]{2,1,0:T(8,128)(2,1)S(1)}, bf16[1,384,768]{2,1,0:T(8,128)(2,1)S(1)}, u32[]{:S(2)}, u32[]{:S(2)}) collective-permute-start(bf16[1,384,768]{2,1,0:T(8,128)(2,1)S(1)} %bitcast.540), channel_id=1, source_target_pairs={{0,4},{4,0},{8,12},{12,8},{16,20},{20,16},{24,28},{28,24},{1,5},{5... | collective-permute-start | bytes 1769480 | tf_op jit(solution)/shard_map/ppermute | solution.py:36
  55.0 23.6 %collective-permute-start.30 = (bf16[1,384,768]{2,1,0:T(8,128)(2,1)}, bf16[1,384,768]{2,1,0:T(8,128)(2,1)}, u32[]{:S(2)}, u32[]{:S(2)}) collective-permute-start(bf16[1,384,768]{2,1,0:T(8,128)(2,1)} %fusion.127), channel_id=1, source_target_pairs={{0,16},{4,20},{8,24},{12,28},{16,0},{20,4},{24,8},{28,12},{1,17},{... | collective-permute-start | bytes 1769480 | tf_op jit(solution)/shard_map/ppermute | solution.py:36
  55.5 25.2 %collective-permute-start.28 = (bf16[1,384,768]{2,1,0:T(8,128)(2,1)}, bf16[1,384,768]{2,1,0:T(8,128)(2,1)}, u32[]{:S(2)}, u32[]{:S(2)}) collective-permute-start(bf16[1,384,768]{2,1,0:T(8,128)(2,1)} %fusion.127), channel_id=1, source_target_pairs={{0,8},{4,12},{8,0},{12,4},{16,24},{20,28},{24,16},{28,20},{1,9},{5... | collective-permute-start | bytes 1769480 | tf_op jit(solution)/shard_map/ppermute | solution.py:36
  65.9 16.4 %collective-permute-start.27 = (bf16[1,384,768]{2,1,0:T(8,128)(2,1)}, bf16[1,384,768]{2,1,0:T(8,128)(2,1)}, u32[]{:S(2)}, u32[]{:S(2)}) collective-permute-start(bf16[1,384,768]{2,1,0:T(8,128)(2,1)} %fusion.127), channel_id=1, source_target_pairs={{0,4},{4,0},{8,12},{12,8},{16,20},{20,16},{24,28},{28,24},{1,5},{5... | collective-permute-start | bytes 1769480 | tf_op jit(solution)/shard_map/ppermute | solution.py:36
  67.5 24.3 %collective-permute-start.6 = (bf16[1,400,768]{2,1,0:T(8,128)(2,1)S(1)}, bf16[1,400,768]{2,1,0:T(8,128)(2,1)}, u32[]{:S(2)}, u32[]{:S(2)}) collective-permute-start(bf16[1,400,768]{2,1,0:T(8,128)(2,1)S(1)} %bitcast.554), channel_id=1, source_target_pairs={{0,16},{4,20},{8,24},{12,28},{16,0},{20,4},{24,8},{28,12},{1,17},{... | collective-permute-start | bytes 1843208 | tf_op jit(solution)/shard_map/ppermute | solution.py:36
  68.1 27.4 %collective-permute-start.4 = (bf16[1,400,768]{2,1,0:T(8,128)(2,1)S(1)}, bf16[1,400,768]{2,1,0:T(8,128)(2,1)S(1)}, u32[]{:S(2)}, u32[]{:S(2)}) collective-permute-start(bf16[1,400,768]{2,1,0:T(8,128)(2,1)S(1)} %bitcast.555), channel_id=1, source_target_pairs={{0,8},{4,12},{8,0},{12,4},{16,24},{20,28},{24,16},{28,20},{1,9},{5... | collective-permute-start | bytes 1843208 | tf_op jit(solution)/shard_map/ppermute | solution.py:36
  78.5 17.1 %collective-permute-start.3 = (bf16[1,400,768]{2,1,0:T(8,128)(2,1)S(1)}, bf16[1,400,768]{2,1,0:T(8,128)(2,1)S(1)}, u32[]{:S(2)}, u32[]{:S(2)}) collective-permute-start(bf16[1,400,768]{2,1,0:T(8,128)(2,1)S(1)} %bitcast.556), channel_id=1, source_target_pairs={{0,4},{4,0},{8,12},{12,8},{16,20},{20,16},{24,28},{28,24},{1,5},{5... | collective-permute-start | bytes 1843208 | tf_op jit(solution)/shard_map/ppermute | solution.py:36
  80.7 18.8 %collective-permute-start.21 = (bf16[1,192,768]{2,1,0:T(8,128)(2,1)S(1)}, bf16[1,192,768]{2,1,0:T(8,128)(2,1)S(1)}, u32[]{:S(2)}, u32[]{:S(2)}) collective-permute-start(bf16[1,192,768]{2,1,0:T(8,128)(2,1)S(1)} %slice.574), channel_id=1, source_target_pairs={{0,8},{4,12},{8,0},{12,4},{16,24},{20,28},{24,16},{28,20},{1,9},{5... | collective-permute-start | bytes 884744 | tf_op jit(solution)/shard_map/ppermute | solution.py:36
  82.3 17.5 %collective-permute-start.20 = (bf16[1,192,768]{2,1,0:T(8,128)(2,1)S(1)}, bf16[1,192,768]{2,1,0:T(8,128)(2,1)S(1)}, u32[]{:S(2)}, u32[]{:S(2)}) collective-permute-start(bf16[1,192,768]{2,1,0:T(8,128)(2,1)S(1)} %slice.573), channel_id=1, source_target_pairs={{0,16},{4,20},{8,24},{12,28},{16,0},{20,4},{24,8},{28,12},{1,17},{... | collective-permute-start | bytes 884744 | tf_op jit(solution)/shard_map/ppermute | solution.py:36
  91.7 14.3 %collective-permute-start.33 = (bf16[1,192,768]{2,1,0:T(8,128)(2,1)S(1)}, bf16[1,192,768]{2,1,0:T(8,128)(2,1)}, u32[]{:S(2)}, u32[]{:S(2)}) collective-permute-start(bf16[1,192,768]{2,1,0:T(8,128)(2,1)S(1)} %slice.577), channel_id=1, source_target_pairs={{0,8},{4,12},{8,0},{12,4},{16,24},{20,28},{24,16},{28,20},{1,9},{5... | collective-permute-start | bytes 884744 | tf_op jit(solution)/shard_map/ppermute | solution.py:36
  95.6 17.7 %collective-permute-start.19 = (bf16[1,384,768]{2,1,0:T(8,128)(2,1)}, bf16[1,384,768]{2,1,0:T(8,128)(2,1)S(1)}, u32[]{:S(2)}, u32[]{:S(2)}) collective-permute-start(bf16[1,384,768]{2,1,0:T(8,128)(2,1)} %collective-permute-done.18), channel_id=1, source_target_pairs={{0,4},{4,0},{8,12},{12,8},{16,20},{20,16},{24,28},{28,24},{1,5},{5... | collective-permute-start | bytes 1769480 | tf_op jit(solution)/shard_map/ppermute | solution.py:36
  99.6 15.0 %collective-permute-start.17 = (bf16[1,384,768]{2,1,0:T(8,128)(2,1)S(1)}, bf16[1,384,768]{2,1,0:T(8,128)(2,1)S(1)}, u32[]{:S(2)}, u32[]{:S(2)}) collective-permute-start(bf16[1,384,768]{2,1,0:T(8,128)(2,1)S(1)} %copy-done.19), channel_id=1, source_target_pairs={{0,4},{4,0},{8,12},{12,8},{16,20},{20,16},{24,28},{28,24},{1,5},{5... | collective-permute-start | bytes 1769480 | tf_op jit(solution)/shard_map/ppermute | solution.py:36
  99.8 12.9 %collective-permute-start.9 = (bf16[1,208,768]{2,1,0:T(8,128)(2,1)S(1)}, bf16[1,208,768]{2,1,0:T(8,128)(2,1)S(1)}, u32[]{:S(2)}, u32[]{:S(2)}) collective-permute-start(bf16[1,208,768]{2,1,0:T(8,128)(2,1)S(1)} %slice.555), channel_id=1, source_target_pairs={{0,8},{4,12},{8,0},{12,4},{16,24},{20,28},{24,16},{28,20},{1,9},{5... | collective-permute-start | bytes 958472 | tf_op jit(solution)/shard_map/ppermute | solution.py:36
  106.7 29.8 %collective-permute-start.31 = (bf16[1,384,768]{2,1,0:T(8,128)(2,1)}, bf16[1,384,768]{2,1,0:T(8,128)(2,1)}, u32[]{:S(2)}, u32[]{:S(2)}) collective-permute-start(bf16[1,384,768]{2,1,0:T(8,128)(2,1)} %collective-permute-done.30), channel_id=1, source_target_pairs={{0,4},{4,0},{8,12},{12,8},{16,20},{20,16},{24,28},{28,24},{1,5},{5... | collective-permute-start | bytes 1769480 | tf_op jit(solution)/shard_map/ppermute | solution.py:36
  113.3 24.8 %collective-permute-start.29 = (bf16[1,384,768]{2,1,0:T(8,128)(2,1)}, bf16[1,384,768]{2,1,0:T(8,128)(2,1)}, u32[]{:S(2)}, u32[]{:S(2)}) collective-permute-start(bf16[1,384,768]{2,1,0:T(8,128)(2,1)} %collective-permute-done.28), channel_id=1, source_target_pairs={{0,4},{4,0},{8,12},{12,8},{16,20},{20,16},{24,28},{28,24},{1,5},{5... | collective-permute-start | bytes 1769480 | tf_op jit(solution)/shard_map/ppermute | solution.py:36
  114.6 30.5 %collective-permute-start.7 = (bf16[1,400,768]{2,1,0:T(8,128)(2,1)}, bf16[1,400,768]{2,1,0:T(8,128)(2,1)}, u32[]{:S(2)}, u32[]{:S(2)}) collective-permute-start(bf16[1,400,768]{2,1,0:T(8,128)(2,1)} %collective-permute-done.6), channel_id=1, source_target_pairs={{0,4},{4,0},{8,12},{12,8},{16,20},{20,16},{24,28},{28,24},{1,5},{5... | collective-permute-start | bytes 1843208 | tf_op jit(solution)/shard_map/ppermute | solution.py:36
  115.2 19.6 %collective-permute-start.35 = (bf16[1,192,768]{2,1,0:T(8,128)(2,1)}, bf16[1,192,768]{2,1,0:T(8,128)(2,1)}, u32[]{:S(2)}, u32[]{:S(2)}) collective-permute-start(bf16[1,192,768]{2,1,0:T(8,128)(2,1)} %collective-permute-done.33), channel_id=1, source_target_pairs={{0,4},{4,0},{8,12},{12,8},{16,20},{20,16},{24,28},{28,24},{1,5},{5... | collective-permute-start | bytes 884744 | tf_op jit(solution)/shard_map/ppermute | solution.py:36
  115.4 19.6 %collective-permute-start.34 = (bf16[1,192,768]{2,1,0:T(8,128)(2,1)}, bf16[1,192,768]{2,1,0:T(8,128)(2,1)}, u32[]{:S(2)}, u32[]{:S(2)}) collective-permute-start(bf16[1,192,768]{2,1,0:T(8,128)(2,1)} %collective-permute-done.32), channel_id=1, source_target_pairs={{0,4},{4,0},{8,12},{12,8},{16,20},{20,16},{24,28},{28,24},{1,5},{5... | collective-permute-start | bytes 884744 | tf_op jit(solution)/shard_map/ppermute | solution.py:36
  134.9 11.6 %collective-permute-start.5 = (bf16[1,400,768]{2,1,0:T(8,128)(2,1)}, bf16[1,400,768]{2,1,0:T(8,128)(2,1)S(1)}, u32[]{:S(2)}, u32[]{:S(2)}) collective-permute-start(bf16[1,400,768]{2,1,0:T(8,128)(2,1)} %copy-done.16), channel_id=1, source_target_pairs={{0,4},{4,0},{8,12},{12,8},{16,20},{20,16},{24,28},{28,24},{1,5},{5... | collective-permute-start | bytes 1843208 | tf_op jit(solution)/shard_map/ppermute | solution.py:36
  135.0 11.7 %collective-permute-start.10 = (bf16[1,192,768]{2,1,0:T(8,128)(2,1)}, bf16[1,192,768]{2,1,0:T(8,128)(2,1)S(1)}, u32[]{:S(2)}, u32[]{:S(2)}) collective-permute-start(bf16[1,192,768]{2,1,0:T(8,128)(2,1)} %copy-done.38), channel_id=1, source_target_pairs={{0,4},{4,0},{8,12},{12,8},{16,20},{20,16},{24,28},{28,24},{1,5},{5... | collective-permute-start | bytes 884744 | tf_op jit(solution)/shard_map/ppermute | solution.py:36
  434.6 17.5 %collective-permute-start.44 = (bf16[1,4,384,768]{3,2,1,0:T(8,128)(2,1)S(1)}, bf16[1,4,384,768]{3,2,1,0:T(8,128)(2,1)S(1)}, u32[]{:S(2)}, u32[]{:S(2)}) collective-permute-start(bf16[1,4,384,768]{3,2,1,0:T(8,128)(2,1)S(1)} %slice_bitcast_fusion.2), channel_id=1, source_target_pairs={{0,4},{4,0},{8,12},{12,8},{16,20},{20,16},{24,28},{28,24},{1,5},{5... | collective-permute-start | bytes 7077896 | tf_op jit(solution)/shard_map/ppermute | solution.py:36
  437.1 18.0 %collective-permute-start.52 = (bf16[1,4,384,768]{3,2,1,0:T(8,128)(2,1)S(1)}, bf16[1,4,384,768]{3,2,1,0:T(8,128)(2,1)S(1)}, u32[]{:S(2)}, u32[]{:S(2)}) collective-permute-start(bf16[1,4,384,768]{3,2,1,0:T(8,128)(2,1)S(1)} %slice_bitcast_fusion), channel_id=1, source_target_pairs={{0,4},{4,0},{8,12},{12,8},{16,20},{20,16},{24,28},{28,24},{1,5},{5... | collective-permute-start | bytes 7077896 | tf_op jit(solution)/shard_map/ppermute | solution.py:36
  453.0 12.1 %collective-permute-start.45 = (bf16[1,192,768]{2,1,0:T(8,128)(2,1)S(1)}, bf16[1,192,768]{2,1,0:T(8,128)(2,1)S(1)}, u32[]{:S(2)}, u32[]{:S(2)}) collective-permute-start(bf16[1,192,768]{2,1,0:T(8,128)(2,1)S(1)} %get-tuple-element.286), channel_id=1, source_target_pairs={{0,16},{4,20},{8,24},{12,28},{16,0},{20,4},{24,8},{28,12},{1,17},{... | collective-permute-start | bytes 884744 | tf_op jit(solution)/shard_map/ppermute | solution.py:36
  456.0 22.5 %collective-permute-start.53 = (bf16[1,192,768]{2,1,0:T(8,128)(2,1)S(1)}, bf16[1,192,768]{2,1,0:T(8,128)(2,1)S(1)}, u32[]{:S(2)}, u32[]{:S(2)}) collective-permute-start(bf16[1,192,768]{2,1,0:T(8,128)(2,1)S(1)} %get-tuple-element.281), channel_id=1, source_target_pairs={{0,16},{4,20},{8,24},{12,28},{16,0},{20,4},{24,8},{28,12},{1,17},{... | collective-permute-start | bytes 884744 | tf_op jit(solution)/shard_map/ppermute | solution.py:36
  457.6 12.3 %collective-permute-start.55 = (bf16[1,192,768]{2,1,0:T(8,128)(2,1)S(1)}, bf16[1,192,768]{2,1,0:T(8,128)(2,1)S(1)}, u32[]{:S(2)}, u32[]{:S(2)}) collective-permute-start(bf16[1,192,768]{2,1,0:T(8,128)(2,1)S(1)} %get-tuple-element.282), channel_id=1, source_target_pairs={{0,8},{4,12},{8,0},{12,4},{16,24},{20,28},{24,16},{28,20},{1,9},{5... | collective-permute-start | bytes 884744 | tf_op jit(solution)/shard_map/ppermute | solution.py:36
  459.0 18.9 %collective-permute-start.37 = (bf16[1,192,768]{2,1,0:T(8,128)(2,1)S(1)}, bf16[1,192,768]{2,1,0:T(8,128)(2,1)S(1)}, u32[]{:S(2)}, u32[]{:S(2)}) collective-permute-start(bf16[1,192,768]{2,1,0:T(8,128)(2,1)S(1)} %get-tuple-element.292), channel_id=1, source_target_pairs={{0,16},{4,20},{8,24},{12,28},{16,0},{20,4},{24,8},{28,12},{1,17},{... | collective-permute-start | bytes 884744 | tf_op jit(solution)/shard_map/ppermute | solution.py:36
  463.5 12.6 %collective-permute-start.39 = (bf16[1,192,768]{2,1,0:T(8,128)(2,1)S(1)}, bf16[1,192,768]{2,1,0:T(8,128)(2,1)S(1)}, u32[]{:S(2)}, u32[]{:S(2)}) collective-permute-start(bf16[1,192,768]{2,1,0:T(8,128)(2,1)S(1)} %get-tuple-element.293), channel_id=1, source_target_pairs={{0,8},{4,12},{8,0},{12,4},{16,24},{20,28},{24,16},{28,20},{1,9},{5... | collective-permute-start | bytes 884744 | tf_op jit(solution)/shard_map/ppermute | solution.py:36
  465.2 23.1 %collective-permute-start.48 = (bf16[1,384,768]{2,1,0:T(8,128)(2,1)S(1)}, bf16[1,384,768]{2,1,0:T(8,128)(2,1)S(1)}, u32[]{:S(2)}, u32[]{:S(2)}) collective-permute-start(bf16[1,384,768]{2,1,0:T(8,128)(2,1)S(1)} %pad_maximum_fusion.4), channel_id=1, source_target_pairs={{0,16},{4,20},{8,24},{12,28},{16,0},{20,4},{24,8},{28,12},{1,17},{... | collective-permute-start | bytes 1769480 | tf_op jit(solution)/shard_map/ppermute | solution.py:36
  469.8 20.0 %collective-permute-start.46 = (bf16[1,384,768]{2,1,0:T(8,128)(2,1)S(1)}, bf16[1,384,768]{2,1,0:T(8,128)(2,1)S(1)}, u32[]{:S(2)}, u32[]{:S(2)}) collective-permute-start(bf16[1,384,768]{2,1,0:T(8,128)(2,1)S(1)} %pad_maximum_fusion.3), channel_id=1, source_target_pairs={{0,8},{4,12},{8,0},{12,4},{16,24},{20,28},{24,16},{28,20},{1,9},{5... | collective-permute-start | bytes 1769480 | tf_op jit(solution)/shard_map/ppermute | solution.py:36
  476.1 48.7 %collective-permute-start.56 = (bf16[1,384,768]{2,1,0:T(8,128)(2,1)}, bf16[1,384,768]{2,1,0:T(8,128)(2,1)}, u32[]{:S(2)}, u32[]{:S(2)}) collective-permute-start(bf16[1,384,768]{2,1,0:T(8,128)(2,1)} %pad_maximum_fusion.6), channel_id=1, source_target_pairs={{0,16},{4,20},{8,24},{12,28},{16,0},{20,4},{24,8},{28,12},{1,17},{... | collective-permute-start | bytes 1769480 | tf_op jit(solution)/shard_map/ppermute | solution.py:36
  477.9 32.3 %collective-permute-start.40 = (bf16[1,384,768]{2,1,0:T(8,128)(2,1)S(1)}, bf16[1,384,768]{2,1,0:T(8,128)(2,1)S(1)}, u32[]{:S(2)}, u32[]{:S(2)}) collective-permute-start(bf16[1,384,768]{2,1,0:T(8,128)(2,1)S(1)} %pad_maximum_fusion.2), channel_id=1, source_target_pairs={{0,16},{4,20},{8,24},{12,28},{16,0},{20,4},{24,8},{28,12},{1,17},{... | collective-permute-start | bytes 1769480 | tf_op jit(solution)/shard_map/ppermute | solution.py:36
  478.5 32.4 %collective-permute-start.38 = (bf16[1,384,768]{2,1,0:T(8,128)(2,1)S(1)}, bf16[1,384,768]{2,1,0:T(8,128)(2,1)S(1)}, u32[]{:S(2)}, u32[]{:S(2)}) collective-permute-start(bf16[1,384,768]{2,1,0:T(8,128)(2,1)S(1)} %pad_maximum_fusion.1), channel_id=1, source_target_pairs={{0,8},{4,12},{8,0},{12,4},{16,24},{20,28},{24,16},{28,20},{1,9},{5... | collective-permute-start | bytes 1769480 | tf_op jit(solution)/shard_map/ppermute | solution.py:36
  488.3 36.9 %collective-permute-start.54 = (bf16[1,384,768]{2,1,0:T(8,128)(2,1)}, bf16[1,384,768]{2,1,0:T(8,128)(2,1)}, u32[]{:S(2)}, u32[]{:S(2)}) collective-permute-start(bf16[1,384,768]{2,1,0:T(8,128)(2,1)} %pad_maximum_fusion.5), channel_id=1, source_target_pairs={{0,8},{4,12},{8,0},{12,4},{16,24},{20,28},{24,16},{28,20},{1,9},{5... | collective-permute-start | bytes 1769480 | tf_op jit(solution)/shard_map/ppermute | solution.py:36
  490.8 55.6 %collective-permute-start.49 = (bf16[96,768]{1,0:T(8,128)(2,1)}, bf16[96,768]{1,0:T(8,128)(2,1)}, u32[]{:S(2)}, u32[]{:S(2)}) collective-permute-start(bf16[96,768]{1,0:T(8,128)(2,1)} %get-tuple-element.283), channel_id=1, source_target_pairs={{0,1},{1,2},{2,3},{3,0},{4,5},{5,6},{6,7},{7,4},{8,9},{9,10},{10,1... | collective-permute-start | bytes 442376 | tf_op jit(solution)/shard_map/ppermute | solution.py:36
  510.2 36.3 %collective-permute-start.51 = (bf16[96,768]{1,0:T(8,128)(2,1)}, bf16[96,768]{1,0:T(8,128)(2,1)}, u32[]{:S(2)}, u32[]{:S(2)}) collective-permute-start(bf16[96,768]{1,0:T(8,128)(2,1)} %get-tuple-element.284), channel_id=1, source_target_pairs={{0,3},{1,0},{2,1},{3,2},{4,7},{5,4},{6,5},{7,6},{8,11},{9,8},{10,9... | collective-permute-start | bytes 442376 | tf_op jit(solution)/shard_map/ppermute | solution.py:36
  524.8 15.1 %collective-permute-start.42 = (bf16[96,768]{1,0:T(8,128)(2,1)}, bf16[96,768]{1,0:T(8,128)(2,1)}, u32[]{:S(2)}, u32[]{:S(2)}) collective-permute-start(bf16[96,768]{1,0:T(8,128)(2,1)} %bitcast.423), channel_id=1, source_target_pairs={{0,2},{1,3},{2,0},{3,1},{4,6},{5,7},{6,4},{7,5},{8,10},{9,11},{10,... | collective-permute-start | bytes 442376 | tf_op jit(solution)/shard_map/ppermute | solution.py:36
  525.3 14.7 %collective-permute-start.41 = (bf16[96,768]{1,0:T(8,128)(2,1)}, bf16[96,768]{1,0:T(8,128)(2,1)}, u32[]{:S(2)}, u32[]{:S(2)}) collective-permute-start(bf16[96,768]{1,0:T(8,128)(2,1)} %bitcast.424), channel_id=1, source_target_pairs={{0,1},{1,2},{2,3},{3,0},{4,5},{5,6},{6,7},{7,4},{8,9},{9,10},{10,1... | collective-permute-start | bytes 442376 | tf_op jit(solution)/shard_map/ppermute | solution.py:36
  530.0 19.0 %collective-permute-start.50 = (bf16[96,768]{1,0:T(8,128)(2,1)}, bf16[96,768]{1,0:T(8,128)(2,1)S(1)}, u32[]{:S(2)}, u32[]{:S(2)}) collective-permute-start(bf16[96,768]{1,0:T(8,128)(2,1)} %get-tuple-element.285), channel_id=1, source_target_pairs={{0,2},{1,3},{2,0},{3,1},{4,6},{5,7},{6,4},{7,5},{8,10},{9,11},{10,... | collective-permute-start | bytes 442376 | tf_op jit(solution)/shard_map/ppermute | solution.py:36
  (93 other events, 1107.0 us)

commit v2 on v1

v2 whole, which is shorter than its diff:
```python
import functools
import math

import jax
import jax.numpy as jnp
from jax import lax
from jax.experimental import pallas as pl
from jax.experimental.pallas import tpu as pltpu
from jax.sharding import PartitionSpec as P

HD = 64
LN_EPSILON = 1e-06
MASKED = -1e30
TILE = 256
F32 = jnp.float32
BF16 = jnp.bfloat16
MIB = 1 << 20


def exchange(value, axis_name, partner):
    size = lax.axis_size(axis_name)
    return lax.ppermute(value, axis_name, [(i, partner(i) % size) for i in range(size)])


def cross(value, bit):
    return exchange(value, "wide", lambda i: i ^ (1 << bit))


def shift(value, step):
    return exchange(value, "narrow", lambda i: i + step)


def wide_bits():
    return lax.axis_size("wide").bit_length() - 1


def by_origin(pieces):
    size = len(pieces)
    backward = jnp.stack(pieces[::-1])
    twice = jnp.concatenate([backward, backward])
    return lax.dynamic_slice_in_dim(twice, size - 1 - lax.axis_index("narrow"), size)


def flip_own(stacked):
    here = lax.axis_index("wide")
    size = stacked.shape[0]
    for bit in range(size.bit_length() - 1):
        halves = stacked.reshape((size >> (bit + 1), 2, 1 << bit) + stacked.shape[1:])
        halves = jnp.where((here >> bit) & 1, halves[:, ::-1], halves)
        stacked = halves.reshape(stacked.shape)
    return stacked


def after(value, *others):
    return lax.optimization_barrier((value, others))[0]


def beside(run, value, sends, moves):
    value, sends = lax.optimization_barrier((value, sends))
    moved = [move(send) for move, send in zip(moves, sends, strict=True)]
    return lax.optimization_barrier((run(value), moved))


def planes():
    return [lambda v: cross(v, 1), lambda v: cross(v, 2)]


def corners():
    return [lambda v: cross(v, 2), lambda v: cross(v, 1)]


def shifts(layers):
    return [lambda v, step=step: shift(v, step) for step in range(1, layers)]


def double(block):
    held = block[None]
    for bit in range(3, wide_bits()):
        held = jnp.concatenate([held, cross(held, bit)])
    return held


def side_by_side(stacked):
    return jnp.concatenate([stacked[i] for i in range(stacked.shape[0])], axis=1)


def direct():
    return lax.axis_size("wide") == 8


def matrices(planes, cores, parts):
    unit = planes[0].shape[1] // parts
    if not direct():
        other = [*jnp.split(cores[0], 3), cores[1]]
        stacked = jnp.stack([jnp.stack(pair, axis=1) for pair in zip(planes, other)], axis=1)
        stacked = flip_own(stacked.reshape((-1,) + planes[0].shape[1:]))
        stacked = stacked.reshape(stacked.shape[0], parts, unit, -1)
        arrays = [stacked[:, m].reshape(-1, stacked.shape[3]) for m in range(parts)]
        return arrays, [[(m, 0, 0, None, unit)] for m in range(parts)]
    spots = [(0, 0, 0), (1, 0, 2), (2, 0, 4), (3, 0, 6), (4, 0, 1), (4, 1, 3), (4, 2, 5), (5, 0, 7)]
    plans = [[(at, index, m * unit, rel, unit) for at, index, rel in spots] for m in range(parts)]
    return [*planes, *cores], plans


def copies(place, refs, plan, target, sems, first):
    made = []
    for at, index, row, rel, unit in plan:
        sem = sems.at[first + len(made)]
        if rel is None:
            made.append(pltpu.make_async_copy(refs[at], target, sem))
        else:
            start = pl.multiple_of((place ^ rel) * unit, 16)
            source = refs[at].at[index, pl.ds(row, unit)]
            made.append(pltpu.make_async_copy(source, target.at[pl.ds(start, unit)], sem))
    return made


def start_all(made):
    for copy in made:
        copy.start()


def wait_all(made):
    for copy in made:
        copy.wait()


def dot(left, right):
    return lax.dot_general(left, right, (((1,), (0,)), ((), ())), preferred_element_type=F32)


def dot_nt(left, right):
    return lax.dot_general(left, right, (((1,), (1,)), ((), ())), preferred_element_type=F32)


def centred_rows(values):
    row_mean = jnp.mean(values, axis=-1, keepdims=True)
    centred = values - row_mean
    row_var = jnp.mean(centred * centred, axis=-1, keepdims=True)
    inverse = lax.rsqrt(row_var + LN_EPSILON)
    return centred * inverse, inverse


def norm_back(grad, unit_rows, inverse, gain):
    scaled = grad * gain
    mean_one = jnp.mean(scaled, axis=-1, keepdims=True)
    mean_two = jnp.mean(scaled * unit_rows, axis=-1, keepdims=True)
    return (scaled - mean_one - unit_rows * mean_two) * inverse


def row_sum(values):
    return jnp.sum(values, axis=0, keepdims=True)


def gelu_pair(values):
    size = jnp.abs(values) * math.sqrt(0.5)
    bell = jnp.exp(values * values * -0.5)
    step = 1.0 / (1.0 + 0.3275911 * size)
    series = step * (-1.453152027 + step * 1.061405429) + 1.421413741
    series = step * (0.254829592 + step * (-0.284496736 + step * series))
    tail = 0.5 * series * bell
    share = jnp.where(values >= 0, 1.0 - tail, tail)
    return values * share, share + values * bell * (1.0 / math.sqrt(2.0 * math.pi))


ANY = pl.BlockSpec(memory_space=pl.ANY)
SMEM = pl.BlockSpec(memory_space=pltpu.SMEM)


def whole(shape):
    return pl.BlockSpec(shape, lambda *_: (0,) * len(shape))


def tile_of(columns):
    return pl.BlockSpec((TILE, columns), lambda i: (i, 0))


def cost(flops, moved, exps=0):
    return pl.CostEstimate(flops=flops, bytes_accessed=moved, transcendentals=exps)


def params(mib, dims=1):
    return pltpu.CompilerParams(
        vmem_limit_bytes=mib * MIB, dimension_semantics=("arbitrary",) * dims
    )


LN1_G, LN1_B, Q_B, V_B, OUT_B, ATTN_S, LN2_G, LN2_B, DOWN_B, MLP_S, UP_B = range(11)


def vector(table, row):
    return table[row : row + 1, :]


def project_kernel(plans, place, rows, table, *refs):
    count = len(refs) - 4 - 2
    sources, (normed, query, key, value, weights, sems) = refs[:count], refs[count:]
    made, first = [], 0
    for m in range(3):
        made.append(copies(place[0], sources, plans[m], weights.at[m], sems, first))
        first += len(plans[m])

    @pl.when(pl.program_id(0) == 0)
    def _():
        for group in made:
            start_all(group)

    unit_rows, _ = centred_rows(rows[...].astype(F32))
    low = (unit_rows * vector(table, LN1_G) + vector(table, LN1_B)).astype(BF16)
    normed[...] = low

    @pl.when(pl.program_id(0) == 0)
    def _():
        for group in made:
            wait_all(group)

    query[...] = ((dot(low, weights[0]) + vector(table, Q_B)) * 0.125).astype(BF16)
    key[...] = dot(low, weights[1]).astype(BF16)
    value[...] = (dot(low, weights[2]) + vector(table, V_B)).astype(BF16)


def project(place, rows, table, group):
    arrays, plans = group
    count, width = rows.shape
    return pl.pallas_call(
        functools.partial(project_kernel, plans),
        grid=(count // TILE,),
        in_specs=[SMEM, tile_of(width), whole(table.shape)] + [ANY] * len(arrays),
        out_specs=[tile_of(width)] * 4,
        out_shape=[jax.ShapeDtypeStruct(rows.shape, BF16)] * 4,
        scratch_shapes=[
            pltpu.VMEM((3, width, width), BF16),
            pltpu.SemaphoreType.DMA((sum(len(p) for p in plans[:3]),)),
        ],
        compiler_params=params(60),
        cost_estimate=cost(6 * count * width * width, 14 * count * width),
        name="project",
    )(place, rows, table, *arrays)


def segments(lengths, pack, position):
    end, segment = 0, jnp.zeros_like(position)
    for slot in range(lengths.shape[1] - 1):
        end = end + lengths[pack, slot]
        segment = segment + (position >= end).astype(jnp.int32)
    return jnp.where(position < end, segment, lengths.shape[1] + position)


def same_segment(lengths, pack, rows):
    down = lax.broadcasted_iota(jnp.int32, (rows, 128), 0)
    along = lax.broadcasted_iota(jnp.int32, (1, rows), 1)
    column = segments(lengths, pack, down)
    row = segments(lengths, pack, along)
    return jnp.concatenate([column] * (rows // 128), axis=1) == row


def head_lanes(shape, head):
    lane = lax.broadcasted_iota(jnp.int32, shape, 1)
    return (lane < HD) if head == 0 else (lane >= HD)


def only(values, head):
    return jnp.where(head_lanes(values.shape, head), values, jnp.zeros_like(values))


def attend_kernel(pack, lengths, query, key, value, *refs):
    attended, log_total = refs[-2:]
    rows = query.shape[0]
    same = same_segment(lengths, pack, rows)
    flat = jnp.transpose(value[...].astype(F32)).astype(BF16)
    mixed = []
    for head in range(2):
        scores = dot_nt(key[...], only(query[...], head))
        scores = jnp.where(same, scores, MASKED)
        top = jnp.max(scores, axis=0, keepdims=True)
        powers = jnp.exp(scores - top)
        total = jnp.sum(powers, axis=0, keepdims=True)
        weights = (powers * (1.0 / total)).astype(BF16)
        mixed.append(dot(flat[head * HD : (head + 1) * HD], weights))
        log_total[0, 0, head : head + 1, :] = top + jnp.log(total)
    attended[...] = jnp.transpose(jnp.concatenate(mixed, axis=0)).astype(BF16)


def pair_block(rows, pack):
    return pl.BlockSpec((rows, 2 * HD), lambda h: (pack, h))


def log_block(rows, pack):
    return pl.BlockSpec((1, 1, 2, rows), lambda h: (pack, h, 0, 0))


def attend(lengths, query, key, value, pack, earlier=()):
    packs = lengths.shape[0]
    count, width = query.shape
    rows, pairs = count // packs, width // (2 * HD)
    return pl.pallas_call(
        functools.partial(attend_kernel, pack),
        grid=(pairs,),
        in_specs=[SMEM] + [pair_block(rows, pack)] * 3 + [ANY] * len(earlier),
        out_specs=[pair_block(rows, pack), log_block(rows, pack)],
        out_shape=[
            jax.ShapeDtypeStruct(query.shape, BF16),
            jax.ShapeDtypeStruct((packs, pairs, 2, rows), F32),
        ],
        input_output_aliases={4 + i: i for i in range(len(earlier))},
        compiler_params=params(60),
        cost_estimate=cost(16 * rows * rows * width, 8 * rows * width, 12 * rows * rows),
        name="attend",
    )(lengths, query, key, value, *earlier)


def attend_back_kernel(pack, lengths, query, key, value, grad, log_total, *refs):
    grad_q, grad_k, grad_v = refs[-3:]
    rows = query.shape[0]
    same = same_segment(lengths, pack, rows)
    flat_key = jnp.transpose(key[...].astype(F32)).astype(BF16)
    by_query, by_key, by_value = [], [], []
    for head in range(2):
        scores = dot_nt(key[...], only(query[...], head))
        probs = jnp.exp(scores - log_total[0, 0, head : head + 1, :])
        probs = jnp.where(same, probs, 0.0)
        by_value.append(dot(probs.astype(BF16), grad[...]))
        grad_probs = dot_nt(value[...], only(grad[...], head))
        centre = jnp.sum(grad_probs * probs, axis=0, keepdims=True)
        grad_scores = (probs * (grad_probs - centre)).astype(BF16)
        by_key.append(dot(grad_scores, query[...]))
        by_query.append(dot(flat_key[head * HD : (head + 1) * HD], grad_scores))
    lanes = head_lanes(by_key[0].shape, 0)
    grad_k[...] = jnp.where(lanes, by_key[0], by_key[1]).astype(BF16)
    grad_v[...] = jnp.where(lanes, by_value[0], by_value[1]).astype(BF16)
    grad_q[...] = jnp.transpose(jnp.concatenate(by_query, axis=0)).astype(BF16) * 0.125


def attend_back(lengths, query, key, value, grad, log_total, pack, earlier=()):
    packs = lengths.shape[0]
    count, width = query.shape
    rows, pairs = count // packs, width // (2 * HD)
    return pl.pallas_call(
        functools.partial(attend_back_kernel, pack),
        grid=(pairs,),
        in_specs=[SMEM]
        + [pair_block(rows, pack)] * 4
        + [log_block(rows, pack)]
        + [ANY] * len(earlier),
        out_specs=[pair_block(rows, pack)] * 3,
        out_shape=[jax.ShapeDtypeStruct(query.shape, BF16)] * 3,
        input_output_aliases={6 + i: i for i in range(len(earlier))},
        compiler_params=params(60),
        cost_estimate=cost(40 * rows * rows * width, 14 * rows * width, 12 * rows * rows),
        name="attend_back",
    )(lengths, query, key, value, grad, log_total, *earlier)


def live_rows(lengths, shape):
    tiles = pl.num_programs(0) // lengths.shape[0]
    step = pl.program_id(0)
    pack = step // tiles
    end = 0
    for slot in range(lengths.shape[1] - 1):
        end = end + lengths[pack, slot]
    position = lax.broadcasted_iota(jnp.int32, shape, 0) + (step - pack * tiles) * shape[0]
    return position < end


def hidden_kernel(plans, size, place, lengths, rows, mixed, cotangent, table, *refs):
    two, refs = refs[:size], refs[size:]
    *up_plans, out_plan = plans
    branch_out, normed, active, slope, grad_down, out_w, up_w, sems = refs
    made = [copies(place[0], two, out_plan, out_w, sems, 0)]
    first = len(out_plan)
    for m, plan in enumerate(up_plans):
        made.append(copies(place[0], two, plan, up_w.at[m], sems, first))
        first += len(plan)

    @pl.when(pl.program_id(0) == 0)
    def _():
        for group in made:
            start_all(group)
        wait_all(made[0])

    branch = dot(mixed[...], out_w[...]) + vector(table, OUT_B)
    branch_out[...] = branch
    middle = rows[...].astype(F32) + vector(table, ATTN_S) * branch
    unit_rows, _ = centred_rows(middle)
    low = (unit_rows * vector(table, LN2_G) + vector(table, LN2_B)).astype(BF16)
    normed[...] = low
    live = live_rows(lengths, cotangent.shape)
    grad_out = jnp.where(live, cotangent[...].astype(F32), 0.0)
    grad_down[...] = (grad_out * vector(table, MLP_S)).astype(BF16)

    @pl.when(pl.program_id(0) == 0)
    def _():
        for group in made[1:]:
            wait_all(group)

    width = low.shape[1]
    for m in range(len(up_plans)):
        part = slice(m * width, (m + 1) * width)
        up = dot(low, up_w[m]) + vector(table, UP_B + m)
        value, rate = gelu_pair(up)
        active[:, part] = value.astype(BF16)
        slope[:, part] = rate.astype(BF16)


def hidden(place, lengths, rows, mixed, cotangent, table, group):
    count, width = rows.shape
    arrays, plans = group
    hidden_units = width * (len(plans) - 1)
    return pl.pallas_call(
        functools.partial(hidden_kernel, plans, len(arrays)),
        grid=(count // TILE,),
        in_specs=[SMEM, SMEM]
        + [tile_of(width)] * 3
        + [whole(table.shape)]
        + [ANY] * len(arrays),
        out_specs=[tile_of(width)] * 2 + [tile_of(hidden_units)] * 2 + [tile_of(width)],
        out_shape=[
            jax.ShapeDtypeStruct(rows.shape, F32),
            jax.ShapeDtypeStruct(rows.shape, BF16),
            jax.ShapeDtypeStruct((count, hidden_units), BF16),
            jax.ShapeDtypeStruct((count, hidden_units), BF16),
            jax.ShapeDtypeStruct(rows.shape, BF16),
        ],
        scratch_shapes=[
            pltpu.VMEM((width, width), BF16),
            pltpu.VMEM((len(plans) - 1, width, width), BF16),
            pltpu.SemaphoreType.DMA((sum(len(p) for p in plans),)),
        ],
        compiler_params=params(60),
        cost_estimate=cost(14 * count * width * hidden_units // 4, 26 * count * width, 2 * count * hidden_units),
        name="hidden",
    )(place, lengths, rows, mixed, cotangent, table, *arrays)


STATS_TWO = 7


def back_kernel(
    two_plans, down_plan, sizes, place, lengths, rows, branch_in, active, slope, grad_down, cotangent,
    table, *refs,
):
    sources, refs = refs[: sum(sizes)], refs[sum(sizes) :]
    two, three = sources[: sizes[0]], sources[sizes[0] :]
    *up_plans, out_plan = two_plans
    result, grad_hidden, grad_middle_out, grad_branch, grad_mixed, stats, hidden_stats = refs[:7]
    out_w, up_w, down_w, sems = refs[7:]
    made = [copies(place[0], three, down_plan, down_w, sems, 0)]
    first = len(down_plan)
    for m, plan in enumerate(up_plans):
        made.append(copies(place[0], two, plan, up_w.at[m], sems, first))
        first += len(plan)
    made.append(copies(place[0], two, out_plan, out_w, sems, first))

    @pl.when(pl.program_id(0) == 0)
    def _():
        for group in made:
            start_all(group)
        stats[...] = jnp.zeros_like(stats)
        hidden_stats[...] = jnp.zeros_like(hidden_stats)
        wait_all(made[0])

    live = live_rows(lengths, cotangent.shape)
    branch = branch_in[...]
    middle = rows[...].astype(F32) + vector(table, ATTN_S) * branch
    down_out = dot(active[...], down_w[...]) + vector(table, DOWN_B)
    result[...] = jnp.where(live, middle + vector(table, MLP_S) * down_out, 0.0).astype(BF16)
    grad_out = jnp.where(live, cotangent[...].astype(F32), 0.0)
    sums = [row_sum(grad_out * down_out), row_sum(grad_down[...].astype(F32))]

    @pl.when(pl.program_id(0) == 0)
    def _():
        for group in made[1:]:
            wait_all(group)

    width = middle.shape[1]
    grad_normed = jnp.zeros(middle.shape, F32)
    for m in range(len(up_plans)):
        part = slice(m * width, (m + 1) * width)
        grad_active = dot_nt(grad_down[...], down_w[part, :])
        low = (grad_active * slope[:, part].astype(F32)).astype(BF16)
        grad_hidden[:, part] = low
        hidden_stats[m : m + 1, :] += row_sum(low.astype(F32))
        grad_normed += dot_nt(low, up_w[m])
    unit_rows, inverse = centred_rows(middle)
    sums += [row_sum(grad_normed * unit_rows), row_sum(grad_normed)]
    grad_middle = grad_out + norm_back(grad_normed, unit_rows, inverse, vector(table, LN2_G))
    grad_middle_out[...] = grad_middle
    low = (grad_middle * vector(table, ATTN_S)).astype(BF16)
    grad_branch[...] = low
    sums += [row_sum(grad_middle * branch), row_sum(low.astype(F32))]
    grad_mixed[...] = dot_nt(low, out_w[...]).astype(BF16)
    for at, total in enumerate(sums):
        stats[at : at + 1, :] += total


def back(place, lengths, rows, branch, active, slope, grad_down, cotangent, table, two, three):
    count, width = rows.shape
    hidden_units = active.shape[1]
    plans = (two[1], three[1][0])
    sizes = (len(two[0]), len(three[0]))
    return pl.pallas_call(
        functools.partial(back_kernel, *plans, sizes),
        grid=(count // TILE,),
        in_specs=[SMEM, SMEM]
        + [tile_of(width)] * 2
        + [tile_of(hidden_units)] * 2
        + [tile_of(width)] * 2
        + [whole(table.shape)]
        + [ANY] * sum(sizes),
        out_specs=[tile_of(width), tile_of(hidden_units)]
        + [tile_of(width)] * 3
        + [whole((8, width)), whole((8, width))],
        out_shape=[
            jax.ShapeDtypeStruct(rows.shape, BF16),
            jax.ShapeDtypeStruct(active.shape, BF16),
            jax.ShapeDtypeStruct(rows.shape, F32),
            jax.ShapeDtypeStruct(rows.shape, BF16),
            jax.ShapeDtypeStruct(rows.shape, BF16),
            jax.ShapeDtypeStruct((8, width), F32),
            jax.ShapeDtypeStruct((8, width), F32),
        ],
        scratch_shapes=[
            pltpu.VMEM((width, width), BF16),
            pltpu.VMEM((len(plans[0]) - 1, width, width), BF16),
            pltpu.VMEM((hidden_units, width), BF16),
            pltpu.SemaphoreType.DMA((sum(len(p) for p in plans[0]) + len(plans[1]),)),
        ],
        compiler_params=params(60),
        cost_estimate=cost(26 * count * width * hidden_units // 4, 40 * count * width),
        name="back",
    )(place, lengths, rows, branch, active, slope, grad_down, cotangent, table, *two[0], *three[0])


def outer_kernel(spread, steps, place, *refs):
    pairs = len(steps)
    lefts, rights, refs = refs[:pairs], refs[pairs : 2 * pairs], refs[2 * pairs :]
    flat = refs[-1]
    step = pl.program_id(0)
    first = 0
    for left, count in zip(lefts, steps):

        @pl.when(step == first)
        def _(left=left):
            for at in range(0, flat.shape[0], 128):
                block = left[:, at : at + 128].astype(F32)
                flat[at : at + 128, :] = jnp.transpose(block).astype(BF16)

        first += count

    def put(right):
        value = dot(flat[...], right[...])
        if not spread:
            refs[0][...] = value.astype(BF16)
            return
        mine, theirs, held = refs[:3]
        plane, core = place[0] // 2, place[0] % 2
        held[...] = value
        unit = flat.shape[0] // 8
        for at in range(4):
            one = pl.multiple_of((2 * at + core) * unit, 8)
            other = pl.multiple_of((2 * at + 1 - core) * unit, 8)
            mine[at ^ plane, 0] = held[pl.ds(one, unit), :].astype(BF16)
            theirs[at ^ plane, 0] = held[pl.ds(other, unit), :].astype(BF16)

    first = 0
    for right, count in zip(rights, steps):

        @pl.when((step >= first) & (step < first + count))
        def _(right=right):
            put(right)

        first += count


def outer(place, pairs, width):
    count, height = pairs[0][0].shape
    steps = [right.shape[1] // width for _, right in pairs]
    total = sum(steps)
    right_specs, first = [], 0
    for own in steps:
        right_specs.append(
            pl.BlockSpec(
                (count, width),
                lambda i, first=first, own=own: (0, jnp.clip(i - first, 0, own - 1)),
            )
        )
        first += own
    scratch = [pltpu.VMEM((height, count), BF16)]
    if direct():
        block = pl.BlockSpec((4, 1, height // 8, width), lambda i: (0, i, 0, 0))
        shape = jax.ShapeDtypeStruct((4, total, height // 8, width), BF16)
        specs, shapes = [block, block], [shape, shape]
        scratch = [pltpu.VMEM((height, width), F32)] + scratch
    else:
        specs = pl.BlockSpec((height, width), lambda i: (0, i))
        shapes = jax.ShapeDtypeStruct((height, total * width), BF16)
    return pl.pallas_call(
        functools.partial(outer_kernel, direct(), steps),
        grid=(total,),
        in_specs=[SMEM] + [whole((count, height))] * len(pairs) + right_specs,
        out_specs=specs,
        out_shape=shapes,
        scratch_shapes=scratch,
        compiler_params=params(60),
        cost_estimate=cost(2 * count * height * total * width, 2 * (count + height) * total * width),
        name="outer",
    )(place, *(left for left, _ in pairs), *(right for _, right in pairs))


def wide_outer_kernel(place, left, right, out, flat):
    @pl.when(pl.program_id(0) == 0)
    def _():
        for at in range(0, flat.shape[0], 128):
            block = left[:, at : at + 128].astype(F32)
            flat[at : at + 128, :] = jnp.transpose(block).astype(BF16)

    out[0] = dot(flat[...], right[...]).astype(BF16)


def wide_outer(place, left, right):
    count, height = left.shape
    columns = right.shape[1]
    steps = 8
    step = columns // steps
    return pl.pallas_call(
        wide_outer_kernel,
        grid=(steps,),
        in_specs=[SMEM, whole(left.shape), pl.BlockSpec((count, step), lambda i: (0, i))],
        out_specs=pl.BlockSpec((1, height, step), lambda i: (i, 0, 0)),
        out_shape=jax.ShapeDtypeStruct((steps, height, step), BF16),
        scratch_shapes=[pltpu.VMEM((height, count), BF16)],
        compiler_params=params(60),
        cost_estimate=cost(2 * count * height * columns, 2 * (count + height) * (height + columns)),
        name="wide_outer",
    )(place, left, right)


def inputs_kernel(plans, place, rows, grad_middle, grad_q, grad_k, grad_v, table, *refs):
    count = len(refs) - 2 - 2
    sources, (grad_rows, stats, weights, sems) = refs[:count], refs[count:]
    made, first = [], 0
    for m in range(3):
        made.append(copies(place[0], sources, plans[m], weights.at[m], sems, first))
        first += len(plans[m])

    @pl.when(pl.program_id(0) == 0)
    def _():
        for group in made:
            start_all(group)
        stats[...] = jnp.zeros_like(stats)
        for group in made:
            wait_all(group)

    grad = dot_nt(grad_q[...], weights[0])
    grad += dot_nt(grad_k[...], weights[1])
    grad += dot_nt(grad_v[...], weights[2])
    unit_rows, inverse = centred_rows(rows[...].astype(F32))
    grad_rows[...] = grad_middle[...] + norm_back(grad, unit_rows, inverse, vector(table, LN1_G))
    sums = [row_sum(grad * unit_rows), row_sum(grad)]
    sums += [row_sum(grad_q[...].astype(F32)), row_sum(grad_v[...].astype(F32))]
    for at, total in enumerate(sums):
        stats[at : at + 1, :] += total


def inputs_back(place, rows, grad_middle, grad_q, grad_k, grad_v, table, group):
    arrays, plans = group
    count, width = rows.shape
    return pl.pallas_call(
        functools.partial(inputs_kernel, plans),
        grid=(count // TILE,),
        in_specs=[SMEM] + [tile_of(width)] * 5 + [whole(table.shape)] + [ANY] * len(arrays),
        out_specs=[tile_of(width), whole((8, width))],
        out_shape=[
            jax.ShapeDtypeStruct(rows.shape, F32),
            jax.ShapeDtypeStruct((8, width), F32),
        ],
        scratch_shapes=[
            pltpu.VMEM((3, width, width), BF16),
            pltpu.SemaphoreType.DMA((sum(len(p) for p in plans[:3]),)),
        ],
        compiler_params=params(60),
        cost_estimate=cost(6 * count * width * width, 20 * count * width),
        name="inputs_back",
    )(place, rows, grad_middle, grad_q, grad_k, grad_v, table, *arrays)


def add_low(left, right):
    return (left.astype(F32) + right.astype(F32)).astype(left.dtype)


def split_cores(stacked):
    stacked = flip_own(stacked)
    pieces = stacked.reshape((-1, 2) + stacked.shape[1:])
    return pieces[:, 0], pieces[:, 1]


def quarters(held):
    held = held.reshape((-1, 4) + held.shape[1:])
    return tuple(held[:, i] for i in range(4))


def halve(total):
    for bit in reversed(range(3, wide_bits())):
        count = total.shape[0] // 2
        total = add_low(total[:count], cross(total[count:], bit))
    return total[0]


def spread_blocks(stacked):
    size = stacked.shape[0]
    here = lax.axis_index("narrow")
    steps = sorted(range(1, size), key=lambda step: min(step, size - step))
    blocks = [
        lax.dynamic_index_in_dim(stacked, lax.rem(here + step, size), keepdims=False)
        for step in steps
    ]
    return blocks, [lambda v, step=step: shift(v, step) for step in steps]


def add_blocks(stacked, moved):
    total = lax.dynamic_index_in_dim(stacked, lax.axis_index("narrow"), keepdims=False)
    total = total.astype(F32)
    for block in moved:
        total = total + block.astype(F32)
    return total


def by_core(grad, parts):
    if direct():
        return tuple(piece.reshape(4, -1, piece.shape[3]) for piece in grad)
    places = lax.axis_size("wide")
    height, columns = grad.shape
    stacked = grad.reshape(places, height // places, parts, columns // parts).transpose(0, 2, 1, 3)
    return split_cores(stacked.reshape(places, -1, columns // parts))


def all_stages():
    stages = []
    for bit in range(lax.axis_size("narrow").bit_length() - 1):
        stages.append(lambda v, bit=bit: exchange(v, "narrow", lambda i: i ^ (1 << bit)))
    for bit in reversed(range(wide_bits())):
        stages.append(lambda v, bit=bit: cross(v, bit))
    return stages


def own_spot(places, layers, piece, width):
    start = (lax.axis_index("wide") * layers + lax.axis_index("narrow")) * piece
    return start // width, start % width


def shards(
    patches, lengths, w_qkv, w_out, w_up, w_down, ln1_gain, ln1_bias, q_bias, v_bias, out_bias, attn_scale,
    ln2_gain, ln2_bias, up_bias, down_bias, mlp_scale, cotangent,
):
    places, layers = lax.axis_size("wide"), lax.axis_size("narrow")
    place = lax.axis_index("wide").astype(jnp.int32).reshape(1)
    short, width = w_up.shape
    part = w_qkv.shape[1]
    quarter = w_out.shape[1]
    packs, pack_rows, _ = patches.shape
    rows = patches.reshape(-1, width)
    cotangent = cotangent.reshape(-1, width)

    small = [ln1_gain, ln1_bias, q_bias, v_bias, out_bias, attn_scale, ln2_gain, ln2_bias, down_bias, mlp_scale]
    small_spot = own_spot(places, layers, ln1_gain.shape[0], width)
    up_spot = own_spot(places, layers, up_bias.shape[0], width)
    table = jnp.zeros((16, width), BF16)
    table = lax.dynamic_update_slice(table, jnp.stack(small), (0, small_spot[1]))
    table = lax.dynamic_update_slice(table, up_bias[None], (UP_B + up_spot[0], up_spot[1]))
    stages = all_stages()

    def spread_table(table, stages):
        for stage in stages:
            table = table + stage(table)
        return table

    one = [w_qkv] * (layers - 1), shifts(layers)
    table, one = beside(lambda v: spread_table(v, stages[2:]), table, *one)
    one = by_origin([w_qkv, *one])
    one = jnp.concatenate(jnp.split(side_by_side(one), 3, axis=1))
    held = double(one)
    up_out = jnp.concatenate([w_up, w_out], axis=1)
    sends = [held, held] + [up_out] * (layers - 1)
    table, moved = beside(
        lambda v: spread_table(v, stages[:2]).astype(F32), table, sends, planes() + shifts(layers)
    )
    near, far, *two = moved
    half = near.shape[1] // 32 * 16
    sends = [near[:, :half], far[:, half:], jnp.concatenate([held, near, far])]
    two, moved = beside(
        lambda v: v, by_origin([up_out, *two]), sends, corners() + [lambda v: cross(v, 0)]
    )
    planes_one = held, near, far, jnp.concatenate(moved[:2], axis=1)
    other_three = moved[2]
    two = jnp.concatenate([two[:, :, :width].reshape(-1, width), side_by_side(two[:, :, width:])])
    held_two = double(two)
    half = two.shape[0] // 32 * 16
    one = matrices(planes_one, (other_three, cross(planes_one[3], 0)), 3)

    first, second = held_two[:, :half], held_two[:, half:]
    (normed, query, key, value), (near_one, far_one) = beside(
        lambda v: project(place, v, table, one), rows, [first, first], planes()
    )
    side_down = jnp.concatenate(jnp.split(w_down, layers, axis=0), axis=1)
    sends = [second, second] + [side_down] * (layers - 1)
    attention, (near_two, far_two, *three) = beside(
        lambda v: attend(lengths, v, key, value, 0), query, sends, planes() + shifts(layers)
    )
    near = jnp.concatenate([near_one, near_two], axis=1)
    far = jnp.concatenate([far_one, far_two], axis=1)
    sends = [near_one, far_two, jnp.concatenate([held_two, near, far])]
    for pack in range(1, packs):
        run = functools.partial(attend, lengths, query, key, value, pack)
        if pack == packs - 1:
            attention, moved = beside(run, attention, sends, corners() + [lambda v: cross(v, 0)])
        else:
            attention = run(attention)
    mixed, log_total = attention
    planes_two = held_two, near, far, jnp.concatenate(moved[:2], axis=1)
    two = matrices(planes_two, (moved[2], cross(planes_two[3], 0)), layers + 1)
    three = by_origin([side_down, *three])
    three = jnp.concatenate(
        [side_by_side(three[:, :, i * quarter : (i + 1) * quarter]) for i in range(layers)]
    )
    held = double(three)
    (branch, normed_two, active, slope, grad_down), (near, far) = beside(
        lambda v: hidden(place, lengths, rows, v, cotangent, table, two), mixed, [held, held], planes()
    )
    half = near.shape[1] // 32 * 16
    sends = [near[:, :half], far[:, half:], jnp.concatenate([held, near, far])]
    grad_w_down, moved = beside(
        lambda v: wide_outer(place, v, active), grad_down, sends, corners() + [lambda v: cross(v, 0)]
    )
    planes_three = held, near, far, jnp.concatenate(moved[:2], axis=1)
    three = matrices(planes_three, (moved[2], cross(planes_three[3], 0)), 1)
    active = after(active, grad_w_down)
    if places != 8:
        grad_w_down = grad_w_down.reshape(8, width, places // 8, -1).transpose(0, 2, 1, 3)
    total_down = lax.psum_scatter(grad_w_down.reshape(places, width, -1), "wide")

    result, grad_hidden, grad_middle, grad_branch, grad_mixed, stats_two, hidden_stats = back(
        place, lengths, rows, branch, active, slope, grad_down, cotangent, table, two, three
    )
    mine, theirs = by_core(
        outer(place, [(normed_two, grad_hidden), (mixed, grad_branch)], width), layers + 1
    )
    grads, (moved,) = beside(
        lambda v: attend_back(lengths, query, key, value, v, log_total, 0),
        grad_mixed,
        [theirs],
        [lambda v: cross(v, 0)],
    )
    own, near, far, corner = quarters(add_low(mine, moved))
    half = own.shape[1] // 32 * 16
    for pack in range(1, packs):
        run = functools.partial(attend_back, lengths, query, key, value, grad_mixed, log_total, pack)
        if pack == packs - 1:
            sends = [corner[:, :half], corner[:, half:]]
            grads, moved = beside(run, grads, sends, planes())
        else:
            grads = run(grads)
    far_part = add_low(far[:, :half], moved[0])
    near_part = add_low(near[:, half:], moved[1])
    grad_w_qkv, (near, far) = beside(
        lambda v: outer(place, [(normed, v)], width),
        jnp.concatenate(grads, axis=1),
        [near[:, :half], far[:, half:]],
        planes(),
    )
    mine, theirs = by_core(grad_w_qkv, 3)
    grad_q, grad_k, grad_v = grads
    near_part, far_part, theirs, total_down, mine = lax.optimization_barrier(
        (near_part, far_part, theirs, total_down, mine)
    )
    sends, moves = spread_blocks(total_down.reshape(layers, quarter, -1))
    (grad_rows, stats_one), moved = beside(
        lambda v: inputs_back(place, rows, grad_middle, v, grad_k, grad_v, table, one),
        grad_q,
        [near_part, far_part, theirs, *sends],
        planes() + [lambda v: cross(v, 0)] + moves,
    )
    near_part, far_part, other, *down = moved

    sums = jnp.concatenate([stats_one, stats_two, hidden_stats])
    total_down = add_blocks(total_down.reshape(layers, quarter, -1), down).T
    near = jnp.concatenate([near, near_part], axis=1).astype(F32)
    far = jnp.concatenate([far_part, far], axis=1).astype(F32)
    total_up = halve((own.astype(F32) + near + far).astype(BF16))
    total_out = total_up[layers * short :].reshape(short, layers, quarter).transpose(1, 0, 2)
    total_up = total_up[: layers * short].reshape(layers, short, width)
    total_up = jnp.concatenate([total_up, total_out], axis=2)
    up_sends, up_moves = spread_blocks(total_up)
    own, near, far, corner = quarters(add_low(mine, other))
    half = own.shape[1] // 32 * 16
    split = len(up_sends) - 1
    sums, moved = beside(
        lambda v: v + stages[-1](v),
        sums,
        [corner[:, :half], corner[:, half:]] + up_sends[:split],
        planes() + up_moves[:split],
    )
    up_parts = moved[2:]
    far = jnp.concatenate([add_low(far[:, :half], moved[0]), far[:, half:]], axis=1)
    near = jnp.concatenate([near[:, :half], add_low(near[:, half:], moved[1])], axis=1)
    sums, moved = beside(
        lambda v: spread_table(v, stages[:-3]), sums, [near, far] + up_sends[split:], planes() + up_moves[split:]
    )
    total_qkv = own.astype(F32) + moved[0].astype(F32) + moved[1].astype(F32)
    total_qkv = halve(total_qkv.astype(BF16))
    total_qkv = jnp.concatenate([total_qkv[i * short : (i + 1) * short] for i in range(3)], axis=1)
    total_qkv = total_qkv.reshape(short, layers, part).transpose(1, 0, 2)
    sends, moves = spread_blocks(total_qkv)
    up_parts += moved[2:]
    sums, moved = beside(lambda v: spread_table(v, stages[-3:-1]), sums, sends, moves)
    total_qkv = add_blocks(total_qkv, moved)
    total_up = add_blocks(total_up, up_parts)

    own = lax.dynamic_slice(sums, (0, small_spot[1]), (16, ln1_gain.shape[0]))
    own_up = lax.dynamic_slice(sums, (16 + up_spot[0], up_spot[1]), (1, up_bias.shape[0]))[0]
    return (
        result.reshape(patches.shape),
        grad_rows.reshape(patches.shape),
        total_qkv,
        total_up[:, width:],
        total_up[:, :width],
        total_down,
        own[0],
        own[1],
        own[2],
        own[3],
        own[13],
        own[12],
        own[10],
        own[11],
        own_up,
        own[9],
        own[8],
    )


def solution(mesh):
    return jax.shard_map(
        shards,
        mesh=mesh,
        in_specs=(
            P(("wide", "narrow"), None, None),
            P(("wide", "narrow"), None),
            P("wide", "narrow"),
            P("wide", "narrow"),
            P("wide", "narrow"),
            P("wide", "narrow"),
            P(("wide", "narrow")),
            P(("wide", "narrow")),
            P(("wide", "narrow")),
            P(("wide", "narrow")),
            P(("wide", "narrow")),
            P(("wide", "narrow")),
            P(("wide", "narrow")),
            P(("wide", "narrow")),
            P(("wide", "narrow")),
            P(("wide", "narrow")),
            P(("wide", "narrow")),
            P(("wide", "narrow"), None, None),
        ),
        out_specs=(
            P(("wide", "narrow"), None, None),
            P(("wide", "narrow"), None, None),
            P("wide", "narrow"),
            P("wide", "narrow"),
            P("wide", "narrow"),
            P("wide", "narrow"),
            P(("wide", "narrow")),
            P(("wide", "narrow")),
            P(("wide", "narrow")),
            P(("wide", "narrow")),
            P(("wide", "narrow")),
            P(("wide", "narrow")),
            P(("wide", "narrow")),
            P(("wide", "narrow")),
            P(("wide", "narrow")),
            P(("wide", "narrow")),
            P(("wide", "narrow")),
        ),
        check_vma=False,
    )
```

time: 564 us -> 361 us (0.64)
  Pallas kernels: 0 us -> 159 us
  matrix products: 145 us -> 0 us
  other arithmetic: 131 us -> 26.2 us
  waiting for transfers between devices: 113 us -> 47.4 us
  local copies, waits for them, and re-layouts: 95.6 us -> 35.6 us
  between operations: 3.12 us -> 15.7 us
    pallas_call x0 -> x11, Pallas kernels: none -> 159 us  [the longest x1 31.4 us: back(): pl.pallas_call(functools.partial(back_kernel, *plans, sizes), grid=(count...]
    dot_general x26 -> x0, matrix products: 145 us -> none  [the longest x1 17.2 us: shards(): jnp.einsum('prd,fd->prf', grad_down, down_back, preferred_element_type=jn...]
    ppermute x67 -> x60, waiting for transfers between devices: 113 us -> 47.4 us  [exchange(): lax.ppermute(value, axis_name, [(i, partner(i) % size) for i in range(siz...]
    convert_element_type x18 -> x7, other arithmetic: 56 us -> 4.95 us  [the longest x4 2.78 us: add_low(): return (left.astype(F32) + right.astype(F32)).astype(left.dtype)]
    select_n x22 -> x0, other arithmetic: 25.7 us -> none  [the longest x21 25.7 us: flip_own(): halves = jnp.where(here >> bit & 1, halves[:, ::-1], halves)]
    reshape x5 -> x2, local copies, waits for them, and re-layouts: 25.6 us -> 0.77 us  [the longest x1 0.57 us: shards(): total_qkv = total_qkv.reshape(short, layers, part).transpose(1, 0, 2)]
    reduce_sum x10 -> x0, other arithmetic: 15 us -> none  [the longest x2 4.35 us: attend(): row_total = jnp.sum(exp_scores, axis=-1, keepdims=True)]
    another operation x23 -> x1, other arithmetic: 15 us -> 0.96 us  [the longest x12 7.31 us: spread_wide(): stacked = jnp.stack(quads, axis=1).reshape((-1,) + block.shape)]
  transfers between devices with their start and end apart: 67 -> 61, of which waited for: 20 -> 18; matrix products, arithmetic and copies ran while one was open for 16% -> 10% of each run, Pallas kernels for 0% -> 45%
where the time goes in v2:
time: 361 us; the launch traced here: 355 us
  Pallas kernels  159 us (44%)
  starting transfers between devices  70.6 us (20%)
  waiting for transfers between devices  47.4 us (13%)
  local copies, waits for them, and re-layouts  35.6 us (10%)
  other arithmetic  26.2 us (7%)
  between operations  15.7 us (4%)
    ppermute x60, starting transfers between devices, exchange(): lax.ppermute(value, axis_name, [(i, partner(i) % size) for i in range(siz...  70.6 us
    ppermute x60, waiting for transfers between devices, exchange(): lax.ppermute(value, axis_name, [(i, partner(i) % size) for i in range(siz...  47.4 us
    pallas_call x1, Pallas kernels, back(): pl.pallas_call(functools.partial(back_kernel, *plans, sizes), grid=(count...  31.4 us
    pallas_call x2, Pallas kernels, attend_back(): pl.pallas_call(functools.partial(attend_back_kernel, pack), grid=(pairs,)...  27.4 us
    pallas_call x1, Pallas kernels, hidden(): pl.pallas_call(functools.partial(hidden_kernel, plans, len(arrays)), grid...  24.5 us
    pallas_call x2, Pallas kernels, outer(): pl.pallas_call(functools.partial(outer_kernel, direct(), steps), grid=(to...  21.7 us
    pallas_call x2, Pallas kernels, attend(): pl.pallas_call(functools.partial(attend_kernel, pack), grid=(pairs,), in_...  21.4 us
    unnamed x108, local copies, waits for them, and re-layouts  16.2 us
  transfers between devices with their start and end apart: 61, of which 18 were waited for; matrix products, arithmetic and copies ran while one was open for 10% of the time, Pallas kernels for 45%

profile of v2, /device:TPU:0, one launch (start us, length us, event | category | flops | bytes accessed | tf_op | source)
XLA Modules:
  0.0 354.9 jit_solution(11735957595881296098)
XLA Ops:
  10.0 3.0 collective-permute-start
  13.0 2.0 collective-permute-start.3
  15.0 2.6 collective-permute-start.4
  28.2 3.1 collective-permute-start.6
  31.3 1.8 collective-permute-done.6
  33.1 1.7 collective-permute-start.7
  34.8 2.0 collective-permute-start.10
  38.1 5.8 %collective-permute-done.7 = bf16[16,768]{1,0:T(8,128)(2,1)S(1)} collective-permute-done((bf16[16,768]{1,0:T(8,128)(2,1)S(1)}, bf16[16,768]{1,0:T(8,128)(2,1)S(1)}, u32[]{:S(2)}, u32[]{:S(2)}) %collective-permute-start.7) | collective-permute-done | bytes 24608 | tf_op jit(solution)/shard_map/ppermute | solution.py:22
  44.5 6.0 %collective-permute-done.11 = bf16[96,960]{1,0:T(8,128)(2,1)S(1)} collective-permute-done((bf16[96,960]{1,0:T(8,128)(2,1)S(1)}, bf16[96,960]{1,0:T(8,128)(2,1)S(1)}, u32[]{:S(2)}, u32[]{:S(2)}) %collective-permute-start.11) | collective-permute-done | bytes 184352 | tf_op jit(solution)/shard_map/ppermute | solution.py:22
  56.5 5.4 %collective-permute-done.13 = bf16[1,144,768]{2,1,0:T(8,128)(2,1)S(1)} collective-permute-done((bf16[1,144,768]{2,1,0:T(8,128)(2,1)}, bf16[1,144,768]{2,1,0:T(8,128)(2,1)S(1)}, u32[]{:S(2)}, u32[]{:S(2)}) %collective-permute-start.13) | collective-permute-done | bytes 221216 | tf_op jit(solution)/shard_map/ppermute | solution.py:22
  66.0 9.5 %project.1 = (bf16[1024,768]{1,0:T(8,128)(2,1)}, bf16[1024,768]{1,0:T(8,128)(2,1)}, bf16[1024,768]{1,0:T(8,128)(2,1)}, bf16[1024,768]{1,0:T(8,128)(2,1)}) custom-call(s32[1]{0:T(128)} %bitcast.place, bf16[1024,768]{1,0:T(8,128)(2,1)} %bitcast.233, f32[16,768]{1,0:T(8,128)} %add_convert_fusion.5.table, bf16[1,288,768]{2,1,0:T(8,128)(2,1)} %copy-done.5, ...), custom_call_target="tpu_custom_call" | custom-call | flops 3623878656 | bytes 11010048 | tf_op jit(solution)/shard_map/project/pallas_call | solution.py:225
  75.5 3.2 collective-permute-start.21
  81.3 1.7 collective-permute-start.19
  84.5 10.7 %attend.2 = (bf16[1024,768]{1,0:T(8,128)(2,1)}, f32[2,6,2,512]{3,2,1,0:T(2,128)}) custom-call(s32[2,6]{1,0:T(2,128)} %lengths.11, bf16[1024,768]{1,0:T(8,128)(2,1)} %get-tuple-element.235.query, bf16[1024,768]{1,0:T(8,128)(2,1)} %get-tuple-element.233.key, bf16[1024,768]{1,0:T(8,128)(2,1)} %get-tuple-element.234.value), custom_call_target="tpu_custom_call" | custom-call | flops 3221225472 | bytes 3145728 | tf_op jit(solution)/shard_map/attend/pallas_call | solution.py:296
  97.8 1.6 bitcast_dynamic-update-slice_fusion.14
  99.4 1.6 bitcast_dynamic-update-slice_fusion.12
  102.4 1.6 bitcast_dynamic-update-slice_fusion.15
  104.0 10.7 %attend.3 = (bf16[1024,768]{1,0:T(8,128)(2,1)}, f32[2,6,2,512]{3,2,1,0:T(2,128)}) custom-call(s32[2,6]{1,0:T(2,128)} %lengths.11, bf16[1024,768]{1,0:T(8,128)(2,1)} %get-tuple-element.235.query, bf16[1024,768]{1,0:T(8,128)(2,1)} %get-tuple-element.233.key, bf16[1024,768]{1,0:T(8,128)(2,1)} %get-tuple-element.234.value, ...), custom_call_target="tpu_custom_call", output_to_operand_aliasing={{0}: (4, {}), {1}: (5, {})} | custom-call | flops 3221225472 | bytes 3145728 | tf_op jit(solution)/shard_map/attend/pallas_call | solution.py:296
  119.4 1.8 collective-permute-start.28
  123.5 24.5 %hidden.1 = (f32[1024,768]{1,0:T(8,128)}, bf16[1024,768]{1,0:T(8,128)(2,1)}, bf16[1024,3072]{1,0:T(8,128)(2,1)}, bf16[1024,3072]{1,0:T(8,128)(2,1)}, bf16[1024,768]{1,0:T(8,128)(2,1)}) custom-call(s32[1]{0:T(128)} %bitcast.place, s32[2,6]{1,0:T(2,128)} %lengths.11, bf16[1024,768]{1,0:T(8,128)(2,1)} %bitcast.234, ...), custom_call_target="tpu_custom_call" | custom-call | flops 8455716864 | bytes 20447232 | tf_op jit(solution)/shard_map/hidden/pallas_call | solution.py:409
  150.8 12.2 %wide_outer.1 = bf16[8,768,384]{2,1,0:T(8,128)(2,1)} custom-call(s32[1]{0:T(128)} %bitcast.place, bf16[1024,768]{1,0:T(8,128)(2,1)} %get-tuple-element.276.left.grad_down, bf16[1024,3072]{1,0:T(8,128)(2,1)} %get-tuple-element.281.right.active), custom_call_target="tpu_custom_call" | custom-call | flops 4831838208 | bytes 13762560 | tf_op jit(solution)/shard_map/wide_outer/pallas_call | solution.py:625
  165.9 31.4 %back.1 = (bf16[1024,768]{1,0:T(8,128)(2,1)}, bf16[1024,3072]{1,0:T(8,128)(2,1)}, f32[1024,768]{1,0:T(8,128)}, bf16[1024,768]{1,0:T(8,128)(2,1)}, bf16[1024,768]...) custom-call(s32[1]{0:T(128)} %bitcast.place, s32[2,6]{1,0:T(2,128)} %lengths.11, bf16[1024,768]{1,0:T(8,128)(2,1)} %bitcast.235, ...), custom_call_target="tpu_custom_call" | custom-call | flops 15703474176 | bytes 31457280 | tf_op jit(solution)/shard_map/back/pallas_call | solution.py:501
  197.3 13.3 %outer.2 = (bf16[4,5,96,768]{3,2,1,0:T(8,128)(2,1)}, bf16[4,5,96,768]{3,2,1,0:T(8,128)(2,1)}) custom-call(s32[1]{0:T(128)} %bitcast.place, bf16[1024,768]{1,0:T(8,128)(2,1)} %get-tuple-element.290.refs_0_, bf16[1024,768]{1,0:T(8,128)(2,1)} %get-tuple-element.260.mixed.refs_1_, bf16[1024,3072]{1,0:T(8,128)(2,1)} %get-tuple-element.291.refs_2_, ...), custom_call_target="tpu_custom_call" | custom-call | flops 6039797760 | bytes 13762560 | tf_op jit(solution)/shard_map/outer/pallas_call | solution.py:597
  210.7 13.6 %attend_back.2 = (bf16[1024,768]{1,0:T(8,128)(2,1)}, bf16[1024,768]{1,0:T(8,128)(2,1)}, bf16[1024,768]{1,0:T(8,128)(2,1)}) custom-call(s32[2,6]{1,0:T(2,128)} %lengths.11, bf16[1024,768]{1,0:T(8,128)(2,1)} %get-tuple-element.235.query, bf16[1024,768]{1,0:T(8,128)(2,1)} %get-tuple-element.233.key, bf16[1024,768]{1,0:T(8,128)(2,1)} %get-tuple-element.234.value, ...), custom_call_target="tpu_custom_call" | custom-call | flops 8053063680 | bytes 5505024 | tf_op jit(solution)/shard_map/attend_back/pallas_call | solution.py:338
  224.3 1.6 copy-done.1
  225.9 3.4 fusion.1
  231.5 1.7 collective-permute-start.35
  234.6 13.8 %attend_back.3 = (bf16[1024,768]{1,0:T(8,128)(2,1)}, bf16[1024,768]{1,0:T(8,128)(2,1)}, bf16[1024,768]{1,0:T(8,128)(2,1)}) custom-call(s32[2,6]{1,0:T(2,128)} %lengths.11, bf16[1024,768]{1,0:T(8,128)(2,1)} %get-tuple-element.235.query, bf16[1024,768]{1,0:T(8,128)(2,1)} %get-tuple-element.233.key, ...), custom_call_target="tpu_custom_call", output_to_operand_aliasing={{0}: (6, {}), {1}: (7, {}), {2}: (8, {})} | custom-call | flops 8053063680 | bytes 5505024 | tf_op jit(solution)/shard_map/attend_back/pallas_call | solution.py:338
  248.4 1.7 slice.324
  250.2 1.7 slice.323
  252.7 4.1 %pad_maximum_fusion.refs_1_ = bf16[1024,2304]{1,0:T(8,128)(2,1)} fusion(bf16[1024,768]{1,0:T(8,128)(2,1)} %get-tuple-element.317.grad_v, bf16[1024,768]{1,0:T(8,128)(2,1)} %get-tuple-element.316.grad_k, bf16[1024,768]{1,0:T(8,128)(2,1)} %get-tuple-element.329.grad_q), kind=kLoop, calls=%fused_computation.2 | loop fusion | flops 14155776 | bytes 9437184 | tf_op jit(solution)/shard_map/concatenate | solution.py:866
  258.5 1.8 add_convert_fusion.2
  260.3 8.4 %outer.3 = (bf16[4,3,96,768]{3,2,1,0:T(8,128)(2,1)}, bf16[4,3,96,768]{3,2,1,0:T(8,128)(2,1)}) custom-call(s32[1]{0:T(128)} %bitcast.place, bf16[1024,768]{1,0:T(8,128)(2,1)} %get-tuple-element.315.refs_0_, bf16[1024,2304]{1,0:T(8,128)(2,1)} %pad_maximum_fusion.refs_1_), custom_call_target="tpu_custom_call" | custom-call | flops 3623878656 | bytes 8257536 | tf_op jit(solution)/shard_map/outer/pallas_call | solution.py:597
  268.8 1.8 dynamic-slice_bitcast_fusion
  271.2 1.6 collective-permute-start.39
  274.2 3.3 collective-permute-start.43
  279.1 11.3 %inputs_back.1 = (f32[1024,768]{1,0:T(8,128)}, f32[8,768]{1,0:T(8,128)}) custom-call(s32[1]{0:T(128)} %bitcast.place, bf16[1024,768]{1,0:T(8,128)(2,1)} %bitcast.236, f32[1024,768]{1,0:T(8,128)} %get-tuple-element.287.grad_middle, bf16[1024,768]{1,0:T(8,128)(2,1)} %get-tuple-element.329.grad_q, bf16[1024,768]{1,0:T(8,128)(2,1)} %get-tuple-element.316.grad_k, ...), custom_call_target="tpu_custom_call" | custom-call | flops 3623878656 | bytes 15728640 | tf_op jit(solution)/shard_map/inputs_back/pallas_call | solution.py:668
  292.2 2.4 fusion.2
  295.6 1.9 collective-permute-start.46
  298.8 3.8 %collective-permute-start.49 = (bf16[96,960]{1,0:T(8,128)(2,1)S(1)}, bf16[96,960]{1,0:T(8,128)(2,1)S(1)}, u32[]{:S(2)}, u32[]{:S(2)}) collective-permute-start(bf16[96,960]{1,0:T(8,128)(2,1)S(1)} %get-tuple-element.352), channel_id=1, source_target_pairs={{0,3},{1,0},{2,1},{3,2},{4,7},{5,4},{6,5},{7,6},{8,11},{9,8},{10,9... | collective-permute-start | bytes 552968 | tf_op jit(solution)/shard_map/ppermute | solution.py:22
  303.9 4.4 %collective-permute-done.48 = bf16[96,960]{1,0:T(8,128)(2,1)S(1)} collective-permute-done((bf16[96,960]{1,0:T(8,128)(2,1)S(1)}, bf16[96,960]{1,0:T(8,128)(2,1)S(1)}, u32[]{:S(2)}, u32[]{:S(2)}) %collective-permute-start.48) | collective-permute-done | bytes 184352 | tf_op jit(solution)/shard_map/ppermute | solution.py:22
  314.3 4.3 %collective-permute-done.50 = f32[24,768]{1,0:T(8,128)S(1)} collective-permute-done((f32[24,768]{1,0:T(8,128)S(1)}, f32[24,768]{1,0:T(8,128)S(1)}, u32[]{:S(2)}, u32[]{:S(2)}) %collective-permute-start.50) | collective-permute-done | bytes 73760 | tf_op jit(solution)/shard_map/ppermute | solution.py:22
  318.6 4.6 %collective-permute-start.51 = (f32[24,768]{1,0:T(8,128)S(1)}, f32[24,768]{1,0:T(8,128)}, u32[]{:S(2)}, u32[]{:S(2)}) collective-permute-start(f32[24,768]{1,0:T(8,128)S(1)} %add.209), channel_id=1, source_target_pairs={{0,2},{1,3},{2,0},{3,1},{4,6},{5,7},{6,4},{7,5},{8,10},{9,11},{10,... | collective-permute-start | bytes 221192 | tf_op jit(solution)/shard_map/ppermute | solution.py:22
  323.2 3.4 collective-permute-done.51
  329.5 1.8 collective-permute-start.55
  331.2 1.8 fusion.14
  333.0 3.8 %collective-permute-start.58 = (bf16[96,576]{1,0:T(8,128)(2,1)S(1)}, bf16[96,576]{1,0:T(8,128)(2,1)S(1)}, u32[]{:S(2)}, u32[]{:S(2)}) collective-permute-start(bf16[96,576]{1,0:T(8,128)(2,1)S(1)} %bitcast.216), channel_id=1, source_target_pairs={{0,3},{1,0},{2,1},{3,2},{4,7},{5,4},{6,5},{7,6},{8,11},{9,8},{10,9... | collective-permute-start | bytes 331784 | tf_op jit(solution)/shard_map/ppermute | solution.py:22
  341.3 4.4 %collective-permute-done.59 = bf16[96,576]{1,0:T(8,128)(2,1)S(1)} collective-permute-done((bf16[96,576]{1,0:T(8,128)(2,1)S(1)}, bf16[96,576]{1,0:T(8,128)(2,1)S(1)}, u32[]{:S(2)}, u32[]{:S(2)}) %collective-permute-start.59) | collective-permute-done | bytes 110624 | tf_op jit(solution)/shard_map/ppermute | solution.py:22
  (273 shorter events, 75.8 us)
Async XLA Ops:
  7.2 261.6 %reduce-scatter.2.cloned.1.call-start = ((), (), s32[]{:S(2)}) async-start(), calls=%async_computation.1 | async-start | bytes 5308416 | tf_op jit(solution)/shard_map/reduce_scatter | solution.py:839
  10.0 8.9 %collective-permute-start = (bf16[16,768]{1,0:T(8,128)(2,1)S(1)}, bf16[16,768]{1,0:T(8,128)(2,1)S(1)}, u32[]{:S(2)}, u32[]{:S(2)}) collective-permute-start(bf16[16,768]{1,0:T(8,128)(2,1)S(1)} %dynamic_update_slice.7), channel_id=1, source_target_pairs={{0,16},{4,20},{8,24},{12,28},{16,0},{20,4},{24,8},{28,12},{1,17},{... | collective-permute-start | bytes 73736 | tf_op jit(solution)/shard_map/ppermute | solution.py:22
  13.0 11.1 %collective-permute-start.3 = (bf16[96,576]{1,0:T(8,128)(2,1)}, bf16[96,576]{1,0:T(8,128)(2,1)S(1)}, u32[]{:S(2)}, u32[]{:S(2)}) collective-permute-start(bf16[96,576]{1,0:T(8,128)(2,1)} %param.20), channel_id=1, source_target_pairs={{0,1},{1,2},{2,3},{3,0},{4,5},{5,6},{6,7},{7,4},{8,9},{9,10},{10,1... | collective-permute-start | bytes 331784 | tf_op jit(solution)/shard_map/ppermute | solution.py:22
  15.0 10.7 %collective-permute-start.4 = (bf16[96,576]{1,0:T(8,128)(2,1)}, bf16[96,576]{1,0:T(8,128)(2,1)S(1)}, u32[]{:S(2)}, u32[]{:S(2)}) collective-permute-start(bf16[96,576]{1,0:T(8,128)(2,1)} %param.20), channel_id=1, source_target_pairs={{0,2},{1,3},{2,0},{3,1},{4,6},{5,7},{6,4},{7,5},{8,10},{9,11},{10,... | collective-permute-start | bytes 331784 | tf_op jit(solution)/shard_map/ppermute | solution.py:22
  17.6 8.1 %collective-permute-start.5 = (bf16[96,576]{1,0:T(8,128)(2,1)}, bf16[96,576]{1,0:T(8,128)(2,1)S(1)}, u32[]{:S(2)}, u32[]{:S(2)}) collective-permute-start(bf16[96,576]{1,0:T(8,128)(2,1)} %param.20), channel_id=1, source_target_pairs={{0,3},{1,0},{2,1},{3,2},{4,7},{5,4},{6,5},{7,6},{8,11},{9,8},{10,9... | collective-permute-start | bytes 331784 | tf_op jit(solution)/shard_map/ppermute | solution.py:22
  26.1 25.8 %collective-permute-start.8 = (bf16[1,288,768]{2,1,0:T(8,128)(2,1)S(1)}, bf16[1,288,768]{2,1,0:T(8,128)(2,1)S(1)}, u32[]{:S(2)}, u32[]{:S(2)}) collective-permute-start(bf16[1,288,768]{2,1,0:T(8,128)(2,1)S(1)} %fusion.8.refs_0_), channel_id=1, source_target_pairs={{0,8},{4,12},{8,0},{12,4},{16,24},{20,28},{24,16},{28,20},{1,9},{5... | collective-permute-start | bytes 1327112 | tf_op jit(solution)/shard_map/ppermute | solution.py:22
  27.6 24.2 %collective-permute-start.9 = (bf16[1,288,768]{2,1,0:T(8,128)(2,1)S(1)}, bf16[1,288,768]{2,1,0:T(8,128)(2,1)S(1)}, u32[]{:S(2)}, u32[]{:S(2)}) collective-permute-start(bf16[1,288,768]{2,1,0:T(8,128)(2,1)S(1)} %fusion.8.refs_0_), channel_id=1, source_target_pairs={{0,16},{4,20},{8,24},{12,28},{16,0},{20,4},{24,8},{28,12},{1,17},{... | collective-permute-start | bytes 1327112 | tf_op jit(solution)/shard_map/ppermute | solution.py:22
  33.1 10.8 %collective-permute-start.7 = (bf16[16,768]{1,0:T(8,128)(2,1)S(1)}, bf16[16,768]{1,0:T(8,128)(2,1)S(1)}, u32[]{:S(2)}, u32[]{:S(2)}) collective-permute-start(bf16[16,768]{1,0:T(8,128)(2,1)S(1)} %add.192), channel_id=1, source_target_pairs={{0,2},{1,3},{2,0},{3,1},{4,6},{5,7},{6,4},{7,5},{8,10},{9,11},{10,... | collective-permute-start | bytes 73736 | tf_op jit(solution)/shard_map/ppermute | solution.py:22
  34.8 9.7 %collective-permute-start.10 = (bf16[96,960]{1,0:T(8,128)(2,1)S(1)}, bf16[96,960]{1,0:T(8,128)(2,1)S(1)}, u32[]{:S(2)}, u32[]{:S(2)}) collective-permute-start(bf16[96,960]{1,0:T(8,128)(2,1)S(1)} %constant_dynamic-update-slice_fusion), channel_id=1, source_target_pairs={{0,1},{1,2},{2,3},{3,0},{4,5},{5,6},{6,7},{7,4},{8,9},{9,10},{10,1... | collective-permute-start | bytes 552968 | tf_op jit(solution)/shard_map/ppermute | solution.py:22
  36.8 13.7 %collective-permute-start.11 = (bf16[96,960]{1,0:T(8,128)(2,1)S(1)}, bf16[96,960]{1,0:T(8,128)(2,1)S(1)}, u32[]{:S(2)}, u32[]{:S(2)}) collective-permute-start(bf16[96,960]{1,0:T(8,128)(2,1)S(1)} %constant_dynamic-update-slice_fusion), channel_id=1, source_target_pairs={{0,2},{1,3},{2,0},{3,1},{4,6},{5,7},{6,4},{7,5},{8,10},{9,11},{10,... | collective-permute-start | bytes 552968 | tf_op jit(solution)/shard_map/ppermute | solution.py:22
  53.8 9.3 %collective-permute-start.15 = (bf16[3,288,768]{2,1,0:T(8,128)(2,1)S(1)}, bf16[3,288,768]{2,1,0:T(8,128)(2,1)}, u32[]{:S(2)}, u32[]{:S(2)}) collective-permute-start(bf16[3,288,768]{2,1,0:T(8,128)(2,1)S(1)} %pad_maximum_fusion.3), channel_id=1, source_target_pairs={{0,4},{4,0},{8,12},{12,8},{16,20},{20,16},{24,28},{28,24},{1,5},{5... | collective-permute-start | bytes 3981320 | tf_op jit(solution)/shard_map/ppermute | solution.py:22
  53.8 8.1 %collective-permute-start.13 = (bf16[1,144,768]{2,1,0:T(8,128)(2,1)}, bf16[1,144,768]{2,1,0:T(8,128)(2,1)S(1)}, u32[]{:S(2)}, u32[]{:S(2)}) collective-permute-start(bf16[1,144,768]{2,1,0:T(8,128)(2,1)} %slice.247), channel_id=1, source_target_pairs={{0,16},{4,20},{8,24},{12,28},{16,0},{20,4},{24,8},{28,12},{1,17},{... | collective-permute-start | bytes 663560 | tf_op jit(solution)/shard_map/ppermute | solution.py:22
  63.5 12.0 %collective-permute-start.17 = (bf16[1,240,768]{2,1,0:T(8,128)(2,1)S(1)}, bf16[1,240,768]{2,1,0:T(8,128)(2,1)S(1)}, u32[]{:S(2)}, u32[]{:S(2)}) collective-permute-start(bf16[1,240,768]{2,1,0:T(8,128)(2,1)S(1)} %get-tuple-element.231), channel_id=1, source_target_pairs={{0,8},{4,12},{8,0},{12,4},{16,24},{20,28},{24,16},{28,20},{1,9},{5... | collective-permute-start | bytes 1105928 | tf_op jit(solution)/shard_map/ppermute | solution.py:22
  64.1 11.4 %collective-permute-start.18 = (bf16[1,240,768]{2,1,0:T(8,128)(2,1)S(1)}, bf16[1,240,768]{2,1,0:T(8,128)(2,1)S(1)}, u32[]{:S(2)}, u32[]{:S(2)}) collective-permute-start(bf16[1,240,768]{2,1,0:T(8,128)(2,1)S(1)} %get-tuple-element.231), channel_id=1, source_target_pairs={{0,16},{4,20},{8,24},{12,28},{16,0},{20,4},{24,8},{28,12},{1,17},{... | collective-permute-start | bytes 1105928 | tf_op jit(solution)/shard_map/ppermute | solution.py:22
  75.5 19.7 %collective-permute-start.21 = (bf16[96,768]{1,0:T(8,128)(2,1)}, bf16[96,768]{1,0:T(8,128)(2,1)S(1)}, u32[]{:S(2)}, u32[]{:S(2)}) collective-permute-start(bf16[96,768]{1,0:T(8,128)(2,1)} %pad_maximum_fusion.10), channel_id=1, source_target_pairs={{0,1},{1,2},{2,3},{3,0},{4,5},{5,6},{6,7},{7,4},{8,9},{9,10},{10,1... | collective-permute-start | bytes 442376 | tf_op jit(solution)/shard_map/ppermute | solution.py:22
  78.7 16.5 %collective-permute-start.22 = (bf16[96,768]{1,0:T(8,128)(2,1)}, bf16[96,768]{1,0:T(8,128)(2,1)S(1)}, u32[]{:S(2)}, u32[]{:S(2)}) collective-permute-start(bf16[96,768]{1,0:T(8,128)(2,1)} %pad_maximum_fusion.10), channel_id=1, source_target_pairs={{0,2},{1,3},{2,0},{3,1},{4,6},{5,7},{6,4},{7,5},{8,10},{9,11},{10,... | collective-permute-start | bytes 442376 | tf_op jit(solution)/shard_map/ppermute | solution.py:22
  80.1 15.2 %collective-permute-start.23 = (bf16[96,768]{1,0:T(8,128)(2,1)}, bf16[96,768]{1,0:T(8,128)(2,1)S(1)}, u32[]{:S(2)}, u32[]{:S(2)}) collective-permute-start(bf16[96,768]{1,0:T(8,128)(2,1)} %pad_maximum_fusion.10), channel_id=1, source_target_pairs={{0,3},{1,0},{2,1},{3,2},{4,7},{5,4},{6,5},{7,6},{8,11},{9,8},{10,9... | collective-permute-start | bytes 442376 | tf_op jit(solution)/shard_map/ppermute | solution.py:22
  81.3 14.0 %collective-permute-start.19 = (bf16[1,240,768]{2,1,0:T(8,128)(2,1)S(1)}, bf16[1,240,768]{2,1,0:T(8,128)(2,1)S(1)}, u32[]{:S(2)}, u32[]{:S(2)}) collective-permute-start(bf16[1,240,768]{2,1,0:T(8,128)(2,1)S(1)} %get-tuple-element.239), channel_id=1, source_target_pairs={{0,8},{4,12},{8,0},{12,4},{16,24},{20,28},{24,16},{28,20},{1,9},{5... | collective-permute-start | bytes 1105928 | tf_op jit(solution)/shard_map/ppermute | solution.py:22
  83.0 12.3 %collective-permute-start.20 = (bf16[1,240,768]{2,1,0:T(8,128)(2,1)S(1)}, bf16[1,240,768]{2,1,0:T(8,128)(2,1)S(1)}, u32[]{:S(2)}, u32[]{:S(2)}) collective-permute-start(bf16[1,240,768]{2,1,0:T(8,128)(2,1)S(1)} %get-tuple-element.239), channel_id=1, source_target_pairs={{0,16},{4,20},{8,24},{12,28},{16,0},{20,4},{24,8},{28,12},{1,17},{... | collective-permute-start | bytes 1105928 | tf_op jit(solution)/shard_map/ppermute | solution.py:22
  97.0 17.7 %collective-permute-start.26 = (bf16[3,480,768]{2,1,0:T(8,128)(2,1)S(1)}, bf16[3,480,768]{2,1,0:T(8,128)(2,1)}, u32[]{:S(2)}, u32[]{:S(2)}) collective-permute-start(bf16[3,480,768]{2,1,0:T(8,128)(2,1)S(1)} %pad_maximum_fusion.1), channel_id=1, source_target_pairs={{0,4},{4,0},{8,12},{12,8},{16,20},{20,16},{24,28},{28,24},{1,5},{5... | collective-permute-start | bytes 6635528 | tf_op jit(solution)/shard_map/ppermute | solution.py:22
  97.0 17.7 %collective-permute-start.24 = (bf16[1,240,768]{2,1,0:T(8,128)(2,1)}, bf16[1,240,768]{2,1,0:T(8,128)(2,1)S(1)}, u32[]{:S(2)}, u32[]{:S(2)}) collective-permute-start(bf16[1,240,768]{2,1,0:T(8,128)(2,1)} %copy-done.16), channel_id=1, source_target_pairs={{0,16},{4,20},{8,24},{12,28},{16,0},{20,4},{24,8},{28,12},{1,17},{... | collective-permute-start | bytes 1105928 | tf_op jit(solution)/shard_map/ppermute | solution.py:22
  97.5 17.2 %collective-permute-start.25 = (bf16[1,240,768]{2,1,0:T(8,128)(2,1)}, bf16[1,240,768]{2,1,0:T(8,128)(2,1)S(1)}, u32[]{:S(2)}, u32[]{:S(2)}) collective-permute-start(bf16[1,240,768]{2,1,0:T(8,128)(2,1)} %copy-done.17), channel_id=1, source_target_pairs={{0,8},{4,12},{8,0},{12,4},{16,24},{20,28},{24,16},{28,20},{1,9},{5... | collective-permute-start | bytes 1105928 | tf_op jit(solution)/shard_map/ppermute | solution.py:22
  119.4 28.6 %collective-permute-start.28 = (bf16[1,384,768]{2,1,0:T(8,128)(2,1)S(1)}, bf16[1,384,768]{2,1,0:T(8,128)(2,1)S(1)}, u32[]{:S(2)}, u32[]{:S(2)}) collective-permute-start(bf16[1,384,768]{2,1,0:T(8,128)(2,1)S(1)} %maximum_bitcast_fusion.1.refs_6_), channel_id=1, source_target_pairs={{0,8},{4,12},{8,0},{12,4},{16,24},{20,28},{24,16},{28,20},{1,9},{5... | collective-permute-start | bytes 1769480 | tf_op jit(solution)/shard_map/ppermute | solution.py:22
  121.1 26.8 %collective-permute-start.29 = (bf16[1,384,768]{2,1,0:T(8,128)(2,1)S(1)}, bf16[1,384,768]{2,1,0:T(8,128)(2,1)S(1)}, u32[]{:S(2)}, u32[]{:S(2)}) collective-permute-start(bf16[1,384,768]{2,1,0:T(8,128)(2,1)S(1)} %maximum_bitcast_fusion.1.refs_6_), channel_id=1, source_target_pairs={{0,16},{4,20},{8,24},{12,28},{16,0},{20,4},{24,8},{28,12},{1,17},{... | collective-permute-start | bytes 1769480 | tf_op jit(solution)/shard_map/ppermute | solution.py:22
  149.8 13.2 %collective-permute-start.32 = (bf16[3,384,768]{2,1,0:T(8,128)(2,1)S(1)}, bf16[3,384,768]{2,1,0:T(8,128)(2,1)}, u32[]{:S(2)}, u32[]{:S(2)}) collective-permute-start(bf16[3,384,768]{2,1,0:T(8,128)(2,1)S(1)} %pad_maximum_fusion.2), channel_id=1, source_target_pairs={{0,4},{4,0},{8,12},{12,8},{16,20},{20,16},{24,28},{28,24},{1,5},{5... | collective-permute-start | bytes 5308424 | tf_op jit(solution)/shard_map/ppermute | solution.py:22
  149.8 13.1 %collective-permute-start.30 = (bf16[1,192,768]{2,1,0:T(8,128)(2,1)}, bf16[1,192,768]{2,1,0:T(8,128)(2,1)S(1)}, u32[]{:S(2)}, u32[]{:S(2)}) collective-permute-start(bf16[1,192,768]{2,1,0:T(8,128)(2,1)} %slice.272), channel_id=1, source_target_pairs={{0,16},{4,20},{8,24},{12,28},{16,0},{20,4},{24,8},{28,12},{1,17},{... | collective-permute-start | bytes 884744 | tf_op jit(solution)/shard_map/ppermute | solution.py:22
  150.4 12.5 %collective-permute-start.31 = (bf16[1,192,768]{2,1,0:T(8,128)(2,1)}, bf16[1,192,768]{2,1,0:T(8,128)(2,1)S(1)}, u32[]{:S(2)}, u32[]{:S(2)}) collective-permute-start(bf16[1,192,768]{2,1,0:T(8,128)(2,1)} %slice.273), channel_id=1, source_target_pairs={{0,8},{4,12},{8,0},{12,4},{16,24},{20,28},{24,16},{28,20},{1,9},{5... | collective-permute-start | bytes 884744 | tf_op jit(solution)/shard_map/ppermute | solution.py:22
  210.6 13.7 %collective-permute-start.34 = (bf16[4,480,768]{2,1,0:T(8,128)(2,1)}, bf16[4,480,768]{2,1,0:T(8,128)(2,1)S(1)}, u32[]{:S(2)}, u32[]{:S(2)}) collective-permute-start(bf16[4,480,768]{2,1,0:T(8,128)(2,1)} %bitcast.229), channel_id=1, source_target_pairs={{0,4},{4,0},{8,12},{12,8},{16,20},{20,16},{24,28},{28,24},{1,5},{5... | collective-permute-start | bytes 8847368 | tf_op jit(solution)/shard_map/ppermute | solution.py:22
  231.5 20.4 %collective-permute-start.35 = (bf16[1,240,768]{2,1,0:T(8,128)(2,1)}, bf16[1,240,768]{2,1,0:T(8,128)(2,1)S(1)}, u32[]{:S(2)}, u32[]{:S(2)}) collective-permute-start(bf16[1,240,768]{2,1,0:T(8,128)(2,1)} %get-tuple-element.310), channel_id=1, source_target_pairs={{0,8},{4,12},{8,0},{12,4},{16,24},{20,28},{24,16},{28,20},{1,9},{5... | collective-permute-start | bytes 1105928 | tf_op jit(solution)/shard_map/ppermute | solution.py:22
  233.2 18.7 %collective-permute-start.36 = (bf16[1,240,768]{2,1,0:T(8,128)(2,1)}, bf16[1,240,768]{2,1,0:T(8,128)(2,1)S(1)}, u32[]{:S(2)}, u32[]{:S(2)}) collective-permute-start(bf16[1,240,768]{2,1,0:T(8,128)(2,1)} %get-tuple-element.311), channel_id=1, source_target_pairs={{0,16},{4,20},{8,24},{12,28},{16,0},{20,4},{24,8},{28,12},{1,17},{... | collective-permute-start | bytes 1105928 | tf_op jit(solution)/shard_map/ppermute | solution.py:22
  256.7 12.0 %collective-permute-start.37 = (bf16[1,240,768]{2,1,0:T(8,128)(2,1)}, bf16[1,240,768]{2,1,0:T(8,128)(2,1)S(1)}, u32[]{:S(2)}, u32[]{:S(2)}) collective-permute-start(bf16[1,240,768]{2,1,0:T(8,128)(2,1)} %slice.323), channel_id=1, source_target_pairs={{0,8},{4,12},{8,0},{12,4},{16,24},{20,28},{24,16},{28,20},{1,9},{5... | collective-permute-start | bytes 1105928 | tf_op jit(solution)/shard_map/ppermute | solution.py:22
  257.4 11.4 %collective-permute-start.38 = (bf16[1,240,768]{2,1,0:T(8,128)(2,1)}, bf16[1,240,768]{2,1,0:T(8,128)(2,1)}, u32[]{:S(2)}, u32[]{:S(2)}) collective-permute-start(bf16[1,240,768]{2,1,0:T(8,128)(2,1)} %slice.324), channel_id=1, source_target_pairs={{0,16},{4,20},{8,24},{12,28},{16,0},{20,4},{24,8},{28,12},{1,17},{... | collective-permute-start | bytes 1105928 | tf_op jit(solution)/shard_map/ppermute | solution.py:22
  270.6 19.9 %collective-permute-start.41 = (bf16[4,288,768]{2,1,0:T(8,128)(2,1)}, bf16[4,288,768]{2,1,0:T(8,128)(2,1)}, u32[]{:S(2)}, u32[]{:S(2)}) collective-permute-start(bf16[4,288,768]{2,1,0:T(8,128)(2,1)} %bitcast.230), channel_id=1, source_target_pairs={{0,4},{4,0},{8,12},{12,8},{16,20},{20,16},{24,28},{28,24},{1,5},{5... | collective-permute-start | bytes 5308424 | tf_op jit(solution)/shard_map/ppermute | solution.py:22
  270.6 8.5 %collective-permute-start.42 = (bf16[192,384]{1,0:T(8,128)(2,1)S(1)}, bf16[192,384]{1,0:T(8,128)(2,1)S(1)}, u32[]{:S(2)}, u32[]{:S(2)}) collective-permute-start(bf16[192,384]{1,0:T(8,128)(2,1)S(1)} %get-tuple-element.335), channel_id=1, source_target_pairs={{0,1},{1,2},{2,3},{3,0},{4,5},{5,6},{6,7},{7,4},{8,9},{9,10},{10,1... | collective-permute-start | bytes 442376 | tf_op jit(solution)/shard_map/ppermute | solution.py:22
  271.2 19.3 %collective-permute-start.39 = (bf16[1,240,768]{2,1,0:T(8,128)(2,1)}, bf16[1,240,768]{2,1,0:T(8,128)(2,1)S(1)}, u32[]{:S(2)}, u32[]{:S(2)}) collective-permute-start(bf16[1,240,768]{2,1,0:T(8,128)(2,1)} %add_convert_fusion.2), channel_id=1, source_target_pairs={{0,8},{4,12},{8,0},{12,4},{16,24},{20,28},{24,16},{28,20},{1,9},{5... | collective-permute-start | bytes 1105928 | tf_op jit(solution)/shard_map/ppermute | solution.py:22
  272.7 17.7 %collective-permute-start.40 = (bf16[1,240,768]{2,1,0:T(8,128)(2,1)}, bf16[1,240,768]{2,1,0:T(8,128)(2,1)}, u32[]{:S(2)}, u32[]{:S(2)}) collective-permute-start(bf16[1,240,768]{2,1,0:T(8,128)(2,1)} %add_convert_fusion.1), channel_id=1, source_target_pairs={{0,16},{4,20},{8,24},{12,28},{16,0},{20,4},{24,8},{28,12},{1,17},{... | collective-permute-start | bytes 1105928 | tf_op jit(solution)/shard_map/ppermute | solution.py:22
  274.2 16.2 %collective-permute-start.43 = (bf16[192,384]{1,0:T(8,128)(2,1)}, bf16[192,384]{1,0:T(8,128)(2,1)S(1)}, u32[]{:S(2)}, u32[]{:S(2)}) collective-permute-start(bf16[192,384]{1,0:T(8,128)(2,1)} %get-tuple-element.336), channel_id=1, source_target_pairs={{0,3},{1,0},{2,1},{3,2},{4,7},{5,4},{6,5},{7,6},{8,11},{9,8},{10,9... | collective-permute-start | bytes 442376 | tf_op jit(solution)/shard_map/ppermute | solution.py:22
  279.1 11.4 %collective-permute-start.44 = (bf16[192,384]{1,0:T(8,128)(2,1)}, bf16[192,384]{1,0:T(8,128)(2,1)}, u32[]{:S(2)}, u32[]{:S(2)}) collective-permute-start(bf16[192,384]{1,0:T(8,128)(2,1)} %get-tuple-element.337), channel_id=1, source_target_pairs={{0,2},{1,3},{2,0},{3,1},{4,6},{5,7},{6,4},{7,5},{8,10},{9,11},{10,... | collective-permute-start | bytes 442376 | tf_op jit(solution)/shard_map/ppermute | solution.py:22
  295.6 14.1 %collective-permute-start.46 = (bf16[1,144,768]{2,1,0:T(8,128)(2,1)S(1)}, bf16[1,144,768]{2,1,0:T(8,128)(2,1)S(1)}, u32[]{:S(2)}, u32[]{:S(2)}) collective-permute-start(bf16[1,144,768]{2,1,0:T(8,128)(2,1)S(1)} %get-tuple-element.349), channel_id=1, source_target_pairs={{0,8},{4,12},{8,0},{12,4},{16,24},{20,28},{24,16},{28,20},{1,9},{5... | collective-permute-start | bytes 663560 | tf_op jit(solution)/shard_map/ppermute | solution.py:22
  297.4 12.3 %collective-permute-start.47 = (bf16[1,144,768]{2,1,0:T(8,128)(2,1)S(1)}, bf16[1,144,768]{2,1,0:T(8,128)(2,1)S(1)}, u32[]{:S(2)}, u32[]{:S(2)}) collective-permute-start(bf16[1,144,768]{2,1,0:T(8,128)(2,1)S(1)} %get-tuple-element.350), channel_id=1, source_target_pairs={{0,16},{4,20},{8,24},{12,28},{16,0},{20,4},{24,8},{28,12},{1,17},{... | collective-permute-start | bytes 663560 | tf_op jit(solution)/shard_map/ppermute | solution.py:22
  298.8 9.5 %collective-permute-start.48 = (bf16[96,960]{1,0:T(8,128)(2,1)S(1)}, bf16[96,960]{1,0:T(8,128)(2,1)S(1)}, u32[]{:S(2)}, u32[]{:S(2)}) collective-permute-start(bf16[96,960]{1,0:T(8,128)(2,1)S(1)} %get-tuple-element.351), channel_id=1, source_target_pairs={{0,1},{1,2},{2,3},{3,0},{4,5},{5,6},{6,7},{7,4},{8,9},{9,10},{10,1... | collective-permute-start | bytes 552968 | tf_op jit(solution)/shard_map/ppermute | solution.py:22
  298.8 10.9 %collective-permute-start.49 = (bf16[96,960]{1,0:T(8,128)(2,1)S(1)}, bf16[96,960]{1,0:T(8,128)(2,1)S(1)}, u32[]{:S(2)}, u32[]{:S(2)}) collective-permute-start(bf16[96,960]{1,0:T(8,128)(2,1)S(1)} %get-tuple-element.352), channel_id=1, source_target_pairs={{0,3},{1,0},{2,1},{3,2},{4,7},{5,4},{6,5},{7,6},{8,11},{9,8},{10,9... | collective-permute-start | bytes 552968 | tf_op jit(solution)/shard_map/ppermute | solution.py:22
  311.5 16.0 %collective-permute-start.52 = (bf16[1,288,768]{2,1,0:T(8,128)(2,1)}, bf16[1,288,768]{2,1,0:T(8,128)(2,1)S(1)}, u32[]{:S(2)}, u32[]{:S(2)}) collective-permute-start(bf16[1,288,768]{2,1,0:T(8,128)(2,1)} %pad_maximum_fusion.7), channel_id=1, source_target_pairs={{0,8},{4,12},{8,0},{12,4},{16,24},{20,28},{24,16},{28,20},{1,9},{5... | collective-permute-start | bytes 1327112 | tf_op jit(solution)/shard_map/ppermute | solution.py:22
  312.2 15.4 %collective-permute-start.53 = (bf16[1,288,768]{2,1,0:T(8,128)(2,1)}, bf16[1,288,768]{2,1,0:T(8,128)(2,1)S(1)}, u32[]{:S(2)}, u32[]{:S(2)}) collective-permute-start(bf16[1,288,768]{2,1,0:T(8,128)(2,1)} %pad_maximum_fusion.8), channel_id=1, source_target_pairs={{0,16},{4,20},{8,24},{12,28},{16,0},{20,4},{24,8},{28,12},{1,17},{... | collective-permute-start | bytes 1327112 | tf_op jit(solution)/shard_map/ppermute | solution.py:22
  312.5 15.0 %collective-permute-start.54 = (bf16[96,960]{1,0:T(8,128)(2,1)}, bf16[96,960]{1,0:T(8,128)(2,1)}, u32[]{:S(2)}, u32[]{:S(2)}) collective-permute-start(bf16[96,960]{1,0:T(8,128)(2,1)} %get-tuple-element.359), channel_id=1, source_target_pairs={{0,2},{1,3},{2,0},{3,1},{4,6},{5,7},{6,4},{7,5},{8,10},{9,11},{10,... | collective-permute-start | bytes 552968 | tf_op jit(solution)/shard_map/ppermute | solution.py:22
  333.0 8.3 %collective-permute-start.57 = (bf16[96,576]{1,0:T(8,128)(2,1)S(1)}, bf16[96,576]{1,0:T(8,128)(2,1)S(1)}, u32[]{:S(2)}, u32[]{:S(2)}) collective-permute-start(bf16[96,576]{1,0:T(8,128)(2,1)S(1)} %bitcast.217), channel_id=1, source_target_pairs={{0,1},{1,2},{2,3},{3,0},{4,5},{5,6},{6,7},{7,4},{8,9},{9,10},{10,1... | collective-permute-start | bytes 331784 | tf_op jit(solution)/shard_map/ppermute | solution.py:22
  333.0 8.3 %collective-permute-start.58 = (bf16[96,576]{1,0:T(8,128)(2,1)S(1)}, bf16[96,576]{1,0:T(8,128)(2,1)S(1)}, u32[]{:S(2)}, u32[]{:S(2)}) collective-permute-start(bf16[96,576]{1,0:T(8,128)(2,1)S(1)} %bitcast.216), channel_id=1, source_target_pairs={{0,3},{1,0},{2,1},{3,2},{4,7},{5,4},{6,5},{7,6},{8,11},{9,8},{10,9... | collective-permute-start | bytes 331784 | tf_op jit(solution)/shard_map/ppermute | solution.py:22
  336.8 8.9 %collective-permute-start.59 = (bf16[96,576]{1,0:T(8,128)(2,1)S(1)}, bf16[96,576]{1,0:T(8,128)(2,1)S(1)}, u32[]{:S(2)}, u32[]{:S(2)}) collective-permute-start(bf16[96,576]{1,0:T(8,128)(2,1)S(1)} %bitcast.215), channel_id=1, source_target_pairs={{0,2},{1,3},{2,0},{3,1},{4,6},{5,7},{6,4},{7,5},{8,10},{9,11},{10,... | collective-permute-start | bytes 331784 | tf_op jit(solution)/shard_map/ppermute | solution.py:22
  (51 other events, 291.1 us)
Sparse Core Ops, SparseCore 0:
  163.2 53.8 reduce-scatter.1

commit v3 on v2

--- a/solution.py
+++ b/solution.py
@@ -61,6 +61,10 @@
     return lax.optimization_barrier((run(value), moved))
 
 
+def beside_loose(run, value, sends, moves):
+    return beside(run, value, sends, moves)
+
+
 def planes():
     return [lambda v: cross(v, 1), lambda v: cross(v, 2)]
 
@@ -88,18 +92,38 @@
     return lax.axis_size("wide") == 8
 
 
-def matrices(planes, cores, parts):
-    unit = planes[0].shape[1] // parts
+def in_order(stacked, parts):
+    places, rows, columns = stacked.shape
+    unit = rows // parts
+    if parts == 1 or not direct():
+        stacked = stacked.reshape(places, parts, unit, columns)
+        arrays = [stacked[:, m].reshape(-1, columns) for m in range(parts)]
+        return arrays, [[(m, 0, 0, None, unit)] for m in range(parts)]
+    return [stacked], [[(0, at, m * unit, at, -unit) for at in range(places)] for m in range(parts)]
+
+
+def matrices(planes, cores, parts, short, long):
+    unit = (planes[0].shape[1] - 16) // parts
+    behind = parts * unit
     if not direct():
         other = [*jnp.split(cores[0], 3), cores[1]]
         stacked = jnp.stack([jnp.stack(pair, axis=1) for pair in zip(planes, other)], axis=1)
         stacked = flip_own(stacked.reshape((-1,) + planes[0].shape[1:]))
-        stacked = stacked.reshape(stacked.shape[0], parts, unit, -1)
+        width = stacked.shape[2]
+        rows = stacked[:, behind:].transpose(1, 0, 2)
+        table = rows[:10, :, :short].reshape(10, width)
+        up = rows[10, :, :long].reshape(-1, width)
+        table = jnp.concatenate([table, up])
+        table = jnp.pad(table, ((0, 16 - table.shape[0]), (0, 0)))
+        stacked = stacked[:, :behind].reshape(stacked.shape[0], parts, unit, -1)
         arrays = [stacked[:, m].reshape(-1, stacked.shape[3]) for m in range(parts)]
-        return arrays, [[(m, 0, 0, None, unit)] for m in range(parts)]
+        plans = [[(m, 0, 0, None, unit)] for m in range(parts)]
+        return (arrays, plans), (table, None)
     spots = [(0, 0, 0), (1, 0, 2), (2, 0, 4), (3, 0, 6), (4, 0, 1), (4, 1, 3), (4, 2, 5), (5, 0, 7)]
     plans = [[(at, index, m * unit, rel, unit) for at, index, rel in spots] for m in range(parts)]
-    return [*planes, *cores], plans
+    rows = jnp.concatenate([piece[:, behind:] for piece in (*planes, *cores)])
+    order = (0, 2, 4, 6, 1, 3, 5, 7)
+    return ([*planes, *cores], plans), (rows, (order, short, long))
 
 
 def copies(place, refs, plan, target, sems, first):
@@ -109,7 +133,8 @@
         if rel is None:
             made.append(pltpu.make_async_copy(refs[at], target, sem))
         else:
-            start = pl.multiple_of((place ^ rel) * unit, 16)
+            start = -rel * unit if unit < 0 else pl.multiple_of((place ^ rel) * unit, 16)
+            unit = abs(unit)
             source = refs[at].at[index, pl.ds(row, unit)]
             made.append(pltpu.make_async_copy(source, target.at[pl.ds(start, unit)], sem))
     return made
@@ -153,13 +178,8 @@
 
 
 def gelu_pair(values):
-    size = jnp.abs(values) * math.sqrt(0.5)
     bell = jnp.exp(values * values * -0.5)
-    step = 1.0 / (1.0 + 0.3275911 * size)
-    series = step * (-1.453152027 + step * 1.061405429) + 1.421413741
-    series = step * (0.254829592 + step * (-0.284496736 + step * series))
-    tail = 0.5 * series * bell
-    share = jnp.where(values >= 0, 1.0 - tail, tail)
+    share = 0.5 + 0.5 * lax.erf(values * math.sqrt(0.5))
     return values * share, share + values * bell * (1.0 / math.sqrt(2.0 * math.pi))
 
 
@@ -192,9 +212,28 @@
     return table[row : row + 1, :]
 
 
-def project_kernel(plans, place, rows, table, *refs):
-    count = len(refs) - 4 - 2
-    sources, (normed, query, key, value, weights, sems) = refs[:count], refs[count:]
+def make_table(place, rows, layout):
+    if layout is None:
+        return rows[...].astype(F32)
+    order, short, long = layout
+    shape = rows.shape[1:]
+    lane = lax.broadcasted_iota(jnp.int32, shape, 1)
+    row = lax.broadcasted_iota(jnp.int32, shape, 0)
+    table = jnp.zeros(shape, F32)
+    for at, rel in enumerate(order):
+        spot = place ^ rel
+        piece = rows[at].astype(F32)
+        table += pltpu.roll(jnp.where((row < UP_B) & (lane < short), piece, 0.0), spot * short, 1)
+        start = spot * long
+        up = jnp.where(lane[:1] < long, piece[UP_B : UP_B + 1], 0.0)
+        up = pltpu.roll(jnp.broadcast_to(up, shape), lax.rem(start, shape[1]), 1)
+        table += jnp.where(row == UP_B + start // shape[1], up, 0.0)
+    return table
+
+
+def project_kernel(plans, layout, place, rows, extras, *refs):
+    count = len(refs) - 5 - 2
+    sources, (normed, query, key, value, table, weights, sems) = refs[:count], refs[count:]
     made, first = [], 0
     for m in range(3):
         made.append(copies(place[0], sources, plans[m], weights.at[m], sems, first))
@@ -204,6 +243,7 @@
     def _():
         for group in made:
             start_all(group)
+        table[...] = make_table(place[0], extras, layout)
 
     unit_rows, _ = centred_rows(rows[...].astype(F32))
     low = (unit_rows * vector(table, LN1_G) + vector(table, LN1_B)).astype(BF16)
@@ -219,15 +259,17 @@
     value[...] = (dot(low, weights[2]) + vector(table, V_B)).astype(BF16)
 
 
-def project(place, rows, table, group):
+def project(place, rows, extras, group):
     arrays, plans = group
+    extras, layout = extras
     count, width = rows.shape
     return pl.pallas_call(
-        functools.partial(project_kernel, plans),
+        functools.partial(project_kernel, plans, layout),
         grid=(count // TILE,),
-        in_specs=[SMEM, tile_of(width), whole(table.shape)] + [ANY] * len(arrays),
-        out_specs=[tile_of(width)] * 4,
-        out_shape=[jax.ShapeDtypeStruct(rows.shape, BF16)] * 4,
+        in_specs=[SMEM, tile_of(width), whole(extras.shape)] + [ANY] * len(arrays),
+        out_specs=[tile_of(width)] * 4 + [whole((16, width))],
+        out_shape=[jax.ShapeDtypeStruct(rows.shape, BF16)] * 4
+        + [jax.ShapeDtypeStruct((16, width), F32)],
         scratch_shapes=[
             pltpu.VMEM((3, width, width), BF16),
             pltpu.SemaphoreType.DMA((sum(len(p) for p in plans[:3]),)),
@@ -235,7 +277,7 @@
         compiler_params=params(60),
         cost_estimate=cost(6 * count * width * width, 14 * count * width),
         name="project",
-    )(place, rows, table, *arrays)
+    )(place, rows, extras, *arrays)
 
 
 def segments(lengths, pack, position):
@@ -304,7 +346,7 @@
         ],
         input_output_aliases={4 + i: i for i in range(len(earlier))},
         compiler_params=params(60),
-        cost_estimate=cost(16 * rows * rows * width, 8 * rows * width, 12 * rows * rows),
+        cost_estimate=cost(16 * rows * rows * width, 8 * rows * width) if earlier else cost(0, 0),
         name="attend",
     )(lengths, query, key, value, *earlier)
 
@@ -388,13 +430,13 @@
     grad_out = jnp.where(live, cotangent[...].astype(F32), 0.0)
     grad_down[...] = (grad_out * vector(table, MLP_S)).astype(BF16)
 
-    @pl.when(pl.program_id(0) == 0)
-    def _():
-        for group in made[1:]:
-            wait_all(group)
-
     width = low.shape[1]
     for m in range(len(up_plans)):
+
+        @pl.when(pl.program_id(0) == 0)
+        def _(m=m):
+            wait_all(made[m + 1])
+
         part = slice(m * width, (m + 1) * width)
         up = dot(low, up_w[m]) + vector(table, UP_B + m)
         value, rate = gelu_pair(up)
@@ -607,6 +649,65 @@
     )(place, *(left for left, _ in pairs), *(right for _, right in pairs))
 
 
+def plain_kernel(steps, *refs):
+    lefts, rights = refs[: len(steps)], refs[len(steps) : -2]
+    out, flat = refs[-2:]
+    step = pl.program_id(0)
+    first, at_right = 0, 0
+    for left, counts in zip(lefts, steps):
+
+        @pl.when(step == first)
+        def _(left=left):
+            for at in range(0, flat.shape[0], 128):
+                block = left[:, at : at + 128].astype(F32)
+                flat[at : at + 128, :] = jnp.transpose(block).astype(BF16)
+
+        for count in counts:
+
+            @pl.when((step >= first) & (step < first + count))
+            def _(right=rights[at_right]):
+                out[...] = dot(flat[...], right[...]).astype(BF16).reshape(out.shape)
+
+            first += count
+            at_right += 1
+
+
+def plain_outer(pairs, width):
+    count, height = pairs[0][0].shape
+    steps = [[right.shape[1] // width for right in rights] for _, rights in pairs]
+    total = sum(sum(counts) for counts in steps)
+    places = lax.axis_size("wide")
+    right_specs, first = [], 0
+    for own in sum(steps, []):
+        right_specs.append(
+            pl.BlockSpec(
+                (count, width),
+                lambda i, first=first, own=own: (0, jnp.clip(i - first, 0, own - 1)),
+            )
+        )
+        first += own
+    if direct():
+        spec = pl.BlockSpec((8, 1, height // 8, width), lambda i: (0, i, 0, 0))
+        shape = jax.ShapeDtypeStruct((8, total, height // 8, width), BF16)
+    else:
+        spec = pl.BlockSpec((height, width), lambda i: (0, i))
+        shape = jax.ShapeDtypeStruct((height, total * width), BF16)
+    out = pl.pallas_call(
+        functools.partial(plain_kernel, steps),
+        grid=(total,),
+        in_specs=[whole((count, height))] * len(pairs) + right_specs,
+        out_specs=spec,
+        out_shape=shape,
+        scratch_shapes=[pltpu.VMEM((height, count), BF16)],
+        compiler_params=params(60),
+        cost_estimate=cost(2 * count * height * total * width, 2 * (count + height) * total * width),
+        name="plain_outer",
+    )(*(left for left, _ in pairs), *(right for _, rights in pairs for right in rights))
+    if not direct():
+        out = out.reshape(places, height // places, total, width).transpose(0, 2, 1, 3)
+    return out.reshape(places, -1, width)
+
+
 def wide_outer_kernel(place, left, right, out, flat):
     @pl.when(pl.program_id(0) == 0)
     def _():
@@ -614,7 +715,10 @@
             block = left[:, at : at + 128].astype(F32)
             flat[at : at + 128, :] = jnp.transpose(block).astype(BF16)
 
-    out[0] = dot(flat[...], right[...]).astype(BF16)
+    value = dot(flat[...], right[...]).astype(BF16)
+    half = value.shape[1] // 2
+    out[0] = value[:, :half]
+    out[1] = value[:, half:]
 
 
 def wide_outer(place, left, right):
@@ -624,9 +728,9 @@
     step = columns // steps
     return pl.pallas_call(
         wide_outer_kernel,
-        grid=(steps,),
-        in_specs=[SMEM, whole(left.shape), pl.BlockSpec((count, step), lambda i: (0, i))],
-        out_specs=pl.BlockSpec((1, height, step), lambda i: (i, 0, 0)),
+        grid=(steps // 2,),
+        in_specs=[SMEM, whole(left.shape), pl.BlockSpec((count, 2 * step), lambda i: (0, i))],
+        out_specs=pl.BlockSpec((2, height, step), lambda i: (i, 0, 0)),
         out_shape=jax.ShapeDtypeStruct((steps, height, step), BF16),
         scratch_shapes=[pltpu.VMEM((height, count), BF16)],
         compiler_params=params(60),
@@ -699,6 +803,41 @@
     return tuple(held[:, i] for i in range(4))
 
 
+def add_kernel(mine, other, own, *halves):
+    for quarter in range(4):
+        total = (mine[quarter].astype(F32) + other[quarter].astype(F32)).astype(BF16)
+        if quarter == 0:
+            own[0] = total
+            continue
+        one, two = halves[2 * quarter - 2], halves[2 * quarter - 1]
+        one[0] = total[: one.shape[1]]
+        two[0] = total[one.shape[1] :]
+
+
+def quarters_added(mine, other):
+    rows, columns = mine.shape[1:]
+    half = rows // 32 * 16
+    if not direct():
+        own, *rest = quarters(add_low(mine, other))
+        return [own] + [(piece[:, :half], piece[:, half:]) for piece in rest]
+    shapes = [jax.ShapeDtypeStruct((1, rows, columns), BF16)]
+    for _ in range(3):
+        shapes.append(jax.ShapeDtypeStruct((1, half, columns), BF16))
+        shapes.append(jax.ShapeDtypeStruct((1, rows - half, columns), BF16))
+    step = columns // 6
+    own, *parts = pl.pallas_call(
+        add_kernel,
+        grid=(6,),
+        in_specs=[pl.BlockSpec((4, rows, step), lambda i: (0, 0, i))] * 2,
+        out_specs=[pl.BlockSpec((1, s.shape[1], step), lambda i: (0, 0, i)) for s in shapes],
+        out_shape=shapes,
+        compiler_params=params(60),
+        cost_estimate=cost(4 * rows * columns, 24 * rows * columns),
+        name="core_add",
+    )(mine, other)
+    return own, parts[0:2], parts[2:4], parts[4:6]
+
+
 def halve(total):
     for bit in reversed(range(3, wide_bits())):
         count = total.shape[0] // 2
@@ -723,6 +862,41 @@
     for block in moved:
         total = total + block.astype(F32)
     return total
+
+
+def column_starts(columns, part, layers):
+    starts = [at * part // 128 * 128 for at in range(layers)]
+    room = max(-(-(at + 1) * part // 128) * 128 - starts[at] for at in range(layers))
+    return [min(start, columns - room) for start in starts], room
+
+
+def columns_blocks(blocks, part, layers):
+    here = lax.axis_index("narrow")
+    starts, room = column_starts(blocks.shape[1], part, layers)
+    choices = [blocks[:, start : start + room] for start in starts]
+
+    def block_of(index):
+        chosen = choices[-1]
+        for at in reversed(range(layers - 1)):
+            chosen = jnp.where(index == at, choices[at], chosen)
+        return chosen
+
+    own, *sends = [block_of(lax.rem(here + step, layers)) for step in range(layers)]
+    return own, sends, shifts(layers)
+
+
+def own_columns(own, moved, part, columns):
+    layers = len(moved) + 1
+    here = lax.axis_index("narrow")
+    starts, _ = column_starts(columns, part, layers)
+    total = own.astype(F32)
+    for block in moved:
+        total = total + block.astype(F32)
+    cuts = [total[:, at * part - start : (at + 1) * part - start] for at, start in enumerate(starts)]
+    result = cuts[-1]
+    for at in reversed(range(layers - 1)):
+        result = jnp.where(here == at, cuts[at], result)
+    return result
 
 
 def by_core(grad, parts):
@@ -762,11 +936,9 @@
     cotangent = cotangent.reshape(-1, width)
 
     small = [ln1_gain, ln1_bias, q_bias, v_bias, out_bias, attn_scale, ln2_gain, ln2_bias, down_bias, mlp_scale]
-    small_spot = own_spot(places, layers, ln1_gain.shape[0], width)
-    up_spot = own_spot(places, layers, up_bias.shape[0], width)
-    table = jnp.zeros((16, width), BF16)
-    table = lax.dynamic_update_slice(table, jnp.stack(small), (0, small_spot[1]))
-    table = lax.dynamic_update_slice(table, up_bias[None], (UP_B + up_spot[0], up_spot[1]))
+    piece, long = ln1_gain.shape[0], up_bias.shape[0]
+    small_spot = own_spot(places, layers, piece, width)
+    up_spot = own_spot(places, layers, long, width)
     stages = all_stages()
 
     def spread_table(table, stages):
@@ -774,65 +946,51 @@
             table = table + stage(table)
         return table
 
-    one = [w_qkv] * (layers - 1), shifts(layers)
-    table, one = beside(lambda v: spread_table(v, stages[2:]), table, *one)
-    one = by_origin([w_qkv, *one])
-    one = jnp.concatenate(jnp.split(side_by_side(one), 3, axis=1))
+    extra = jnp.pad(jnp.stack(small), ((0, 0), (0, part - piece)))
+    extra = jnp.concatenate([extra, jnp.pad(up_bias[None], ((0, 5), (0, part - long)))])
+    early = jnp.concatenate([w_qkv, extra])
+
+    moved = [move(early) for move in shifts(layers)]
+    one = by_origin([early, *moved])
+    extra = side_by_side(one[:, short : short + 10, :piece])
+    extra = jnp.pad(extra, ((0, 6), (0, width - layers * piece)))
+    long_row = side_by_side(one[:, short + 10 : short + 11, :long])
+    long_row = jnp.pad(long_row, ((10, 5), (0, width - layers * long)))
+    one = side_by_side(one[:, :short])
+    one = jnp.concatenate([*jnp.split(one, 3, axis=1), extra + long_row])
     held = double(one)
     up_out = jnp.concatenate([w_up, w_out], axis=1)
     sends = [held, held] + [up_out] * (layers - 1)
-    table, moved = beside(
-        lambda v: spread_table(v, stages[:2]).astype(F32), table, sends, planes() + shifts(layers)
-    )
-    near, far, *two = moved
+    (up_out,), (near, far, *two) = beside(lambda v: v, (up_out,), sends, planes() + shifts(layers))
     half = near.shape[1] // 32 * 16
     sends = [near[:, :half], far[:, half:], jnp.concatenate([held, near, far])]
-    two, moved = beside(
-        lambda v: v, by_origin([up_out, *two]), sends, corners() + [lambda v: cross(v, 0)]
+    two = by_origin([up_out, *two])
+    two = jnp.concatenate([two[:, :, :width].reshape(-1, width), side_by_side(two[:, :, width:])])
+    two, sends = lax.optimization_barrier((two, sends))
+    two = in_order(lax.all_gather(two, "wide"), layers + 1)
+    moves = corners() + [lambda v: cross(v, 0)]
+    moved = lax.optimization_barrier([move(send) for move, send in zip(moves, sends)])
+    planes_one = held, near, far, jnp.concatenate(moved[:2], axis=1)
+    one, extras = matrices(planes_one, (moved[2], cross(planes_one[3], 0)), 3, layers * piece, layers * long)
+    side_down = jnp.concatenate(jnp.split(w_down, layers, axis=0), axis=1)
+
+    (normed, query, key, value, table), three = beside(
+        lambda v: project(place, v, extras, one), rows, [side_down] * (layers - 1), shifts(layers)
     )
-    planes_one = held, near, far, jnp.concatenate(moved[:2], axis=1)
-    other_three = moved[2]
-    two = jnp.concatenate([two[:, :, :width].reshape(-1, width), side_by_side(two[:, :, width:])])
-    held_two = double(two)
-    half = two.shape[0] // 32 * 16
-    one = matrices(planes_one, (other_three, cross(planes_one[3], 0)), 3)
-
-    first, second = held_two[:, :half], held_two[:, half:]
-    (normed, query, key, value), (near_one, far_one) = beside(
-        lambda v: project(place, v, table, one), rows, [first, first], planes()
-    )
-    side_down = jnp.concatenate(jnp.split(w_down, layers, axis=0), axis=1)
-    sends = [second, second] + [side_down] * (layers - 1)
-    attention, (near_two, far_two, *three) = beside(
-        lambda v: attend(lengths, v, key, value, 0), query, sends, planes() + shifts(layers)
-    )
-    near = jnp.concatenate([near_one, near_two], axis=1)
-    far = jnp.concatenate([far_one, far_two], axis=1)
-    sends = [near_one, far_two, jnp.concatenate([held_two, near, far])]
-    for pack in range(1, packs):
-        run = functools.partial(attend, lengths, query, key, value, pack)
-        if pack == packs - 1:
-            attention, moved = beside(run, attention, sends, corners() + [lambda v: cross(v, 0)])
-        else:
-            attention = run(attention)
-    mixed, log_total = attention
-    planes_two = held_two, near, far, jnp.concatenate(moved[:2], axis=1)
-    two = matrices(planes_two, (moved[2], cross(planes_two[3], 0)), layers + 1)
     three = by_origin([side_down, *three])
     three = jnp.concatenate(
         [side_by_side(three[:, :, i * quarter : (i + 1) * quarter]) for i in range(layers)]
     )
-    held = double(three)
-    (branch, normed_two, active, slope, grad_down), (near, far) = beside(
-        lambda v: hidden(place, lengths, rows, v, cotangent, table, two), mixed, [held, held], planes()
+    query, three = lax.optimization_barrier((query, three))
+    three = in_order(lax.all_gather(three, "wide"), 1)
+    attention = attend(lengths, query, key, value, 0)
+    for pack in range(1, packs):
+        attention = attend(lengths, query, key, value, pack, attention)
+    mixed, log_total = attention
+    branch, normed_two, active, slope, grad_down = hidden(
+        place, lengths, rows, mixed, cotangent, table, two
     )
-    half = near.shape[1] // 32 * 16
-    sends = [near[:, :half], far[:, half:], jnp.concatenate([held, near, far])]
-    grad_w_down, moved = beside(
-        lambda v: wide_outer(place, v, active), grad_down, sends, corners() + [lambda v: cross(v, 0)]
-    )
-    planes_three = held, near, far, jnp.concatenate(moved[:2], axis=1)
-    three = matrices(planes_three, (moved[2], cross(planes_three[3], 0)), 1)
+    grad_w_down = wide_outer(place, grad_down, active)
     active = after(active, grad_w_down)
     if places != 8:
         grad_w_down = grad_w_down.reshape(8, width, places // 8, -1).transpose(0, 2, 1, 3)
@@ -844,76 +1002,52 @@
     mine, theirs = by_core(
         outer(place, [(normed_two, grad_hidden), (mixed, grad_branch)], width), layers + 1
     )
-    grads, (moved,) = beside(
+    grads, (other,) = beside(
         lambda v: attend_back(lengths, query, key, value, v, log_total, 0),
         grad_mixed,
         [theirs],
         [lambda v: cross(v, 0)],
     )
-    own, near, far, corner = quarters(add_low(mine, moved))
-    half = own.shape[1] // 32 * 16
+    own_up, near, far, corner = quarters_added(mine, other)
     for pack in range(1, packs):
         run = functools.partial(attend_back, lengths, query, key, value, grad_mixed, log_total, pack)
         if pack == packs - 1:
-            sends = [corner[:, :half], corner[:, half:]]
-            grads, moved = beside(run, grads, sends, planes())
+            sends = [corner[0], corner[1], near[0], far[1]]
+            grads, moved = beside(run, grads, sends, planes() + planes())
         else:
             grads = run(grads)
-    far_part = add_low(far[:, :half], moved[0])
-    near_part = add_low(near[:, half:], moved[1])
-    grad_w_qkv, (near, far) = beside(
-        lambda v: outer(place, [(normed, v)], width),
-        jnp.concatenate(grads, axis=1),
-        [near[:, :half], far[:, half:]],
-        planes(),
+    near_one, far_two = moved[2:]
+    sends = [add_low(near[1], moved[1]), add_low(far[0], moved[0])]
+    grads, sends = lax.optimization_barrier((grads, sends))
+    grad_w_qkv, (near_two, far_one) = beside(
+        lambda v: plain_outer([(normed, v)], width), grads, sends, planes()
     )
-    mine, theirs = by_core(grad_w_qkv, 3)
+    total_qkv = lax.psum_scatter(grad_w_qkv, "wide")
+    own_up = own_up.astype(F32) + jnp.concatenate([near_one, near_two], axis=1).astype(F32)
+    own_up = own_up + jnp.concatenate([far_one, far_two], axis=1).astype(F32)
+    total_up = halve(own_up.astype(BF16))
+    total_out = total_up[layers * short :].reshape(short, layers, quarter).transpose(1, 0, 2)
+    total_up = total_up[: layers * short].reshape(layers, short, width)
+    total_up = jnp.concatenate([total_up, total_out], axis=2)
+    total_down = total_down.reshape(layers, quarter, -1)
+    sends, moves = spread_blocks(total_up)
+    down_sends, down_moves = spread_blocks(total_down)
     grad_q, grad_k, grad_v = grads
-    near_part, far_part, theirs, total_down, mine = lax.optimization_barrier(
-        (near_part, far_part, theirs, total_down, mine)
-    )
-    sends, moves = spread_blocks(total_down.reshape(layers, quarter, -1))
     (grad_rows, stats_one), moved = beside(
         lambda v: inputs_back(place, rows, grad_middle, v, grad_k, grad_v, table, one),
         grad_q,
-        [near_part, far_part, theirs, *sends],
-        planes() + [lambda v: cross(v, 0)] + moves,
+        sends + down_sends,
+        moves + down_moves,
     )
-    near_part, far_part, other, *down = moved
-
-    sums = jnp.concatenate([stats_one, stats_two, hidden_stats])
-    total_down = add_blocks(total_down.reshape(layers, quarter, -1), down).T
-    near = jnp.concatenate([near, near_part], axis=1).astype(F32)
-    far = jnp.concatenate([far_part, far], axis=1).astype(F32)
-    total_up = halve((own.astype(F32) + near + far).astype(BF16))
-    total_out = total_up[layers * short :].reshape(short, layers, quarter).transpose(1, 0, 2)
-    total_up = total_up[: layers * short].reshape(layers, short, width)
-    total_up = jnp.concatenate([total_up, total_out], axis=2)
-    up_sends, up_moves = spread_blocks(total_up)
-    own, near, far, corner = quarters(add_low(mine, other))
-    half = own.shape[1] // 32 * 16
-    split = len(up_sends) - 1
-    sums, moved = beside(
-        lambda v: v + stages[-1](v),
-        sums,
-        [corner[:, :half], corner[:, half:]] + up_sends[:split],
-        planes() + up_moves[:split],
-    )
-    up_parts = moved[2:]
-    far = jnp.concatenate([add_low(far[:, :half], moved[0]), far[:, half:]], axis=1)
-    near = jnp.concatenate([near[:, :half], add_low(near[:, half:], moved[1])], axis=1)
-    sums, moved = beside(
-        lambda v: spread_table(v, stages[:-3]), sums, [near, far] + up_sends[split:], planes() + up_moves[split:]
-    )
-    total_qkv = own.astype(F32) + moved[0].astype(F32) + moved[1].astype(F32)
-    total_qkv = halve(total_qkv.astype(BF16))
-    total_qkv = jnp.concatenate([total_qkv[i * short : (i + 1) * short] for i in range(3)], axis=1)
-    total_qkv = total_qkv.reshape(short, layers, part).transpose(1, 0, 2)
-    sends, moves = spread_blocks(total_qkv)
-    up_parts += moved[2:]
-    sums, moved = beside(lambda v: spread_table(v, stages[-3:-1]), sums, sends, moves)
-    total_qkv = add_blocks(total_qkv, moved)
+    up_parts, down_parts = moved[: len(sends)], moved[len(sends) :]
     total_up = add_blocks(total_up, up_parts)
+    total_down = add_blocks(total_down, down_parts).T
+    sums = spread_table(jnp.concatenate([stats_one, stats_two, hidden_stats]), stages[2:])
+    total_qkv = after(total_qkv, sums)
+    blocks = jnp.concatenate([total_qkv[i * short : (i + 1) * short] for i in range(3)], axis=1)
+    own_block, sends, moves = columns_blocks(blocks, part, layers)
+    sums, moved = beside(lambda v: spread_table(v, stages[:2]), sums, sends, moves)
+    total_qkv = own_columns(own_block, moved, part, blocks.shape[1])
 
     own = lax.dynamic_slice(sums, (0, small_spot[1]), (16, ln1_gain.shape[0]))
     own_up = lax.dynamic_slice(sums, (16 + up_spot[0], up_spot[1]), (1, up_bias.shape[0]))[0]

time: 361 us -> 313 us (0.87); the launches traced: 355 us -> 312 us
  starting transfers between devices: 70.6 us -> 46.6 us
  waiting for transfers between devices: 47.4 us -> 66.2 us
  local copies, waits for them, and re-layouts: 35.6 us -> 18.3 us
  other arithmetic: 26.2 us -> 9.83 us
    ppermute x60 -> x36, starting transfers between devices: 70.6 us -> 46.1 us  [exchange(): lax.ppermute(value, axis_name, [(i, partner(i) % size) for i in range(siz...]
    ppermute x60 -> x36, waiting for transfers between devices: 47.4 us -> 64.3 us  [exchange(): lax.ppermute(value, axis_name, [(i, partner(i) % size) for i in range(siz...]
    pallas_call x2 -> x4, Pallas kernels: 21.7 us -> 34.4 us  [the longest x1 10.4 us: project(): pl.pallas_call(functools.partial(project_kernel, plans, layout), grid=(co...]
    pallas_call x2 -> x1, Pallas kernels: 21.7 us -> 13.2 us  [outer(): pl.pallas_call(functools.partial(outer_kernel, direct(), steps), grid=(to...]
    unnamed x108 -> x67, local copies, waits for them, and re-layouts: 16.2 us -> 8.99 us
    reshape x2 -> x0, other arithmetic: 5.84 us -> none  [quarters(): held = held.reshape((-1, 4) + held.shape[1:])]
    pallas_call x1, Pallas kernels: 24.5 us -> 19.3 us  [hidden(): pl.pallas_call(functools.partial(hidden_kernel, plans, len(arrays)), grid...]
    slice x7 -> x0, local copies, waits for them, and re-layouts: 4.51 us -> none  [the longest x2 1.76 us: shards(): near[:, :half]]
  transfers between devices with their start and end apart: 61 -> 40, of which waited for: 18 -> 14; matrix products, arithmetic and copies ran while one was open for 10% -> 5% of each run, Pallas kernels for 45% -> 50%
where the time goes in v3:
time: 313 us; the launch traced here: 312 us
  Pallas kernels  157 us (50%)
  waiting for transfers between devices  66.2 us (21%)
  starting transfers between devices  46.6 us (15%)
  local copies, waits for them, and re-layouts  18.3 us (6%)
  between operations  14.6 us (5%)
  other arithmetic  9.83 us (3%)
    ppermute x36, waiting for transfers between devices, exchange(): lax.ppermute(value, axis_name, [(i, partner(i) % size) for i in range(siz...  64.3 us
    ppermute x36, starting transfers between devices, exchange(): lax.ppermute(value, axis_name, [(i, partner(i) % size) for i in range(siz...  46.1 us
    pallas_call x1, Pallas kernels, back(): pl.pallas_call(functools.partial(back_kernel, *plans, sizes), grid=(count...  29.9 us
    pallas_call x2, Pallas kernels, attend_back(): pl.pallas_call(functools.partial(attend_back_kernel, pack), grid=(pairs,)...  27.1 us
    pallas_call x2, Pallas kernels, attend(): pl.pallas_call(functools.partial(attend_kernel, pack), grid=(pairs,), in_...  21.4 us
    pallas_call x1, Pallas kernels, hidden(): pl.pallas_call(functools.partial(hidden_kernel, plans, len(arrays)), grid...  19.3 us
    pallas_call x1, Pallas kernels, outer(): pl.pallas_call(functools.partial(outer_kernel, direct(), steps), grid=(to...  13.2 us
    pallas_call x1, Pallas kernels, inputs_back(): pl.pallas_call(functools.partial(inputs_kernel, plans), grid=(count // TI...  11.4 us
  transfers between devices with their start and end apart: 40, of which 14 were waited for; matrix products, arithmetic and copies ran while one was open for 5% of the time, Pallas kernels for 50%

profile of v3, /device:TPU:0, one launch (start us, length us, event | category | flops | bytes accessed | tf_op | source)
XLA Modules:
  0.0 312.3 jit_solution(14244845308103787875)
XLA Ops:
  7.3 1.5 stack.82
  9.7 5.1 %collective-permute-start = (bf16[112,576]{1,0:T(8,128)(2,1)S(1)}, bf16[112,576]{1,0:T(8,128)(2,1)S(1)}, u32[]{:S(2)}, u32[]{:S(2)}) collective-permute-start(bf16[112,576]{1,0:T(8,128)(2,1)S(1)} %fusion.22), channel_id=1, source_target_pairs={{0,3},{1,0},{2,1},{3,2},{4,7},{5,4},{6,5},{7,6},{8,11},{9,8},{10,9... | collective-permute-start | bytes 387080 | tf_op jit(solution)/shard_map/ppermute | solution.py:22
  16.8 2.2 collective-permute-done
  19.0 7.9 %collective-permute-done.1 = bf16[112,576]{1,0:T(8,128)(2,1)S(1)} collective-permute-done((bf16[112,576]{1,0:T(8,128)(2,1)S(1)}, bf16[112,576]{1,0:T(8,128)(2,1)S(1)}, u32[]{:S(2)}, u32[]{:S(2)}) %collective-permute-start.1) | collective-permute-done | bytes 129056 | tf_op jit(solution)/shard_map/ppermute | solution.py:22
  27.6 1.6 collective-permute-start.3
  29.1 1.5 collective-permute-start.4
  31.5 1.9 collective-permute-start.6
  33.4 2.9 collective-permute-start.7
  36.3 4.0 %collective-permute-done.5 = bf16[96,960]{1,0:T(8,128)(2,1)S(1)} collective-permute-done((bf16[96,960]{1,0:T(8,128)(2,1)S(1)}, bf16[96,960]{1,0:T(8,128)(2,1)S(1)}, u32[]{:S(2)}, u32[]{:S(2)}) %collective-permute-start.5) | collective-permute-done | bytes 184352 | tf_op jit(solution)/shard_map/ppermute | solution.py:22
  40.3 6.3 %collective-permute-done.6 = bf16[96,960]{1,0:T(8,128)(2,1)S(1)} collective-permute-done((bf16[96,960]{1,0:T(8,128)(2,1)S(1)}, bf16[96,960]{1,0:T(8,128)(2,1)S(1)}, u32[]{:S(2)}, u32[]{:S(2)}) %collective-permute-start.6) | collective-permute-done | bytes 184352 | tf_op jit(solution)/shard_map/ppermute | solution.py:22
  51.8 4.1 %collective-permute-start.12 = (bf16[96,768]{1,0:T(8,128)(2,1)}, bf16[96,768]{1,0:T(8,128)(2,1)S(1)}, u32[]{:S(2)}, u32[]{:S(2)}) collective-permute-start(bf16[96,768]{1,0:T(8,128)(2,1)} %pad_maximum_fusion.5), channel_id=1, source_target_pairs={{0,1},{1,2},{2,3},{3,0},{4,5},{5,6},{6,7},{7,4},{8,9},{9,10},{10,1... | collective-permute-start | bytes 442376 | tf_op jit(solution)/shard_map/ppermute | solution.py:22
  55.9 2.2 collective-permute-start.13
  60.4 10.8 %collective-permute-done.8 = bf16[1,144,768]{2,1,0:T(8,128)(2,1)S(1)} collective-permute-done((bf16[1,144,768]{2,1,0:T(8,128)(2,1)}, bf16[1,144,768]{2,1,0:T(8,128)(2,1)S(1)}, u32[]{:S(2)}, u32[]{:S(2)}) %collective-permute-start.8) | collective-permute-done | bytes 221216 | tf_op jit(solution)/shard_map/ppermute | solution.py:22
  72.6 1.5 constant_dynamic-update-slice_fusion.3
  74.9 10.4 %project.1 = (bf16[1024,768]{1,0:T(8,128)(2,1)}, bf16[1024,768]{1,0:T(8,128)(2,1)}, bf16[1024,768]{1,0:T(8,128)(2,1)}, bf16[1024,768]{1,0:T(8,128)(2,1)}, f32[16,768]{1,0:T(8,128)}) custom-call(s32[1]{0:T(128)} %bitcast.place, bf16[1024,768]{1,0:T(8,128)(2,1)} %bitcast.204, bf16[8,16,768]{2,1,0:T(8,128)(2,1)} %constant_dynamic-update-slice_fusion.2.extras, ...), custom_call_target="tpu_custom_call" | custom-call | flops 3623878656 | bytes 11010048 | tf_op jit(solution)/shard_map/project/pallas_call | solution.py:266
  87.2 10.7 %attend.2 = (bf16[1024,768]{1,0:T(8,128)(2,1)}, f32[2,6,2,512]{3,2,1,0:T(2,128)}) custom-call(s32[2,6]{1,0:T(2,128)} %lengths.11, bf16[1024,768]{1,0:T(8,128)(2,1)} %get-tuple-element.175.query, bf16[1024,768]{1,0:T(8,128)(2,1)} %get-tuple-element.176.key, bf16[1024,768]{1,0:T(8,128)(2,1)} %get-tuple-element.177.value), custom_call_target="tpu_custom_call" | custom-call | tf_op jit(solution)/shard_map/attend/pallas_call | solution.py:338
  98.0 10.7 %attend.3 = (bf16[1024,768]{1,0:T(8,128)(2,1)}, f32[2,6,2,512]{3,2,1,0:T(2,128)}) custom-call(s32[2,6]{1,0:T(2,128)} %lengths.11, bf16[1024,768]{1,0:T(8,128)(2,1)} %get-tuple-element.175.query, bf16[1024,768]{1,0:T(8,128)(2,1)} %get-tuple-element.176.key, bf16[1024,768]{1,0:T(8,128)(2,1)} %get-tuple-element.177.value, ...), custom_call_target="tpu_custom_call", output_to_operand_aliasing={{0}: (4, {}), {1}: (5, {})} | custom-call | flops 3221225472 | bytes 3145728 | tf_op jit(solution)/shard_map/attend/pallas_call | solution.py:338
  108.6 19.3 %hidden.1 = (f32[1024,768]{1,0:T(8,128)}, bf16[1024,768]{1,0:T(8,128)(2,1)}, bf16[1024,3072]{1,0:T(8,128)(2,1)}, bf16[1024,3072]{1,0:T(8,128)(2,1)}, bf16[1024,768]{1,0:T(8,128)(2,1)}) custom-call(s32[1]{0:T(128)} %bitcast.place, s32[2,6]{1,0:T(2,128)} %lengths.11, bf16[1024,768]{1,0:T(8,128)(2,1)} %bitcast.205, ...), custom_call_target="tpu_custom_call" | custom-call | flops 8455716864 | bytes 20447232 | tf_op jit(solution)/shard_map/hidden/pallas_call | solution.py:451
  128.0 9.6 %wide_outer.1 = bf16[8,768,384]{2,1,0:T(8,128)(2,1)} custom-call(s32[1]{0:T(128)} %bitcast.place, bf16[1024,768]{1,0:T(8,128)(2,1)} %get-tuple-element.185.left.grad_down, bf16[1024,3072]{1,0:T(8,128)(2,1)} %get-tuple-element.186.right.active), custom_call_target="tpu_custom_call" | custom-call | flops 4831838208 | bytes 13762560 | tf_op jit(solution)/shard_map/wide_outer/pallas_call | solution.py:729
  138.0 29.9 %back.1 = (bf16[1024,768]{1,0:T(8,128)(2,1)}, bf16[1024,3072]{1,0:T(8,128)(2,1)}, f32[1024,768]{1,0:T(8,128)}, bf16[1024,768]{1,0:T(8,128)(2,1)}, bf16[1024,768]...) custom-call(s32[1]{0:T(128)} %bitcast.place, s32[2,6]{1,0:T(2,128)} %lengths.11, bf16[1024,768]{1,0:T(8,128)(2,1)} %bitcast.206, ...), custom_call_target="tpu_custom_call" | custom-call | flops 15703474176 | bytes 31457280 | tf_op jit(solution)/shard_map/back/pallas_call | solution.py:543
  167.8 13.2 %outer.1 = (bf16[4,5,96,768]{3,2,1,0:T(8,128)(2,1)}, bf16[4,5,96,768]{3,2,1,0:T(8,128)(2,1)}) custom-call(s32[1]{0:T(128)} %bitcast.place, bf16[1024,768]{1,0:T(8,128)(2,1)} %get-tuple-element.193.refs_0_, bf16[1024,768]{1,0:T(8,128)(2,1)} %get-tuple-element.180.mixed.refs_1_, bf16[1024,3072]{1,0:T(8,128)(2,1)} %get-tuple-element.194.refs_2_, ...), custom_call_target="tpu_custom_call" | custom-call | flops 6039797760 | bytes 13762560 | tf_op jit(solution)/shard_map/outer/pallas_call | solution.py:639
  181.6 13.5 %attend_back.2 = (bf16[1024,768]{1,0:T(8,128)(2,1)}, bf16[1024,768]{1,0:T(8,128)(2,1)}, bf16[1024,768]{1,0:T(8,128)(2,1)}) custom-call(s32[2,6]{1,0:T(2,128)} %lengths.11, bf16[1024,768]{1,0:T(8,128)(2,1)} %get-tuple-element.175.query, bf16[1024,768]{1,0:T(8,128)(2,1)} %get-tuple-element.176.key, bf16[1024,768]{1,0:T(8,128)(2,1)} %get-tuple-element.177.value, ...), custom_call_target="tpu_custom_call" | custom-call | flops 8053063680 | bytes 5505024 | tf_op jit(solution)/shard_map/attend_back/pallas_call | solution.py:380
  195.1 1.5 copy-done.1
  196.7 5.9 %core_add.1 = (bf16[1,480,768]{2,1,0:T(8,128)(2,1)}, bf16[1,240,768]{2,1,0:T(8,128)(2,1)}, bf16[1,240,768]{2,1,0:T(8,128)(2,1)}, bf16[1,240,768]{2,1,0:T(8,128)(...) custom-call(bf16[4,480,768]{2,1,0:T(8,128)(2,1)} %bitcast.180, ...), custom_call_target="tpu_custom_call" | custom-call | flops 1474560 | bytes 8847360 | tf_op jit(solution)/shard_map/core_add/pallas_call | solution.py:828
  202.6 1.4 collective-permute-start.16
  204.3 1.3 collective-permute-start.18
  205.5 1.1 collective-permute-start.19
  206.7 13.6 %attend_back.3 = (bf16[1024,768]{1,0:T(8,128)(2,1)}, bf16[1024,768]{1,0:T(8,128)(2,1)}, bf16[1024,768]{1,0:T(8,128)(2,1)}) custom-call(s32[2,6]{1,0:T(2,128)} %lengths.11, bf16[1024,768]{1,0:T(8,128)(2,1)} %get-tuple-element.175.query, bf16[1024,768]{1,0:T(8,128)(2,1)} %get-tuple-element.176.key, ...), custom_call_target="tpu_custom_call", output_to_operand_aliasing={{0}: (6, {}), {1}: (7, {}), {2}: (8, {})} | custom-call | flops 8053063680 | bytes 5505024 | tf_op jit(solution)/shard_map/attend_back/pallas_call | solution.py:380
  223.2 1.1 collective-permute-start.21
  224.4 8.6 %plain_outer.1 = bf16[8,3,96,768]{3,2,1,0:T(8,128)(2,1)} custom-call(bf16[1024,768]{1,0:T(8,128)(2,1)} %get-tuple-element.231.refs_0_, bf16[1024,768]{1,0:T(8,128)(2,1)} %get-tuple-element.240.refs_1_.grad_q, bf16[1024,768]{1,0:T(8,128)(2,1)} %get-tuple-element.241.refs_2_.grad_k, bf16[1024,768]{1,0:T(8,128)(2,1)} %get-tuple-element.242.refs_3_.grad_v), custom_call_target="tpu_custom_call" | custom-call | flops 3623878656 | bytes 8257536 | tf_op jit(solution)/shard_map/plain_outer/pallas_call | solution.py:695
  235.9 1.8 collective-permute-start.25
  237.7 1.2 collective-permute-start.22
  239.0 2.6 collective-permute-start.23
  241.9 1.5 collective-permute-start.26
  243.4 1.2 collective-permute-done.25
  244.6 1.6 collective-permute-start.27
  246.2 11.4 %inputs_back.1 = (f32[1024,768]{1,0:T(8,128)}, f32[8,768]{1,0:T(8,128)}) custom-call(s32[1]{0:T(128)} %bitcast.place, bf16[1024,768]{1,0:T(8,128)(2,1)} %bitcast.207, f32[1024,768]{1,0:T(8,128)} %get-tuple-element.190.grad_middle, bf16[1024,768]{1,0:T(8,128)(2,1)} %get-tuple-element.240.refs_1_.grad_q, bf16[1024,768]{1,0:T(8,128)(2,1)} %get-tuple-element.241.refs_2_.grad_k, ...), custom_call_target="tpu_custom_call" | custom-call | flops 3623878656 | bytes 15728640 | tf_op jit(solution)/shard_map/inputs_back/pallas_call | solution.py:772
  257.6 10.8 %collective-permute-done.27 = bf16[192,384]{1,0:T(8,128)(2,1)S(1)} collective-permute-done((bf16[192,384]{1,0:T(8,128)(2,1)S(1)}, bf16[192,384]{1,0:T(8,128)(2,1)S(1)}, u32[]{:S(2)}, u32[]{:S(2)}) %collective-permute-start.27) | collective-permute-done | bytes 147488 | tf_op jit(solution)/shard_map/ppermute | solution.py:22
  269.9 3.7 %collective-permute-done.28 = f32[24,768]{1,0:T(8,128)S(1)} collective-permute-done((f32[24,768]{1,0:T(8,128)S(1)}, f32[24,768]{1,0:T(8,128)S(1)}, u32[]{:S(2)}, u32[]{:S(2)}) %collective-permute-start.28) | collective-permute-done | bytes 73760 | tf_op jit(solution)/shard_map/ppermute | solution.py:22
  274.4 5.1 %collective-permute-done.29 = f32[24,768]{1,0:T(8,128)S(1)} collective-permute-done((f32[24,768]{1,0:T(8,128)S(1)}, f32[24,768]{1,0:T(8,128)S(1)}, u32[]{:S(2)}, u32[]{:S(2)}) %collective-permute-start.29) | collective-permute-done | bytes 73760 | tf_op jit(solution)/shard_map/ppermute | solution.py:22
  279.7 1.1 collective-permute-done.30
  280.9 1.7 reduce-scatter.5.cloned.1.call-done
  282.6 1.1 fusion.52
  285.3 1.8 collective-permute-start.33
  287.1 1.4 collective-permute-start.34
  288.6 2.8 collective-permute-start.35
  291.5 1.7 fusion.9
  294.6 9.0 %collective-permute-done.32 = f32[24,768]{1,0:T(8,128)S(1)} collective-permute-done((f32[24,768]{1,0:T(8,128)S(1)}, f32[24,768]{1,0:T(8,128)S(1)}, u32[]{:S(2)}, u32[]{:S(2)}) %collective-permute-start.32) | collective-permute-done | bytes 73760 | tf_op jit(solution)/shard_map/ppermute | solution.py:22
  (165 shorter events, 30.5 us)
Async XLA Ops:
  7.2 19.8 %copy-start.16 = (bf16[96]{0:T(256)(128)(2,1)S(1)}, bf16[96]{0:T(256)(128)(2,1)}, u32[]{:S(2)}) copy-start(bf16[96]{0:T(256)(128)(2,1)} %param.32) | copy-start | bytes 580
  7.2 19.8 %copy-start.4 = (bf16[96,576]{1,0:T(8,128)(2,1)S(1)}, bf16[96,576]{1,0:T(8,128)(2,1)}, u32[]{:S(2)}) copy-start(bf16[96,576]{1,0:T(8,128)(2,1)} %param.20) | copy-start | bytes 331780
  7.2 101.4 %all-gather.5.cloned.1.call-start = ((), (), s32[]{:S(2)}) async-start(), calls=%async_computation.4 | async-start | bytes 6635520 | tf_op jit(solution)/shard_map/all_gather | solution.py:970
  9.7 9.3 %collective-permute-start = (bf16[112,576]{1,0:T(8,128)(2,1)S(1)}, bf16[112,576]{1,0:T(8,128)(2,1)S(1)}, u32[]{:S(2)}, u32[]{:S(2)}) collective-permute-start(bf16[112,576]{1,0:T(8,128)(2,1)S(1)} %fusion.22), channel_id=1, source_target_pairs={{0,3},{1,0},{2,1},{3,2},{4,7},{5,4},{6,5},{7,6},{8,11},{9,8},{10,9... | collective-permute-start | bytes 387080 | tf_op jit(solution)/shard_map/ppermute | solution.py:22
  14.8 12.1 %collective-permute-start.1 = (bf16[112,576]{1,0:T(8,128)(2,1)S(1)}, bf16[112,576]{1,0:T(8,128)(2,1)S(1)}, u32[]{:S(2)}, u32[]{:S(2)}) collective-permute-start(bf16[112,576]{1,0:T(8,128)(2,1)S(1)} %fusion.22), channel_id=1, source_target_pairs={{0,2},{1,3},{2,0},{3,1},{4,6},{5,7},{6,4},{7,5},{8,10},{9,11},{10,... | collective-permute-start | bytes 387080 | tf_op jit(solution)/shard_map/ppermute | solution.py:22
  14.8 12.1 %collective-permute-start.2 = (bf16[112,576]{1,0:T(8,128)(2,1)S(1)}, bf16[112,576]{1,0:T(8,128)(2,1)S(1)}, u32[]{:S(2)}, u32[]{:S(2)}) collective-permute-start(bf16[112,576]{1,0:T(8,128)(2,1)S(1)} %fusion.22), channel_id=1, source_target_pairs={{0,1},{1,2},{2,3},{3,0},{4,5},{5,6},{6,7},{7,4},{8,9},{9,10},{10,1... | collective-permute-start | bytes 387080 | tf_op jit(solution)/shard_map/ppermute | solution.py:22
  27.6 31.1 %copy-start.2 = (bf16[1,304,768]{2,1,0:T(8,128)(2,1)}, bf16[1,304,768]{2,1,0:T(8,128)(2,1)S(1)}, u32[]{:S(2)}) copy-start(bf16[1,304,768]{2,1,0:T(8,128)(2,1)S(1)} %fusion.2.refs_0_) | copy-start | bytes 1400836
  27.6 19.1 %collective-permute-start.3 = (bf16[1,304,768]{2,1,0:T(8,128)(2,1)S(1)}, bf16[1,304,768]{2,1,0:T(8,128)(2,1)S(1)}, u32[]{:S(2)}, u32[]{:S(2)}) collective-permute-start(bf16[1,304,768]{2,1,0:T(8,128)(2,1)S(1)} %fusion.2.refs_0_), channel_id=1, source_target_pairs={{0,8},{4,12},{8,0},{12,4},{16,24},{20,28},{24,16},{28,20},{1,9},{5... | collective-permute-start | bytes 1400840 | tf_op jit(solution)/shard_map/ppermute | solution.py:22
  29.1 17.5 %collective-permute-start.4 = (bf16[1,304,768]{2,1,0:T(8,128)(2,1)S(1)}, bf16[1,304,768]{2,1,0:T(8,128)(2,1)S(1)}, u32[]{:S(2)}, u32[]{:S(2)}) collective-permute-start(bf16[1,304,768]{2,1,0:T(8,128)(2,1)S(1)} %fusion.2.refs_0_), channel_id=1, source_target_pairs={{0,16},{4,20},{8,24},{12,28},{16,0},{20,4},{24,8},{28,12},{1,17},{... | collective-permute-start | bytes 1400840 | tf_op jit(solution)/shard_map/ppermute | solution.py:22
  30.6 9.7 %collective-permute-start.5 = (bf16[96,960]{1,0:T(8,128)(2,1)S(1)}, bf16[96,960]{1,0:T(8,128)(2,1)S(1)}, u32[]{:S(2)}, u32[]{:S(2)}) collective-permute-start(bf16[96,960]{1,0:T(8,128)(2,1)S(1)} %pad_maximum_fusion.4), channel_id=1, source_target_pairs={{0,1},{1,2},{2,3},{3,0},{4,5},{5,6},{6,7},{7,4},{8,9},{9,10},{10,1... | collective-permute-start | bytes 552968 | tf_op jit(solution)/shard_map/ppermute | solution.py:22
  31.5 15.2 %collective-permute-start.6 = (bf16[96,960]{1,0:T(8,128)(2,1)S(1)}, bf16[96,960]{1,0:T(8,128)(2,1)S(1)}, u32[]{:S(2)}, u32[]{:S(2)}) collective-permute-start(bf16[96,960]{1,0:T(8,128)(2,1)S(1)} %pad_maximum_fusion.4), channel_id=1, source_target_pairs={{0,2},{1,3},{2,0},{3,1},{4,6},{5,7},{6,4},{7,5},{8,10},{9,11},{10,... | collective-permute-start | bytes 552968 | tf_op jit(solution)/shard_map/ppermute | solution.py:22
  33.4 13.2 %collective-permute-start.7 = (bf16[96,960]{1,0:T(8,128)(2,1)S(1)}, bf16[96,960]{1,0:T(8,128)(2,1)S(1)}, u32[]{:S(2)}, u32[]{:S(2)}) collective-permute-start(bf16[96,960]{1,0:T(8,128)(2,1)S(1)} %pad_maximum_fusion.4), channel_id=1, source_target_pairs={{0,3},{1,0},{2,1},{3,2},{4,7},{5,4},{6,5},{7,6},{8,11},{9,8},{10,9... | collective-permute-start | bytes 552968 | tf_op jit(solution)/shard_map/ppermute | solution.py:22
  47.3 24.0 %copy-start.3 = (bf16[1,304,768]{2,1,0:T(8,128)(2,1)}, bf16[1,304,768]{2,1,0:T(8,128)(2,1)S(1)}, u32[]{:S(2)}) copy-start(bf16[1,304,768]{2,1,0:T(8,128)(2,1)S(1)} %collective-permute-done.4.refs_2_) | copy-start | bytes 1400836
  50.3 87.6 %all-gather.7.cloned.1.call-start = ((), (), s32[]{:S(2)}) async-start(), calls=%async_computation.5 | async-start | bytes 5308416 | tf_op jit(solution)/shard_map/all_gather | solution.py:985
  50.4 20.8 %collective-permute-start.10 = (bf16[3,304,768]{2,1,0:T(8,128)(2,1)S(1)}, bf16[3,304,768]{2,1,0:T(8,128)(2,1)}, u32[]{:S(2)}, u32[]{:S(2)}) collective-permute-start(bf16[3,304,768]{2,1,0:T(8,128)(2,1)S(1)} %pad_maximum_fusion), channel_id=1, source_target_pairs={{0,4},{4,0},{8,12},{12,8},{16,20},{20,16},{24,28},{28,24},{1,5},{5... | collective-permute-start | bytes 4202504 | tf_op jit(solution)/shard_map/ppermute | solution.py:22
  51.8 33.5 %collective-permute-start.12 = (bf16[96,768]{1,0:T(8,128)(2,1)}, bf16[96,768]{1,0:T(8,128)(2,1)S(1)}, u32[]{:S(2)}, u32[]{:S(2)}) collective-permute-start(bf16[96,768]{1,0:T(8,128)(2,1)} %pad_maximum_fusion.5), channel_id=1, source_target_pairs={{0,1},{1,2},{2,3},{3,0},{4,5},{5,6},{6,7},{7,4},{8,9},{9,10},{10,1... | collective-permute-start | bytes 442376 | tf_op jit(solution)/shard_map/ppermute | solution.py:22
  55.9 29.4 %collective-permute-start.13 = (bf16[96,768]{1,0:T(8,128)(2,1)}, bf16[96,768]{1,0:T(8,128)(2,1)S(1)}, u32[]{:S(2)}, u32[]{:S(2)}) collective-permute-start(bf16[96,768]{1,0:T(8,128)(2,1)} %pad_maximum_fusion.5), channel_id=1, source_target_pairs={{0,2},{1,3},{2,0},{3,1},{4,6},{5,7},{6,4},{7,5},{8,10},{9,11},{10,... | collective-permute-start | bytes 442376 | tf_op jit(solution)/shard_map/ppermute | solution.py:22
  58.1 13.1 %collective-permute-start.9 = (bf16[1,160,768]{2,1,0:T(8,128)(2,1)S(1)}, bf16[1,160,768]{2,1,0:T(8,128)(2,1)S(1)}, u32[]{:S(2)}, u32[]{:S(2)}) collective-permute-start(bf16[1,160,768]{2,1,0:T(8,128)(2,1)S(1)} %copy-done.12), channel_id=1, source_target_pairs={{0,8},{4,12},{8,0},{12,4},{16,24},{20,28},{24,16},{28,20},{1,9},{5... | collective-permute-start | bytes 737288 | tf_op jit(solution)/shard_map/ppermute | solution.py:22
  59.2 11.9 %collective-permute-start.8 = (bf16[1,144,768]{2,1,0:T(8,128)(2,1)}, bf16[1,144,768]{2,1,0:T(8,128)(2,1)S(1)}, u32[]{:S(2)}, u32[]{:S(2)}) collective-permute-start(bf16[1,144,768]{2,1,0:T(8,128)(2,1)} %slice.263), channel_id=1, source_target_pairs={{0,16},{4,20},{8,24},{12,28},{16,0},{20,4},{24,8},{28,12},{1,17},{... | collective-permute-start | bytes 663560 | tf_op jit(solution)/shard_map/ppermute | solution.py:22
  71.2 14.2 %collective-permute-start.14 = (bf16[96,768]{1,0:T(8,128)(2,1)}, bf16[96,768]{1,0:T(8,128)(2,1)S(1)}, u32[]{:S(2)}, u32[]{:S(2)}) collective-permute-start(bf16[96,768]{1,0:T(8,128)(2,1)} %pad_maximum_fusion.5), channel_id=1, source_target_pairs={{0,3},{1,0},{2,1},{3,2},{4,7},{5,4},{6,5},{7,6},{8,11},{9,8},{10,9... | collective-permute-start | bytes 442376 | tf_op jit(solution)/shard_map/ppermute | solution.py:22
  71.2 2.9 collective-permute-start.11
  87.0 147.8 %reduce-scatter.3.cloned.1.call-start = ((), (), s32[]{:S(2)}) async-start(), calls=%async_computation.2 | async-start | bytes 5308416 | tf_op jit(solution)/shard_map/reduce_scatter | solution.py:997
  137.7 144.9 %reduce-scatter.5.cloned.1.call-start = ((), (), s32[]{:S(2)}) async-start(), calls=%async_computation.3 | async-start | bytes 3981312 | tf_op jit(solution)/shard_map/reduce_scatter | solution.py:1025
  181.0 14.1 %collective-permute-start.15 = (bf16[4,480,768]{2,1,0:T(8,128)(2,1)}, bf16[4,480,768]{2,1,0:T(8,128)(2,1)S(1)}, u32[]{:S(2)}, u32[]{:S(2)}) collective-permute-start(bf16[4,480,768]{2,1,0:T(8,128)(2,1)} %bitcast.201), channel_id=1, source_target_pairs={{0,4},{4,0},{8,12},{12,8},{16,20},{20,16},{24,28},{28,24},{1,5},{5... | collective-permute-start | bytes 8847368 | tf_op jit(solution)/shard_map/ppermute | solution.py:22
  202.5 19.8 %copy-start.9 = (bf16[1,240,768]{2,1,0:T(8,128)(2,1)S(1)}, bf16[1,240,768]{2,1,0:T(8,128)(2,1)}, u32[]{:S(2)}) copy-start(bf16[1,240,768]{2,1,0:T(8,128)(2,1)} %get-tuple-element.224) | copy-start | bytes 1105924
  202.5 19.8 %copy-start.10 = (bf16[1,240,768]{2,1,0:T(8,128)(2,1)S(1)}, bf16[1,240,768]{2,1,0:T(8,128)(2,1)}, u32[]{:S(2)}) copy-start(bf16[1,240,768]{2,1,0:T(8,128)(2,1)} %get-tuple-element.226) | copy-start | bytes 1105924
  202.6 17.7 %collective-permute-start.16 = (bf16[1,240,768]{2,1,0:T(8,128)(2,1)}, bf16[1,240,768]{2,1,0:T(8,128)(2,1)S(1)}, u32[]{:S(2)}, u32[]{:S(2)}) collective-permute-start(bf16[1,240,768]{2,1,0:T(8,128)(2,1)} %get-tuple-element.217), channel_id=1, source_target_pairs={{0,8},{4,12},{8,0},{12,4},{16,24},{20,28},{24,16},{28,20},{1,9},{5... | collective-permute-start | bytes 1105928 | tf_op jit(solution)/shard_map/ppermute | solution.py:22
  204.0 16.3 %collective-permute-start.17 = (bf16[1,240,768]{2,1,0:T(8,128)(2,1)}, bf16[1,240,768]{2,1,0:T(8,128)(2,1)S(1)}, u32[]{:S(2)}, u32[]{:S(2)}) collective-permute-start(bf16[1,240,768]{2,1,0:T(8,128)(2,1)} %get-tuple-element.218), channel_id=1, source_target_pairs={{0,16},{4,20},{8,24},{12,28},{16,0},{20,4},{24,8},{28,12},{1,17},{... | collective-permute-start | bytes 1105928 | tf_op jit(solution)/shard_map/ppermute | solution.py:22
  204.3 17.0 %collective-permute-start.18 = (bf16[1,240,768]{2,1,0:T(8,128)(2,1)}, bf16[1,240,768]{2,1,0:T(8,128)(2,1)S(1)}, u32[]{:S(2)}, u32[]{:S(2)}) collective-permute-start(bf16[1,240,768]{2,1,0:T(8,128)(2,1)} %get-tuple-element.219), channel_id=1, source_target_pairs={{0,8},{4,12},{8,0},{12,4},{16,24},{20,28},{24,16},{28,20},{1,9},{5... | collective-permute-start | bytes 1105928 | tf_op jit(solution)/shard_map/ppermute | solution.py:22
  205.5 16.8 %collective-permute-start.19 = (bf16[1,240,768]{2,1,0:T(8,128)(2,1)}, bf16[1,240,768]{2,1,0:T(8,128)(2,1)S(1)}, u32[]{:S(2)}, u32[]{:S(2)}) collective-permute-start(bf16[1,240,768]{2,1,0:T(8,128)(2,1)} %get-tuple-element.220), channel_id=1, source_target_pairs={{0,16},{4,20},{8,24},{12,28},{16,0},{20,4},{24,8},{28,12},{1,17},{... | collective-permute-start | bytes 1105928 | tf_op jit(solution)/shard_map/ppermute | solution.py:22
  222.5 10.4 %collective-permute-start.20 = (bf16[1,240,768]{2,1,0:T(8,128)(2,1)S(1)}, bf16[1,240,768]{2,1,0:T(8,128)(2,1)S(1)}, u32[]{:S(2)}, u32[]{:S(2)}) collective-permute-start(bf16[1,240,768]{2,1,0:T(8,128)(2,1)S(1)} %get-tuple-element.235), channel_id=1, source_target_pairs={{0,8},{4,12},{8,0},{12,4},{16,24},{20,28},{24,16},{28,20},{1,9},{5... | collective-permute-start | bytes 1105928 | tf_op jit(solution)/shard_map/ppermute | solution.py:22
  223.2 9.7 %collective-permute-start.21 = (bf16[1,240,768]{2,1,0:T(8,128)(2,1)S(1)}, bf16[1,240,768]{2,1,0:T(8,128)(2,1)S(1)}, u32[]{:S(2)}, u32[]{:S(2)}) collective-permute-start(bf16[1,240,768]{2,1,0:T(8,128)(2,1)S(1)} %get-tuple-element.236), channel_id=1, source_target_pairs={{0,16},{4,20},{8,24},{12,28},{16,0},{20,4},{24,8},{28,12},{1,17},{... | collective-permute-start | bytes 1105928 | tf_op jit(solution)/shard_map/ppermute | solution.py:22
  235.9 8.7 %collective-permute-start.25 = (bf16[192,384]{1,0:T(8,128)(2,1)S(1)}, bf16[192,384]{1,0:T(8,128)(2,1)S(1)}, u32[]{:S(2)}, u32[]{:S(2)}) collective-permute-start(bf16[192,384]{1,0:T(8,128)(2,1)S(1)} %get-tuple-element.248), channel_id=1, source_target_pairs={{0,1},{1,2},{2,3},{3,0},{4,5},{5,6},{6,7},{7,4},{8,9},{9,10},{10,1... | collective-permute-start | bytes 442376 | tf_op jit(solution)/shard_map/ppermute | solution.py:22
  237.7 30.7 %collective-permute-start.22 = (bf16[96,960]{1,0:T(8,128)(2,1)S(1)}, bf16[96,960]{1,0:T(8,128)(2,1)S(1)}, u32[]{:S(2)}, u32[]{:S(2)}) collective-permute-start(bf16[96,960]{1,0:T(8,128)(2,1)S(1)} %get-tuple-element.245), channel_id=1, source_target_pairs={{0,1},{1,2},{2,3},{3,0},{4,5},{5,6},{6,7},{7,4},{8,9},{9,10},{10,1... | collective-permute-start | bytes 552968 | tf_op jit(solution)/shard_map/ppermute | solution.py:22
  239.0 29.5 %collective-permute-start.23 = (bf16[96,960]{1,0:T(8,128)(2,1)S(1)}, bf16[96,960]{1,0:T(8,128)(2,1)S(1)}, u32[]{:S(2)}, u32[]{:S(2)}) collective-permute-start(bf16[96,960]{1,0:T(8,128)(2,1)S(1)} %get-tuple-element.246), channel_id=1, source_target_pairs={{0,3},{1,0},{2,1},{3,2},{4,7},{5,4},{6,5},{7,6},{8,11},{9,8},{10,9... | collective-permute-start | bytes 552968 | tf_op jit(solution)/shard_map/ppermute | solution.py:22
  241.5 26.9 %collective-permute-start.24 = (bf16[96,960]{1,0:T(8,128)(2,1)S(1)}, bf16[96,960]{1,0:T(8,128)(2,1)S(1)}, u32[]{:S(2)}, u32[]{:S(2)}) collective-permute-start(bf16[96,960]{1,0:T(8,128)(2,1)S(1)} %get-tuple-element.247), channel_id=1, source_target_pairs={{0,2},{1,3},{2,0},{3,1},{4,6},{5,7},{6,4},{7,5},{8,10},{9,11},{10,... | collective-permute-start | bytes 552968 | tf_op jit(solution)/shard_map/ppermute | solution.py:22
  241.9 15.7 %collective-permute-start.26 = (bf16[192,384]{1,0:T(8,128)(2,1)S(1)}, bf16[192,384]{1,0:T(8,128)(2,1)S(1)}, u32[]{:S(2)}, u32[]{:S(2)}) collective-permute-start(bf16[192,384]{1,0:T(8,128)(2,1)S(1)} %get-tuple-element.249), channel_id=1, source_target_pairs={{0,3},{1,0},{2,1},{3,2},{4,7},{5,4},{6,5},{7,6},{8,11},{9,8},{10,9... | collective-permute-start | bytes 442376 | tf_op jit(solution)/shard_map/ppermute | solution.py:22
  244.6 23.8 %collective-permute-start.27 = (bf16[192,384]{1,0:T(8,128)(2,1)S(1)}, bf16[192,384]{1,0:T(8,128)(2,1)S(1)}, u32[]{:S(2)}, u32[]{:S(2)}) collective-permute-start(bf16[192,384]{1,0:T(8,128)(2,1)S(1)} %get-tuple-element.250), channel_id=1, source_target_pairs={{0,2},{1,3},{2,0},{3,1},{4,6},{5,7},{6,4},{7,5},{8,10},{9,11},{10,... | collective-permute-start | bytes 442376 | tf_op jit(solution)/shard_map/ppermute | solution.py:22
  246.2 23.0 %copy-start.15 = (f32[8,768]{1,0:T(8,128)S(1)}, f32[8,768]{1,0:T(8,128)}, u32[]{:S(2)}) copy-start(f32[8,768]{1,0:T(8,128)} %get-tuple-element.254) | copy-start | bytes 73732
  246.2 23.0 %copy-start.14 = (f32[8,768]{1,0:T(8,128)S(1)}, f32[8,768]{1,0:T(8,128)}, u32[]{:S(2)}) copy-start(f32[8,768]{1,0:T(8,128)} %get-tuple-element.255) | copy-start | bytes 73732
  269.2 4.4 %collective-permute-start.28 = (f32[24,768]{1,0:T(8,128)S(1)}, f32[24,768]{1,0:T(8,128)S(1)}, u32[]{:S(2)}, u32[]{:S(2)}) collective-permute-start(f32[24,768]{1,0:T(8,128)S(1)} %constant_dynamic-update-slice_fusion.8), channel_id=1, source_target_pairs={{0,16},{4,20},{8,24},{12,28},{16,0},{20,4},{24,8},{28,12},{1,17},{... | collective-permute-start | bytes 221192 | tf_op jit(solution)/shard_map/ppermute | solution.py:22
  273.6 5.9 %collective-permute-start.29 = (f32[24,768]{1,0:T(8,128)S(1)}, f32[24,768]{1,0:T(8,128)S(1)}, u32[]{:S(2)}, u32[]{:S(2)}) collective-permute-start(f32[24,768]{1,0:T(8,128)S(1)} %add.143), channel_id=1, source_target_pairs={{0,8},{4,12},{8,0},{12,4},{16,24},{20,28},{24,16},{28,20},{1,9},{5... | collective-permute-start | bytes 221192 | tf_op jit(solution)/shard_map/ppermute | solution.py:22
  279.5 1.3 collective-permute-start.30
  284.9 6.6 %collective-permute-start.31 = (f32[24,768]{1,0:T(8,128)S(1)}, f32[24,768]{1,0:T(8,128)S(1)}, u32[]{:S(2)}, u32[]{:S(2)}) collective-permute-start(f32[24,768]{1,0:T(8,128)S(1)} %add.145), channel_id=1, source_target_pairs={{0,1},{1,0},{2,3},{3,2},{4,5},{5,4},{6,7},{7,6},{8,9},{9,8},{10,11... | collective-permute-start | bytes 221192 | tf_op jit(solution)/shard_map/ppermute | solution.py:22
  285.3 18.3 %collective-permute-start.33 = (bf16[96,640]{1,0:T(8,128)(2,1)S(1)}, bf16[96,640]{1,0:T(8,128)(2,1)S(1)}, u32[]{:S(2)}, u32[]{:S(2)}) collective-permute-start(bf16[96,640]{1,0:T(8,128)(2,1)S(1)} %get-tuple-element.258), channel_id=1, source_target_pairs={{0,1},{1,2},{2,3},{3,0},{4,5},{5,6},{6,7},{7,4},{8,9},{9,10},{10,1... | collective-permute-start | bytes 368648 | tf_op jit(solution)/shard_map/ppermute | solution.py:22
  287.1 16.5 %collective-permute-start.34 = (bf16[96,640]{1,0:T(8,128)(2,1)S(1)}, bf16[96,640]{1,0:T(8,128)(2,1)S(1)}, u32[]{:S(2)}, u32[]{:S(2)}) collective-permute-start(bf16[96,640]{1,0:T(8,128)(2,1)S(1)} %get-tuple-element.259), channel_id=1, source_target_pairs={{0,2},{1,3},{2,0},{3,1},{4,6},{5,7},{6,4},{7,5},{8,10},{9,11},{10,... | collective-permute-start | bytes 368648 | tf_op jit(solution)/shard_map/ppermute | solution.py:22
  288.6 15.1 %collective-permute-start.35 = (bf16[96,640]{1,0:T(8,128)(2,1)S(1)}, bf16[96,640]{1,0:T(8,128)(2,1)S(1)}, u32[]{:S(2)}, u32[]{:S(2)}) collective-permute-start(bf16[96,640]{1,0:T(8,128)(2,1)S(1)} %get-tuple-element.260), channel_id=1, source_target_pairs={{0,3},{1,0},{2,1},{3,2},{4,7},{5,4},{6,5},{7,6},{8,11},{9,8},{10,9... | collective-permute-start | bytes 368648 | tf_op jit(solution)/shard_map/ppermute | solution.py:22
  291.4 12.2 %collective-permute-start.32 = (f32[24,768]{1,0:T(8,128)S(1)}, f32[24,768]{1,0:T(8,128)S(1)}, u32[]{:S(2)}, u32[]{:S(2)}) collective-permute-start(f32[24,768]{1,0:T(8,128)S(1)} %add.146), channel_id=1, source_target_pairs={{0,2},{1,3},{2,0},{3,1},{4,6},{5,7},{6,4},{7,5},{8,10},{9,11},{10,... | collective-permute-start | bytes 221192 | tf_op jit(solution)/shard_map/ppermute | solution.py:22
  (10 other events, 33.9 us)
Sparse Core Ops, SparseCore 0:
  50.4 46.5 all-gather.4
  99.0 38.9 all-gather.6
  141.4 53.8 reduce-scatter.2
  233.1 49.4 reduce-scatter.4

commit v4 on v3

--- a/solution.py
+++ b/solution.py
@@ -121,9 +121,7 @@
         return (arrays, plans), (table, None)
     spots = [(0, 0, 0), (1, 0, 2), (2, 0, 4), (3, 0, 6), (4, 0, 1), (4, 1, 3), (4, 2, 5), (5, 0, 7)]
     plans = [[(at, index, m * unit, rel, unit) for at, index, rel in spots] for m in range(parts)]
-    rows = jnp.concatenate([piece[:, behind:] for piece in (*planes, *cores)])
-    order = (0, 2, 4, 6, 1, 3, 5, 7)
-    return ([*planes, *cores], plans), (rows, (order, short, long))
+    return ([*planes, *cores], plans), (None, (spots, behind, short, long))
 
 
 def copies(place, refs, plan, target, sems, first):
@@ -212,17 +210,15 @@
     return table[row : row + 1, :]
 
 
-def make_table(place, rows, layout):
-    if layout is None:
-        return rows[...].astype(F32)
-    order, short, long = layout
-    shape = rows.shape[1:]
+def make_table(place, pieces, layout):
+    spots, _, short, long = layout
+    shape = pieces.shape[1:]
     lane = lax.broadcasted_iota(jnp.int32, shape, 1)
     row = lax.broadcasted_iota(jnp.int32, shape, 0)
     table = jnp.zeros(shape, F32)
-    for at, rel in enumerate(order):
+    for at, (_, _, rel) in enumerate(spots):
         spot = place ^ rel
-        piece = rows[at].astype(F32)
+        piece = pieces[at].astype(F32)
         table += pltpu.roll(jnp.where((row < UP_B) & (lane < short), piece, 0.0), spot * short, 1)
         start = spot * long
         up = jnp.where(lane[:1] < long, piece[UP_B : UP_B + 1], 0.0)
@@ -232,8 +228,9 @@
 
 
 def project_kernel(plans, layout, place, rows, extras, *refs):
-    count = len(refs) - 5 - 2
-    sources, (normed, query, key, value, table, weights, sems) = refs[:count], refs[count:]
+    count = len(refs) - 5 - 4
+    sources, refs = refs[:count], refs[count:]
+    normed, query, key, value, table, weights, pieces, sems, piece_sems = refs
     made, first = [], 0
     for m in range(3):
         made.append(copies(place[0], sources, plans[m], weights.at[m], sems, first))
@@ -243,7 +240,16 @@
     def _():
         for group in made:
             start_all(group)
-        table[...] = make_table(place[0], extras, layout)
+        if layout is None:
+            table[...] = extras[...].astype(F32)
+            return
+        brought = []
+        for at, (source, index, _) in enumerate(layout[0]):
+            piece = sources[source].at[index, pl.ds(layout[1], 16)]
+            brought.append(pltpu.make_async_copy(piece, pieces.at[at], piece_sems.at[at]))
+        start_all(brought)
+        wait_all(brought)
+        table[...] = make_table(place[0], pieces, layout)
 
     unit_rows, _ = centred_rows(rows[...].astype(F32))
     low = (unit_rows * vector(table, LN1_G) + vector(table, LN1_B)).astype(BF16)
@@ -263,6 +269,8 @@
     arrays, plans = group
     extras, layout = extras
     count, width = rows.shape
+    if extras is None:
+        extras = jnp.zeros((16, width), BF16)
     return pl.pallas_call(
         functools.partial(project_kernel, plans, layout),
         grid=(count // TILE,),
@@ -272,7 +280,9 @@
         + [jax.ShapeDtypeStruct((16, width), F32)],
         scratch_shapes=[
             pltpu.VMEM((3, width, width), BF16),
+            pltpu.VMEM((8, 16, width), BF16),
             pltpu.SemaphoreType.DMA((sum(len(p) for p in plans[:3]),)),
+            pltpu.SemaphoreType.DMA((8,)),
         ],
         compiler_params=params(60),
         cost_estimate=cost(6 * count * width * width, 14 * count * width),
@@ -306,7 +316,7 @@
 
 
 def attend_kernel(pack, lengths, query, key, value, *refs):
-    attended, log_total = refs[-2:]
+    attended, kept = refs[-2:]
     rows = query.shape[0]
     same = same_segment(lengths, pack, rows)
     flat = jnp.transpose(value[...].astype(F32)).astype(BF16)
@@ -319,7 +329,7 @@
         total = jnp.sum(powers, axis=0, keepdims=True)
         weights = (powers * (1.0 / total)).astype(BF16)
         mixed.append(dot(flat[head * HD : (head + 1) * HD], weights))
-        log_total[0, 0, head : head + 1, :] = top + jnp.log(total)
+        kept[head] = weights
     attended[...] = jnp.transpose(jnp.concatenate(mixed, axis=0)).astype(BF16)
 
 
@@ -327,8 +337,8 @@
     return pl.BlockSpec((rows, 2 * HD), lambda h: (pack, h))
 
 
-def log_block(rows, pack):
-    return pl.BlockSpec((1, 1, 2, rows), lambda h: (pack, h, 0, 0))
+def kept_block(rows):
+    return pl.BlockSpec((2, rows, rows), lambda h: (h, 0, 0))
 
 
 def attend(lengths, query, key, value, pack, earlier=()):
@@ -339,10 +349,10 @@
         functools.partial(attend_kernel, pack),
         grid=(pairs,),
         in_specs=[SMEM] + [pair_block(rows, pack)] * 3 + [ANY] * len(earlier),
-        out_specs=[pair_block(rows, pack), log_block(rows, pack)],
+        out_specs=[pair_block(rows, pack), kept_block(rows)],
         out_shape=[
             jax.ShapeDtypeStruct(query.shape, BF16),
-            jax.ShapeDtypeStruct((packs, pairs, 2, rows), F32),
+            jax.ShapeDtypeStruct((2 * pairs, rows, rows), BF16),
         ],
         input_output_aliases={4 + i: i for i in range(len(earlier))},
         compiler_params=params(60),
@@ -351,17 +361,14 @@
     )(lengths, query, key, value, *earlier)
 
 
-def attend_back_kernel(pack, lengths, query, key, value, grad, log_total, *refs):
+def attend_back_kernel(query, key, value, grad, kept, *refs):
     grad_q, grad_k, grad_v = refs[-3:]
-    rows = query.shape[0]
-    same = same_segment(lengths, pack, rows)
     flat_key = jnp.transpose(key[...].astype(F32)).astype(BF16)
     by_query, by_key, by_value = [], [], []
     for head in range(2):
-        scores = dot_nt(key[...], only(query[...], head))
-        probs = jnp.exp(scores - log_total[0, 0, head : head + 1, :])
-        probs = jnp.where(same, probs, 0.0)
-        by_value.append(dot(probs.astype(BF16), grad[...]))
+        weights = kept[head]
+        probs = weights.astype(F32)
+        by_value.append(dot(weights, grad[...]))
         grad_probs = dot_nt(value[...], only(grad[...], head))
         centre = jnp.sum(grad_probs * probs, axis=0, keepdims=True)
         grad_scores = (probs * (grad_probs - centre)).astype(BF16)
@@ -373,24 +380,20 @@
     grad_q[...] = jnp.transpose(jnp.concatenate(by_query, axis=0)).astype(BF16) * 0.125
 
 
-def attend_back(lengths, query, key, value, grad, log_total, pack, earlier=()):
-    packs = lengths.shape[0]
-    count, width = query.shape
-    rows, pairs = count // packs, width // (2 * HD)
+def attend_back(query, key, value, grad, kept, pack, earlier=()):
+    pairs, rows = kept.shape[0] // 2, kept.shape[1]
+    width = query.shape[1]
     return pl.pallas_call(
-        functools.partial(attend_back_kernel, pack),
+        attend_back_kernel,
         grid=(pairs,),
-        in_specs=[SMEM]
-        + [pair_block(rows, pack)] * 4
-        + [log_block(rows, pack)]
-        + [ANY] * len(earlier),
+        in_specs=[pair_block(rows, pack)] * 4 + [kept_block(rows)] + [ANY] * len(earlier),
         out_specs=[pair_block(rows, pack)] * 3,
         out_shape=[jax.ShapeDtypeStruct(query.shape, BF16)] * 3,
-        input_output_aliases={6 + i: i for i in range(len(earlier))},
+        input_output_aliases={5 + i: i for i in range(len(earlier))},
         compiler_params=params(60),
-        cost_estimate=cost(40 * rows * rows * width, 14 * rows * width, 12 * rows * rows),
+        cost_estimate=cost(32 * rows * rows * width, 14 * rows * width, 0),
         name="attend_back",
-    )(lengths, query, key, value, grad, log_total, *earlier)
+    )(query, key, value, grad, kept, *earlier)
 
 
 def live_rows(lengths, shape):
@@ -404,11 +407,11 @@
     return position < end
 
 
-def hidden_kernel(plans, size, place, lengths, rows, mixed, cotangent, table, *refs):
-    two, refs = refs[:size], refs[size:]
-    *up_plans, out_plan = plans
+def hidden_kernel(out_plan, up_plans, sizes, place, lengths, rows, mixed, cotangent, table, *refs):
+    sources, refs = refs[: sum(sizes)], refs[sum(sizes) :]
+    one, two = sources[: sizes[0]], sources[sizes[0] :]
     branch_out, normed, active, slope, grad_down, out_w, up_w, sems = refs
-    made = [copies(place[0], two, out_plan, out_w, sems, 0)]
+    made = [copies(place[0], one, out_plan, out_w, sems, 0)]
     first = len(out_plan)
     for m, plan in enumerate(up_plans):
         made.append(copies(place[0], two, plan, up_w.at[m], sems, first))
@@ -444,17 +447,18 @@
         slope[:, part] = rate.astype(BF16)
 
 
-def hidden(place, lengths, rows, mixed, cotangent, table, group):
+def hidden(place, lengths, rows, mixed, cotangent, table, group_one, group_two):
     count, width = rows.shape
-    arrays, plans = group
-    hidden_units = width * (len(plans) - 1)
+    hidden_units = width * len(group_two[1])
+    out_plan, up_plans = group_one[1][3], group_two[1]
+    sizes = (len(group_one[0]), len(group_two[0]))
     return pl.pallas_call(
-        functools.partial(hidden_kernel, plans, len(arrays)),
+        functools.partial(hidden_kernel, out_plan, up_plans, sizes),
         grid=(count // TILE,),
         in_specs=[SMEM, SMEM]
         + [tile_of(width)] * 3
         + [whole(table.shape)]
-        + [ANY] * len(arrays),
+        + [ANY] * sum(sizes),
         out_specs=[tile_of(width)] * 2 + [tile_of(hidden_units)] * 2 + [tile_of(width)],
         out_shape=[
             jax.ShapeDtypeStruct(rows.shape, F32),
@@ -465,25 +469,25 @@
         ],
         scratch_shapes=[
             pltpu.VMEM((width, width), BF16),
-            pltpu.VMEM((len(plans) - 1, width, width), BF16),
-            pltpu.SemaphoreType.DMA((sum(len(p) for p in plans),)),
+            pltpu.VMEM((len(up_plans), width, width), BF16),
+            pltpu.SemaphoreType.DMA((len(out_plan) + sum(len(p) for p in up_plans),)),
         ],
         compiler_params=params(60),
         cost_estimate=cost(14 * count * width * hidden_units // 4, 26 * count * width, 2 * count * hidden_units),
         name="hidden",
-    )(place, lengths, rows, mixed, cotangent, table, *arrays)
+    )(place, lengths, rows, mixed, cotangent, table, *group_one[0], *group_two[0])
 
 
 STATS_TWO = 7
 
 
 def back_kernel(
-    two_plans, down_plan, sizes, place, lengths, rows, branch_in, active, slope, grad_down, cotangent,
+    out_plan, up_plans, down_plan, sizes, place, lengths, rows, branch_in, active, slope, grad_down, cotangent,
     table, *refs,
 ):
     sources, refs = refs[: sum(sizes)], refs[sum(sizes) :]
-    two, three = sources[: sizes[0]], sources[sizes[0] :]
-    *up_plans, out_plan = two_plans
+    one, two = sources[: sizes[0]], sources[sizes[0] : sizes[0] + sizes[1]]
+    three = sources[sizes[0] + sizes[1] :]
     result, grad_hidden, grad_middle_out, grad_branch, grad_mixed, stats, hidden_stats = refs[:7]
     out_w, up_w, down_w, sems = refs[7:]
     made = [copies(place[0], three, down_plan, down_w, sems, 0)]
@@ -491,7 +495,7 @@
     for m, plan in enumerate(up_plans):
         made.append(copies(place[0], two, plan, up_w.at[m], sems, first))
         first += len(plan)
-    made.append(copies(place[0], two, out_plan, out_w, sems, first))
+    made.append(copies(place[0], one, out_plan, out_w, sems, first))
 
     @pl.when(pl.program_id(0) == 0)
     def _():
@@ -535,11 +539,11 @@
         stats[at : at + 1, :] += total
 
 
-def back(place, lengths, rows, branch, active, slope, grad_down, cotangent, table, two, three):
+def back(place, lengths, rows, branch, active, slope, grad_down, cotangent, table, one, two, three):
     count, width = rows.shape
     hidden_units = active.shape[1]
-    plans = (two[1], three[1][0])
-    sizes = (len(two[0]), len(three[0]))
+    plans = (one[1][3], two[1], three[1][0])
+    sizes = (len(one[0]), len(two[0]), len(three[0]))
     return pl.pallas_call(
         functools.partial(back_kernel, *plans, sizes),
         grid=(count // TILE,),
@@ -563,63 +567,71 @@
         ],
         scratch_shapes=[
             pltpu.VMEM((width, width), BF16),
-            pltpu.VMEM((len(plans[0]) - 1, width, width), BF16),
+            pltpu.VMEM((len(plans[1]), width, width), BF16),
             pltpu.VMEM((hidden_units, width), BF16),
-            pltpu.SemaphoreType.DMA((sum(len(p) for p in plans[0]) + len(plans[1]),)),
+            pltpu.SemaphoreType.DMA(
+                (len(plans[0]) + sum(len(p) for p in plans[1]) + len(plans[2]),)
+            ),
         ],
         compiler_params=params(60),
         cost_estimate=cost(26 * count * width * hidden_units // 4, 40 * count * width),
         name="back",
-    )(place, lengths, rows, branch, active, slope, grad_down, cotangent, table, *two[0], *three[0])
+    )(place, lengths, rows, branch, active, slope, grad_down, cotangent, table, *one[0], *two[0], *three[0])
 
 
 def outer_kernel(spread, steps, place, *refs):
-    pairs = len(steps)
-    lefts, rights, refs = refs[:pairs], refs[pairs : 2 * pairs], refs[2 * pairs :]
+    lefts, refs = refs[: len(steps)], refs[len(steps) :]
+    count = sum(len(own) for own in steps)
+    rights, refs = refs[:count], refs[count:]
     flat = refs[-1]
     step = pl.program_id(0)
-    first = 0
-    for left, count in zip(lefts, steps):
-
-        @pl.when(step == first)
-        def _(left=left):
-            for at in range(0, flat.shape[0], 128):
-                block = left[:, at : at + 128].astype(F32)
-                flat[at : at + 128, :] = jnp.transpose(block).astype(BF16)
-
-        first += count
 
     def put(right):
         value = dot(flat[...], right[...])
         if not spread:
             refs[0][...] = value.astype(BF16)
             return
-        mine, theirs, held = refs[:3]
-        plane, core = place[0] // 2, place[0] % 2
-        held[...] = value
+        mine, theirs = refs[:2]
         unit = flat.shape[0] // 8
+        value = value.astype(BF16)
         for at in range(4):
-            one = pl.multiple_of((2 * at + core) * unit, 8)
-            other = pl.multiple_of((2 * at + 1 - core) * unit, 8)
-            mine[at ^ plane, 0] = held[pl.ds(one, unit), :].astype(BF16)
-            theirs[at ^ plane, 0] = held[pl.ds(other, unit), :].astype(BF16)
-
-    first = 0
-    for right, count in zip(rights, steps):
-
-        @pl.when((step >= first) & (step < first + count))
-        def _(right=right):
-            put(right)
-
-        first += count
+            mine[at, 0] = value[2 * at * unit : (2 * at + 1) * unit]
+            theirs[at, 0] = value[(2 * at + 1) * unit : (2 * at + 2) * unit]
+
+    first, at_right = 0, 0
+    for left, own in zip(lefts, steps):
+
+        @pl.when(step == first)
+        def _(left=left):
+            for at in range(0, flat.shape[0], 128):
+                block = left[:, at : at + 128].astype(F32)
+                turned = jnp.transpose(block).astype(BF16)
+                if spread:
+                    refs[2][at : at + 128, :] = turned
+                else:
+                    flat[at : at + 128, :] = turned
+            if spread:
+                unit = flat.shape[0] // 8
+                for rel in range(8):
+                    start = pl.multiple_of((place[0] ^ rel) * unit, 16)
+                    flat[rel * unit : (rel + 1) * unit, :] = refs[2][pl.ds(start, unit), :]
+
+        for count in own:
+
+            @pl.when((step >= first) & (step < first + count))
+            def _(right=rights[at_right]):
+                put(right)
+
+            first += count
+            at_right += 1
 
 
 def outer(place, pairs, width):
     count, height = pairs[0][0].shape
-    steps = [right.shape[1] // width for _, right in pairs]
-    total = sum(steps)
+    steps = [[right.shape[1] // width for right in rights] for _, rights in pairs]
+    total = sum(sum(own) for own in steps)
     right_specs, first = [], 0
-    for own in steps:
+    for own in sum(steps, []):
         right_specs.append(
             pl.BlockSpec(
                 (count, width),
@@ -632,7 +644,7 @@
         block = pl.BlockSpec((4, 1, height // 8, width), lambda i: (0, i, 0, 0))
         shape = jax.ShapeDtypeStruct((4, total, height // 8, width), BF16)
         specs, shapes = [block, block], [shape, shape]
-        scratch = [pltpu.VMEM((height, width), F32)] + scratch
+        scratch = scratch * 2
     else:
         specs = pl.BlockSpec((height, width), lambda i: (0, i))
         shapes = jax.ShapeDtypeStruct((height, total * width), BF16)
@@ -646,66 +658,7 @@
         compiler_params=params(60),
         cost_estimate=cost(2 * count * height * total * width, 2 * (count + height) * total * width),
         name="outer",
-    )(place, *(left for left, _ in pairs), *(right for _, right in pairs))
-
-
-def plain_kernel(steps, *refs):
-    lefts, rights = refs[: len(steps)], refs[len(steps) : -2]
-    out, flat = refs[-2:]
-    step = pl.program_id(0)
-    first, at_right = 0, 0
-    for left, counts in zip(lefts, steps):
-
-        @pl.when(step == first)
-        def _(left=left):
-            for at in range(0, flat.shape[0], 128):
-                block = left[:, at : at + 128].astype(F32)
-                flat[at : at + 128, :] = jnp.transpose(block).astype(BF16)
-
-        for count in counts:
-
-            @pl.when((step >= first) & (step < first + count))
-            def _(right=rights[at_right]):
-                out[...] = dot(flat[...], right[...]).astype(BF16).reshape(out.shape)
-
-            first += count
-            at_right += 1
-
-
-def plain_outer(pairs, width):
-    count, height = pairs[0][0].shape
-    steps = [[right.shape[1] // width for right in rights] for _, rights in pairs]
-    total = sum(sum(counts) for counts in steps)
-    places = lax.axis_size("wide")
-    right_specs, first = [], 0
-    for own in sum(steps, []):
-        right_specs.append(
-            pl.BlockSpec(
-                (count, width),
-                lambda i, first=first, own=own: (0, jnp.clip(i - first, 0, own - 1)),
-            )
-        )
-        first += own
-    if direct():
-        spec = pl.BlockSpec((8, 1, height // 8, width), lambda i: (0, i, 0, 0))
-        shape = jax.ShapeDtypeStruct((8, total, height // 8, width), BF16)
-    else:
-        spec = pl.BlockSpec((height, width), lambda i: (0, i))
-        shape = jax.ShapeDtypeStruct((height, total * width), BF16)
-    out = pl.pallas_call(
-        functools.partial(plain_kernel, steps),
-        grid=(total,),
-        in_specs=[whole((count, height))] * len(pairs) + right_specs,
-        out_specs=spec,
-        out_shape=shape,
-        scratch_shapes=[pltpu.VMEM((height, count), BF16)],
-        compiler_params=params(60),
-        cost_estimate=cost(2 * count * height * total * width, 2 * (count + height) * total * width),
-        name="plain_outer",
-    )(*(left for left, _ in pairs), *(right for _, rights in pairs for right in rights))
-    if not direct():
-        out = out.reshape(places, height // places, total, width).transpose(0, 2, 1, 3)
-    return out.reshape(places, -1, width)
+    )(place, *(left for left, _ in pairs), *(right for _, rights in pairs for right in rights))
 
 
 def wide_outer_kernel(place, left, right, out, flat):
@@ -803,39 +756,57 @@
     return tuple(held[:, i] for i in range(4))
 
 
-def add_kernel(mine, other, own, *halves):
-    for quarter in range(4):
-        total = (mine[quarter].astype(F32) + other[quarter].astype(F32)).astype(BF16)
-        if quarter == 0:
-            own[0] = total
-            continue
-        one, two = halves[2 * quarter - 2], halves[2 * quarter - 1]
-        one[0] = total[: one.shape[1]]
-        two[0] = total[one.shape[1] :]
-
-
-def quarters_added(mine, other):
+def add_kernel(mine, other, own, by_x, by_y, near, far):
+    total = (mine[...].astype(F32) + other[...].astype(F32)).astype(BF16)
+    own[0] = total[0]
+
+    @pl.when(pl.program_id(0) == 0)
+    def _():
+        by_x[0] = total[3]
+        by_x[1] = total[1]
+        far[0] = total[2]
+
+    @pl.when(pl.program_id(0) == 1)
+    def _():
+        by_y[0] = total[3]
+        by_y[1] = total[2]
+        near[0] = total[1]
+
+
+def sums_of_cores(mine, other):
     rows, columns = mine.shape[1:]
-    half = rows // 32 * 16
+    half = rows // 2
     if not direct():
-        own, *rest = quarters(add_low(mine, other))
-        return [own] + [(piece[:, :half], piece[:, half:]) for piece in rest]
-    shapes = [jax.ShapeDtypeStruct((1, rows, columns), BF16)]
-    for _ in range(3):
-        shapes.append(jax.ShapeDtypeStruct((1, half, columns), BF16))
-        shapes.append(jax.ShapeDtypeStruct((1, rows - half, columns), BF16))
-    step = columns // 6
-    own, *parts = pl.pallas_call(
+        own, near, far, corner = quarters(add_low(mine, other))
+        by_x = jnp.stack([corner[:, :half], near[:, :half]], axis=1)
+        by_y = jnp.stack([corner[:, half:], far[:, half:]], axis=1)
+        return own, by_x, by_y, near[:, half:], far[:, :half]
+    sizes = [rows, 2 * half, 2 * half, half, half]
+    whole_out = [(1, rows, columns), (2, half, columns), (2, half, columns), (1, half, columns), (1, half, columns)]
+    own, by_x, by_y, near, far = pl.pallas_call(
         add_kernel,
-        grid=(6,),
-        in_specs=[pl.BlockSpec((4, rows, step), lambda i: (0, 0, i))] * 2,
-        out_specs=[pl.BlockSpec((1, s.shape[1], step), lambda i: (0, 0, i)) for s in shapes],
-        out_shape=shapes,
+        grid=(2,),
+        in_specs=[pl.BlockSpec((4, half, columns), lambda i: (0, i, 0))] * 2,
+        out_specs=[pl.BlockSpec((1, half, columns), lambda i: (0, i, 0))]
+        + [whole(shape) for shape in whole_out[1:]],
+        out_shape=[jax.ShapeDtypeStruct(shape, BF16) for shape in whole_out],
         compiler_params=params(60),
         cost_estimate=cost(4 * rows * columns, 24 * rows * columns),
         name="core_add",
     )(mine, other)
-    return own, parts[0:2], parts[2:4], parts[4:6]
+    return own, by_x[None], by_y[None], near, far
+
+
+def second_sends(held, first):
+    by_x, by_y = first
+    return [add_low(held[3], by_y[:, 0]), add_low(held[4], by_x[:, 0])]
+
+
+def own_sum(own, first, second):
+    (by_x, by_y), (near, far) = first, second
+    total = own.astype(F32) + jnp.concatenate([by_x[:, 1], near], axis=1).astype(F32)
+    total = total + jnp.concatenate([far, by_y[:, 1]], axis=1).astype(F32)
+    return total.astype(BF16)
 
 
 def halve(total):
@@ -908,15 +879,6 @@
     return split_cores(stacked.reshape(places, -1, columns // parts))
 
 
-def all_stages():
-    stages = []
-    for bit in range(lax.axis_size("narrow").bit_length() - 1):
-        stages.append(lambda v, bit=bit: exchange(v, "narrow", lambda i: i ^ (1 << bit)))
-    for bit in reversed(range(wide_bits())):
-        stages.append(lambda v, bit=bit: cross(v, bit))
-    return stages
-
-
 def own_spot(places, layers, piece, width):
     start = (lax.axis_index("wide") * layers + lax.axis_index("narrow")) * piece
     return start // width, start % width
@@ -939,16 +901,10 @@
     piece, long = ln1_gain.shape[0], up_bias.shape[0]
     small_spot = own_spot(places, layers, piece, width)
     up_spot = own_spot(places, layers, long, width)
-    stages = all_stages()
-
-    def spread_table(table, stages):
-        for stage in stages:
-            table = table + stage(table)
-        return table
-
     extra = jnp.pad(jnp.stack(small), ((0, 0), (0, part - piece)))
     extra = jnp.concatenate([extra, jnp.pad(up_bias[None], ((0, 5), (0, part - long)))])
-    early = jnp.concatenate([w_qkv, extra])
+    extra = jnp.pad(extra, ((0, 0), (0, quarter)))
+    early = jnp.concatenate([jnp.concatenate([w_qkv, w_out], axis=1), extra])
 
     moved = [move(early) for move in shifts(layers)]
     one = by_origin([early, *moved])
@@ -956,23 +912,23 @@
     extra = jnp.pad(extra, ((0, 6), (0, width - layers * piece)))
     long_row = side_by_side(one[:, short + 10 : short + 11, :long])
     long_row = jnp.pad(long_row, ((10, 5), (0, width - layers * long)))
-    one = side_by_side(one[:, :short])
-    one = jnp.concatenate([*jnp.split(one, 3, axis=1), extra + long_row])
+    qkv, out = side_by_side(one[:, :short, :part]), side_by_side(one[:, :short, part:])
+    one = jnp.concatenate([*jnp.split(qkv, 3, axis=1), out, extra + long_row])
     held = double(one)
-    up_out = jnp.concatenate([w_up, w_out], axis=1)
-    sends = [held, held] + [up_out] * (layers - 1)
-    (up_out,), (near, far, *two) = beside(lambda v: v, (up_out,), sends, planes() + shifts(layers))
+    sends = [held, held] + [w_up] * (layers - 1)
+    (near, far, *two) = [move(send) for move, send in zip(planes() + shifts(layers), sends)]
+    near, far, two = lax.optimization_barrier((near, far, two))
     half = near.shape[1] // 32 * 16
     sends = [near[:, :half], far[:, half:], jnp.concatenate([held, near, far])]
-    two = by_origin([up_out, *two])
-    two = jnp.concatenate([two[:, :, :width].reshape(-1, width), side_by_side(two[:, :, width:])])
+    two = by_origin([w_up, *two]).reshape(-1, width)
     two, sends = lax.optimization_barrier((two, sends))
-    two = in_order(lax.all_gather(two, "wide"), layers + 1)
+    two = in_order(lax.all_gather(two, "wide"), layers)
     moves = corners() + [lambda v: cross(v, 0)]
     moved = lax.optimization_barrier([move(send) for move, send in zip(moves, sends)])
     planes_one = held, near, far, jnp.concatenate(moved[:2], axis=1)
-    one, extras = matrices(planes_one, (moved[2], cross(planes_one[3], 0)), 3, layers * piece, layers * long)
     side_down = jnp.concatenate(jnp.split(w_down, layers, axis=0), axis=1)
+    side_down = after(side_down, moved)
+    one, extras = matrices(planes_one, (moved[2], cross(planes_one[3], 0)), 4, layers * piece, layers * long)
 
     (normed, query, key, value, table), three = beside(
         lambda v: project(place, v, extras, one), rows, [side_down] * (layers - 1), shifts(layers)
@@ -983,12 +939,14 @@
     )
     query, three = lax.optimization_barrier((query, three))
     three = in_order(lax.all_gather(three, "wide"), 1)
-    attention = attend(lengths, query, key, value, 0)
-    for pack in range(1, packs):
-        attention = attend(lengths, query, key, value, pack, attention)
-    mixed, log_total = attention
+    kept, mixed = [], ()
+    for pack in range(packs):
+        mixed, weights = attend(lengths, query, key, value, pack, mixed)
+        mixed = (mixed,)
+        kept.append(weights)
+    (mixed,) = mixed
     branch, normed_two, active, slope, grad_down = hidden(
-        place, lengths, rows, mixed, cotangent, table, two
+        place, lengths, rows, mixed, cotangent, table, one, two
     )
     grad_w_down = wide_outer(place, grad_down, active)
     active = after(active, grad_w_down)
@@ -997,57 +955,68 @@
     total_down = lax.psum_scatter(grad_w_down.reshape(places, width, -1), "wide")
 
     result, grad_hidden, grad_middle, grad_branch, grad_mixed, stats_two, hidden_stats = back(
-        place, lengths, rows, branch, active, slope, grad_down, cotangent, table, two, three
+        place, lengths, rows, branch, active, slope, grad_down, cotangent, table, one, two, three
     )
     mine, theirs = by_core(
-        outer(place, [(normed_two, grad_hidden), (mixed, grad_branch)], width), layers + 1
+        outer(place, [(normed_two, [grad_hidden]), (mixed, [grad_branch])], width), layers + 1
     )
     grads, (other,) = beside(
-        lambda v: attend_back(lengths, query, key, value, v, log_total, 0),
+        lambda v: attend_back(query, key, value, v, kept[0], 0),
         grad_mixed,
         [theirs],
         [lambda v: cross(v, 0)],
     )
-    own_up, near, far, corner = quarters_added(mine, other)
+    up_held = sums_of_cores(mine, other)
+    total_down, grads = lax.optimization_barrier((total_down, grads))
+    total_down = lax.psum_scatter(total_down.reshape(layers, quarter, -1), "narrow")
     for pack in range(1, packs):
-        run = functools.partial(attend_back, lengths, query, key, value, grad_mixed, log_total, pack)
+        run = functools.partial(attend_back, query, key, value, grad_mixed, kept[pack], pack)
         if pack == packs - 1:
-            sends = [corner[0], corner[1], near[0], far[1]]
-            grads, moved = beside(run, grads, sends, planes() + planes())
+            grads, moved = beside(run, grads, up_held[1:3], planes())
         else:
             grads = run(grads)
-    near_one, far_two = moved[2:]
-    sends = [add_low(near[1], moved[1]), add_low(far[0], moved[0])]
+    up_moved, sends = moved, second_sends(up_held, moved)
     grads, sends = lax.optimization_barrier((grads, sends))
-    grad_w_qkv, (near_two, far_one) = beside(
-        lambda v: plain_outer([(normed, v)], width), grads, sends, planes()
-    )
-    total_qkv = lax.psum_scatter(grad_w_qkv, "wide")
-    own_up = own_up.astype(F32) + jnp.concatenate([near_one, near_two], axis=1).astype(F32)
-    own_up = own_up + jnp.concatenate([far_one, far_two], axis=1).astype(F32)
-    total_up = halve(own_up.astype(BF16))
+    mine_theirs, moved = beside(
+        lambda v: outer(place, [(normed, v)], width), grads, sends, planes()
+    )
+    mine_theirs, total_down = lax.optimization_barrier((mine_theirs, total_down))
+    mine, theirs = by_core(mine_theirs, 3)
+    total_up = halve(own_sum(up_held[0], up_moved, moved))
     total_out = total_up[layers * short :].reshape(short, layers, quarter).transpose(1, 0, 2)
     total_up = total_up[: layers * short].reshape(layers, short, width)
     total_up = jnp.concatenate([total_up, total_out], axis=2)
-    total_down = total_down.reshape(layers, quarter, -1)
-    sends, moves = spread_blocks(total_up)
-    down_sends, down_moves = spread_blocks(total_down)
+    up_sends, up_moves = spread_blocks(total_up)
+    up_sends, (other,) = beside(lambda v: v, up_sends, [theirs], [lambda v: cross(v, 0)])
+    held = sums_of_cores(mine, other)
     grad_q, grad_k, grad_v = grads
     (grad_rows, stats_one), moved = beside(
         lambda v: inputs_back(place, rows, grad_middle, v, grad_k, grad_v, table, one),
         grad_q,
-        sends + down_sends,
-        moves + down_moves,
-    )
-    up_parts, down_parts = moved[: len(sends)], moved[len(sends) :]
-    total_up = add_blocks(total_up, up_parts)
-    total_down = add_blocks(total_down, down_parts).T
-    sums = spread_table(jnp.concatenate([stats_one, stats_two, hidden_stats]), stages[2:])
-    total_qkv = after(total_qkv, sums)
+        [*held[1:3], *up_sends],
+        planes() + up_moves,
+    )
+    first, up_parts = moved[:2], moved[2:]
+    sums = jnp.concatenate([stats_one, stats_two, hidden_stats])
+    others = [sums] * (layers - 1)
+    sums, moved = beside(
+        lambda v: v, sums, [*second_sends(held, first), *others], planes() + shifts(layers)
+    )
+    second = moved[:2]
+    for piece_sums in moved[2:]:
+        sums = sums + piece_sums
+    total_qkv = halve(own_sum(held[0], first, second))
     blocks = jnp.concatenate([total_qkv[i * short : (i + 1) * short] for i in range(3)], axis=1)
     own_block, sends, moves = columns_blocks(blocks, part, layers)
-    sums, moved = beside(lambda v: spread_table(v, stages[:2]), sums, sends, moves)
-    total_qkv = own_columns(own_block, moved, part, blocks.shape[1])
+    both = [lambda v: exchange(v, "wide", lambda i: i ^ 6)]
+    sums, moved = beside(lambda v: v, sums, [*sends, sums, sums, sums], moves + planes() + both)
+    total_qkv = own_columns(own_block, moved[: layers - 1], part, blocks.shape[1])
+    for piece_sums in moved[layers - 1 :]:
+        sums = sums + piece_sums
+    for bit in (0, *range(3, wide_bits())):
+        sums = sums + cross(sums, bit)
+    total_up = add_blocks(total_up, up_parts)
+    total_down = total_down.astype(F32).T
 
     own = lax.dynamic_slice(sums, (0, small_spot[1]), (16, ln1_gain.shape[0]))
     own_up = lax.dynamic_slice(sums, (16 + up_spot[0], up_spot[1]), (1, up_bias.shape[0]))[0]

time: 313 us -> 290 us (0.927)
  waiting for transfers between devices: 66.2 us -> 51.2 us
  local copies, waits for them, and re-layouts: 18.3 us -> 11.1 us
    ppermute x36 -> x38, waiting for transfers between devices: 64.3 us -> 51.1 us  [exchange(): lax.ppermute(value, axis_name, [(i, partner(i) % size) for i in range(siz...]
    pallas_call x5, Pallas kernels: 60.9 us -> 50.9 us  [the longest x2 23.3 us: attend_back(): pl.pallas_call(attend_back_kernel, grid=(pairs,), in_specs=[pair_block(ro...]
    pallas_call x1 -> x2, Pallas kernels: 13.2 us -> 21.7 us  [outer(): pl.pallas_call(functools.partial(outer_kernel, direct(), steps), grid=(to...]
    unnamed x67 -> x73, local copies, waits for them, and re-layouts: 8.99 us -> 4.35 us
    ppermute x36 -> x38, starting transfers between devices: 46.1 us -> 47.8 us  [exchange(): lax.ppermute(value, axis_name, [(i, partner(i) % size) for i in range(siz...]
  transfers between devices with their start and end apart: 40 -> 42, of which waited for: 14 -> 17; matrix products, arithmetic and copies ran while one was open for 5% -> 2% of each run, Pallas kernels for 50% -> 53%
where the time goes in v4:
time: 290 us; the launch traced here: 289 us
  Pallas kernels  156 us (54%)
  waiting for transfers between devices  51.2 us (18%)
  starting transfers between devices  48.4 us (17%)
  between operations  14.6 us (5%)
  local copies, waits for them, and re-layouts  11.1 us (4%)
  other arithmetic  7.85 us (3%)
    ppermute x38, waiting for transfers between devices, exchange(): lax.ppermute(value, axis_name, [(i, partner(i) % size) for i in range(siz...  51.1 us
    ppermute x38, starting transfers between devices, exchange(): lax.ppermute(value, axis_name, [(i, partner(i) % size) for i in range(siz...  47.8 us
    pallas_call x1, Pallas kernels, back(): pl.pallas_call(functools.partial(back_kernel, *plans, sizes), grid=(count...  30.1 us
    pallas_call x2, Pallas kernels, attend_back(): pl.pallas_call(attend_back_kernel, grid=(pairs,), in_specs=[pair_block(ro...  23.3 us
    pallas_call x2, Pallas kernels, attend(): pl.pallas_call(functools.partial(attend_kernel, pack), grid=(pairs,), in_...  22.4 us
    pallas_call x2, Pallas kernels, outer(): pl.pallas_call(functools.partial(outer_kernel, direct(), steps), grid=(to...  21.7 us
    pallas_call x1, Pallas kernels, hidden(): pl.pallas_call(functools.partial(hidden_kernel, out_plan, up_plans, sizes...  19.3 us
    pallas_call x1, Pallas kernels, inputs_back(): pl.pallas_call(functools.partial(inputs_kernel, plans), grid=(count // TI...  11.3 us
  transfers between devices with their start and end apart: 42, of which 17 were waited for; matrix products, arithmetic and copies ran while one was open for 2% of the time, Pallas kernels for 53%

profile of v4, /device:TPU:0, one launch (start us, length us, event | category | flops | bytes accessed | tf_op | source)
XLA Modules:
  0.0 289.3 jit_solution(13038189940435422625)
XLA Ops:
  7.3 1.5 stack.82
  10.4 5.1 %collective-permute-start = (bf16[112,768]{1,0:T(8,128)(2,1)S(1)}, bf16[112,768]{1,0:T(8,128)(2,1)S(1)}, u32[]{:S(2)}, u32[]{:S(2)}) collective-permute-start(bf16[112,768]{1,0:T(8,128)(2,1)S(1)} %fusion.16), channel_id=1, source_target_pairs={{0,3},{1,0},{2,1},{3,2},{4,7},{5,4},{6,5},{7,6},{8,11},{9,8},{10,9... | collective-permute-start | bytes 516104 | tf_op jit(solution)/shard_map/ppermute | solution.py:22
  16.6 3.8 %collective-permute-done = bf16[112,768]{1,0:T(8,128)(2,1)S(1)} collective-permute-done((bf16[112,768]{1,0:T(8,128)(2,1)S(1)}, bf16[112,768]{1,0:T(8,128)(2,1)S(1)}, u32[]{:S(2)}, u32[]{:S(2)}) %collective-permute-start) | collective-permute-done | bytes 172064 | tf_op jit(solution)/shard_map/ppermute | solution.py:22
  20.4 9.7 %collective-permute-done.1 = bf16[112,768]{1,0:T(8,128)(2,1)S(1)} collective-permute-done((bf16[112,768]{1,0:T(8,128)(2,1)S(1)}, bf16[112,768]{1,0:T(8,128)(2,1)S(1)}, u32[]{:S(2)}, u32[]{:S(2)}) %collective-permute-start.1) | collective-permute-done | bytes 172064 | tf_op jit(solution)/shard_map/ppermute | solution.py:22
  31.3 1.6 collective-permute-start.3
  32.8 1.5 collective-permute-start.4
  35.2 1.9 collective-permute-start.6
  37.1 2.9 %collective-permute-start.7 = (bf16[96,768]{1,0:T(8,128)(2,1)S(1)}, bf16[96,768]{1,0:T(8,128)(2,1)S(1)}, u32[]{:S(2)}, u32[]{:S(2)}) collective-permute-start(bf16[96,768]{1,0:T(8,128)(2,1)S(1)} %copy-done.10), channel_id=1, source_target_pairs={{0,3},{1,0},{2,1},{3,2},{4,7},{5,4},{6,5},{7,6},{8,11},{9,8},{10,9... | collective-permute-start | bytes 442376 | tf_op jit(solution)/shard_map/ppermute | solution.py:22
  40.0 2.9 %collective-permute-done.5 = bf16[96,768]{1,0:T(8,128)(2,1)S(1)} collective-permute-done((bf16[96,768]{1,0:T(8,128)(2,1)S(1)}, bf16[96,768]{1,0:T(8,128)(2,1)S(1)}, u32[]{:S(2)}, u32[]{:S(2)}) %collective-permute-start.5) | collective-permute-done | bytes 147488 | tf_op jit(solution)/shard_map/ppermute | solution.py:22
  43.0 4.5 %collective-permute-done.6 = bf16[96,768]{1,0:T(8,128)(2,1)S(1)} collective-permute-done((bf16[96,768]{1,0:T(8,128)(2,1)S(1)}, bf16[96,768]{1,0:T(8,128)(2,1)S(1)}, u32[]{:S(2)}, u32[]{:S(2)}) %collective-permute-start.6) | collective-permute-done | bytes 147488 | tf_op jit(solution)/shard_map/ppermute | solution.py:22
  48.0 1.4 pad_maximum_fusion
  51.3 1.5 collective-permute-start.8
  52.8 7.6 %collective-permute-done.8 = bf16[1,192,768]{2,1,0:T(8,128)(2,1)S(1)} collective-permute-done((bf16[1,192,768]{2,1,0:T(8,128)(2,1)S(1)}, bf16[1,192,768]{2,1,0:T(8,128)(2,1)S(1)}, u32[]{:S(2)}, u32[]{:S(2)}) %collective-permute-start.8) | collective-permute-done | bytes 294944 | tf_op jit(solution)/shard_map/ppermute | solution.py:22
  61.5 3.6 %collective-permute-start.12 = (bf16[96,768]{1,0:T(8,128)(2,1)S(1)}, bf16[96,768]{1,0:T(8,128)(2,1)S(1)}, u32[]{:S(2)}, u32[]{:S(2)}) collective-permute-start(bf16[96,768]{1,0:T(8,128)(2,1)S(1)} %pad_maximum_fusion.4), channel_id=1, source_target_pairs={{0,1},{1,2},{2,3},{3,0},{4,5},{5,6},{6,7},{7,4},{8,9},{9,10},{10,1... | collective-permute-start | bytes 442376 | tf_op jit(solution)/shard_map/ppermute | solution.py:22
  65.1 2.0 collective-permute-start.13
  68.4 10.1 %project.1 = (bf16[1024,768]{1,0:T(8,128)(2,1)}, bf16[1024,768]{1,0:T(8,128)(2,1)}, bf16[1024,768]{1,0:T(8,128)(2,1)}, bf16[1024,768]{1,0:T(8,128)(2,1)}, f32[16,768]{1,0:T(8,128)}) custom-call(s32[1]{0:T(128)} %bitcast.place, bf16[1024,768]{1,0:T(8,128)(2,1)} %bitcast.209, bf16[16,768]{1,0:T(8,128)(2,1)} %broadcast.21.extras, ...), custom_call_target="tpu_custom_call" | custom-call | flops 3623878656 | bytes 11010048 | tf_op jit(solution)/shard_map/project/pallas_call | solution.py:274
  80.3 11.2 %attend.2 = (bf16[1024,768]{1,0:T(8,128)(2,1)}, bf16[12,512,512]{2,1,0:T(8,128)(2,1)}) custom-call(s32[2,6]{1,0:T(2,128)} %lengths.7, bf16[1024,768]{1,0:T(8,128)(2,1)} %get-tuple-element.195.query, bf16[1024,768]{1,0:T(8,128)(2,1)} %get-tuple-element.196.key, bf16[1024,768]{1,0:T(8,128)(2,1)} %get-tuple-element.197.value), custom_call_target="tpu_custom_call" | custom-call | tf_op jit(solution)/shard_map/attend/pallas_call | solution.py:348
  91.5 11.2 %attend.3 = (bf16[1024,768]{1,0:T(8,128)(2,1)}, bf16[12,512,512]{2,1,0:T(8,128)(2,1)}) custom-call(s32[2,6]{1,0:T(2,128)} %lengths.7, bf16[1024,768]{1,0:T(8,128)(2,1)} %get-tuple-element.195.query, bf16[1024,768]{1,0:T(8,128)(2,1)} %get-tuple-element.196.key, bf16[1024,768]{1,0:T(8,128)(2,1)} %get-tuple-element.197.value, ...), custom_call_target="tpu_custom_call", output_to_operand_aliasing={{0}: (4, {})} | custom-call | flops 3221225472 | bytes 3145728 | tf_op jit(solution)/shard_map/attend/pallas_call | solution.py:348
  102.7 19.3 %hidden.1 = (f32[1024,768]{1,0:T(8,128)}, bf16[1024,768]{1,0:T(8,128)(2,1)}, bf16[1024,3072]{1,0:T(8,128)(2,1)}, bf16[1024,3072]{1,0:T(8,128)(2,1)}, bf16[1024,768]{1,0:T(8,128)(2,1)}) custom-call(s32[1]{0:T(128)} %bitcast.place, s32[2,6]{1,0:T(2,128)} %lengths.7, bf16[1024,768]{1,0:T(8,128)(2,1)} %bitcast.210, ...), custom_call_target="tpu_custom_call" | custom-call | flops 8455716864 | bytes 20447232 | tf_op jit(solution)/shard_map/hidden/pallas_call | solution.py:455
  122.0 9.6 %wide_outer.1 = bf16[8,768,384]{2,1,0:T(8,128)(2,1)} custom-call(s32[1]{0:T(128)} %bitcast.place, bf16[1024,768]{1,0:T(8,128)(2,1)} %get-tuple-element.204.left.grad_down, bf16[1024,3072]{1,0:T(8,128)(2,1)} %get-tuple-element.205.right.active), custom_call_target="tpu_custom_call" | custom-call | flops 4831838208 | bytes 13762560 | tf_op jit(solution)/shard_map/wide_outer/pallas_call | solution.py:682
  132.0 30.1 %back.1 = (bf16[1024,768]{1,0:T(8,128)(2,1)}, bf16[1024,3072]{1,0:T(8,128)(2,1)}, f32[1024,768]{1,0:T(8,128)}, bf16[1024,768]{1,0:T(8,128)(2,1)}, bf16[1024,768]...) custom-call(s32[1]{0:T(128)} %bitcast.place, s32[2,6]{1,0:T(2,128)} %lengths.7, bf16[1024,768]{1,0:T(8,128)(2,1)} %bitcast.211, ...), custom_call_target="tpu_custom_call" | custom-call | flops 15703474176 | bytes 31457280 | tf_op jit(solution)/shard_map/back/pallas_call | solution.py:547
  162.1 12.8 %outer.2 = (bf16[4,5,96,768]{3,2,1,0:T(8,128)(2,1)}, bf16[4,5,96,768]{3,2,1,0:T(8,128)(2,1)}) custom-call(s32[1]{0:T(128)} %bitcast.place, bf16[1024,768]{1,0:T(8,128)(2,1)} %get-tuple-element.212.refs_0_, bf16[1024,768]{1,0:T(8,128)(2,1)} %get-tuple-element.199.mixed.refs_1_, bf16[1024,3072]{1,0:T(8,128)(2,1)} %get-tuple-element.213.refs_2_, ...), custom_call_target="tpu_custom_call" | custom-call | flops 6039797760 | bytes 13762560 | tf_op jit(solution)/shard_map/outer/pallas_call | solution.py:651
  174.9 11.7 %attend_back.2 = (bf16[1024,768]{1,0:T(8,128)(2,1)}, bf16[1024,768]{1,0:T(8,128)(2,1)}, bf16[1024,768]{1,0:T(8,128)(2,1)}) custom-call(bf16[1024,768]{1,0:T(8,128)(2,1)} %get-tuple-element.195.query, bf16[1024,768]{1,0:T(8,128)(2,1)} %get-tuple-element.196.key, bf16[1024,768]{1,0:T(8,128)(2,1)} %get-tuple-element.197.value, ...), custom_call_target="tpu_custom_call" | custom-call | flops 6442450944 | bytes 5505024 | tf_op jit(solution)/shard_map/attend_back/pallas_call | solution.py:386
  186.6 1.6 copy-done.3
  188.2 4.9 %core_add.2 = (bf16[1,480,768]{2,1,0:T(8,128)(2,1)}, bf16[2,240,768]{2,1,0:T(8,128)(2,1)}, bf16[2,240,768]{2,1,0:T(8,128)(2,1)}, bf16[1,240,768]{2,1,0:T(8,128)(2,1)}, bf16[1,240,768]{2,1,0:T(8,128)(2,1)}) custom-call(bf16[4,480,768]{2,1,0:T(8,128)(2,1)} %bitcast.204, bf16[4,480,768]{2,1,0:T(8,128)(2,1)} %copy-done.3), custom_call_target="tpu_custom_call" | custom-call | flops 1474560 | bytes 8847360 | tf_op jit(solution)/shard_map/core_add/pallas_call | solution.py:786
  193.5 1.7 collective-permute-start.17
  195.3 11.6 %attend_back.3 = (bf16[1024,768]{1,0:T(8,128)(2,1)}, bf16[1024,768]{1,0:T(8,128)(2,1)}, bf16[1024,768]{1,0:T(8,128)(2,1)}) custom-call(bf16[1024,768]{1,0:T(8,128)(2,1)} %get-tuple-element.195.query, bf16[1024,768]{1,0:T(8,128)(2,1)} %get-tuple-element.196.key, ...), custom_call_target="tpu_custom_call", output_to_operand_aliasing={{0}: (5, {}), {1}: (6, {}), {2}: (7, {})} | custom-call | flops 6442450944 | bytes 5505024 | tf_op jit(solution)/shard_map/attend_back/pallas_call | solution.py:386
  206.9 5.3 %collective-permute-done.16 = bf16[1,2,240,768]{3,2,1,0:T(8,128)(2,1)S(1)} collective-permute-done((bf16[1,2,240,768]{3,2,1,0:T(8,128)(2,1)}, bf16[1,2,240,768]{3,2,1,0:T(8,128)(2,1)S(1)}, u32[]{:S(2)}, u32[]{:S(2)}) %collective-permute-start.16) | collective-permute-done | bytes 737312 | tf_op jit(solution)/shard_map/ppermute | solution.py:22
  212.8 1.4 collective-permute-start.18
  215.3 8.8 %outer.3 = (bf16[4,3,96,768]{3,2,1,0:T(8,128)(2,1)}, bf16[4,3,96,768]{3,2,1,0:T(8,128)(2,1)}) custom-call(s32[1]{0:T(128)} %bitcast.place, bf16[1024,768]{1,0:T(8,128)(2,1)} %get-tuple-element.248.refs_0_, bf16[1024,768]{1,0:T(8,128)(2,1)} %get-tuple-element.274.refs_1_.grad_q, bf16[1024,768]{1,0:T(8,128)(2,1)} %get-tuple-element.275.refs_2_.grad_k, ...), custom_call_target="tpu_custom_call" | custom-call | flops 3623878656 | bytes 8257536 | tf_op jit(solution)/shard_map/outer/pallas_call | solution.py:651
  224.9 3.9 %collective-permute-done.20.other = bf16[4,288,768]{2,1,0:T(8,128)(2,1)S(1)} collective-permute-done((bf16[4,288,768]{2,1,0:T(8,128)(2,1)}, bf16[4,288,768]{2,1,0:T(8,128)(2,1)S(1)}, u32[]{:S(2)}, u32[]{:S(2)}) %collective-permute-start.20) | collective-permute-done | bytes 1769504 | tf_op jit(solution)/shard_map/ppermute | solution.py:22
  230.0 3.5 %core_add.3 = (bf16[1,288,768]{2,1,0:T(8,128)(2,1)}, bf16[2,144,768]{2,1,0:T(8,128)(2,1)}, bf16[2,144,768]{2,1,0:T(8,128)(2,1)}, bf16[1,144,768]{2,1,0:T(8,128)(2,1)}, bf16[1,144,768]{2,1,0:T(8,128)(2,1)}) custom-call(bf16[4,288,768]{2,1,0:T(8,128)(2,1)} %bitcast.206, bf16[4,288,768]{2,1,0:T(8,128)(2,1)} %copy-done.5), custom_call_target="tpu_custom_call" | custom-call | flops 884736 | bytes 5308416 | tf_op jit(solution)/shard_map/core_add/pallas_call | solution.py:786
  233.4 1.4 collective-permute-start.21
  236.0 1.5 collective-permute-start.23
  237.5 2.4 collective-permute-start.24
  239.9 11.3 %inputs_back.1 = (f32[1024,768]{1,0:T(8,128)}, f32[8,768]{1,0:T(8,128)}) custom-call(s32[1]{0:T(128)} %bitcast.place, bf16[1024,768]{1,0:T(8,128)(2,1)} %bitcast.212, f32[1024,768]{1,0:T(8,128)} %get-tuple-element.209.grad_middle, bf16[1024,768]{1,0:T(8,128)(2,1)} %get-tuple-element.274.refs_1_.grad_q, bf16[1024,768]{1,0:T(8,128)(2,1)} %get-tuple-element.275.refs_2_.grad_k, ...), custom_call_target="tpu_custom_call" | custom-call | flops 3623878656 | bytes 15728640 | tf_op jit(solution)/shard_map/inputs_back/pallas_call | solution.py:725
  251.3 4.7 %collective-permute-done.25 = bf16[96,960]{1,0:T(8,128)(2,1)S(1)} collective-permute-done((bf16[96,960]{1,0:T(8,128)(2,1)S(1)}, bf16[96,960]{1,0:T(8,128)(2,1)S(1)}, u32[]{:S(2)}, u32[]{:S(2)}) %collective-permute-start.25) | collective-permute-done | bytes 184352 | tf_op jit(solution)/shard_map/ppermute | solution.py:22
  256.8 1.4 collective-permute-start.26
  259.1 1.7 collective-permute-start.29
  260.8 2.1 collective-permute-start.30
  262.9 3.0 %collective-permute-done.28 = f32[24,768]{1,0:T(8,128)S(1)} collective-permute-done((f32[24,768]{1,0:T(8,128)S(1)}, f32[24,768]{1,0:T(8,128)S(1)}, u32[]{:S(2)}, u32[]{:S(2)}) %collective-permute-start.28) | collective-permute-done | bytes 73760 | tf_op jit(solution)/shard_map/ppermute | solution.py:22
  265.9 1.5 collective-permute-done.29
  269.3 1.4 collective-permute-start.31
  270.6 1.2 collective-permute-start.32
  271.9 1.2 collective-permute-start.33
  273.1 1.4 collective-permute-start.35
  274.5 1.5 collective-permute-start.36
  278.1 1.7 collective-permute-done.36
  (180 shorter events, 24.9 us)
Async XLA Ops:
  7.2 23.0 %copy-start.7 = (bf16[96,576]{1,0:T(8,128)(2,1)S(1)}, bf16[96,576]{1,0:T(8,128)(2,1)}, u32[]{:S(2)}) copy-start(bf16[96,576]{1,0:T(8,128)(2,1)} %param.20) | copy-start | bytes 331780
  7.2 23.0 %copy-start.12 = (bf16[96,192]{1,0:T(8,128)(2,1)S(1)}, bf16[96,192]{1,0:T(8,128)(2,1)}, u32[]{:S(2)}) copy-start(bf16[96,192]{1,0:T(8,128)(2,1)} %param.21) | copy-start | bytes 110596
  7.2 95.5 %all-gather.5.cloned.1.call-start = ((), (), s32[]{:S(2)}) async-start(), calls=%async_computation.4 | async-start | bytes 5308416 | tf_op jit(solution)/shard_map/all_gather | solution.py:925
  10.4 9.9 %collective-permute-start = (bf16[112,768]{1,0:T(8,128)(2,1)S(1)}, bf16[112,768]{1,0:T(8,128)(2,1)S(1)}, u32[]{:S(2)}, u32[]{:S(2)}) collective-permute-start(bf16[112,768]{1,0:T(8,128)(2,1)S(1)} %fusion.16), channel_id=1, source_target_pairs={{0,3},{1,0},{2,1},{3,2},{4,7},{5,4},{6,5},{7,6},{8,11},{9,8},{10,9... | collective-permute-start | bytes 516104 | tf_op jit(solution)/shard_map/ppermute | solution.py:22
  15.6 14.6 %collective-permute-start.1 = (bf16[112,768]{1,0:T(8,128)(2,1)S(1)}, bf16[112,768]{1,0:T(8,128)(2,1)S(1)}, u32[]{:S(2)}, u32[]{:S(2)}) collective-permute-start(bf16[112,768]{1,0:T(8,128)(2,1)S(1)} %fusion.16), channel_id=1, source_target_pairs={{0,2},{1,3},{2,0},{3,1},{4,6},{5,7},{6,4},{7,5},{8,10},{9,11},{10,... | collective-permute-start | bytes 516104 | tf_op jit(solution)/shard_map/ppermute | solution.py:22
  15.6 14.6 %collective-permute-start.2 = (bf16[112,768]{1,0:T(8,128)(2,1)S(1)}, bf16[112,768]{1,0:T(8,128)(2,1)S(1)}, u32[]{:S(2)}, u32[]{:S(2)}) collective-permute-start(bf16[112,768]{1,0:T(8,128)(2,1)S(1)} %fusion.16), channel_id=1, source_target_pairs={{0,1},{1,2},{2,3},{3,0},{4,5},{5,6},{6,7},{7,4},{8,9},{9,10},{10,1... | collective-permute-start | bytes 516104 | tf_op jit(solution)/shard_map/ppermute | solution.py:22
  31.3 18.2 %copy-start.2 = (bf16[400,768]{1,0:T(8,128)(2,1)}, bf16[400,768]{1,0:T(8,128)(2,1)S(1)}, u32[]{:S(2)}) copy-start(bf16[400,768]{1,0:T(8,128)(2,1)S(1)} %constant_dynamic-update-slice_fusion) | copy-start | bytes 1843204
  31.3 16.3 %collective-permute-start.3 = (bf16[1,400,768]{2,1,0:T(8,128)(2,1)S(1)}, bf16[1,400,768]{2,1,0:T(8,128)(2,1)S(1)}, u32[]{:S(2)}, u32[]{:S(2)}) collective-permute-start(bf16[1,400,768]{2,1,0:T(8,128)(2,1)S(1)} %bitcast.197), channel_id=1, source_target_pairs={{0,8},{4,12},{8,0},{12,4},{16,24},{20,28},{24,16},{28,20},{1,9},{5... | collective-permute-start | bytes 1843208 | tf_op jit(solution)/shard_map/ppermute | solution.py:22
  32.8 15.2 %collective-permute-start.4 = (bf16[1,400,768]{2,1,0:T(8,128)(2,1)S(1)}, bf16[1,400,768]{2,1,0:T(8,128)(2,1)S(1)}, u32[]{:S(2)}, u32[]{:S(2)}) collective-permute-start(bf16[1,400,768]{2,1,0:T(8,128)(2,1)S(1)} %bitcast.198), channel_id=1, source_target_pairs={{0,16},{4,20},{8,24},{12,28},{16,0},{20,4},{24,8},{28,12},{1,17},{... | collective-permute-start | bytes 1843208 | tf_op jit(solution)/shard_map/ppermute | solution.py:22
  34.3 8.6 %collective-permute-start.5 = (bf16[96,768]{1,0:T(8,128)(2,1)S(1)}, bf16[96,768]{1,0:T(8,128)(2,1)S(1)}, u32[]{:S(2)}, u32[]{:S(2)}) collective-permute-start(bf16[96,768]{1,0:T(8,128)(2,1)S(1)} %copy-done.10), channel_id=1, source_target_pairs={{0,1},{1,2},{2,3},{3,0},{4,5},{5,6},{6,7},{7,4},{8,9},{9,10},{10,1... | collective-permute-start | bytes 442376 | tf_op jit(solution)/shard_map/ppermute | solution.py:22
  35.2 12.3 %collective-permute-start.6 = (bf16[96,768]{1,0:T(8,128)(2,1)S(1)}, bf16[96,768]{1,0:T(8,128)(2,1)S(1)}, u32[]{:S(2)}, u32[]{:S(2)}) collective-permute-start(bf16[96,768]{1,0:T(8,128)(2,1)S(1)} %copy-done.10), channel_id=1, source_target_pairs={{0,2},{1,3},{2,0},{3,1},{4,6},{5,7},{6,4},{7,5},{8,10},{9,11},{10,... | collective-permute-start | bytes 442376 | tf_op jit(solution)/shard_map/ppermute | solution.py:22
  37.1 10.4 %collective-permute-start.7 = (bf16[96,768]{1,0:T(8,128)(2,1)S(1)}, bf16[96,768]{1,0:T(8,128)(2,1)S(1)}, u32[]{:S(2)}, u32[]{:S(2)}) collective-permute-start(bf16[96,768]{1,0:T(8,128)(2,1)S(1)} %copy-done.10), channel_id=1, source_target_pairs={{0,3},{1,0},{2,1},{3,2},{4,7},{5,4},{6,5},{7,6},{8,11},{9,8},{10,9... | collective-permute-start | bytes 442376 | tf_op jit(solution)/shard_map/ppermute | solution.py:22
  50.6 81.4 %all-gather.7.cloned.1.call-start = ((), (), s32[]{:S(2)}) async-start(), calls=%async_computation.5 | async-start | bytes 5308416 | tf_op jit(solution)/shard_map/all_gather | solution.py:941
  50.6 10.0 %collective-permute-start.10 = (bf16[3,400,768]{2,1,0:T(8,128)(2,1)}, bf16[3,400,768]{2,1,0:T(8,128)(2,1)S(1)}, u32[]{:S(2)}, u32[]{:S(2)}) collective-permute-start(bf16[3,400,768]{2,1,0:T(8,128)(2,1)} %pad_maximum_fusion), channel_id=1, source_target_pairs={{0,4},{4,0},{8,12},{12,8},{16,20},{20,16},{24,28},{28,24},{1,5},{5... | collective-permute-start | bytes 5529608 | tf_op jit(solution)/shard_map/ppermute | solution.py:22
  50.7 10.0 %collective-permute-start.9 = (bf16[1,208,768]{2,1,0:T(8,128)(2,1)S(1)}, bf16[1,208,768]{2,1,0:T(8,128)(2,1)S(1)}, u32[]{:S(2)}, u32[]{:S(2)}) collective-permute-start(bf16[1,208,768]{2,1,0:T(8,128)(2,1)S(1)} %slice.270), channel_id=1, source_target_pairs={{0,8},{4,12},{8,0},{12,4},{16,24},{20,28},{24,16},{28,20},{1,9},{5... | collective-permute-start | bytes 958472 | tf_op jit(solution)/shard_map/ppermute | solution.py:22
  51.3 9.1 %collective-permute-start.8 = (bf16[1,192,768]{2,1,0:T(8,128)(2,1)S(1)}, bf16[1,192,768]{2,1,0:T(8,128)(2,1)S(1)}, u32[]{:S(2)}, u32[]{:S(2)}) collective-permute-start(bf16[1,192,768]{2,1,0:T(8,128)(2,1)S(1)} %slice.269), channel_id=1, source_target_pairs={{0,16},{4,20},{8,24},{12,28},{16,0},{20,4},{24,8},{28,12},{1,17},{... | collective-permute-start | bytes 884744 | tf_op jit(solution)/shard_map/ppermute | solution.py:22
  60.7 6.8 %collective-permute-start.11 = (bf16[1,400,768]{2,1,0:T(8,128)(2,1)S(1)}, bf16[1,400,768]{2,1,0:T(8,128)(2,1)S(1)}, u32[]{:S(2)}, u32[]{:S(2)}) collective-permute-start(bf16[1,400,768]{2,1,0:T(8,128)(2,1)S(1)} %constant_dynamic-update-slice_fusion.1.refs_3_), channel_id=1, source_target_pairs={{0,4},{4,0},{8,12},{12,8},{16,20},{20,16},{24,28},{28,24},{1,5},{5... | collective-permute-start | bytes 1843208 | tf_op jit(solution)/shard_map/ppermute | solution.py:22
  61.5 17.1 %collective-permute-start.12 = (bf16[96,768]{1,0:T(8,128)(2,1)S(1)}, bf16[96,768]{1,0:T(8,128)(2,1)S(1)}, u32[]{:S(2)}, u32[]{:S(2)}) collective-permute-start(bf16[96,768]{1,0:T(8,128)(2,1)S(1)} %pad_maximum_fusion.4), channel_id=1, source_target_pairs={{0,1},{1,2},{2,3},{3,0},{4,5},{5,6},{6,7},{7,4},{8,9},{9,10},{10,1... | collective-permute-start | bytes 442376 | tf_op jit(solution)/shard_map/ppermute | solution.py:22
  65.1 13.5 %collective-permute-start.13 = (bf16[96,768]{1,0:T(8,128)(2,1)S(1)}, bf16[96,768]{1,0:T(8,128)(2,1)S(1)}, u32[]{:S(2)}, u32[]{:S(2)}) collective-permute-start(bf16[96,768]{1,0:T(8,128)(2,1)S(1)} %pad_maximum_fusion.4), channel_id=1, source_target_pairs={{0,2},{1,3},{2,0},{3,1},{4,6},{5,7},{6,4},{7,5},{8,10},{9,11},{10,... | collective-permute-start | bytes 442376 | tf_op jit(solution)/shard_map/ppermute | solution.py:22
  67.1 11.5 %collective-permute-start.14 = (bf16[96,768]{1,0:T(8,128)(2,1)S(1)}, bf16[96,768]{1,0:T(8,128)(2,1)S(1)}, u32[]{:S(2)}, u32[]{:S(2)}) collective-permute-start(bf16[96,768]{1,0:T(8,128)(2,1)S(1)} %pad_maximum_fusion.4), channel_id=1, source_target_pairs={{0,3},{1,0},{2,1},{3,2},{4,7},{5,4},{6,5},{7,6},{8,11},{9,8},{10,9... | collective-permute-start | bytes 442376 | tf_op jit(solution)/shard_map/ppermute | solution.py:22
  80.1 112.9 %reduce-scatter.3.cloned.1.call-start = ((), (), s32[]{:S(2)}) async-start(), calls=%async_computation.2 | async-start | bytes 5308416 | tf_op jit(solution)/shard_map/reduce_scatter | solution.py:955
  131.7 93.1 %reduce-scatter.5.cloned.1.call-start = ((), (), s32[]{:S(2)}) async-start(), calls=%async_computation.3 | async-start | bytes 737280 | tf_op jit(solution)/shard_map/reduce_scatter | solution.py:971
  174.9 11.7 %collective-permute-start.15 = (bf16[4,480,768]{2,1,0:T(8,128)(2,1)}, bf16[4,480,768]{2,1,0:T(8,128)(2,1)S(1)}, u32[]{:S(2)}, u32[]{:S(2)}) collective-permute-start(bf16[4,480,768]{2,1,0:T(8,128)(2,1)} %bitcast.229), channel_id=1, source_target_pairs={{0,4},{4,0},{8,12},{12,8},{16,20},{20,16},{24,28},{28,24},{1,5},{5... | collective-permute-start | bytes 8847368 | tf_op jit(solution)/shard_map/ppermute | solution.py:22
  193.0 19.2 %collective-permute-start.16 = (bf16[1,2,240,768]{3,2,1,0:T(8,128)(2,1)}, bf16[1,2,240,768]{3,2,1,0:T(8,128)(2,1)S(1)}, u32[]{:S(2)}, u32[]{:S(2)}) collective-permute-start(bf16[1,2,240,768]{3,2,1,0:T(8,128)(2,1)} %bitcast.234), channel_id=1, source_target_pairs={{0,8},{4,12},{8,0},{12,4},{16,24},{20,28},{24,16},{28,20},{1,9},{5... | collective-permute-start | bytes 2211848 | tf_op jit(solution)/shard_map/ppermute | solution.py:22
  193.5 19.1 %collective-permute-start.17 = (bf16[1,2,240,768]{3,2,1,0:T(8,128)(2,1)}, bf16[1,2,240,768]{3,2,1,0:T(8,128)(2,1)S(1)}, u32[]{:S(2)}, u32[]{:S(2)}) collective-permute-start(bf16[1,2,240,768]{3,2,1,0:T(8,128)(2,1)} %bitcast.233), channel_id=1, source_target_pairs={{0,16},{4,20},{8,24},{12,28},{16,0},{20,4},{24,8},{28,12},{1,17},{... | collective-permute-start | bytes 2211848 | tf_op jit(solution)/shard_map/ppermute | solution.py:22
  195.3 17.3 %copy-start.13 = (bf16[1,240,768]{2,1,0:T(8,128)(2,1)S(1)}, bf16[1,240,768]{2,1,0:T(8,128)(2,1)}, u32[]{:S(2)}) copy-start(bf16[1,240,768]{2,1,0:T(8,128)(2,1)} %get-tuple-element.243) | copy-start | bytes 1105924
  195.3 17.3 %copy-start.14 = (bf16[1,240,768]{2,1,0:T(8,128)(2,1)S(1)}, bf16[1,240,768]{2,1,0:T(8,128)(2,1)}, u32[]{:S(2)}) copy-start(bf16[1,240,768]{2,1,0:T(8,128)(2,1)} %get-tuple-element.245) | copy-start | bytes 1105924
  212.8 11.3 %collective-permute-start.18 = (bf16[1,240,768]{2,1,0:T(8,128)(2,1)S(1)}, bf16[1,240,768]{2,1,0:T(8,128)(2,1)S(1)}, u32[]{:S(2)}, u32[]{:S(2)}) collective-permute-start(bf16[1,240,768]{2,1,0:T(8,128)(2,1)S(1)} %get-tuple-element.254), channel_id=1, source_target_pairs={{0,8},{4,12},{8,0},{12,4},{16,24},{20,28},{24,16},{28,20},{1,9},{5... | collective-permute-start | bytes 1105928 | tf_op jit(solution)/shard_map/ppermute | solution.py:22
  214.2 9.8 %collective-permute-start.19 = (bf16[1,240,768]{2,1,0:T(8,128)(2,1)S(1)}, bf16[1,240,768]{2,1,0:T(8,128)(2,1)S(1)}, u32[]{:S(2)}, u32[]{:S(2)}) collective-permute-start(bf16[1,240,768]{2,1,0:T(8,128)(2,1)S(1)} %get-tuple-element.255), channel_id=1, source_target_pairs={{0,16},{4,20},{8,24},{12,28},{16,0},{20,4},{24,8},{28,12},{1,17},{... | collective-permute-start | bytes 1105928 | tf_op jit(solution)/shard_map/ppermute | solution.py:22
  224.8 4.0 %collective-permute-start.20 = (bf16[4,288,768]{2,1,0:T(8,128)(2,1)}, bf16[4,288,768]{2,1,0:T(8,128)(2,1)S(1)}, u32[]{:S(2)}, u32[]{:S(2)}) collective-permute-start(bf16[4,288,768]{2,1,0:T(8,128)(2,1)} %bitcast.230), channel_id=1, source_target_pairs={{0,4},{4,0},{8,12},{12,8},{16,20},{20,16},{24,28},{28,24},{1,5},{5... | collective-permute-start | bytes 5308424 | tf_op jit(solution)/shard_map/ppermute | solution.py:22
  233.4 22.5 %collective-permute-start.21 = (bf16[1,2,144,768]{3,2,1,0:T(8,128)(2,1)}, bf16[1,2,144,768]{3,2,1,0:T(8,128)(2,1)S(1)}, u32[]{:S(2)}, u32[]{:S(2)}) collective-permute-start(bf16[1,2,144,768]{3,2,1,0:T(8,128)(2,1)} %bitcast.236), channel_id=1, source_target_pairs={{0,8},{4,12},{8,0},{12,4},{16,24},{20,28},{24,16},{28,20},{1,9},{5... | collective-permute-start | bytes 1327112 | tf_op jit(solution)/shard_map/ppermute | solution.py:22
  234.9 21.1 %collective-permute-start.22 = (bf16[1,2,144,768]{3,2,1,0:T(8,128)(2,1)}, bf16[1,2,144,768]{3,2,1,0:T(8,128)(2,1)S(1)}, u32[]{:S(2)}, u32[]{:S(2)}) collective-permute-start(bf16[1,2,144,768]{3,2,1,0:T(8,128)(2,1)} %bitcast.235), channel_id=1, source_target_pairs={{0,16},{4,20},{8,24},{12,28},{16,0},{20,4},{24,8},{28,12},{1,17},{... | collective-permute-start | bytes 1327112 | tf_op jit(solution)/shard_map/ppermute | solution.py:22
  236.0 15.2 %collective-permute-start.23 = (bf16[96,960]{1,0:T(8,128)(2,1)S(1)}, bf16[96,960]{1,0:T(8,128)(2,1)S(1)}, u32[]{:S(2)}, u32[]{:S(2)}) collective-permute-start(bf16[96,960]{1,0:T(8,128)(2,1)S(1)} %get-tuple-element.281), channel_id=1, source_target_pairs={{0,1},{1,2},{2,3},{3,0},{4,5},{5,6},{6,7},{7,4},{8,9},{9,10},{10,1... | collective-permute-start | bytes 552968 | tf_op jit(solution)/shard_map/ppermute | solution.py:22
  237.5 13.8 %collective-permute-start.24 = (bf16[96,960]{1,0:T(8,128)(2,1)S(1)}, bf16[96,960]{1,0:T(8,128)(2,1)S(1)}, u32[]{:S(2)}, u32[]{:S(2)}) collective-permute-start(bf16[96,960]{1,0:T(8,128)(2,1)S(1)} %get-tuple-element.282), channel_id=1, source_target_pairs={{0,3},{1,0},{2,1},{3,2},{4,7},{5,4},{6,5},{7,6},{8,11},{9,8},{10,9... | collective-permute-start | bytes 552968 | tf_op jit(solution)/shard_map/ppermute | solution.py:22
  239.9 16.1 %collective-permute-start.25 = (bf16[96,960]{1,0:T(8,128)(2,1)S(1)}, bf16[96,960]{1,0:T(8,128)(2,1)S(1)}, u32[]{:S(2)}, u32[]{:S(2)}) collective-permute-start(bf16[96,960]{1,0:T(8,128)(2,1)S(1)} %get-tuple-element.283), channel_id=1, source_target_pairs={{0,2},{1,3},{2,0},{3,1},{4,6},{5,7},{6,4},{7,5},{8,10},{9,11},{10,... | collective-permute-start | bytes 552968 | tf_op jit(solution)/shard_map/ppermute | solution.py:22
  239.9 16.9 %copy-start.16 = (bf16[1,144,768]{2,1,0:T(8,128)(2,1)S(1)}, bf16[1,144,768]{2,1,0:T(8,128)(2,1)}, u32[]{:S(2)}) copy-start(bf16[1,144,768]{2,1,0:T(8,128)(2,1)} %get-tuple-element.292) | copy-start | bytes 663556
  256.8 10.6 %collective-permute-start.26 = (bf16[1,144,768]{2,1,0:T(8,128)(2,1)S(1)}, bf16[1,144,768]{2,1,0:T(8,128)(2,1)S(1)}, u32[]{:S(2)}, u32[]{:S(2)}) collective-permute-start(bf16[1,144,768]{2,1,0:T(8,128)(2,1)S(1)} %fusion.3), channel_id=1, source_target_pairs={{0,8},{4,12},{8,0},{12,4},{16,24},{20,28},{24,16},{28,20},{1,9},{5... | collective-permute-start | bytes 663560 | tf_op jit(solution)/shard_map/ppermute | solution.py:22
  258.3 9.1 %collective-permute-start.27 = (bf16[1,144,768]{2,1,0:T(8,128)(2,1)S(1)}, bf16[1,144,768]{2,1,0:T(8,128)(2,1)S(1)}, u32[]{:S(2)}, u32[]{:S(2)}) collective-permute-start(bf16[1,144,768]{2,1,0:T(8,128)(2,1)S(1)} %fusion.2), channel_id=1, source_target_pairs={{0,16},{4,20},{8,24},{12,28},{16,0},{20,4},{24,8},{28,12},{1,17},{... | collective-permute-start | bytes 663560 | tf_op jit(solution)/shard_map/ppermute | solution.py:22
  259.1 6.8 %collective-permute-start.28 = (f32[24,768]{1,0:T(8,128)S(1)}, f32[24,768]{1,0:T(8,128)S(1)}, u32[]{:S(2)}, u32[]{:S(2)}) collective-permute-start(f32[24,768]{1,0:T(8,128)S(1)} %pad_maximum_fusion.7), channel_id=1, source_target_pairs={{0,1},{1,2},{2,3},{3,0},{4,5},{5,6},{6,7},{7,4},{8,9},{9,10},{10,1... | collective-permute-start | bytes 221192 | tf_op jit(solution)/shard_map/ppermute | solution.py:22
  259.1 8.3 %collective-permute-start.29 = (f32[24,768]{1,0:T(8,128)S(1)}, f32[24,768]{1,0:T(8,128)S(1)}, u32[]{:S(2)}, u32[]{:S(2)}) collective-permute-start(f32[24,768]{1,0:T(8,128)S(1)} %pad_maximum_fusion.7), channel_id=1, source_target_pairs={{0,2},{1,3},{2,0},{3,1},{4,6},{5,7},{6,4},{7,5},{8,10},{9,11},{10,... | collective-permute-start | bytes 221192 | tf_op jit(solution)/shard_map/ppermute | solution.py:22
  260.8 6.6 %collective-permute-start.30 = (f32[24,768]{1,0:T(8,128)S(1)}, f32[24,768]{1,0:T(8,128)S(1)}, u32[]{:S(2)}, u32[]{:S(2)}) collective-permute-start(f32[24,768]{1,0:T(8,128)S(1)} %pad_maximum_fusion.7), channel_id=1, source_target_pairs={{0,3},{1,0},{2,1},{3,2},{4,7},{5,4},{6,5},{7,6},{8,11},{9,8},{10,9... | collective-permute-start | bytes 221192 | tf_op jit(solution)/shard_map/ppermute | solution.py:22
  267.8 6.6 %collective-permute-start.34 = (f32[24,768]{1,0:T(8,128)S(1)}, f32[24,768]{1,0:T(8,128)S(1)}, u32[]{:S(2)}, u32[]{:S(2)}) collective-permute-start(f32[24,768]{1,0:T(8,128)S(1)} %add_add_fusion.1), channel_id=1, source_target_pairs={{0,8},{4,12},{8,0},{12,4},{16,24},{20,28},{24,16},{28,20},{1,9},{5... | collective-permute-start | bytes 221192 | tf_op jit(solution)/shard_map/ppermute | solution.py:22
  269.3 10.5 %collective-permute-start.31 = (bf16[96,640]{1,0:T(8,128)(2,1)S(1)}, bf16[96,640]{1,0:T(8,128)(2,1)S(1)}, u32[]{:S(2)}, u32[]{:S(2)}) collective-permute-start(bf16[96,640]{1,0:T(8,128)(2,1)S(1)} %get-tuple-element.306), channel_id=1, source_target_pairs={{0,1},{1,2},{2,3},{3,0},{4,5},{5,6},{6,7},{7,4},{8,9},{9,10},{10,1... | collective-permute-start | bytes 368648 | tf_op jit(solution)/shard_map/ppermute | solution.py:22
  270.6 9.6 %collective-permute-start.32 = (bf16[96,640]{1,0:T(8,128)(2,1)S(1)}, bf16[96,640]{1,0:T(8,128)(2,1)S(1)}, u32[]{:S(2)}, u32[]{:S(2)}) collective-permute-start(bf16[96,640]{1,0:T(8,128)(2,1)S(1)} %get-tuple-element.307), channel_id=1, source_target_pairs={{0,2},{1,3},{2,0},{3,1},{4,6},{5,7},{6,4},{7,5},{8,10},{9,11},{10,... | collective-permute-start | bytes 368648 | tf_op jit(solution)/shard_map/ppermute | solution.py:22
  271.9 8.3 %collective-permute-start.33 = (bf16[96,640]{1,0:T(8,128)(2,1)S(1)}, bf16[96,640]{1,0:T(8,128)(2,1)S(1)}, u32[]{:S(2)}, u32[]{:S(2)}) collective-permute-start(bf16[96,640]{1,0:T(8,128)(2,1)S(1)} %get-tuple-element.308), channel_id=1, source_target_pairs={{0,3},{1,0},{2,1},{3,2},{4,7},{5,4},{6,5},{7,6},{8,11},{9,8},{10,9... | collective-permute-start | bytes 368648 | tf_op jit(solution)/shard_map/ppermute | solution.py:22
  273.1 5.0 %collective-permute-start.35 = (f32[24,768]{1,0:T(8,128)S(1)}, f32[24,768]{1,0:T(8,128)S(1)}, u32[]{:S(2)}, u32[]{:S(2)}) collective-permute-start(f32[24,768]{1,0:T(8,128)S(1)} %add_add_fusion.1), channel_id=1, source_target_pairs={{0,16},{4,20},{8,24},{12,28},{16,0},{20,4},{24,8},{28,12},{1,17},{... | collective-permute-start | bytes 221192 | tf_op jit(solution)/shard_map/ppermute | solution.py:22
  274.5 5.3 %collective-permute-start.36 = (f32[24,768]{1,0:T(8,128)S(1)}, f32[24,768]{1,0:T(8,128)S(1)}, u32[]{:S(2)}, u32[]{:S(2)}) collective-permute-start(f32[24,768]{1,0:T(8,128)S(1)} %add_add_fusion.1), channel_id=1, source_target_pairs={{0,24},{4,28},{8,16},{12,20},{16,8},{20,12},{24,0},{28,4},{1,25},{... | collective-permute-start | bytes 221192 | tf_op jit(solution)/shard_map/ppermute | solution.py:22
  280.2 1.3 collective-permute-start.37
  (18 other events, 105.6 us)
Sparse Core Ops, SparseCore 0:
  50.7 38.7 all-gather.4
  91.4 38.9 all-gather.6
  133.8 53.8 reduce-scatter.2
  195.4 21.6 reduce-scatter.4

commit v5 on v4

--- a/solution.py
+++ b/solution.py
@@ -9,6 +9,7 @@
 from jax.sharding import PartitionSpec as P
 
 HD = 64
+HEADS = 4
 LN_EPSILON = 1e-06
 MASKED = -1e30
 TILE = 256
@@ -308,7 +309,14 @@
 
 def head_lanes(shape, head):
     lane = lax.broadcasted_iota(jnp.int32, shape, 1)
-    return (lane < HD) if head == 0 else (lane >= HD)
+    return (lane >= head * HD) & (lane < (head + 1) * HD)
+
+
+def by_lanes(heads):
+    chosen = heads[-1]
+    for head in reversed(range(len(heads) - 1)):
+        chosen = jnp.where(head_lanes(chosen.shape, head), heads[head], chosen)
+    return chosen
 
 
 def only(values, head):
@@ -321,7 +329,7 @@
     same = same_segment(lengths, pack, rows)
     flat = jnp.transpose(value[...].astype(F32)).astype(BF16)
     mixed = []
-    for head in range(2):
+    for head in range(HEADS):
         scores = dot_nt(key[...], only(query[...], head))
         scores = jnp.where(same, scores, MASKED)
         top = jnp.max(scores, axis=0, keepdims=True)
@@ -333,18 +341,18 @@
     attended[...] = jnp.transpose(jnp.concatenate(mixed, axis=0)).astype(BF16)
 
 
-def pair_block(rows, pack):
-    return pl.BlockSpec((rows, 2 * HD), lambda h: (pack, h))
-
-
-def kept_block(rows):
-    return pl.BlockSpec((2, rows, rows), lambda h: (h, 0, 0))
+def pair_block(rows, pack, first=0):
+    return pl.BlockSpec((rows, HEADS * HD), lambda h: (pack, h + first))
+
+
+def kept_block(rows, first=0):
+    return pl.BlockSpec((HEADS, rows, rows), lambda h: (h + first, 0, 0))
 
 
 def attend(lengths, query, key, value, pack, earlier=()):
     packs = lengths.shape[0]
     count, width = query.shape
-    rows, pairs = count // packs, width // (2 * HD)
+    rows, pairs = count // packs, width // (HEADS * HD)
     return pl.pallas_call(
         functools.partial(attend_kernel, pack),
         grid=(pairs,),
@@ -352,7 +360,7 @@
         out_specs=[pair_block(rows, pack), kept_block(rows)],
         out_shape=[
             jax.ShapeDtypeStruct(query.shape, BF16),
-            jax.ShapeDtypeStruct((2 * pairs, rows, rows), BF16),
+            jax.ShapeDtypeStruct((HEADS * pairs, rows, rows), BF16),
         ],
         input_output_aliases={4 + i: i for i in range(len(earlier))},
         compiler_params=params(60),
@@ -365,7 +373,7 @@
     grad_q, grad_k, grad_v = refs[-3:]
     flat_key = jnp.transpose(key[...].astype(F32)).astype(BF16)
     by_query, by_key, by_value = [], [], []
-    for head in range(2):
+    for head in range(HEADS):
         weights = kept[head]
         probs = weights.astype(F32)
         by_value.append(dot(weights, grad[...]))
@@ -374,24 +382,26 @@
         grad_scores = (probs * (grad_probs - centre)).astype(BF16)
         by_key.append(dot(grad_scores, query[...]))
         by_query.append(dot(flat_key[head * HD : (head + 1) * HD], grad_scores))
-    lanes = head_lanes(by_key[0].shape, 0)
-    grad_k[...] = jnp.where(lanes, by_key[0], by_key[1]).astype(BF16)
-    grad_v[...] = jnp.where(lanes, by_value[0], by_value[1]).astype(BF16)
+    grad_k[...] = by_lanes(by_key).astype(BF16)
+    grad_v[...] = by_lanes(by_value).astype(BF16)
     grad_q[...] = jnp.transpose(jnp.concatenate(by_query, axis=0)).astype(BF16) * 0.125
 
 
-def attend_back(query, key, value, grad, kept, pack, earlier=()):
-    pairs, rows = kept.shape[0] // 2, kept.shape[1]
+def attend_back(query, key, value, grad, kept, pack, first, last, earlier=()):
+    rows = kept.shape[1]
     width = query.shape[1]
+    part = last - first
     return pl.pallas_call(
         attend_back_kernel,
-        grid=(pairs,),
-        in_specs=[pair_block(rows, pack)] * 4 + [kept_block(rows)] + [ANY] * len(earlier),
-        out_specs=[pair_block(rows, pack)] * 3,
+        grid=(part,),
+        in_specs=[pair_block(rows, pack, first)] * 4
+        + [kept_block(rows, first)]
+        + [ANY] * len(earlier),
+        out_specs=[pair_block(rows, pack, first)] * 3,
         out_shape=[jax.ShapeDtypeStruct(query.shape, BF16)] * 3,
         input_output_aliases={5 + i: i for i in range(len(earlier))},
         compiler_params=params(60),
-        cost_estimate=cost(32 * rows * rows * width, 14 * rows * width, 0),
+        cost_estimate=cost(32 * rows * rows * HEADS * HD * part, 14 * rows * HEADS * HD * part, 0),
         name="attend_back",
     )(query, key, value, grad, kept, *earlier)
 
@@ -478,7 +488,7 @@
     )(place, lengths, rows, mixed, cotangent, table, *group_one[0], *group_two[0])
 
 
-STATS_TWO = 7
+STATS_UP, STATS_ONE = 6, 10
 
 
 def back_kernel(
@@ -488,8 +498,8 @@
     sources, refs = refs[: sum(sizes)], refs[sum(sizes) :]
     one, two = sources[: sizes[0]], sources[sizes[0] : sizes[0] + sizes[1]]
     three = sources[sizes[0] + sizes[1] :]
-    result, grad_hidden, grad_middle_out, grad_branch, grad_mixed, stats, hidden_stats = refs[:7]
-    out_w, up_w, down_w, sems = refs[7:]
+    result, grad_hidden, grad_middle_out, grad_branch, grad_mixed, stats = refs[:6]
+    out_w, up_w, down_w, sems = refs[6:]
     made = [copies(place[0], three, down_plan, down_w, sems, 0)]
     first = len(down_plan)
     for m, plan in enumerate(up_plans):
@@ -502,7 +512,6 @@
         for group in made:
             start_all(group)
         stats[...] = jnp.zeros_like(stats)
-        hidden_stats[...] = jnp.zeros_like(hidden_stats)
         wait_all(made[0])
 
     live = live_rows(lengths, cotangent.shape)
@@ -525,7 +534,7 @@
         grad_active = dot_nt(grad_down[...], down_w[part, :])
         low = (grad_active * slope[:, part].astype(F32)).astype(BF16)
         grad_hidden[:, part] = low
-        hidden_stats[m : m + 1, :] += row_sum(low.astype(F32))
+        stats[STATS_UP + m : STATS_UP + m + 1, :] += row_sum(low.astype(F32))
         grad_normed += dot_nt(low, up_w[m])
     unit_rows, inverse = centred_rows(middle)
     sums += [row_sum(grad_normed * unit_rows), row_sum(grad_normed)]
@@ -555,15 +564,14 @@
         + [ANY] * sum(sizes),
         out_specs=[tile_of(width), tile_of(hidden_units)]
         + [tile_of(width)] * 3
-        + [whole((8, width)), whole((8, width))],
+        + [whole((16, width))],
         out_shape=[
             jax.ShapeDtypeStruct(rows.shape, BF16),
             jax.ShapeDtypeStruct(active.shape, BF16),
             jax.ShapeDtypeStruct(rows.shape, F32),
             jax.ShapeDtypeStruct(rows.shape, BF16),
             jax.ShapeDtypeStruct(rows.shape, BF16),
-            jax.ShapeDtypeStruct((8, width), F32),
-            jax.ShapeDtypeStruct((8, width), F32),
+            jax.ShapeDtypeStruct((16, width), F32),
         ],
         scratch_shapes=[
             pltpu.VMEM((width, width), BF16),
@@ -692,7 +700,7 @@
     )(place, left, right)
 
 
-def inputs_kernel(plans, place, rows, grad_middle, grad_q, grad_k, grad_v, table, *refs):
+def inputs_kernel(plans, place, rows, grad_middle, grad_q, grad_k, grad_v, table, earlier, *refs):
     count = len(refs) - 2 - 2
     sources, (grad_rows, stats, weights, sems) = refs[:count], refs[count:]
     made, first = [], 0
@@ -704,7 +712,7 @@
     def _():
         for group in made:
             start_all(group)
-        stats[...] = jnp.zeros_like(stats)
+        stats[...] = earlier[...]
         for group in made:
             wait_all(group)
 
@@ -716,20 +724,20 @@
     sums = [row_sum(grad * unit_rows), row_sum(grad)]
     sums += [row_sum(grad_q[...].astype(F32)), row_sum(grad_v[...].astype(F32))]
     for at, total in enumerate(sums):
-        stats[at : at + 1, :] += total
-
-
-def inputs_back(place, rows, grad_middle, grad_q, grad_k, grad_v, table, group):
+        stats[STATS_ONE + at : STATS_ONE + at + 1, :] += total
+
+
+def inputs_back(place, rows, grad_middle, grad_q, grad_k, grad_v, table, earlier, group):
     arrays, plans = group
     count, width = rows.shape
     return pl.pallas_call(
         functools.partial(inputs_kernel, plans),
         grid=(count // TILE,),
-        in_specs=[SMEM] + [tile_of(width)] * 5 + [whole(table.shape)] + [ANY] * len(arrays),
-        out_specs=[tile_of(width), whole((8, width))],
+        in_specs=[SMEM] + [tile_of(width)] * 5 + [whole(table.shape)] * 2 + [ANY] * len(arrays),
+        out_specs=[tile_of(width), whole((16, width))],
         out_shape=[
             jax.ShapeDtypeStruct(rows.shape, F32),
-            jax.ShapeDtypeStruct((8, width), F32),
+            jax.ShapeDtypeStruct((16, width), F32),
         ],
         scratch_shapes=[
             pltpu.VMEM((3, width, width), BF16),
@@ -738,7 +746,7 @@
         compiler_params=params(60),
         cost_estimate=cost(6 * count * width * width, 20 * count * width),
         name="inputs_back",
-    )(place, rows, grad_middle, grad_q, grad_k, grad_v, table, *arrays)
+    )(place, rows, grad_middle, grad_q, grad_k, grad_v, table, earlier, *arrays)
 
 
 def add_low(left, right):
@@ -759,14 +767,15 @@
 def add_kernel(mine, other, own, by_x, by_y, near, far):
     total = (mine[...].astype(F32) + other[...].astype(F32)).astype(BF16)
     own[0] = total[0]
-
-    @pl.when(pl.program_id(0) == 0)
+    early = pl.program_id(0) < pl.num_programs(0) // 2
+
+    @pl.when(early)
     def _():
         by_x[0] = total[3]
         by_x[1] = total[1]
         far[0] = total[2]
 
-    @pl.when(pl.program_id(0) == 1)
+    @pl.when(jnp.logical_not(early))
     def _():
         by_y[0] = total[3]
         by_y[1] = total[2]
@@ -781,16 +790,26 @@
         by_x = jnp.stack([corner[:, :half], near[:, :half]], axis=1)
         by_y = jnp.stack([corner[:, half:], far[:, half:]], axis=1)
         return own, by_x, by_y, near[:, half:], far[:, :half]
-    sizes = [rows, 2 * half, 2 * half, half, half]
-    whole_out = [(1, rows, columns), (2, half, columns), (2, half, columns), (1, half, columns), (1, half, columns)]
+    shapes = [(1, rows, columns), (2, half, columns), (2, half, columns), (1, half, columns), (1, half, columns)]
+    steps = 2
+    step = rows // steps
+    spots = [
+        lambda i: i,
+        lambda i: jnp.minimum(i, steps // 2 - 1),
+        lambda i: jnp.maximum(i - steps // 2, 0),
+        lambda i: jnp.maximum(i - steps // 2, 0),
+        lambda i: jnp.minimum(i, steps // 2 - 1),
+    ]
     own, by_x, by_y, near, far = pl.pallas_call(
         add_kernel,
-        grid=(2,),
-        in_specs=[pl.BlockSpec((4, half, columns), lambda i: (0, i, 0))] * 2,
-        out_specs=[pl.BlockSpec((1, half, columns), lambda i: (0, i, 0))]
-        + [whole(shape) for shape in whole_out[1:]],
-        out_shape=[jax.ShapeDtypeStruct(shape, BF16) for shape in whole_out],
-        compiler_params=params(60),
+        grid=(steps,),
+        in_specs=[pl.BlockSpec((4, step, columns), lambda i: (0, i, 0))] * 2,
+        out_specs=[
+            pl.BlockSpec((shape[0], step, columns), lambda i, spot=spot: (0, spot(i), 0))
+            for shape, spot in zip(shapes, spots)
+        ],
+        out_shape=[jax.ShapeDtypeStruct(shape, BF16) for shape in shapes],
+        compiler_params=params(24),
         cost_estimate=cost(4 * rows * columns, 24 * rows * columns),
         name="core_add",
     )(mine, other)
@@ -954,28 +973,30 @@
         grad_w_down = grad_w_down.reshape(8, width, places // 8, -1).transpose(0, 2, 1, 3)
     total_down = lax.psum_scatter(grad_w_down.reshape(places, width, -1), "wide")
 
-    result, grad_hidden, grad_middle, grad_branch, grad_mixed, stats_two, hidden_stats = back(
+    result, grad_hidden, grad_middle, grad_branch, grad_mixed, stats = back(
         place, lengths, rows, branch, active, slope, grad_down, cotangent, table, one, two, three
     )
     mine, theirs = by_core(
         outer(place, [(normed_two, [grad_hidden]), (mixed, [grad_branch])], width), layers + 1
     )
+    def heads_back(grads, value, spans):
+        for pack, first, last in spans:
+            grads = attend_back(query, key, value_rows, value, kept[pack], pack, first, last, grads)
+        return grads
+
+    groups = width // (HEADS * HD)
+    spans = [(0, 0, 1), (0, 1, groups)] + [(pack, 0, groups) for pack in range(1, packs)]
+    value_rows = value
     grads, (other,) = beside(
-        lambda v: attend_back(query, key, value, v, kept[0], 0),
-        grad_mixed,
-        [theirs],
-        [lambda v: cross(v, 0)],
+        lambda v: heads_back((), v, spans[:1]), grad_mixed, [theirs], [lambda v: cross(v, 0)]
     )
     up_held = sums_of_cores(mine, other)
     total_down, grads = lax.optimization_barrier((total_down, grads))
     total_down = lax.psum_scatter(total_down.reshape(layers, quarter, -1), "narrow")
-    for pack in range(1, packs):
-        run = functools.partial(attend_back, query, key, value, grad_mixed, kept[pack], pack)
-        if pack == packs - 1:
-            grads, moved = beside(run, grads, up_held[1:3], planes())
-        else:
-            grads = run(grads)
-    up_moved, sends = moved, second_sends(up_held, moved)
+    grads, up_moved = beside(
+        lambda v: heads_back(v, grad_mixed, spans[1:]), grads, up_held[1:3], planes()
+    )
+    sends = second_sends(up_held, up_moved)
     grads, sends = lax.optimization_barrier((grads, sends))
     mine_theirs, moved = beside(
         lambda v: outer(place, [(normed, v)], width), grads, sends, planes()
@@ -986,18 +1007,16 @@
     total_out = total_up[layers * short :].reshape(short, layers, quarter).transpose(1, 0, 2)
     total_up = total_up[: layers * short].reshape(layers, short, width)
     total_up = jnp.concatenate([total_up, total_out], axis=2)
-    up_sends, up_moves = spread_blocks(total_up)
-    up_sends, (other,) = beside(lambda v: v, up_sends, [theirs], [lambda v: cross(v, 0)])
-    held = sums_of_cores(mine, other)
+    total_up, theirs = lax.optimization_barrier((total_up, theirs))
+    total_up = lax.psum_scatter(total_up, "narrow")
+    held = sums_of_cores(mine, cross(theirs, 0))
     grad_q, grad_k, grad_v = grads
-    (grad_rows, stats_one), moved = beside(
-        lambda v: inputs_back(place, rows, grad_middle, v, grad_k, grad_v, table, one),
+    (grad_rows, sums), first = beside(
+        lambda v: inputs_back(place, rows, grad_middle, v, grad_k, grad_v, table, stats, one),
         grad_q,
-        [*held[1:3], *up_sends],
-        planes() + up_moves,
-    )
-    first, up_parts = moved[:2], moved[2:]
-    sums = jnp.concatenate([stats_one, stats_two, hidden_stats])
+        held[1:3],
+        planes(),
+    )
     others = [sums] * (layers - 1)
     sums, moved = beside(
         lambda v: v, sums, [*second_sends(held, first), *others], planes() + shifts(layers)
@@ -1009,17 +1028,22 @@
     blocks = jnp.concatenate([total_qkv[i * short : (i + 1) * short] for i in range(3)], axis=1)
     own_block, sends, moves = columns_blocks(blocks, part, layers)
     both = [lambda v: exchange(v, "wide", lambda i: i ^ 6)]
-    sums, moved = beside(lambda v: v, sums, [*sends, sums, sums, sums], moves + planes() + both)
+
+    def last_part(value):
+        sums, total_up, total_down = value
+        return sums, total_up.astype(F32), total_down.astype(F32).T
+
+    (sums, total_up, total_down), moved = beside(
+        last_part, (sums, total_up, total_down), [*sends, sums, sums, sums], moves + planes() + both
+    )
     total_qkv = own_columns(own_block, moved[: layers - 1], part, blocks.shape[1])
     for piece_sums in moved[layers - 1 :]:
         sums = sums + piece_sums
     for bit in (0, *range(3, wide_bits())):
         sums = sums + cross(sums, bit)
-    total_up = add_blocks(total_up, up_parts)
-    total_down = total_down.astype(F32).T
-
-    own = lax.dynamic_slice(sums, (0, small_spot[1]), (16, ln1_gain.shape[0]))
-    own_up = lax.dynamic_slice(sums, (16 + up_spot[0], up_spot[1]), (1, up_bias.shape[0]))[0]
+
+    own = lax.dynamic_slice(sums, (0, small_spot[1]), (16, piece))
+    own_up = lax.dynamic_slice(sums, (STATS_UP + up_spot[0], up_spot[1]), (1, long))[0]
     return (
         result.reshape(patches.shape),
         grad_rows.reshape(patches.shape),
@@ -1027,17 +1051,17 @@
         total_up[:, width:],
         total_up[:, :width],
         total_down,
-        own[0],
-        own[1],
+        own[STATS_ONE],
+        own[STATS_ONE + 1],
+        own[STATS_ONE + 2],
+        own[STATS_ONE + 3],
+        own[5],
+        own[4],
         own[2],
         own[3],
-        own[13],
-        own[12],
-        own[10],
-        own[11],
         own_up,
-        own[9],
-        own[8],
+        own[1],
+        own[0],
     )
 
 

time: 290 us -> 286 us (0.986); the launches traced: 289 us -> 281 us
  waiting for transfers between devices: 51.2 us -> 46.9 us
  starting transfers between devices: 48.4 us -> 45.2 us
  Pallas kernels: 156 us -> 153 us
    ppermute x38 -> x35, waiting for transfers between devices: 51.1 us -> 42.8 us  [exchange(): lax.ppermute(value, axis_name, [(i, partner(i) % size) for i in range(siz...]
    ppermute x38 -> x35, starting transfers between devices: 47.8 us -> 44.2 us  [exchange(): lax.ppermute(value, axis_name, [(i, partner(i) % size) for i in range(siz...]
    pallas_call x4 -> x5, Pallas kernels: 31.6 us -> 29.3 us  [the longest x3 25.4 us: attend_back(): pl.pallas_call(attend_back_kernel, grid=(part,), in_specs=[pair_block(row...]
  transfers between devices with their start and end apart: 42 -> 40, of which waited for: 17 -> 16; matrix products, arithmetic and copies ran while one was open for 2% -> 3% of each run, Pallas kernels for 53% -> 54%
where the time goes in v5:
time: 286 us; the launch traced here: 281 us
  Pallas kernels  153 us (53%)
  waiting for transfers between devices  46.9 us (16%)
  starting transfers between devices  45.2 us (16%)
  between operations  14.7 us (5%)
  other arithmetic  10.3 us (4%)
  local copies, waits for them, and re-layouts  10 us (3%)
    ppermute x35, starting transfers between devices, exchange(): lax.ppermute(value, axis_name, [(i, partner(i) % size) for i in range(siz...  44.2 us
    ppermute x35, waiting for transfers between devices, exchange(): lax.ppermute(value, axis_name, [(i, partner(i) % size) for i in range(siz...  42.8 us
    pallas_call x1, Pallas kernels, back(): pl.pallas_call(functools.partial(back_kernel, *plans, sizes), grid=(count...  30.2 us
    pallas_call x3, Pallas kernels, attend_back(): pl.pallas_call(attend_back_kernel, grid=(part,), in_specs=[pair_block(row...  25.4 us
    pallas_call x2, Pallas kernels, attend(): pl.pallas_call(functools.partial(attend_kernel, pack), grid=(pairs,), in_...  21.9 us
    pallas_call x2, Pallas kernels, outer(): pl.pallas_call(functools.partial(outer_kernel, direct(), steps), grid=(to...  21.5 us
    pallas_call x1, Pallas kernels, hidden(): pl.pallas_call(functools.partial(hidden_kernel, out_plan, up_plans, sizes...  19.3 us
    pallas_call x1, Pallas kernels, inputs_back(): pl.pallas_call(functools.partial(inputs_kernel, plans), grid=(count // TI...  11.5 us
  transfers between devices with their start and end apart: 40, of which 16 were waited for; matrix products, arithmetic and copies ran while one was open for 3% of the time, Pallas kernels for 54%

profile of v5, /device:TPU:0, one launch (start us, length us, event | category | flops | bytes accessed | tf_op | source)
XLA Modules:
  0.0 280.6 jit_solution(14588793649367672754)
XLA Ops:
  7.3 1.5 stack.82
  10.4 5.1 %collective-permute-start = (bf16[112,768]{1,0:T(8,128)(2,1)S(1)}, bf16[112,768]{1,0:T(8,128)(2,1)S(1)}, u32[]{:S(2)}, u32[]{:S(2)}) collective-permute-start(bf16[112,768]{1,0:T(8,128)(2,1)S(1)} %fusion.6), channel_id=1, source_target_pairs={{0,3},{1,0},{2,1},{3,2},{4,7},{5,4},{6,5},{7,6},{8,11},{9,8},{10,9... | collective-permute-start | bytes 516104 | tf_op jit(solution)/shard_map/ppermute | solution.py:23
  16.6 3.8 %collective-permute-done = bf16[112,768]{1,0:T(8,128)(2,1)S(1)} collective-permute-done((bf16[112,768]{1,0:T(8,128)(2,1)S(1)}, bf16[112,768]{1,0:T(8,128)(2,1)S(1)}, u32[]{:S(2)}, u32[]{:S(2)}) %collective-permute-start) | collective-permute-done | bytes 172064 | tf_op jit(solution)/shard_map/ppermute | solution.py:23
  20.4 9.7 %collective-permute-done.1 = bf16[112,768]{1,0:T(8,128)(2,1)S(1)} collective-permute-done((bf16[112,768]{1,0:T(8,128)(2,1)S(1)}, bf16[112,768]{1,0:T(8,128)(2,1)S(1)}, u32[]{:S(2)}, u32[]{:S(2)}) %collective-permute-start.1) | collective-permute-done | bytes 172064 | tf_op jit(solution)/shard_map/ppermute | solution.py:23
  31.3 1.6 collective-permute-start.3
  32.8 1.5 collective-permute-start.4
  35.2 1.9 collective-permute-start.6
  37.1 2.9 %collective-permute-start.7 = (bf16[96,768]{1,0:T(8,128)(2,1)S(1)}, bf16[96,768]{1,0:T(8,128)(2,1)S(1)}, u32[]{:S(2)}, u32[]{:S(2)}) collective-permute-start(bf16[96,768]{1,0:T(8,128)(2,1)S(1)} %copy-done.13), channel_id=1, source_target_pairs={{0,3},{1,0},{2,1},{3,2},{4,7},{5,4},{6,5},{7,6},{8,11},{9,8},{10,9... | collective-permute-start | bytes 442376 | tf_op jit(solution)/shard_map/ppermute | solution.py:23
  40.0 2.9 %collective-permute-done.5 = bf16[96,768]{1,0:T(8,128)(2,1)S(1)} collective-permute-done((bf16[96,768]{1,0:T(8,128)(2,1)S(1)}, bf16[96,768]{1,0:T(8,128)(2,1)S(1)}, u32[]{:S(2)}, u32[]{:S(2)}) %collective-permute-start.5) | collective-permute-done | bytes 147488 | tf_op jit(solution)/shard_map/ppermute | solution.py:23
  43.0 4.5 %collective-permute-done.6 = bf16[96,768]{1,0:T(8,128)(2,1)S(1)} collective-permute-done((bf16[96,768]{1,0:T(8,128)(2,1)S(1)}, bf16[96,768]{1,0:T(8,128)(2,1)S(1)}, u32[]{:S(2)}, u32[]{:S(2)}) %collective-permute-start.6) | collective-permute-done | bytes 147488 | tf_op jit(solution)/shard_map/ppermute | solution.py:23
  48.0 1.4 pad_maximum_fusion
  51.3 1.5 collective-permute-start.8
  52.8 7.6 %collective-permute-done.8 = bf16[1,192,768]{2,1,0:T(8,128)(2,1)S(1)} collective-permute-done((bf16[1,192,768]{2,1,0:T(8,128)(2,1)S(1)}, bf16[1,192,768]{2,1,0:T(8,128)(2,1)S(1)}, u32[]{:S(2)}, u32[]{:S(2)}) %collective-permute-start.8) | collective-permute-done | bytes 294944 | tf_op jit(solution)/shard_map/ppermute | solution.py:23
  61.4 3.6 %collective-permute-start.12 = (bf16[96,768]{1,0:T(8,128)(2,1)S(1)}, bf16[96,768]{1,0:T(8,128)(2,1)S(1)}, u32[]{:S(2)}, u32[]{:S(2)}) collective-permute-start(bf16[96,768]{1,0:T(8,128)(2,1)S(1)} %pad_maximum_fusion.5), channel_id=1, source_target_pairs={{0,1},{1,2},{2,3},{3,0},{4,5},{5,6},{6,7},{7,4},{8,9},{9,10},{10,1... | collective-permute-start | bytes 442376 | tf_op jit(solution)/shard_map/ppermute | solution.py:23
  65.1 2.0 collective-permute-start.13
  68.4 10.1 %project.1 = (bf16[1024,768]{1,0:T(8,128)(2,1)}, bf16[1024,768]{1,0:T(8,128)(2,1)}, bf16[1024,768]{1,0:T(8,128)(2,1)}, bf16[1024,768]{1,0:T(8,128)(2,1)}, f32[16,768]{1,0:T(8,128)}) custom-call(s32[1]{0:T(128)} %bitcast.place, bf16[1024,768]{1,0:T(8,128)(2,1)} %bitcast.200, bf16[16,768]{1,0:T(8,128)(2,1)} %broadcast.21.extras, ...), custom_call_target="tpu_custom_call" | custom-call | flops 3623878656 | bytes 11010048 | tf_op jit(solution)/shard_map/project/pallas_call | solution.py:275
  78.9 1.1 maximum_maximum_fusion
  80.3 11.0 %attend.2 = (bf16[1024,768]{1,0:T(8,128)(2,1)}, bf16[12,512,512]{2,1,0:T(8,128)(2,1)}) custom-call(s32[2,6]{1,0:T(2,128)} %lengths.7, bf16[1024,768]{1,0:T(8,128)(2,1)} %get-tuple-element.189.query, bf16[1024,768]{1,0:T(8,128)(2,1)} %get-tuple-element.190.key, bf16[1024,768]{1,0:T(8,128)(2,1)} %get-tuple-element.191.value), custom_call_target="tpu_custom_call" | custom-call | tf_op jit(solution)/shard_map/attend/pallas_call | solution.py:356
  91.3 10.9 %attend.3 = (bf16[1024,768]{1,0:T(8,128)(2,1)}, bf16[12,512,512]{2,1,0:T(8,128)(2,1)}) custom-call(s32[2,6]{1,0:T(2,128)} %lengths.7, bf16[1024,768]{1,0:T(8,128)(2,1)} %get-tuple-element.189.query, bf16[1024,768]{1,0:T(8,128)(2,1)} %get-tuple-element.190.key, bf16[1024,768]{1,0:T(8,128)(2,1)} %get-tuple-element.191.value, ...), custom_call_target="tpu_custom_call", output_to_operand_aliasing={{0}: (4, {})} | custom-call | flops 3221225472 | bytes 3145728 | tf_op jit(solution)/shard_map/attend/pallas_call | solution.py:356
  102.2 19.3 %hidden.1 = (f32[1024,768]{1,0:T(8,128)}, bf16[1024,768]{1,0:T(8,128)(2,1)}, bf16[1024,3072]{1,0:T(8,128)(2,1)}, bf16[1024,3072]{1,0:T(8,128)(2,1)}, bf16[1024,768]{1,0:T(8,128)(2,1)}) custom-call(s32[1]{0:T(128)} %bitcast.place, s32[2,6]{1,0:T(2,128)} %lengths.7, bf16[1024,768]{1,0:T(8,128)(2,1)} %bitcast.201, ...), custom_call_target="tpu_custom_call" | custom-call | flops 8455716864 | bytes 20447232 | tf_op jit(solution)/shard_map/hidden/pallas_call | solution.py:465
  121.5 9.6 %wide_outer.1 = bf16[8,768,384]{2,1,0:T(8,128)(2,1)} custom-call(s32[1]{0:T(128)} %bitcast.place, bf16[1024,768]{1,0:T(8,128)(2,1)} %get-tuple-element.198.left.grad_down, bf16[1024,3072]{1,0:T(8,128)(2,1)} %get-tuple-element.199.right.active), custom_call_target="tpu_custom_call" | custom-call | flops 4831838208 | bytes 13762560 | tf_op jit(solution)/shard_map/wide_outer/pallas_call | solution.py:690
  131.4 30.2 %back.1 = (bf16[1024,768]{1,0:T(8,128)(2,1)}, bf16[1024,3072]{1,0:T(8,128)(2,1)}, f32[1024,768]{1,0:T(8,128)}, bf16[1024,768]{1,0:T(8,128)(2,1)}, bf16[1024,768]{1,0:T(8,128)(2,1)}, /*index=5*/f32[16,768]{1,0:T(8,128)}) custom-call(s32[1]{0:T(128)} %bitcast.place, s32[2,6]{1,0:T(2,128)} %lengths.7, bf16[1024,768]{1,0:T(8,128)(2,1)} %bitcast.202, ...), custom_call_target="tpu_custom_call" | custom-call | flops 15703474176 | bytes 31457280 | tf_op jit(solution)/shard_map/back/pallas_call | solution.py:556
  161.6 12.8 %outer.2 = (bf16[4,5,96,768]{3,2,1,0:T(8,128)(2,1)}, bf16[4,5,96,768]{3,2,1,0:T(8,128)(2,1)}) custom-call(s32[1]{0:T(128)} %bitcast.place, bf16[1024,768]{1,0:T(8,128)(2,1)} %get-tuple-element.207.refs_0_, bf16[1024,768]{1,0:T(8,128)(2,1)} %get-tuple-element.193.mixed.refs_1_, bf16[1024,3072]{1,0:T(8,128)(2,1)} %get-tuple-element.208.refs_2_, ...), custom_call_target="tpu_custom_call" | custom-call | flops 6039797760 | bytes 13762560 | tf_op jit(solution)/shard_map/outer/pallas_call | solution.py:659
  174.4 5.7 %attend_back.3 = (bf16[1024,768]{1,0:T(8,128)(2,1)}, bf16[1024,768]{1,0:T(8,128)(2,1)}, bf16[1024,768]{1,0:T(8,128)(2,1)}) custom-call(bf16[1024,768]{1,0:T(8,128)(2,1)} %get-tuple-element.189.query, bf16[1024,768]{1,0:T(8,128)(2,1)} %get-tuple-element.190.key, bf16[1024,768]{1,0:T(8,128)(2,1)} %get-tuple-element.191.value, ...), custom_call_target="tpu_custom_call" | custom-call | flops 2147483648 | bytes 1835008 | tf_op jit(solution)/shard_map/attend_back/pallas_call | solution.py:394
  180.1 2.8 %core_add.2 = (bf16[1,480,768]{2,1,0:T(8,128)(2,1)S(1)}, bf16[2,240,768]{2,1,0:T(8,128)(2,1)S(1)}, bf16[2,240,768]{2,1,0:T(8,128)(2,1)S(1)}, bf16[1,240,768]{2,1,0:T(8,128)(2,1)S(1)}, bf16[1,240,768]{2,1,0:T(8,128)(2,1)S(1)}) custom-call(bf16[4,480,768]{2,1,0:T(8,128)(2,1)S(1)} %bitcast.185, bf16[4,480,768]{2,1,0:T(8,128)(2,1)} %collective-permute-done.15.other), custom_call_target="tpu_custom_call" | custom-call | flops 1474560 | bytes 8847360 | tf_op jit(solution)/shard_map/core_add/pallas_call | solution.py:803
  185.4 2.3 reduce-scatter.4.cloned.1.call-done
  187.7 1.4 collective-permute-start.16
  190.2 8.4 %attend_back.4 = (bf16[1024,768]{1,0:T(8,128)(2,1)}, bf16[1024,768]{1,0:T(8,128)(2,1)}, bf16[1024,768]{1,0:T(8,128)(2,1)}) custom-call(bf16[1024,768]{1,0:T(8,128)(2,1)} %get-tuple-element.189.query, bf16[1024,768]{1,0:T(8,128)(2,1)} %get-tuple-element.190.key, ...), custom_call_target="tpu_custom_call", output_to_operand_aliasing={{0}: (5, {}), {1}: (6, {}), {2}: (7, {})} | custom-call | flops 4294967296 | bytes 3670016 | tf_op jit(solution)/shard_map/attend_back/pallas_call | solution.py:394
  198.7 11.3 %attend_back.5 = (bf16[1024,768]{1,0:T(8,128)(2,1)}, bf16[1024,768]{1,0:T(8,128)(2,1)}, bf16[1024,768]{1,0:T(8,128)(2,1)}) custom-call(bf16[1024,768]{1,0:T(8,128)(2,1)} %get-tuple-element.189.query, bf16[1024,768]{1,0:T(8,128)(2,1)} %get-tuple-element.190.key, ...), custom_call_target="tpu_custom_call", output_to_operand_aliasing={{0}: (5, {}), {1}: (6, {}), {2}: (7, {})} | custom-call | flops 6442450944 | bytes 5505024 | tf_op jit(solution)/shard_map/attend_back/pallas_call | solution.py:394
  210.9 1.4 collective-permute-start.18
  213.0 8.7 %outer.3 = (bf16[4,3,96,768]{3,2,1,0:T(8,128)(2,1)}, bf16[4,3,96,768]{3,2,1,0:T(8,128)(2,1)}) custom-call(s32[1]{0:T(128)} %bitcast.place, bf16[1024,768]{1,0:T(8,128)(2,1)} %get-tuple-element.245.refs_0_, bf16[1024,768]{1,0:T(8,128)(2,1)} %get-tuple-element.264.refs_1_.grad_q, bf16[1024,768]{1,0:T(8,128)(2,1)} %get-tuple-element.265.refs_2_.grad_k, ...), custom_call_target="tpu_custom_call" | custom-call | flops 3623878656 | bytes 8257536 | tf_op jit(solution)/shard_map/outer/pallas_call | solution.py:659
  223.4 3.9 %collective-permute-done.20.other = bf16[4,288,768]{2,1,0:T(8,128)(2,1)S(1)} collective-permute-done((bf16[4,288,768]{2,1,0:T(8,128)(2,1)}, bf16[4,288,768]{2,1,0:T(8,128)(2,1)S(1)}, u32[]{:S(2)}, u32[]{:S(2)}) %collective-permute-start.20) | collective-permute-done | bytes 1769504 | tf_op jit(solution)/shard_map/ppermute | solution.py:23
  228.4 1.4 collective-permute-start.21
  230.5 11.5 %inputs_back.1 = (f32[1024,768]{1,0:T(8,128)}, f32[16,768]{1,0:T(8,128)}) custom-call(s32[1]{0:T(128)} %bitcast.place, bf16[1024,768]{1,0:T(8,128)(2,1)} %bitcast.203, f32[1024,768]{1,0:T(8,128)} %get-tuple-element.203.grad_middle, bf16[1024,768]{1,0:T(8,128)(2,1)} %get-tuple-element.264.refs_1_.grad_q, bf16[1024,768]{1,0:T(8,128)(2,1)} %get-tuple-element.265.refs_2_.grad_k, ...), custom_call_target="tpu_custom_call" | custom-call | flops 3623878656 | bytes 15728640 | tf_op jit(solution)/shard_map/inputs_back/pallas_call | solution.py:733
  242.2 1.4 collective-permute-start.23
  244.3 1.5 collective-permute-start.25
  245.8 2.4 collective-permute-start.26
  248.2 1.4 collective-permute-start.27
  249.7 2.3 collective-permute-done.25
  252.0 2.9 %collective-permute-done.26 = f32[16,768]{1,0:T(8,128)S(1)} collective-permute-done((f32[16,768]{1,0:T(8,128)S(1)}, f32[16,768]{1,0:T(8,128)S(1)}, u32[]{:S(2)}, u32[]{:S(2)}) %collective-permute-start.26) | collective-permute-done | bytes 49184 | tf_op jit(solution)/shard_map/ppermute | solution.py:23
  255.2 1.6 reduce-scatter.8.cloned.1.call-done
  256.9 1.5 collective-permute-start.31
  258.3 1.1 collective-permute-start.28
  259.4 1.4 collective-permute-start.29
  260.8 1.4 collective-permute-start.30
  262.2 1.6 collective-permute-start.32
  266.7 2.0 collective-permute-done.33
  268.8 1.4 collective-permute-done.29
  (165 shorter events, 26.3 us)
Async XLA Ops:
  7.2 23.0 %copy-start.11 = (bf16[96,576]{1,0:T(8,128)(2,1)S(1)}, bf16[96,576]{1,0:T(8,128)(2,1)}, u32[]{:S(2)}) copy-start(bf16[96,576]{1,0:T(8,128)(2,1)} %param.20) | copy-start | bytes 331780
  7.2 23.0 %copy-start.14 = (bf16[96,192]{1,0:T(8,128)(2,1)S(1)}, bf16[96,192]{1,0:T(8,128)(2,1)}, u32[]{:S(2)}) copy-start(bf16[96,192]{1,0:T(8,128)(2,1)} %param.21) | copy-start | bytes 110596
  7.2 94.9 %all-gather.5.cloned.1.call-start = ((), (), s32[]{:S(2)}) async-start(), calls=%async_computation.6 | async-start | bytes 5308416 | tf_op jit(solution)/shard_map/all_gather | solution.py:944
  10.4 9.9 %collective-permute-start = (bf16[112,768]{1,0:T(8,128)(2,1)S(1)}, bf16[112,768]{1,0:T(8,128)(2,1)S(1)}, u32[]{:S(2)}, u32[]{:S(2)}) collective-permute-start(bf16[112,768]{1,0:T(8,128)(2,1)S(1)} %fusion.6), channel_id=1, source_target_pairs={{0,3},{1,0},{2,1},{3,2},{4,7},{5,4},{6,5},{7,6},{8,11},{9,8},{10,9... | collective-permute-start | bytes 516104 | tf_op jit(solution)/shard_map/ppermute | solution.py:23
  15.6 14.6 %collective-permute-start.1 = (bf16[112,768]{1,0:T(8,128)(2,1)S(1)}, bf16[112,768]{1,0:T(8,128)(2,1)S(1)}, u32[]{:S(2)}, u32[]{:S(2)}) collective-permute-start(bf16[112,768]{1,0:T(8,128)(2,1)S(1)} %fusion.6), channel_id=1, source_target_pairs={{0,2},{1,3},{2,0},{3,1},{4,6},{5,7},{6,4},{7,5},{8,10},{9,11},{10,... | collective-permute-start | bytes 516104 | tf_op jit(solution)/shard_map/ppermute | solution.py:23
  15.6 14.6 %collective-permute-start.2 = (bf16[112,768]{1,0:T(8,128)(2,1)S(1)}, bf16[112,768]{1,0:T(8,128)(2,1)S(1)}, u32[]{:S(2)}, u32[]{:S(2)}) collective-permute-start(bf16[112,768]{1,0:T(8,128)(2,1)S(1)} %fusion.6), channel_id=1, source_target_pairs={{0,1},{1,2},{2,3},{3,0},{4,5},{5,6},{6,7},{7,4},{8,9},{9,10},{10,1... | collective-permute-start | bytes 516104 | tf_op jit(solution)/shard_map/ppermute | solution.py:23
  31.3 18.2 %copy-start.8 = (bf16[400,768]{1,0:T(8,128)(2,1)}, bf16[400,768]{1,0:T(8,128)(2,1)S(1)}, u32[]{:S(2)}) copy-start(bf16[400,768]{1,0:T(8,128)(2,1)S(1)} %constant_dynamic-update-slice_fusion) | copy-start | bytes 1843204
  31.3 16.3 %collective-permute-start.3 = (bf16[1,400,768]{2,1,0:T(8,128)(2,1)S(1)}, bf16[1,400,768]{2,1,0:T(8,128)(2,1)S(1)}, u32[]{:S(2)}, u32[]{:S(2)}) collective-permute-start(bf16[1,400,768]{2,1,0:T(8,128)(2,1)S(1)} %bitcast.191), channel_id=1, source_target_pairs={{0,8},{4,12},{8,0},{12,4},{16,24},{20,28},{24,16},{28,20},{1,9},{5... | collective-permute-start | bytes 1843208 | tf_op jit(solution)/shard_map/ppermute | solution.py:23
  32.8 15.2 %collective-permute-start.4 = (bf16[1,400,768]{2,1,0:T(8,128)(2,1)S(1)}, bf16[1,400,768]{2,1,0:T(8,128)(2,1)S(1)}, u32[]{:S(2)}, u32[]{:S(2)}) collective-permute-start(bf16[1,400,768]{2,1,0:T(8,128)(2,1)S(1)} %bitcast.192), channel_id=1, source_target_pairs={{0,16},{4,20},{8,24},{12,28},{16,0},{20,4},{24,8},{28,12},{1,17},{... | collective-permute-start | bytes 1843208 | tf_op jit(solution)/shard_map/ppermute | solution.py:23
  34.3 8.6 %collective-permute-start.5 = (bf16[96,768]{1,0:T(8,128)(2,1)S(1)}, bf16[96,768]{1,0:T(8,128)(2,1)S(1)}, u32[]{:S(2)}, u32[]{:S(2)}) collective-permute-start(bf16[96,768]{1,0:T(8,128)(2,1)S(1)} %copy-done.13), channel_id=1, source_target_pairs={{0,1},{1,2},{2,3},{3,0},{4,5},{5,6},{6,7},{7,4},{8,9},{9,10},{10,1... | collective-permute-start | bytes 442376 | tf_op jit(solution)/shard_map/ppermute | solution.py:23
  35.2 12.3 %collective-permute-start.6 = (bf16[96,768]{1,0:T(8,128)(2,1)S(1)}, bf16[96,768]{1,0:T(8,128)(2,1)S(1)}, u32[]{:S(2)}, u32[]{:S(2)}) collective-permute-start(bf16[96,768]{1,0:T(8,128)(2,1)S(1)} %copy-done.13), channel_id=1, source_target_pairs={{0,2},{1,3},{2,0},{3,1},{4,6},{5,7},{6,4},{7,5},{8,10},{9,11},{10,... | collective-permute-start | bytes 442376 | tf_op jit(solution)/shard_map/ppermute | solution.py:23
  37.1 10.4 %collective-permute-start.7 = (bf16[96,768]{1,0:T(8,128)(2,1)S(1)}, bf16[96,768]{1,0:T(8,128)(2,1)S(1)}, u32[]{:S(2)}, u32[]{:S(2)}) collective-permute-start(bf16[96,768]{1,0:T(8,128)(2,1)S(1)} %copy-done.13), channel_id=1, source_target_pairs={{0,3},{1,0},{2,1},{3,2},{4,7},{5,4},{6,5},{7,6},{8,11},{9,8},{10,9... | collective-permute-start | bytes 442376 | tf_op jit(solution)/shard_map/ppermute | solution.py:23
  49.7 11.1 %copy-start.15 = (bf16[384,192]{0,1:T(8,128)(2,1)S(1)}, bf16[384,192]{0,1:T(8,128)(2,1)}, u32[]{:S(2)}) copy-start(bf16[384,192]{0,1:T(8,128)(2,1)} %param.23) | copy-start | bytes 442372
  50.6 80.9 %all-gather.7.cloned.1.call-start = ((), (), s32[]{:S(2)}) async-start(), calls=%async_computation.7 | async-start | bytes 5308416 | tf_op jit(solution)/shard_map/all_gather | solution.py:960
  50.6 10.0 %collective-permute-start.10 = (bf16[3,400,768]{2,1,0:T(8,128)(2,1)}, bf16[3,400,768]{2,1,0:T(8,128)(2,1)S(1)}, u32[]{:S(2)}, u32[]{:S(2)}) collective-permute-start(bf16[3,400,768]{2,1,0:T(8,128)(2,1)} %pad_maximum_fusion), channel_id=1, source_target_pairs={{0,4},{4,0},{8,12},{12,8},{16,20},{20,16},{24,28},{28,24},{1,5},{5... | collective-permute-start | bytes 5529608 | tf_op jit(solution)/shard_map/ppermute | solution.py:23
  50.7 10.0 %collective-permute-start.9 = (bf16[1,208,768]{2,1,0:T(8,128)(2,1)S(1)}, bf16[1,208,768]{2,1,0:T(8,128)(2,1)S(1)}, u32[]{:S(2)}, u32[]{:S(2)}) collective-permute-start(bf16[1,208,768]{2,1,0:T(8,128)(2,1)S(1)} %slice.270), channel_id=1, source_target_pairs={{0,8},{4,12},{8,0},{12,4},{16,24},{20,28},{24,16},{28,20},{1,9},{5... | collective-permute-start | bytes 958472 | tf_op jit(solution)/shard_map/ppermute | solution.py:23
  51.3 9.1 %collective-permute-start.8 = (bf16[1,192,768]{2,1,0:T(8,128)(2,1)S(1)}, bf16[1,192,768]{2,1,0:T(8,128)(2,1)S(1)}, u32[]{:S(2)}, u32[]{:S(2)}) collective-permute-start(bf16[1,192,768]{2,1,0:T(8,128)(2,1)S(1)} %slice.269), channel_id=1, source_target_pairs={{0,16},{4,20},{8,24},{12,28},{16,0},{20,4},{24,8},{28,12},{1,17},{... | collective-permute-start | bytes 884744 | tf_op jit(solution)/shard_map/ppermute | solution.py:23
  60.6 7.6 %copy-start.9 = (bf16[3,400,768]{2,1,0:T(8,128)(2,1)}, bf16[3,400,768]{2,1,0:T(8,128)(2,1)S(1)}, u32[]{:S(2)}) copy-start(bf16[3,400,768]{2,1,0:T(8,128)(2,1)S(1)} %collective-permute-done.10.refs_4_) | copy-start | bytes 5529604
  60.7 7.5 %copy-start.10 = (bf16[1,400,768]{2,1,0:T(8,128)(2,1)}, bf16[1,400,768]{2,1,0:T(8,128)(2,1)S(1)}, u32[]{:S(2)}) copy-start(bf16[1,400,768]{2,1,0:T(8,128)(2,1)S(1)} %constant_dynamic-update-slice_fusion.1.refs_3_) | copy-start | bytes 1843204
  60.7 6.8 %collective-permute-start.11 = (bf16[1,400,768]{2,1,0:T(8,128)(2,1)S(1)}, bf16[1,400,768]{2,1,0:T(8,128)(2,1)S(1)}, u32[]{:S(2)}, u32[]{:S(2)}) collective-permute-start(bf16[1,400,768]{2,1,0:T(8,128)(2,1)S(1)} %constant_dynamic-update-slice_fusion.1.refs_3_), channel_id=1, source_target_pairs={{0,4},{4,0},{8,12},{12,8},{16,20},{20,16},{24,28},{28,24},{1,5},{5... | collective-permute-start | bytes 1843208 | tf_op jit(solution)/shard_map/ppermute | solution.py:23
  61.4 17.1 %collective-permute-start.12 = (bf16[96,768]{1,0:T(8,128)(2,1)S(1)}, bf16[96,768]{1,0:T(8,128)(2,1)S(1)}, u32[]{:S(2)}, u32[]{:S(2)}) collective-permute-start(bf16[96,768]{1,0:T(8,128)(2,1)S(1)} %pad_maximum_fusion.5), channel_id=1, source_target_pairs={{0,1},{1,2},{2,3},{3,0},{4,5},{5,6},{6,7},{7,4},{8,9},{9,10},{10,1... | collective-permute-start | bytes 442376 | tf_op jit(solution)/shard_map/ppermute | solution.py:23
  65.1 13.4 %collective-permute-start.13 = (bf16[96,768]{1,0:T(8,128)(2,1)S(1)}, bf16[96,768]{1,0:T(8,128)(2,1)S(1)}, u32[]{:S(2)}, u32[]{:S(2)}) collective-permute-start(bf16[96,768]{1,0:T(8,128)(2,1)S(1)} %pad_maximum_fusion.5), channel_id=1, source_target_pairs={{0,2},{1,3},{2,0},{3,1},{4,6},{5,7},{6,4},{7,5},{8,10},{9,11},{10,... | collective-permute-start | bytes 442376 | tf_op jit(solution)/shard_map/ppermute | solution.py:23
  67.1 11.5 %collective-permute-start.14 = (bf16[96,768]{1,0:T(8,128)(2,1)S(1)}, bf16[96,768]{1,0:T(8,128)(2,1)S(1)}, u32[]{:S(2)}, u32[]{:S(2)}) collective-permute-start(bf16[96,768]{1,0:T(8,128)(2,1)S(1)} %pad_maximum_fusion.5), channel_id=1, source_target_pairs={{0,3},{1,0},{2,1},{3,2},{4,7},{5,4},{6,5},{7,6},{8,11},{9,8},{10,9... | collective-permute-start | bytes 442376 | tf_op jit(solution)/shard_map/ppermute | solution.py:23
  80.1 107.6 %reduce-scatter.4.cloned.1.call-start = ((), (), s32[]{:S(2)}) async-start(), calls=%async_computation.3 | async-start | bytes 5308416 | tf_op jit(solution)/shard_map/reduce_scatter | solution.py:974
  131.1 92.3 %reduce-scatter.6.cloned.1.call-start = ((), (), s32[]{:S(2)}) async-start(), calls=%async_computation.4 | async-start | bytes 737280 | tf_op jit(solution)/shard_map/reduce_scatter | solution.py:995
  174.4 5.7 %collective-permute-start.15 = (bf16[4,480,768]{2,1,0:T(8,128)(2,1)}, bf16[4,480,768]{2,1,0:T(8,128)(2,1)}, u32[]{:S(2)}, u32[]{:S(2)}) collective-permute-start(bf16[4,480,768]{2,1,0:T(8,128)(2,1)} %bitcast.222), channel_id=1, source_target_pairs={{0,4},{4,0},{8,12},{12,8},{16,20},{20,16},{24,28},{28,24},{1,5},{5... | collective-permute-start | bytes 8847368 | tf_op jit(solution)/shard_map/ppermute | solution.py:23
  187.7 22.2 %collective-permute-start.16 = (bf16[1,2,240,768]{3,2,1,0:T(8,128)(2,1)}, bf16[1,2,240,768]{3,2,1,0:T(8,128)(2,1)S(1)}, u32[]{:S(2)}, u32[]{:S(2)}) collective-permute-start(bf16[1,2,240,768]{3,2,1,0:T(8,128)(2,1)} %bitcast.188), channel_id=1, source_target_pairs={{0,8},{4,12},{8,0},{12,4},{16,24},{20,28},{24,16},{28,20},{1,9},{5... | collective-permute-start | bytes 2211848 | tf_op jit(solution)/shard_map/ppermute | solution.py:23
  189.2 20.8 %collective-permute-start.17 = (bf16[1,2,240,768]{3,2,1,0:T(8,128)(2,1)}, bf16[1,2,240,768]{3,2,1,0:T(8,128)(2,1)S(1)}, u32[]{:S(2)}, u32[]{:S(2)}) collective-permute-start(bf16[1,2,240,768]{3,2,1,0:T(8,128)(2,1)} %bitcast.187), channel_id=1, source_target_pairs={{0,16},{4,20},{8,24},{12,28},{16,0},{20,4},{24,8},{28,12},{1,17},{... | collective-permute-start | bytes 2211848 | tf_op jit(solution)/shard_map/ppermute | solution.py:23
  189.8 67.1 %reduce-scatter.8.cloned.1.call-start = ((), (), s32[]{:S(2)}) async-start(), calls=%async_computation.5 | async-start | bytes 983040 | tf_op jit(solution)/shard_map/reduce_scatter | solution.py:1011
  198.7 11.3 %copy-start.3 = (bf16[1,240,768]{2,1,0:T(8,128)(2,1)S(1)}, bf16[1,240,768]{2,1,0:T(8,128)(2,1)}, u32[]{:S(2)}) copy-start(bf16[1,240,768]{2,1,0:T(8,128)(2,1)} %copy-done.2) | copy-start | bytes 1105924
  210.9 10.8 %collective-permute-start.18 = (bf16[1,240,768]{2,1,0:T(8,128)(2,1)}, bf16[1,240,768]{2,1,0:T(8,128)(2,1)S(1)}, u32[]{:S(2)}, u32[]{:S(2)}) collective-permute-start(bf16[1,240,768]{2,1,0:T(8,128)(2,1)} %get-tuple-element.251), channel_id=1, source_target_pairs={{0,8},{4,12},{8,0},{12,4},{16,24},{20,28},{24,16},{28,20},{1,9},{5... | collective-permute-start | bytes 1105928 | tf_op jit(solution)/shard_map/ppermute | solution.py:23
  212.3 9.5 %collective-permute-start.19 = (bf16[1,240,768]{2,1,0:T(8,128)(2,1)S(1)}, bf16[1,240,768]{2,1,0:T(8,128)(2,1)S(1)}, u32[]{:S(2)}, u32[]{:S(2)}) collective-permute-start(bf16[1,240,768]{2,1,0:T(8,128)(2,1)S(1)} %get-tuple-element.252), channel_id=1, source_target_pairs={{0,16},{4,20},{8,24},{12,28},{16,0},{20,4},{24,8},{28,12},{1,17},{... | collective-permute-start | bytes 1105928 | tf_op jit(solution)/shard_map/ppermute | solution.py:23
  223.4 3.9 %collective-permute-start.20 = (bf16[4,288,768]{2,1,0:T(8,128)(2,1)}, bf16[4,288,768]{2,1,0:T(8,128)(2,1)S(1)}, u32[]{:S(2)}, u32[]{:S(2)}) collective-permute-start(bf16[4,288,768]{2,1,0:T(8,128)(2,1)} %bitcast.223), channel_id=1, source_target_pairs={{0,4},{4,0},{8,12},{12,8},{16,20},{20,16},{24,28},{28,24},{1,5},{5... | collective-permute-start | bytes 5308424 | tf_op jit(solution)/shard_map/ppermute | solution.py:23
  228.4 13.7 %collective-permute-start.21 = (bf16[1,2,144,768]{3,2,1,0:T(8,128)(2,1)S(1)}, bf16[1,2,144,768]{3,2,1,0:T(8,128)(2,1)S(1)}, u32[]{:S(2)}, u32[]{:S(2)}) collective-permute-start(bf16[1,2,144,768]{3,2,1,0:T(8,128)(2,1)S(1)} %bitcast.190), channel_id=1, source_target_pairs={{0,8},{4,12},{8,0},{12,4},{16,24},{20,28},{24,16},{28,20},{1,9},{5... | collective-permute-start | bytes 1327112 | tf_op jit(solution)/shard_map/ppermute | solution.py:23
  229.8 12.3 %collective-permute-start.22 = (bf16[1,2,144,768]{3,2,1,0:T(8,128)(2,1)S(1)}, bf16[1,2,144,768]{3,2,1,0:T(8,128)(2,1)S(1)}, u32[]{:S(2)}, u32[]{:S(2)}) collective-permute-start(bf16[1,2,144,768]{3,2,1,0:T(8,128)(2,1)S(1)} %bitcast.189), channel_id=1, source_target_pairs={{0,16},{4,20},{8,24},{12,28},{16,0},{20,4},{24,8},{28,12},{1,17},{... | collective-permute-start | bytes 1327112 | tf_op jit(solution)/shard_map/ppermute | solution.py:23
  242.2 12.6 %collective-permute-start.23 = (bf16[1,144,768]{2,1,0:T(8,128)(2,1)S(1)}, bf16[1,144,768]{2,1,0:T(8,128)(2,1)S(1)}, u32[]{:S(2)}, u32[]{:S(2)}) collective-permute-start(bf16[1,144,768]{2,1,0:T(8,128)(2,1)S(1)} %fusion.3), channel_id=1, source_target_pairs={{0,8},{4,12},{8,0},{12,4},{16,24},{20,28},{24,16},{28,20},{1,9},{5... | collective-permute-start | bytes 663560 | tf_op jit(solution)/shard_map/ppermute | solution.py:23
  243.7 11.2 %collective-permute-start.24 = (bf16[1,144,768]{2,1,0:T(8,128)(2,1)S(1)}, bf16[1,144,768]{2,1,0:T(8,128)(2,1)S(1)}, u32[]{:S(2)}, u32[]{:S(2)}) collective-permute-start(bf16[1,144,768]{2,1,0:T(8,128)(2,1)S(1)} %fusion.2), channel_id=1, source_target_pairs={{0,16},{4,20},{8,24},{12,28},{16,0},{20,4},{24,8},{28,12},{1,17},{... | collective-permute-start | bytes 663560 | tf_op jit(solution)/shard_map/ppermute | solution.py:23
  244.3 7.7 %collective-permute-start.25 = (f32[16,768]{1,0:T(8,128)S(1)}, f32[16,768]{1,0:T(8,128)S(1)}, u32[]{:S(2)}, u32[]{:S(2)}) collective-permute-start(f32[16,768]{1,0:T(8,128)S(1)} %copy-done.17), channel_id=1, source_target_pairs={{0,1},{1,2},{2,3},{3,0},{4,5},{5,6},{6,7},{7,4},{8,9},{9,10},{10,1... | collective-permute-start | bytes 147464 | tf_op jit(solution)/shard_map/ppermute | solution.py:23
  245.8 9.0 %collective-permute-start.26 = (f32[16,768]{1,0:T(8,128)S(1)}, f32[16,768]{1,0:T(8,128)S(1)}, u32[]{:S(2)}, u32[]{:S(2)}) collective-permute-start(f32[16,768]{1,0:T(8,128)S(1)} %copy-done.17), channel_id=1, source_target_pairs={{0,2},{1,3},{2,0},{3,1},{4,6},{5,7},{6,4},{7,5},{8,10},{9,11},{10,... | collective-permute-start | bytes 147464 | tf_op jit(solution)/shard_map/ppermute | solution.py:23
  248.2 6.6 %collective-permute-start.27 = (f32[16,768]{1,0:T(8,128)S(1)}, f32[16,768]{1,0:T(8,128)S(1)}, u32[]{:S(2)}, u32[]{:S(2)}) collective-permute-start(f32[16,768]{1,0:T(8,128)S(1)} %copy-done.17), channel_id=1, source_target_pairs={{0,3},{1,0},{2,1},{3,2},{4,7},{5,4},{6,5},{7,6},{8,11},{9,8},{10,9... | collective-permute-start | bytes 147464 | tf_op jit(solution)/shard_map/ppermute | solution.py:23
  255.1 9.1 %copy-start.16 = (bf16[1,192,384]{2,1,0:T(8,128)(2,1)S(1)}, bf16[1,192,384]{2,1,0:T(8,128)(2,1)}, u32[]{:S(2)}) copy-start(bf16[1,192,384]{2,1,0:T(8,128)(2,1)} %reduce-scatter.6.cloned.1.call-done) | copy-start | bytes 442372
  256.9 6.9 %collective-permute-start.31 = (f32[16,768]{1,0:T(8,128)S(1)}, f32[16,768]{1,0:T(8,128)S(1)}, u32[]{:S(2)}, u32[]{:S(2)}) collective-permute-start(f32[16,768]{1,0:T(8,128)S(1)} %add_add_fusion.1), channel_id=1, source_target_pairs={{0,8},{4,12},{8,0},{12,4},{16,24},{20,28},{24,16},{28,20},{1,9},{5... | collective-permute-start | bytes 147464 | tf_op jit(solution)/shard_map/ppermute | solution.py:23
  258.3 10.4 %collective-permute-start.28 = (bf16[96,640]{1,0:T(8,128)(2,1)S(1)}, bf16[96,640]{1,0:T(8,128)(2,1)S(1)}, u32[]{:S(2)}, u32[]{:S(2)}) collective-permute-start(bf16[96,640]{1,0:T(8,128)(2,1)S(1)} %get-tuple-element.296), channel_id=1, source_target_pairs={{0,1},{1,2},{2,3},{3,0},{4,5},{5,6},{6,7},{7,4},{8,9},{9,10},{10,1... | collective-permute-start | bytes 368648 | tf_op jit(solution)/shard_map/ppermute | solution.py:23
  259.4 10.7 %collective-permute-start.29 = (bf16[96,640]{1,0:T(8,128)(2,1)S(1)}, bf16[96,640]{1,0:T(8,128)(2,1)S(1)}, u32[]{:S(2)}, u32[]{:S(2)}) collective-permute-start(bf16[96,640]{1,0:T(8,128)(2,1)S(1)} %get-tuple-element.297), channel_id=1, source_target_pairs={{0,2},{1,3},{2,0},{3,1},{4,6},{5,7},{6,4},{7,5},{8,10},{9,11},{10,... | collective-permute-start | bytes 368648 | tf_op jit(solution)/shard_map/ppermute | solution.py:23
  260.8 9.4 %collective-permute-start.30 = (bf16[96,640]{1,0:T(8,128)(2,1)S(1)}, bf16[96,640]{1,0:T(8,128)(2,1)S(1)}, u32[]{:S(2)}, u32[]{:S(2)}) collective-permute-start(bf16[96,640]{1,0:T(8,128)(2,1)S(1)} %get-tuple-element.298), channel_id=1, source_target_pairs={{0,3},{1,0},{2,1},{3,2},{4,7},{5,4},{6,5},{7,6},{8,11},{9,8},{10,9... | collective-permute-start | bytes 368648 | tf_op jit(solution)/shard_map/ppermute | solution.py:23
  262.2 4.6 %collective-permute-start.32 = (f32[16,768]{1,0:T(8,128)S(1)}, f32[16,768]{1,0:T(8,128)S(1)}, u32[]{:S(2)}, u32[]{:S(2)}) collective-permute-start(f32[16,768]{1,0:T(8,128)S(1)} %add_add_fusion.1), channel_id=1, source_target_pairs={{0,16},{4,20},{8,24},{12,28},{16,0},{20,4},{24,8},{28,12},{1,17},{... | collective-permute-start | bytes 147464 | tf_op jit(solution)/shard_map/ppermute | solution.py:23
  263.8 5.0 %collective-permute-start.33 = (f32[16,768]{1,0:T(8,128)S(1)}, f32[16,768]{1,0:T(8,128)S(1)}, u32[]{:S(2)}, u32[]{:S(2)}) collective-permute-start(f32[16,768]{1,0:T(8,128)S(1)} %add_add_fusion.1), channel_id=1, source_target_pairs={{0,24},{4,28},{8,16},{12,20},{16,8},{20,12},{24,0},{28,4},{1,25},{... | collective-permute-start | bytes 147464 | tf_op jit(solution)/shard_map/ppermute | solution.py:23
  270.2 2.4 collective-permute-start.34
  (10 other events, 23.8 us)
Sparse Core Ops, SparseCore 0:
  50.7 38.8 all-gather.4
  91.4 38.9 all-gather.6
  133.8 53.8 reduce-scatter.3
  190.0 21.9 reduce-scatter.5
  230.6 26.2 reduce-scatter.7

commit v6 on v5

--- a/solution.py
+++ b/solution.py
@@ -151,6 +151,10 @@
 
 def dot(left, right):
     return lax.dot_general(left, right, (((1,), (0,)), ((), ())), preferred_element_type=F32)
+
+
+def dot_tn(left, right):
+    return lax.dot_general(left, right, (((0,), (0,)), ((), ())), preferred_element_type=F32)
 
 
 def dot_nt(left, right):
@@ -590,45 +594,32 @@
 def outer_kernel(spread, steps, place, *refs):
     lefts, refs = refs[: len(steps)], refs[len(steps) :]
     count = sum(len(own) for own in steps)
-    rights, refs = refs[:count], refs[count:]
-    flat = refs[-1]
+    rights, outs = refs[:count], refs[count:]
     step = pl.program_id(0)
 
-    def put(right):
-        value = dot(flat[...], right[...])
+    def put(left, right):
+        value = dot_tn(left[...], right[...]).astype(BF16)
         if not spread:
-            refs[0][...] = value.astype(BF16)
+            outs[0][...] = value
             return
-        mine, theirs = refs[:2]
-        unit = flat.shape[0] // 8
-        value = value.astype(BF16)
-        for at in range(4):
-            mine[at, 0] = value[2 * at * unit : (2 * at + 1) * unit]
-            theirs[at, 0] = value[(2 * at + 1) * unit : (2 * at + 2) * unit]
+        plane, core = place[0] // 2, place[0] % 2
+        unit = value.shape[0] // 8
+        for own in range(2):
+
+            @pl.when(core == own)
+            def _(own=own):
+                for at in range(4):
+                    for out, part in zip(outs, (own, 1 - own)):
+                        first = (2 * at + part) * unit
+                        out[at ^ plane, 0] = value[first : first + unit]
 
     first, at_right = 0, 0
     for left, own in zip(lefts, steps):
-
-        @pl.when(step == first)
-        def _(left=left):
-            for at in range(0, flat.shape[0], 128):
-                block = left[:, at : at + 128].astype(F32)
-                turned = jnp.transpose(block).astype(BF16)
-                if spread:
-                    refs[2][at : at + 128, :] = turned
-                else:
-                    flat[at : at + 128, :] = turned
-            if spread:
-                unit = flat.shape[0] // 8
-                for rel in range(8):
-                    start = pl.multiple_of((place[0] ^ rel) * unit, 16)
-                    flat[rel * unit : (rel + 1) * unit, :] = refs[2][pl.ds(start, unit), :]
-
         for count in own:
 
             @pl.when((step >= first) & (step < first + count))
-            def _(right=rights[at_right]):
-                put(right)
+            def _(left=left, right=rights[at_right]):
+                put(left, right)
 
             first += count
             at_right += 1
@@ -647,12 +638,10 @@
             )
         )
         first += own
-    scratch = [pltpu.VMEM((height, count), BF16)]
     if direct():
         block = pl.BlockSpec((4, 1, height // 8, width), lambda i: (0, i, 0, 0))
         shape = jax.ShapeDtypeStruct((4, total, height // 8, width), BF16)
         specs, shapes = [block, block], [shape, shape]
-        scratch = scratch * 2
     else:
         specs = pl.BlockSpec((height, width), lambda i: (0, i))
         shapes = jax.ShapeDtypeStruct((height, total * width), BF16)
@@ -662,21 +651,14 @@
         in_specs=[SMEM] + [whole((count, height))] * len(pairs) + right_specs,
         out_specs=specs,
         out_shape=shapes,
-        scratch_shapes=scratch,
-        compiler_params=params(60),
+        compiler_params=params(54),
         cost_estimate=cost(2 * count * height * total * width, 2 * (count + height) * total * width),
         name="outer",
     )(place, *(left for left, _ in pairs), *(right for _, rights in pairs for right in rights))
 
 
-def wide_outer_kernel(place, left, right, out, flat):
-    @pl.when(pl.program_id(0) == 0)
-    def _():
-        for at in range(0, flat.shape[0], 128):
-            block = left[:, at : at + 128].astype(F32)
-            flat[at : at + 128, :] = jnp.transpose(block).astype(BF16)
-
-    value = dot(flat[...], right[...]).astype(BF16)
+def wide_outer_kernel(left, right, out):
+    value = dot_tn(left[...], right[...]).astype(BF16)
     half = value.shape[1] // 2
     out[0] = value[:, :half]
     out[1] = value[:, half:]
@@ -690,14 +672,13 @@
     return pl.pallas_call(
         wide_outer_kernel,
         grid=(steps // 2,),
-        in_specs=[SMEM, whole(left.shape), pl.BlockSpec((count, 2 * step), lambda i: (0, i))],
+        in_specs=[whole(left.shape), pl.BlockSpec((count, 2 * step), lambda i: (0, i))],
         out_specs=pl.BlockSpec((2, height, step), lambda i: (i, 0, 0)),
         out_shape=jax.ShapeDtypeStruct((steps, height, step), BF16),
-        scratch_shapes=[pltpu.VMEM((height, count), BF16)],
         compiler_params=params(60),
         cost_estimate=cost(2 * count * height * columns, 2 * (count + height) * (height + columns)),
         name="wide_outer",
-    )(place, left, right)
+    )(left, right)
 
 
 def inputs_kernel(plans, place, rows, grad_middle, grad_q, grad_k, grad_v, table, earlier, *refs):
@@ -985,7 +966,7 @@
         return grads
 
     groups = width // (HEADS * HD)
-    spans = [(0, 0, 1), (0, 1, groups)] + [(pack, 0, groups) for pack in range(1, packs)]
+    spans = [(0, 0, groups - 1), (0, groups - 1, groups)] + [(pack, 0, groups) for pack in range(1, packs)]
     value_rows = value
     grads, (other,) = beside(
         lambda v: heads_back((), v, spans[:1]), grad_mixed, [theirs], [lambda v: cross(v, 0)]

time: 286 us -> 283 us (0.990)
  transfers between devices with their start and end apart: 40 -> 40, of which waited for: 16 -> 16; matrix products, arithmetic and copies ran while one was open for 3% -> 3% of each run, Pallas kernels for 54% -> 55%
where the time goes in v6:
time: 283 us; the launch traced here: 277 us
  Pallas kernels  152 us (54%)
  waiting for transfers between devices  45.4 us (16%)
  starting transfers between devices  44.8 us (16%)
  between operations  15 us (5%)
  local copies, waits for them, and re-layouts  10 us (4%)
  other arithmetic  9.54 us (3%)
    ppermute x35, starting transfers between devices, exchange(): lax.ppermute(value, axis_name, [(i, partner(i) % size) for i in range(siz...  44.2 us
    ppermute x35, waiting for transfers between devices, exchange(): lax.ppermute(value, axis_name, [(i, partner(i) % size) for i in range(siz...  43.4 us
    pallas_call x1, Pallas kernels, back(): pl.pallas_call(functools.partial(back_kernel, *plans, sizes), grid=(count...  30.1 us
    pallas_call x3, Pallas kernels, attend_back(): pl.pallas_call(attend_back_kernel, grid=(part,), in_specs=[pair_block(row...  25.6 us
    pallas_call x2, Pallas kernels, attend(): pl.pallas_call(functools.partial(attend_kernel, pack), grid=(pairs,), in_...  21.9 us
    pallas_call x2, Pallas kernels, outer(): pl.pallas_call(functools.partial(outer_kernel, direct(), steps), grid=(to...  20.9 us
    pallas_call x1, Pallas kernels, hidden(): pl.pallas_call(functools.partial(hidden_kernel, out_plan, up_plans, sizes...  19.3 us
    pallas_call x1, Pallas kernels, inputs_back(): pl.pallas_call(functools.partial(inputs_kernel, plans), grid=(count // TI...  11.4 us
  transfers between devices with their start and end apart: 40, of which 16 were waited for; matrix products, arithmetic and copies ran while one was open for 3% of the time, Pallas kernels for 55%

profile of v6, /device:TPU:0, one launch (start us, length us, event | category | flops | bytes accessed | tf_op | source)
XLA Modules:
  0.0 277.2 jit_solution(5085135626584063875)
XLA Ops:
  7.3 1.5 stack.82
  10.4 5.1 %collective-permute-start = (bf16[112,768]{1,0:T(8,128)(2,1)S(1)}, bf16[112,768]{1,0:T(8,128)(2,1)S(1)}, u32[]{:S(2)}, u32[]{:S(2)}) collective-permute-start(bf16[112,768]{1,0:T(8,128)(2,1)S(1)} %fusion.6), channel_id=1, source_target_pairs={{0,3},{1,0},{2,1},{3,2},{4,7},{5,4},{6,5},{7,6},{8,11},{9,8},{10,9... | collective-permute-start | bytes 516104 | tf_op jit(solution)/shard_map/ppermute | solution.py:23
  16.6 3.8 %collective-permute-done = bf16[112,768]{1,0:T(8,128)(2,1)S(1)} collective-permute-done((bf16[112,768]{1,0:T(8,128)(2,1)S(1)}, bf16[112,768]{1,0:T(8,128)(2,1)S(1)}, u32[]{:S(2)}, u32[]{:S(2)}) %collective-permute-start) | collective-permute-done | bytes 172064 | tf_op jit(solution)/shard_map/ppermute | solution.py:23
  20.4 9.7 %collective-permute-done.1 = bf16[112,768]{1,0:T(8,128)(2,1)S(1)} collective-permute-done((bf16[112,768]{1,0:T(8,128)(2,1)S(1)}, bf16[112,768]{1,0:T(8,128)(2,1)S(1)}, u32[]{:S(2)}, u32[]{:S(2)}) %collective-permute-start.1) | collective-permute-done | bytes 172064 | tf_op jit(solution)/shard_map/ppermute | solution.py:23
  31.3 1.6 collective-permute-start.3
  32.8 1.5 collective-permute-start.4
  35.2 1.9 collective-permute-start.6
  37.1 2.9 %collective-permute-start.7 = (bf16[96,768]{1,0:T(8,128)(2,1)S(1)}, bf16[96,768]{1,0:T(8,128)(2,1)S(1)}, u32[]{:S(2)}, u32[]{:S(2)}) collective-permute-start(bf16[96,768]{1,0:T(8,128)(2,1)S(1)} %copy-done.13), channel_id=1, source_target_pairs={{0,3},{1,0},{2,1},{3,2},{4,7},{5,4},{6,5},{7,6},{8,11},{9,8},{10,9... | collective-permute-start | bytes 442376 | tf_op jit(solution)/shard_map/ppermute | solution.py:23
  40.0 2.9 %collective-permute-done.5 = bf16[96,768]{1,0:T(8,128)(2,1)S(1)} collective-permute-done((bf16[96,768]{1,0:T(8,128)(2,1)S(1)}, bf16[96,768]{1,0:T(8,128)(2,1)S(1)}, u32[]{:S(2)}, u32[]{:S(2)}) %collective-permute-start.5) | collective-permute-done | bytes 147488 | tf_op jit(solution)/shard_map/ppermute | solution.py:23
  43.0 4.5 %collective-permute-done.6 = bf16[96,768]{1,0:T(8,128)(2,1)S(1)} collective-permute-done((bf16[96,768]{1,0:T(8,128)(2,1)S(1)}, bf16[96,768]{1,0:T(8,128)(2,1)S(1)}, u32[]{:S(2)}, u32[]{:S(2)}) %collective-permute-start.6) | collective-permute-done | bytes 147488 | tf_op jit(solution)/shard_map/ppermute | solution.py:23
  48.0 1.4 pad_maximum_fusion
  51.3 1.5 collective-permute-start.8
  52.8 7.6 %collective-permute-done.8 = bf16[1,192,768]{2,1,0:T(8,128)(2,1)S(1)} collective-permute-done((bf16[1,192,768]{2,1,0:T(8,128)(2,1)S(1)}, bf16[1,192,768]{2,1,0:T(8,128)(2,1)S(1)}, u32[]{:S(2)}, u32[]{:S(2)}) %collective-permute-start.8) | collective-permute-done | bytes 294944 | tf_op jit(solution)/shard_map/ppermute | solution.py:23
  61.4 3.6 %collective-permute-start.12 = (bf16[96,768]{1,0:T(8,128)(2,1)S(1)}, bf16[96,768]{1,0:T(8,128)(2,1)S(1)}, u32[]{:S(2)}, u32[]{:S(2)}) collective-permute-start(bf16[96,768]{1,0:T(8,128)(2,1)S(1)} %pad_maximum_fusion.5), channel_id=1, source_target_pairs={{0,1},{1,2},{2,3},{3,0},{4,5},{5,6},{6,7},{7,4},{8,9},{9,10},{10,1... | collective-permute-start | bytes 442376 | tf_op jit(solution)/shard_map/ppermute | solution.py:23
  65.1 2.0 collective-permute-start.13
  68.4 10.1 %project.1 = (bf16[1024,768]{1,0:T(8,128)(2,1)}, bf16[1024,768]{1,0:T(8,128)(2,1)}, bf16[1024,768]{1,0:T(8,128)(2,1)}, bf16[1024,768]{1,0:T(8,128)(2,1)}, f32[16,768]{1,0:T(8,128)}) custom-call(s32[1]{0:T(128)} %bitcast.place, bf16[1024,768]{1,0:T(8,128)(2,1)} %bitcast.200, bf16[16,768]{1,0:T(8,128)(2,1)} %broadcast.21.extras, ...), custom_call_target="tpu_custom_call" | custom-call | flops 3623878656 | bytes 11010048 | tf_op jit(solution)/shard_map/project/pallas_call | solution.py:279
  78.9 1.1 maximum_maximum_fusion
  80.3 11.0 %attend.2 = (bf16[1024,768]{1,0:T(8,128)(2,1)}, bf16[12,512,512]{2,1,0:T(8,128)(2,1)}) custom-call(s32[2,6]{1,0:T(2,128)} %lengths.7, bf16[1024,768]{1,0:T(8,128)(2,1)} %get-tuple-element.189.query, bf16[1024,768]{1,0:T(8,128)(2,1)} %get-tuple-element.190.key, bf16[1024,768]{1,0:T(8,128)(2,1)} %get-tuple-element.191.value), custom_call_target="tpu_custom_call" | custom-call | tf_op jit(solution)/shard_map/attend/pallas_call | solution.py:360
  91.3 10.9 %attend.3 = (bf16[1024,768]{1,0:T(8,128)(2,1)}, bf16[12,512,512]{2,1,0:T(8,128)(2,1)}) custom-call(s32[2,6]{1,0:T(2,128)} %lengths.7, bf16[1024,768]{1,0:T(8,128)(2,1)} %get-tuple-element.189.query, bf16[1024,768]{1,0:T(8,128)(2,1)} %get-tuple-element.190.key, bf16[1024,768]{1,0:T(8,128)(2,1)} %get-tuple-element.191.value, ...), custom_call_target="tpu_custom_call", output_to_operand_aliasing={{0}: (4, {})} | custom-call | flops 3221225472 | bytes 3145728 | tf_op jit(solution)/shard_map/attend/pallas_call | solution.py:360
  102.2 19.3 %hidden.1 = (f32[1024,768]{1,0:T(8,128)}, bf16[1024,768]{1,0:T(8,128)(2,1)}, bf16[1024,3072]{1,0:T(8,128)(2,1)}, bf16[1024,3072]{1,0:T(8,128)(2,1)}, bf16[1024,768]{1,0:T(8,128)(2,1)}) custom-call(s32[1]{0:T(128)} %bitcast.place, s32[2,6]{1,0:T(2,128)} %lengths.7, bf16[1024,768]{1,0:T(8,128)(2,1)} %bitcast.201, ...), custom_call_target="tpu_custom_call" | custom-call | flops 8455716864 | bytes 20447232 | tf_op jit(solution)/shard_map/hidden/pallas_call | solution.py:469
  121.5 9.2 %wide_outer.1 = bf16[8,768,384]{2,1,0:T(8,128)(2,1)} custom-call(bf16[1024,768]{1,0:T(8,128)(2,1)} %get-tuple-element.198.left.grad_down, bf16[1024,3072]{1,0:T(8,128)(2,1)} %get-tuple-element.199.right.active), custom_call_target="tpu_custom_call" | custom-call | flops 4831838208 | bytes 13762560 | tf_op jit(solution)/shard_map/wide_outer/pallas_call | solution.py:672
  131.1 30.1 %back.1 = (bf16[1024,768]{1,0:T(8,128)(2,1)}, bf16[1024,3072]{1,0:T(8,128)(2,1)}, f32[1024,768]{1,0:T(8,128)}, bf16[1024,768]{1,0:T(8,128)(2,1)}, bf16[1024,768]{1,0:T(8,128)(2,1)}, /*index=5*/f32[16,768]{1,0:T(8,128)}) custom-call(s32[1]{0:T(128)} %bitcast.place, s32[2,6]{1,0:T(2,128)} %lengths.7, bf16[1024,768]{1,0:T(8,128)(2,1)} %bitcast.202, ...), custom_call_target="tpu_custom_call" | custom-call | flops 15703474176 | bytes 31457280 | tf_op jit(solution)/shard_map/back/pallas_call | solution.py:560
  161.2 12.2 %outer.2 = (bf16[4,5,96,768]{3,2,1,0:T(8,128)(2,1)}, bf16[4,5,96,768]{3,2,1,0:T(8,128)(2,1)}) custom-call(s32[1]{0:T(128)} %bitcast.place, bf16[1024,768]{1,0:T(8,128)(2,1)} %get-tuple-element.207.refs_0_, bf16[1024,768]{1,0:T(8,128)(2,1)} %get-tuple-element.193.mixed.refs_1_, bf16[1024,3072]{1,0:T(8,128)(2,1)} %get-tuple-element.208.refs_2_, ...), custom_call_target="tpu_custom_call" | custom-call | flops 6039797760 | bytes 13762560 | tf_op jit(solution)/shard_map/outer/pallas_call | solution.py:648
  173.4 8.5 %attend_back.3 = (bf16[1024,768]{1,0:T(8,128)(2,1)}, bf16[1024,768]{1,0:T(8,128)(2,1)}, bf16[1024,768]{1,0:T(8,128)(2,1)}) custom-call(bf16[1024,768]{1,0:T(8,128)(2,1)} %get-tuple-element.189.query, bf16[1024,768]{1,0:T(8,128)(2,1)} %get-tuple-element.190.key, bf16[1024,768]{1,0:T(8,128)(2,1)} %get-tuple-element.191.value, ...), custom_call_target="tpu_custom_call" | custom-call | flops 4294967296 | bytes 3670016 | tf_op jit(solution)/shard_map/attend_back/pallas_call | solution.py:398
  182.0 2.8 %core_add.2 = (bf16[1,480,768]{2,1,0:T(8,128)(2,1)S(1)}, bf16[2,240,768]{2,1,0:T(8,128)(2,1)S(1)}, bf16[2,240,768]{2,1,0:T(8,128)(2,1)S(1)}, bf16[1,240,768]{2,1,0:T(8,128)(2,1)S(1)}, bf16[1,240,768]{2,1,0:T(8,128)(2,1)S(1)}) custom-call(bf16[4,480,768]{2,1,0:T(8,128)(2,1)S(1)} %bitcast.185, bf16[4,480,768]{2,1,0:T(8,128)(2,1)} %collective-permute-done.15.other), custom_call_target="tpu_custom_call" | custom-call | flops 1474560 | bytes 8847360 | tf_op jit(solution)/shard_map/core_add/pallas_call | solution.py:784
  187.7 1.4 collective-permute-start.16
  189.8 5.6 %attend_back.4 = (bf16[1024,768]{1,0:T(8,128)(2,1)}, bf16[1024,768]{1,0:T(8,128)(2,1)}, bf16[1024,768]{1,0:T(8,128)(2,1)}) custom-call(bf16[1024,768]{1,0:T(8,128)(2,1)} %get-tuple-element.189.query, bf16[1024,768]{1,0:T(8,128)(2,1)} %get-tuple-element.190.key, ...), custom_call_target="tpu_custom_call", output_to_operand_aliasing={{0}: (5, {}), {1}: (6, {}), {2}: (7, {})} | custom-call | flops 2147483648 | bytes 1835008 | tf_op jit(solution)/shard_map/attend_back/pallas_call | solution.py:398
  195.4 11.5 %attend_back.5 = (bf16[1024,768]{1,0:T(8,128)(2,1)}, bf16[1024,768]{1,0:T(8,128)(2,1)}, bf16[1024,768]{1,0:T(8,128)(2,1)}) custom-call(bf16[1024,768]{1,0:T(8,128)(2,1)} %get-tuple-element.189.query, bf16[1024,768]{1,0:T(8,128)(2,1)} %get-tuple-element.190.key, ...), custom_call_target="tpu_custom_call", output_to_operand_aliasing={{0}: (5, {}), {1}: (6, {}), {2}: (7, {})} | custom-call | flops 6442450944 | bytes 5505024 | tf_op jit(solution)/shard_map/attend_back/pallas_call | solution.py:398
  207.5 1.1 collective-permute-start.18
  209.6 8.7 %outer.3 = (bf16[4,3,96,768]{3,2,1,0:T(8,128)(2,1)}, bf16[4,3,96,768]{3,2,1,0:T(8,128)(2,1)}) custom-call(s32[1]{0:T(128)} %bitcast.place, bf16[1024,768]{1,0:T(8,128)(2,1)} %get-tuple-element.245.refs_0_, bf16[1024,768]{1,0:T(8,128)(2,1)} %get-tuple-element.264.refs_1_.grad_q, bf16[1024,768]{1,0:T(8,128)(2,1)} %get-tuple-element.265.refs_2_.grad_k, ...), custom_call_target="tpu_custom_call" | custom-call | flops 3623878656 | bytes 8257536 | tf_op jit(solution)/shard_map/outer/pallas_call | solution.py:648
  219.9 3.9 %collective-permute-done.20.other = bf16[4,288,768]{2,1,0:T(8,128)(2,1)S(1)} collective-permute-done((bf16[4,288,768]{2,1,0:T(8,128)(2,1)}, bf16[4,288,768]{2,1,0:T(8,128)(2,1)S(1)}, u32[]{:S(2)}, u32[]{:S(2)}) %collective-permute-start.20) | collective-permute-done | bytes 1769504 | tf_op jit(solution)/shard_map/ppermute | solution.py:23
  223.8 1.0 core_add.3
  224.9 1.1 collective-permute-start.21
  227.0 11.4 %inputs_back.1 = (f32[1024,768]{1,0:T(8,128)}, f32[16,768]{1,0:T(8,128)}) custom-call(s32[1]{0:T(128)} %bitcast.place, bf16[1024,768]{1,0:T(8,128)(2,1)} %bitcast.203, f32[1024,768]{1,0:T(8,128)} %get-tuple-element.203.grad_middle, bf16[1024,768]{1,0:T(8,128)(2,1)} %get-tuple-element.264.refs_1_.grad_q, bf16[1024,768]{1,0:T(8,128)(2,1)} %get-tuple-element.265.refs_2_.grad_k, ...), custom_call_target="tpu_custom_call" | custom-call | flops 3623878656 | bytes 15728640 | tf_op jit(solution)/shard_map/inputs_back/pallas_call | solution.py:714
  238.5 1.2 collective-permute-start.23
  240.7 2.5 collective-permute-start.25
  243.2 1.3 collective-permute-start.26
  244.5 1.5 collective-permute-start.27
  246.0 2.3 collective-permute-done.25
  248.3 3.2 %collective-permute-done.26 = f32[16,768]{1,0:T(8,128)S(1)} collective-permute-done((f32[16,768]{1,0:T(8,128)S(1)}, f32[16,768]{1,0:T(8,128)S(1)}, u32[]{:S(2)}, u32[]{:S(2)}) %collective-permute-start.26) | collective-permute-done | bytes 49184 | tf_op jit(solution)/shard_map/ppermute | solution.py:23
  251.9 1.4 reduce-scatter.8.cloned.1.call-done
  253.3 1.4 collective-permute-start.31
  254.8 1.1 collective-permute-start.28
  255.9 1.3 collective-permute-start.29
  257.3 1.3 collective-permute-start.30
  258.6 1.6 collective-permute-start.32
  263.2 2.1 collective-permute-done.33
  265.3 1.3 collective-permute-done.29
  (165 shorter events, 25.6 us)
Async XLA Ops:
  7.2 23.0 %copy-start.11 = (bf16[96,576]{1,0:T(8,128)(2,1)S(1)}, bf16[96,576]{1,0:T(8,128)(2,1)}, u32[]{:S(2)}) copy-start(bf16[96,576]{1,0:T(8,128)(2,1)} %param.20) | copy-start | bytes 331780
  7.2 23.0 %copy-start.14 = (bf16[96,192]{1,0:T(8,128)(2,1)S(1)}, bf16[96,192]{1,0:T(8,128)(2,1)}, u32[]{:S(2)}) copy-start(bf16[96,192]{1,0:T(8,128)(2,1)} %param.21) | copy-start | bytes 110596
  7.2 95.0 %all-gather.5.cloned.1.call-start = ((), (), s32[]{:S(2)}) async-start(), calls=%async_computation.6 | async-start | bytes 5308416 | tf_op jit(solution)/shard_map/all_gather | solution.py:925
  10.4 9.9 %collective-permute-start = (bf16[112,768]{1,0:T(8,128)(2,1)S(1)}, bf16[112,768]{1,0:T(8,128)(2,1)S(1)}, u32[]{:S(2)}, u32[]{:S(2)}) collective-permute-start(bf16[112,768]{1,0:T(8,128)(2,1)S(1)} %fusion.6), channel_id=1, source_target_pairs={{0,3},{1,0},{2,1},{3,2},{4,7},{5,4},{6,5},{7,6},{8,11},{9,8},{10,9... | collective-permute-start | bytes 516104 | tf_op jit(solution)/shard_map/ppermute | solution.py:23
  15.6 14.6 %collective-permute-start.1 = (bf16[112,768]{1,0:T(8,128)(2,1)S(1)}, bf16[112,768]{1,0:T(8,128)(2,1)S(1)}, u32[]{:S(2)}, u32[]{:S(2)}) collective-permute-start(bf16[112,768]{1,0:T(8,128)(2,1)S(1)} %fusion.6), channel_id=1, source_target_pairs={{0,2},{1,3},{2,0},{3,1},{4,6},{5,7},{6,4},{7,5},{8,10},{9,11},{10,... | collective-permute-start | bytes 516104 | tf_op jit(solution)/shard_map/ppermute | solution.py:23
  15.6 14.6 %collective-permute-start.2 = (bf16[112,768]{1,0:T(8,128)(2,1)S(1)}, bf16[112,768]{1,0:T(8,128)(2,1)S(1)}, u32[]{:S(2)}, u32[]{:S(2)}) collective-permute-start(bf16[112,768]{1,0:T(8,128)(2,1)S(1)} %fusion.6), channel_id=1, source_target_pairs={{0,1},{1,2},{2,3},{3,0},{4,5},{5,6},{6,7},{7,4},{8,9},{9,10},{10,1... | collective-permute-start | bytes 516104 | tf_op jit(solution)/shard_map/ppermute | solution.py:23
  31.3 18.2 %copy-start.8 = (bf16[400,768]{1,0:T(8,128)(2,1)}, bf16[400,768]{1,0:T(8,128)(2,1)S(1)}, u32[]{:S(2)}) copy-start(bf16[400,768]{1,0:T(8,128)(2,1)S(1)} %constant_dynamic-update-slice_fusion) | copy-start | bytes 1843204
  31.3 16.3 %collective-permute-start.3 = (bf16[1,400,768]{2,1,0:T(8,128)(2,1)S(1)}, bf16[1,400,768]{2,1,0:T(8,128)(2,1)S(1)}, u32[]{:S(2)}, u32[]{:S(2)}) collective-permute-start(bf16[1,400,768]{2,1,0:T(8,128)(2,1)S(1)} %bitcast.191), channel_id=1, source_target_pairs={{0,8},{4,12},{8,0},{12,4},{16,24},{20,28},{24,16},{28,20},{1,9},{5... | collective-permute-start | bytes 1843208 | tf_op jit(solution)/shard_map/ppermute | solution.py:23
  32.8 15.2 %collective-permute-start.4 = (bf16[1,400,768]{2,1,0:T(8,128)(2,1)S(1)}, bf16[1,400,768]{2,1,0:T(8,128)(2,1)S(1)}, u32[]{:S(2)}, u32[]{:S(2)}) collective-permute-start(bf16[1,400,768]{2,1,0:T(8,128)(2,1)S(1)} %bitcast.192), channel_id=1, source_target_pairs={{0,16},{4,20},{8,24},{12,28},{16,0},{20,4},{24,8},{28,12},{1,17},{... | collective-permute-start | bytes 1843208 | tf_op jit(solution)/shard_map/ppermute | solution.py:23
  34.3 8.6 %collective-permute-start.5 = (bf16[96,768]{1,0:T(8,128)(2,1)S(1)}, bf16[96,768]{1,0:T(8,128)(2,1)S(1)}, u32[]{:S(2)}, u32[]{:S(2)}) collective-permute-start(bf16[96,768]{1,0:T(8,128)(2,1)S(1)} %copy-done.13), channel_id=1, source_target_pairs={{0,1},{1,2},{2,3},{3,0},{4,5},{5,6},{6,7},{7,4},{8,9},{9,10},{10,1... | collective-permute-start | bytes 442376 | tf_op jit(solution)/shard_map/ppermute | solution.py:23
  35.2 12.3 %collective-permute-start.6 = (bf16[96,768]{1,0:T(8,128)(2,1)S(1)}, bf16[96,768]{1,0:T(8,128)(2,1)S(1)}, u32[]{:S(2)}, u32[]{:S(2)}) collective-permute-start(bf16[96,768]{1,0:T(8,128)(2,1)S(1)} %copy-done.13), channel_id=1, source_target_pairs={{0,2},{1,3},{2,0},{3,1},{4,6},{5,7},{6,4},{7,5},{8,10},{9,11},{10,... | collective-permute-start | bytes 442376 | tf_op jit(solution)/shard_map/ppermute | solution.py:23
  37.1 10.4 %collective-permute-start.7 = (bf16[96,768]{1,0:T(8,128)(2,1)S(1)}, bf16[96,768]{1,0:T(8,128)(2,1)S(1)}, u32[]{:S(2)}, u32[]{:S(2)}) collective-permute-start(bf16[96,768]{1,0:T(8,128)(2,1)S(1)} %copy-done.13), channel_id=1, source_target_pairs={{0,3},{1,0},{2,1},{3,2},{4,7},{5,4},{6,5},{7,6},{8,11},{9,8},{10,9... | collective-permute-start | bytes 442376 | tf_op jit(solution)/shard_map/ppermute | solution.py:23
  49.7 11.1 %copy-start.15 = (bf16[384,192]{0,1:T(8,128)(2,1)S(1)}, bf16[384,192]{0,1:T(8,128)(2,1)}, u32[]{:S(2)}) copy-start(bf16[384,192]{0,1:T(8,128)(2,1)} %param.23) | copy-start | bytes 442372
  50.6 80.5 %all-gather.7.cloned.1.call-start = ((), (), s32[]{:S(2)}) async-start(), calls=%async_computation.7 | async-start | bytes 5308416 | tf_op jit(solution)/shard_map/all_gather | solution.py:941
  50.6 10.0 %collective-permute-start.10 = (bf16[3,400,768]{2,1,0:T(8,128)(2,1)}, bf16[3,400,768]{2,1,0:T(8,128)(2,1)S(1)}, u32[]{:S(2)}, u32[]{:S(2)}) collective-permute-start(bf16[3,400,768]{2,1,0:T(8,128)(2,1)} %pad_maximum_fusion), channel_id=1, source_target_pairs={{0,4},{4,0},{8,12},{12,8},{16,20},{20,16},{24,28},{28,24},{1,5},{5... | collective-permute-start | bytes 5529608 | tf_op jit(solution)/shard_map/ppermute | solution.py:23
  50.7 10.0 %collective-permute-start.9 = (bf16[1,208,768]{2,1,0:T(8,128)(2,1)S(1)}, bf16[1,208,768]{2,1,0:T(8,128)(2,1)S(1)}, u32[]{:S(2)}, u32[]{:S(2)}) collective-permute-start(bf16[1,208,768]{2,1,0:T(8,128)(2,1)S(1)} %slice.270), channel_id=1, source_target_pairs={{0,8},{4,12},{8,0},{12,4},{16,24},{20,28},{24,16},{28,20},{1,9},{5... | collective-permute-start | bytes 958472 | tf_op jit(solution)/shard_map/ppermute | solution.py:23
  51.3 9.1 %collective-permute-start.8 = (bf16[1,192,768]{2,1,0:T(8,128)(2,1)S(1)}, bf16[1,192,768]{2,1,0:T(8,128)(2,1)S(1)}, u32[]{:S(2)}, u32[]{:S(2)}) collective-permute-start(bf16[1,192,768]{2,1,0:T(8,128)(2,1)S(1)} %slice.269), channel_id=1, source_target_pairs={{0,16},{4,20},{8,24},{12,28},{16,0},{20,4},{24,8},{28,12},{1,17},{... | collective-permute-start | bytes 884744 | tf_op jit(solution)/shard_map/ppermute | solution.py:23
  60.6 7.6 %copy-start.9 = (bf16[3,400,768]{2,1,0:T(8,128)(2,1)}, bf16[3,400,768]{2,1,0:T(8,128)(2,1)S(1)}, u32[]{:S(2)}) copy-start(bf16[3,400,768]{2,1,0:T(8,128)(2,1)S(1)} %collective-permute-done.10.refs_4_) | copy-start | bytes 5529604
  60.7 6.8 %collective-permute-start.11 = (bf16[1,400,768]{2,1,0:T(8,128)(2,1)S(1)}, bf16[1,400,768]{2,1,0:T(8,128)(2,1)S(1)}, u32[]{:S(2)}, u32[]{:S(2)}) collective-permute-start(bf16[1,400,768]{2,1,0:T(8,128)(2,1)S(1)} %constant_dynamic-update-slice_fusion.1.refs_3_), channel_id=1, source_target_pairs={{0,4},{4,0},{8,12},{12,8},{16,20},{20,16},{24,28},{28,24},{1,5},{5... | collective-permute-start | bytes 1843208 | tf_op jit(solution)/shard_map/ppermute | solution.py:23
  61.4 17.1 %collective-permute-start.12 = (bf16[96,768]{1,0:T(8,128)(2,1)S(1)}, bf16[96,768]{1,0:T(8,128)(2,1)S(1)}, u32[]{:S(2)}, u32[]{:S(2)}) collective-permute-start(bf16[96,768]{1,0:T(8,128)(2,1)S(1)} %pad_maximum_fusion.5), channel_id=1, source_target_pairs={{0,1},{1,2},{2,3},{3,0},{4,5},{5,6},{6,7},{7,4},{8,9},{9,10},{10,1... | collective-permute-start | bytes 442376 | tf_op jit(solution)/shard_map/ppermute | solution.py:23
  65.1 13.4 %collective-permute-start.13 = (bf16[96,768]{1,0:T(8,128)(2,1)S(1)}, bf16[96,768]{1,0:T(8,128)(2,1)S(1)}, u32[]{:S(2)}, u32[]{:S(2)}) collective-permute-start(bf16[96,768]{1,0:T(8,128)(2,1)S(1)} %pad_maximum_fusion.5), channel_id=1, source_target_pairs={{0,2},{1,3},{2,0},{3,1},{4,6},{5,7},{6,4},{7,5},{8,10},{9,11},{10,... | collective-permute-start | bytes 442376 | tf_op jit(solution)/shard_map/ppermute | solution.py:23
  67.1 11.5 %collective-permute-start.14 = (bf16[96,768]{1,0:T(8,128)(2,1)S(1)}, bf16[96,768]{1,0:T(8,128)(2,1)S(1)}, u32[]{:S(2)}, u32[]{:S(2)}) collective-permute-start(bf16[96,768]{1,0:T(8,128)(2,1)S(1)} %pad_maximum_fusion.5), channel_id=1, source_target_pairs={{0,3},{1,0},{2,1},{3,2},{4,7},{5,4},{6,5},{7,6},{8,11},{9,8},{10,9... | collective-permute-start | bytes 442376 | tf_op jit(solution)/shard_map/ppermute | solution.py:23
  80.1 107.6 %reduce-scatter.4.cloned.1.call-start = ((), (), s32[]{:S(2)}) async-start(), calls=%async_computation.3 | async-start | bytes 5308416 | tf_op jit(solution)/shard_map/reduce_scatter | solution.py:955
  130.8 89.1 %reduce-scatter.6.cloned.1.call-start = ((), (), s32[]{:S(2)}) async-start(), calls=%async_computation.4 | async-start | bytes 737280 | tf_op jit(solution)/shard_map/reduce_scatter | solution.py:976
  173.4 8.6 %collective-permute-start.15 = (bf16[4,480,768]{2,1,0:T(8,128)(2,1)}, bf16[4,480,768]{2,1,0:T(8,128)(2,1)}, u32[]{:S(2)}, u32[]{:S(2)}) collective-permute-start(bf16[4,480,768]{2,1,0:T(8,128)(2,1)} %bitcast.222), channel_id=1, source_target_pairs={{0,4},{4,0},{8,12},{12,8},{16,20},{20,16},{24,28},{28,24},{1,5},{5... | collective-permute-start | bytes 8847368 | tf_op jit(solution)/shard_map/ppermute | solution.py:23
  173.4 8.6 %copy-start = (bf16[4,5,96,768]{3,2,1,0:T(8,128)(2,1)S(1)}, bf16[4,5,96,768]{3,2,1,0:T(8,128)(2,1)}, u32[]{:S(2)}) copy-start(bf16[4,5,96,768]{3,2,1,0:T(8,128)(2,1)} %get-tuple-element.222) | copy-start | bytes 8847364
  187.7 19.2 %collective-permute-start.16 = (bf16[1,2,240,768]{3,2,1,0:T(8,128)(2,1)}, bf16[1,2,240,768]{3,2,1,0:T(8,128)(2,1)S(1)}, u32[]{:S(2)}, u32[]{:S(2)}) collective-permute-start(bf16[1,2,240,768]{3,2,1,0:T(8,128)(2,1)} %bitcast.188), channel_id=1, source_target_pairs={{0,8},{4,12},{8,0},{12,4},{16,24},{20,28},{24,16},{28,20},{1,9},{5... | collective-permute-start | bytes 2211848 | tf_op jit(solution)/shard_map/ppermute | solution.py:23
  189.1 18.2 %collective-permute-start.17 = (bf16[1,2,240,768]{3,2,1,0:T(8,128)(2,1)}, bf16[1,2,240,768]{3,2,1,0:T(8,128)(2,1)S(1)}, u32[]{:S(2)}, u32[]{:S(2)}) collective-permute-start(bf16[1,2,240,768]{3,2,1,0:T(8,128)(2,1)} %bitcast.187), channel_id=1, source_target_pairs={{0,16},{4,20},{8,24},{12,28},{16,0},{20,4},{24,8},{28,12},{1,17},{... | collective-permute-start | bytes 2211848 | tf_op jit(solution)/shard_map/ppermute | solution.py:23
  189.8 63.6 %reduce-scatter.8.cloned.1.call-start = ((), (), s32[]{:S(2)}) async-start(), calls=%async_computation.5 | async-start | bytes 983040 | tf_op jit(solution)/shard_map/reduce_scatter | solution.py:992
  195.4 11.9 %copy-start.3 = (bf16[1,240,768]{2,1,0:T(8,128)(2,1)S(1)}, bf16[1,240,768]{2,1,0:T(8,128)(2,1)}, u32[]{:S(2)}) copy-start(bf16[1,240,768]{2,1,0:T(8,128)(2,1)} %copy-done.2) | copy-start | bytes 1105924
  207.5 10.8 %collective-permute-start.18 = (bf16[1,240,768]{2,1,0:T(8,128)(2,1)S(1)}, bf16[1,240,768]{2,1,0:T(8,128)(2,1)S(1)}, u32[]{:S(2)}, u32[]{:S(2)}) collective-permute-start(bf16[1,240,768]{2,1,0:T(8,128)(2,1)S(1)} %get-tuple-element.251), channel_id=1, source_target_pairs={{0,8},{4,12},{8,0},{12,4},{16,24},{20,28},{24,16},{28,20},{1,9},{5... | collective-permute-start | bytes 1105928 | tf_op jit(solution)/shard_map/ppermute | solution.py:23
  208.6 9.7 %collective-permute-start.19 = (bf16[1,240,768]{2,1,0:T(8,128)(2,1)S(1)}, bf16[1,240,768]{2,1,0:T(8,128)(2,1)S(1)}, u32[]{:S(2)}, u32[]{:S(2)}) collective-permute-start(bf16[1,240,768]{2,1,0:T(8,128)(2,1)S(1)} %get-tuple-element.252), channel_id=1, source_target_pairs={{0,16},{4,20},{8,24},{12,28},{16,0},{20,4},{24,8},{28,12},{1,17},{... | collective-permute-start | bytes 1105928 | tf_op jit(solution)/shard_map/ppermute | solution.py:23
  219.9 3.9 %collective-permute-start.20 = (bf16[4,288,768]{2,1,0:T(8,128)(2,1)}, bf16[4,288,768]{2,1,0:T(8,128)(2,1)S(1)}, u32[]{:S(2)}, u32[]{:S(2)}) collective-permute-start(bf16[4,288,768]{2,1,0:T(8,128)(2,1)} %bitcast.223), channel_id=1, source_target_pairs={{0,4},{4,0},{8,12},{12,8},{16,20},{20,16},{24,28},{28,24},{1,5},{5... | collective-permute-start | bytes 5308424 | tf_op jit(solution)/shard_map/ppermute | solution.py:23
  224.9 13.5 %collective-permute-start.21 = (bf16[1,2,144,768]{3,2,1,0:T(8,128)(2,1)S(1)}, bf16[1,2,144,768]{3,2,1,0:T(8,128)(2,1)S(1)}, u32[]{:S(2)}, u32[]{:S(2)}) collective-permute-start(bf16[1,2,144,768]{3,2,1,0:T(8,128)(2,1)S(1)} %bitcast.190), channel_id=1, source_target_pairs={{0,8},{4,12},{8,0},{12,4},{16,24},{20,28},{24,16},{28,20},{1,9},{5... | collective-permute-start | bytes 1327112 | tf_op jit(solution)/shard_map/ppermute | solution.py:23
  226.0 12.4 %collective-permute-start.22 = (bf16[1,2,144,768]{3,2,1,0:T(8,128)(2,1)S(1)}, bf16[1,2,144,768]{3,2,1,0:T(8,128)(2,1)S(1)}, u32[]{:S(2)}, u32[]{:S(2)}) collective-permute-start(bf16[1,2,144,768]{3,2,1,0:T(8,128)(2,1)S(1)} %bitcast.189), channel_id=1, source_target_pairs={{0,16},{4,20},{8,24},{12,28},{16,0},{20,4},{24,8},{28,12},{1,17},{... | collective-permute-start | bytes 1327112 | tf_op jit(solution)/shard_map/ppermute | solution.py:23
  238.5 13.0 %collective-permute-start.23 = (bf16[1,144,768]{2,1,0:T(8,128)(2,1)S(1)}, bf16[1,144,768]{2,1,0:T(8,128)(2,1)S(1)}, u32[]{:S(2)}, u32[]{:S(2)}) collective-permute-start(bf16[1,144,768]{2,1,0:T(8,128)(2,1)S(1)} %fusion.3), channel_id=1, source_target_pairs={{0,8},{4,12},{8,0},{12,4},{16,24},{20,28},{24,16},{28,20},{1,9},{5... | collective-permute-start | bytes 663560 | tf_op jit(solution)/shard_map/ppermute | solution.py:23
  239.8 11.8 %collective-permute-start.24 = (bf16[1,144,768]{2,1,0:T(8,128)(2,1)S(1)}, bf16[1,144,768]{2,1,0:T(8,128)(2,1)S(1)}, u32[]{:S(2)}, u32[]{:S(2)}) collective-permute-start(bf16[1,144,768]{2,1,0:T(8,128)(2,1)S(1)} %fusion.2), channel_id=1, source_target_pairs={{0,16},{4,20},{8,24},{12,28},{16,0},{20,4},{24,8},{28,12},{1,17},{... | collective-permute-start | bytes 663560 | tf_op jit(solution)/shard_map/ppermute | solution.py:23
  240.7 7.7 %collective-permute-start.25 = (f32[16,768]{1,0:T(8,128)S(1)}, f32[16,768]{1,0:T(8,128)S(1)}, u32[]{:S(2)}, u32[]{:S(2)}) collective-permute-start(f32[16,768]{1,0:T(8,128)S(1)} %copy-done.17), channel_id=1, source_target_pairs={{0,1},{1,2},{2,3},{3,0},{4,5},{5,6},{6,7},{7,4},{8,9},{9,10},{10,1... | collective-permute-start | bytes 147464 | tf_op jit(solution)/shard_map/ppermute | solution.py:23
  243.2 8.3 %collective-permute-start.26 = (f32[16,768]{1,0:T(8,128)S(1)}, f32[16,768]{1,0:T(8,128)S(1)}, u32[]{:S(2)}, u32[]{:S(2)}) collective-permute-start(f32[16,768]{1,0:T(8,128)S(1)} %copy-done.17), channel_id=1, source_target_pairs={{0,2},{1,3},{2,0},{3,1},{4,6},{5,7},{6,4},{7,5},{8,10},{9,11},{10,... | collective-permute-start | bytes 147464 | tf_op jit(solution)/shard_map/ppermute | solution.py:23
  244.5 7.0 %collective-permute-start.27 = (f32[16,768]{1,0:T(8,128)S(1)}, f32[16,768]{1,0:T(8,128)S(1)}, u32[]{:S(2)}, u32[]{:S(2)}) collective-permute-start(f32[16,768]{1,0:T(8,128)S(1)} %copy-done.17), channel_id=1, source_target_pairs={{0,3},{1,0},{2,1},{3,2},{4,7},{5,4},{6,5},{7,6},{8,11},{9,8},{10,9... | collective-permute-start | bytes 147464 | tf_op jit(solution)/shard_map/ppermute | solution.py:23
  251.7 8.9 %copy-start.16 = (bf16[1,192,384]{2,1,0:T(8,128)(2,1)S(1)}, bf16[1,192,384]{2,1,0:T(8,128)(2,1)}, u32[]{:S(2)}) copy-start(bf16[1,192,384]{2,1,0:T(8,128)(2,1)} %reduce-scatter.6.cloned.1.call-done) | copy-start | bytes 442372
  253.3 6.9 %collective-permute-start.31 = (f32[16,768]{1,0:T(8,128)S(1)}, f32[16,768]{1,0:T(8,128)S(1)}, u32[]{:S(2)}, u32[]{:S(2)}) collective-permute-start(f32[16,768]{1,0:T(8,128)S(1)} %add_add_fusion.1), channel_id=1, source_target_pairs={{0,8},{4,12},{8,0},{12,4},{16,24},{20,28},{24,16},{28,20},{1,9},{5... | collective-permute-start | bytes 147464 | tf_op jit(solution)/shard_map/ppermute | solution.py:23
  254.8 10.5 %collective-permute-start.28 = (bf16[96,640]{1,0:T(8,128)(2,1)S(1)}, bf16[96,640]{1,0:T(8,128)(2,1)S(1)}, u32[]{:S(2)}, u32[]{:S(2)}) collective-permute-start(bf16[96,640]{1,0:T(8,128)(2,1)S(1)} %get-tuple-element.296), channel_id=1, source_target_pairs={{0,1},{1,2},{2,3},{3,0},{4,5},{5,6},{6,7},{7,4},{8,9},{9,10},{10,1... | collective-permute-start | bytes 368648 | tf_op jit(solution)/shard_map/ppermute | solution.py:23
  255.9 10.6 %collective-permute-start.29 = (bf16[96,640]{1,0:T(8,128)(2,1)S(1)}, bf16[96,640]{1,0:T(8,128)(2,1)S(1)}, u32[]{:S(2)}, u32[]{:S(2)}) collective-permute-start(bf16[96,640]{1,0:T(8,128)(2,1)S(1)} %get-tuple-element.297), channel_id=1, source_target_pairs={{0,2},{1,3},{2,0},{3,1},{4,6},{5,7},{6,4},{7,5},{8,10},{9,11},{10,... | collective-permute-start | bytes 368648 | tf_op jit(solution)/shard_map/ppermute | solution.py:23
  257.3 9.3 %collective-permute-start.30 = (bf16[96,640]{1,0:T(8,128)(2,1)S(1)}, bf16[96,640]{1,0:T(8,128)(2,1)S(1)}, u32[]{:S(2)}, u32[]{:S(2)}) collective-permute-start(bf16[96,640]{1,0:T(8,128)(2,1)S(1)} %get-tuple-element.298), channel_id=1, source_target_pairs={{0,3},{1,0},{2,1},{3,2},{4,7},{5,4},{6,5},{7,6},{8,11},{9,8},{10,9... | collective-permute-start | bytes 368648 | tf_op jit(solution)/shard_map/ppermute | solution.py:23
  258.6 4.6 %collective-permute-start.32 = (f32[16,768]{1,0:T(8,128)S(1)}, f32[16,768]{1,0:T(8,128)S(1)}, u32[]{:S(2)}, u32[]{:S(2)}) collective-permute-start(f32[16,768]{1,0:T(8,128)S(1)} %add_add_fusion.1), channel_id=1, source_target_pairs={{0,16},{4,20},{8,24},{12,28},{16,0},{20,4},{24,8},{28,12},{1,17},{... | collective-permute-start | bytes 147464 | tf_op jit(solution)/shard_map/ppermute | solution.py:23
  260.3 5.0 %collective-permute-start.33 = (f32[16,768]{1,0:T(8,128)S(1)}, f32[16,768]{1,0:T(8,128)S(1)}, u32[]{:S(2)}, u32[]{:S(2)}) collective-permute-start(f32[16,768]{1,0:T(8,128)S(1)} %add_add_fusion.1), channel_id=1, source_target_pairs={{0,24},{4,28},{8,16},{12,20},{16,8},{20,12},{24,0},{28,4},{1,25},{... | collective-permute-start | bytes 147464 | tf_op jit(solution)/shard_map/ppermute | solution.py:23
  266.6 2.4 collective-permute-start.34
  (10 other events, 25.6 us)
Sparse Core Ops, SparseCore 0:
  50.7 38.8 all-gather.4
  91.4 38.9 all-gather.6
  133.8 53.8 reduce-scatter.3
  190.0 21.9 reduce-scatter.5
  227.1 26.1 reduce-scatter.7

commit v7 on v6

--- a/solution.py
+++ b/solution.py
@@ -998,9 +998,9 @@
         held[1:3],
         planes(),
     )
-    others = [sums] * (layers - 1)
+    both = [lambda v: exchange(v, "wide", lambda i: i ^ 6)]
     sums, moved = beside(
-        lambda v: v, sums, [*second_sends(held, first), *others], planes() + shifts(layers)
+        lambda v: v, sums, [*second_sends(held, first), sums, sums, sums], planes() + planes() + both
     )
     second = moved[:2]
     for piece_sums in moved[2:]:
@@ -1008,14 +1008,12 @@
     total_qkv = halve(own_sum(held[0], first, second))
     blocks = jnp.concatenate([total_qkv[i * short : (i + 1) * short] for i in range(3)], axis=1)
     own_block, sends, moves = columns_blocks(blocks, part, layers)
-    both = [lambda v: exchange(v, "wide", lambda i: i ^ 6)]
-
     def last_part(value):
         sums, total_up, total_down = value
         return sums, total_up.astype(F32), total_down.astype(F32).T
 
     (sums, total_up, total_down), moved = beside(
-        last_part, (sums, total_up, total_down), [*sends, sums, sums, sums], moves + planes() + both
+        last_part, (sums, total_up, total_down), [*sends, *[sums] * (layers - 1)], moves + shifts(layers)
     )
     total_qkv = own_columns(own_block, moved[: layers - 1], part, blocks.shape[1])
     for piece_sums in moved[layers - 1 :]:

time: 283 us -> 283 us (level)
  transfers between devices with their start and end apart: 40 -> 40, of which waited for: 16 -> 14; matrix products, arithmetic and copies ran while one was open for 3% -> 3% of each run, Pallas kernels for 55% -> 55%
where the time goes in v7:
time: 283 us; the launch traced here: 278 us
  Pallas kernels  152 us (54%)
  waiting for transfers between devices  46.3 us (16%)
  starting transfers between devices  44.5 us (16%)
  between operations  15 us (5%)
  local copies, waits for them, and re-layouts  10 us (4%)
  other arithmetic  9.55 us (3%)
    ppermute x35, waiting for transfers between devices, exchange(): lax.ppermute(value, axis_name, [(i, partner(i) % size) for i in range(siz...  44.3 us
    ppermute x35, starting transfers between devices, exchange(): lax.ppermute(value, axis_name, [(i, partner(i) % size) for i in range(siz...  43.9 us
    pallas_call x1, Pallas kernels, back(): pl.pallas_call(functools.partial(back_kernel, *plans, sizes), grid=(count...  30.1 us
    pallas_call x3, Pallas kernels, attend_back(): pl.pallas_call(attend_back_kernel, grid=(part,), in_specs=[pair_block(row...  25.6 us
    pallas_call x2, Pallas kernels, attend(): pl.pallas_call(functools.partial(attend_kernel, pack), grid=(pairs,), in_...  21.9 us
    pallas_call x2, Pallas kernels, outer(): pl.pallas_call(functools.partial(outer_kernel, direct(), steps), grid=(to...  20.9 us
    pallas_call x1, Pallas kernels, hidden(): pl.pallas_call(functools.partial(hidden_kernel, out_plan, up_plans, sizes...  19.3 us
    pallas_call x1, Pallas kernels, inputs_back(): pl.pallas_call(functools.partial(inputs_kernel, plans), grid=(count // TI...  11.4 us
  transfers between devices with their start and end apart: 40, of which 14 were waited for; matrix products, arithmetic and copies ran while one was open for 3% of the time, Pallas kernels for 55%

profile of v7, /device:TPU:0, one launch (start us, length us, event | category | flops | bytes accessed | tf_op | source)
XLA Modules:
  0.0 277.8 jit_solution(15148497799698814479)
XLA Ops:
  7.3 1.5 stack.82
  9.4 1.0 fusion.6
  10.4 5.1 %collective-permute-start = (bf16[112,768]{1,0:T(8,128)(2,1)S(1)}, bf16[112,768]{1,0:T(8,128)(2,1)S(1)}, u32[]{:S(2)}, u32[]{:S(2)}) collective-permute-start(bf16[112,768]{1,0:T(8,128)(2,1)S(1)} %fusion.6), channel_id=1, source_target_pairs={{0,3},{1,0},{2,1},{3,2},{4,7},{5,4},{6,5},{7,6},{8,11},{9,8},{10,9... | collective-permute-start | bytes 516104 | tf_op jit(solution)/shard_map/ppermute | solution.py:23
  15.6 1.0 collective-permute-start.2
  16.6 3.8 %collective-permute-done = bf16[112,768]{1,0:T(8,128)(2,1)S(1)} collective-permute-done((bf16[112,768]{1,0:T(8,128)(2,1)S(1)}, bf16[112,768]{1,0:T(8,128)(2,1)S(1)}, u32[]{:S(2)}, u32[]{:S(2)}) %collective-permute-start) | collective-permute-done | bytes 172064 | tf_op jit(solution)/shard_map/ppermute | solution.py:23
  20.4 9.7 %collective-permute-done.1 = bf16[112,768]{1,0:T(8,128)(2,1)S(1)} collective-permute-done((bf16[112,768]{1,0:T(8,128)(2,1)S(1)}, bf16[112,768]{1,0:T(8,128)(2,1)S(1)}, u32[]{:S(2)}, u32[]{:S(2)}) %collective-permute-start.1) | collective-permute-done | bytes 172064 | tf_op jit(solution)/shard_map/ppermute | solution.py:23
  31.3 1.6 collective-permute-start.3
  32.8 1.5 collective-permute-start.4
  35.2 1.9 collective-permute-start.6
  37.1 2.9 %collective-permute-start.7 = (bf16[96,768]{1,0:T(8,128)(2,1)S(1)}, bf16[96,768]{1,0:T(8,128)(2,1)S(1)}, u32[]{:S(2)}, u32[]{:S(2)}) collective-permute-start(bf16[96,768]{1,0:T(8,128)(2,1)S(1)} %copy-done.13), channel_id=1, source_target_pairs={{0,3},{1,0},{2,1},{3,2},{4,7},{5,4},{6,5},{7,6},{8,11},{9,8},{10,9... | collective-permute-start | bytes 442376 | tf_op jit(solution)/shard_map/ppermute | solution.py:23
  40.0 2.9 %collective-permute-done.5 = bf16[96,768]{1,0:T(8,128)(2,1)S(1)} collective-permute-done((bf16[96,768]{1,0:T(8,128)(2,1)S(1)}, bf16[96,768]{1,0:T(8,128)(2,1)S(1)}, u32[]{:S(2)}, u32[]{:S(2)}) %collective-permute-start.5) | collective-permute-done | bytes 147488 | tf_op jit(solution)/shard_map/ppermute | solution.py:23
  43.0 4.5 %collective-permute-done.6 = bf16[96,768]{1,0:T(8,128)(2,1)S(1)} collective-permute-done((bf16[96,768]{1,0:T(8,128)(2,1)S(1)}, bf16[96,768]{1,0:T(8,128)(2,1)S(1)}, u32[]{:S(2)}, u32[]{:S(2)}) %collective-permute-start.6) | collective-permute-done | bytes 147488 | tf_op jit(solution)/shard_map/ppermute | solution.py:23
  48.0 1.4 pad_maximum_fusion
  51.3 1.5 collective-permute-start.8
  52.8 7.6 %collective-permute-done.8 = bf16[1,192,768]{2,1,0:T(8,128)(2,1)S(1)} collective-permute-done((bf16[1,192,768]{2,1,0:T(8,128)(2,1)S(1)}, bf16[1,192,768]{2,1,0:T(8,128)(2,1)S(1)}, u32[]{:S(2)}, u32[]{:S(2)}) %collective-permute-start.8) | collective-permute-done | bytes 294944 | tf_op jit(solution)/shard_map/ppermute | solution.py:23
  61.4 3.6 %collective-permute-start.12 = (bf16[96,768]{1,0:T(8,128)(2,1)S(1)}, bf16[96,768]{1,0:T(8,128)(2,1)S(1)}, u32[]{:S(2)}, u32[]{:S(2)}) collective-permute-start(bf16[96,768]{1,0:T(8,128)(2,1)S(1)} %pad_maximum_fusion.5), channel_id=1, source_target_pairs={{0,1},{1,2},{2,3},{3,0},{4,5},{5,6},{6,7},{7,4},{8,9},{9,10},{10,1... | collective-permute-start | bytes 442376 | tf_op jit(solution)/shard_map/ppermute | solution.py:23
  65.1 2.0 collective-permute-start.13
  68.4 10.1 %project.1 = (bf16[1024,768]{1,0:T(8,128)(2,1)}, bf16[1024,768]{1,0:T(8,128)(2,1)}, bf16[1024,768]{1,0:T(8,128)(2,1)}, bf16[1024,768]{1,0:T(8,128)(2,1)}, f32[16,768]{1,0:T(8,128)}) custom-call(s32[1]{0:T(128)} %bitcast.place, bf16[1024,768]{1,0:T(8,128)(2,1)} %bitcast.200, bf16[16,768]{1,0:T(8,128)(2,1)} %broadcast.21.extras, ...), custom_call_target="tpu_custom_call" | custom-call | flops 3623878656 | bytes 11010048 | tf_op jit(solution)/shard_map/project/pallas_call | solution.py:279
  78.9 1.1 maximum_maximum_fusion
  80.3 11.0 %attend.2 = (bf16[1024,768]{1,0:T(8,128)(2,1)}, bf16[12,512,512]{2,1,0:T(8,128)(2,1)}) custom-call(s32[2,6]{1,0:T(2,128)} %lengths.7, bf16[1024,768]{1,0:T(8,128)(2,1)} %get-tuple-element.189.query, bf16[1024,768]{1,0:T(8,128)(2,1)} %get-tuple-element.190.key, bf16[1024,768]{1,0:T(8,128)(2,1)} %get-tuple-element.191.value), custom_call_target="tpu_custom_call" | custom-call | tf_op jit(solution)/shard_map/attend/pallas_call | solution.py:360
  91.3 10.9 %attend.3 = (bf16[1024,768]{1,0:T(8,128)(2,1)}, bf16[12,512,512]{2,1,0:T(8,128)(2,1)}) custom-call(s32[2,6]{1,0:T(2,128)} %lengths.7, bf16[1024,768]{1,0:T(8,128)(2,1)} %get-tuple-element.189.query, bf16[1024,768]{1,0:T(8,128)(2,1)} %get-tuple-element.190.key, bf16[1024,768]{1,0:T(8,128)(2,1)} %get-tuple-element.191.value, ...), custom_call_target="tpu_custom_call", output_to_operand_aliasing={{0}: (4, {})} | custom-call | flops 3221225472 | bytes 3145728 | tf_op jit(solution)/shard_map/attend/pallas_call | solution.py:360
  102.2 19.3 %hidden.1 = (f32[1024,768]{1,0:T(8,128)}, bf16[1024,768]{1,0:T(8,128)(2,1)}, bf16[1024,3072]{1,0:T(8,128)(2,1)}, bf16[1024,3072]{1,0:T(8,128)(2,1)}, bf16[1024,768]{1,0:T(8,128)(2,1)}) custom-call(s32[1]{0:T(128)} %bitcast.place, s32[2,6]{1,0:T(2,128)} %lengths.7, bf16[1024,768]{1,0:T(8,128)(2,1)} %bitcast.201, ...), custom_call_target="tpu_custom_call" | custom-call | flops 8455716864 | bytes 20447232 | tf_op jit(solution)/shard_map/hidden/pallas_call | solution.py:469
  121.5 9.2 %wide_outer.1 = bf16[8,768,384]{2,1,0:T(8,128)(2,1)} custom-call(bf16[1024,768]{1,0:T(8,128)(2,1)} %get-tuple-element.198.left.grad_down, bf16[1024,3072]{1,0:T(8,128)(2,1)} %get-tuple-element.199.right.active), custom_call_target="tpu_custom_call" | custom-call | flops 4831838208 | bytes 13762560 | tf_op jit(solution)/shard_map/wide_outer/pallas_call | solution.py:672
  131.1 30.1 %back.1 = (bf16[1024,768]{1,0:T(8,128)(2,1)}, bf16[1024,3072]{1,0:T(8,128)(2,1)}, f32[1024,768]{1,0:T(8,128)}, bf16[1024,768]{1,0:T(8,128)(2,1)}, bf16[1024,768]{1,0:T(8,128)(2,1)}, /*index=5*/f32[16,768]{1,0:T(8,128)}) custom-call(s32[1]{0:T(128)} %bitcast.place, s32[2,6]{1,0:T(2,128)} %lengths.7, bf16[1024,768]{1,0:T(8,128)(2,1)} %bitcast.202, ...), custom_call_target="tpu_custom_call" | custom-call | flops 15703474176 | bytes 31457280 | tf_op jit(solution)/shard_map/back/pallas_call | solution.py:560
  161.2 12.2 %outer.2 = (bf16[4,5,96,768]{3,2,1,0:T(8,128)(2,1)}, bf16[4,5,96,768]{3,2,1,0:T(8,128)(2,1)}) custom-call(s32[1]{0:T(128)} %bitcast.place, bf16[1024,768]{1,0:T(8,128)(2,1)} %get-tuple-element.207.refs_0_, bf16[1024,768]{1,0:T(8,128)(2,1)} %get-tuple-element.193.mixed.refs_1_, bf16[1024,3072]{1,0:T(8,128)(2,1)} %get-tuple-element.208.refs_2_, ...), custom_call_target="tpu_custom_call" | custom-call | flops 6039797760 | bytes 13762560 | tf_op jit(solution)/shard_map/outer/pallas_call | solution.py:648
  173.4 8.5 %attend_back.3 = (bf16[1024,768]{1,0:T(8,128)(2,1)}, bf16[1024,768]{1,0:T(8,128)(2,1)}, bf16[1024,768]{1,0:T(8,128)(2,1)}) custom-call(bf16[1024,768]{1,0:T(8,128)(2,1)} %get-tuple-element.189.query, bf16[1024,768]{1,0:T(8,128)(2,1)} %get-tuple-element.190.key, bf16[1024,768]{1,0:T(8,128)(2,1)} %get-tuple-element.191.value, ...), custom_call_target="tpu_custom_call" | custom-call | flops 4294967296 | bytes 3670016 | tf_op jit(solution)/shard_map/attend_back/pallas_call | solution.py:398
  182.0 2.8 %core_add.2 = (bf16[1,480,768]{2,1,0:T(8,128)(2,1)S(1)}, bf16[2,240,768]{2,1,0:T(8,128)(2,1)S(1)}, bf16[2,240,768]{2,1,0:T(8,128)(2,1)S(1)}, bf16[1,240,768]{2,1,0:T(8,128)(2,1)S(1)}, bf16[1,240,768]{2,1,0:T(8,128)(2,1)S(1)}) custom-call(bf16[4,480,768]{2,1,0:T(8,128)(2,1)S(1)} %bitcast.185, bf16[4,480,768]{2,1,0:T(8,128)(2,1)} %collective-permute-done.15.other), custom_call_target="tpu_custom_call" | custom-call | flops 1474560 | bytes 8847360 | tf_op jit(solution)/shard_map/core_add/pallas_call | solution.py:784
  187.7 1.4 collective-permute-start.16
  189.8 5.6 %attend_back.4 = (bf16[1024,768]{1,0:T(8,128)(2,1)}, bf16[1024,768]{1,0:T(8,128)(2,1)}, bf16[1024,768]{1,0:T(8,128)(2,1)}) custom-call(bf16[1024,768]{1,0:T(8,128)(2,1)} %get-tuple-element.189.query, bf16[1024,768]{1,0:T(8,128)(2,1)} %get-tuple-element.190.key, ...), custom_call_target="tpu_custom_call", output_to_operand_aliasing={{0}: (5, {}), {1}: (6, {}), {2}: (7, {})} | custom-call | flops 2147483648 | bytes 1835008 | tf_op jit(solution)/shard_map/attend_back/pallas_call | solution.py:398
  195.4 11.5 %attend_back.5 = (bf16[1024,768]{1,0:T(8,128)(2,1)}, bf16[1024,768]{1,0:T(8,128)(2,1)}, bf16[1024,768]{1,0:T(8,128)(2,1)}) custom-call(bf16[1024,768]{1,0:T(8,128)(2,1)} %get-tuple-element.189.query, bf16[1024,768]{1,0:T(8,128)(2,1)} %get-tuple-element.190.key, ...), custom_call_target="tpu_custom_call", output_to_operand_aliasing={{0}: (5, {}), {1}: (6, {}), {2}: (7, {})} | custom-call | flops 6442450944 | bytes 5505024 | tf_op jit(solution)/shard_map/attend_back/pallas_call | solution.py:398
  207.5 1.1 collective-permute-start.18
  209.6 8.7 %outer.3 = (bf16[4,3,96,768]{3,2,1,0:T(8,128)(2,1)}, bf16[4,3,96,768]{3,2,1,0:T(8,128)(2,1)}) custom-call(s32[1]{0:T(128)} %bitcast.place, bf16[1024,768]{1,0:T(8,128)(2,1)} %get-tuple-element.245.refs_0_, bf16[1024,768]{1,0:T(8,128)(2,1)} %get-tuple-element.264.refs_1_.grad_q, bf16[1024,768]{1,0:T(8,128)(2,1)} %get-tuple-element.265.refs_2_.grad_k, ...), custom_call_target="tpu_custom_call" | custom-call | flops 3623878656 | bytes 8257536 | tf_op jit(solution)/shard_map/outer/pallas_call | solution.py:648
  218.9 1.0 pad_maximum_fusion.1
  219.9 3.9 %collective-permute-done.20.other = bf16[4,288,768]{2,1,0:T(8,128)(2,1)S(1)} collective-permute-done((bf16[4,288,768]{2,1,0:T(8,128)(2,1)}, bf16[4,288,768]{2,1,0:T(8,128)(2,1)S(1)}, u32[]{:S(2)}, u32[]{:S(2)}) %collective-permute-start.20) | collective-permute-done | bytes 1769504 | tf_op jit(solution)/shard_map/ppermute | solution.py:23
  223.8 1.0 core_add.3
  224.9 1.1 collective-permute-start.21
  227.0 11.4 %inputs_back.1 = (f32[1024,768]{1,0:T(8,128)}, f32[16,768]{1,0:T(8,128)}) custom-call(s32[1]{0:T(128)} %bitcast.place, bf16[1024,768]{1,0:T(8,128)(2,1)} %bitcast.203, f32[1024,768]{1,0:T(8,128)} %get-tuple-element.203.grad_middle, bf16[1024,768]{1,0:T(8,128)(2,1)} %get-tuple-element.264.refs_1_.grad_q, bf16[1024,768]{1,0:T(8,128)(2,1)} %get-tuple-element.265.refs_2_.grad_k, ...), custom_call_target="tpu_custom_call" | custom-call | flops 3623878656 | bytes 15728640 | tf_op jit(solution)/shard_map/inputs_back/pallas_call | solution.py:714
  238.5 1.2 collective-permute-start.23
  240.7 1.1 collective-permute-start.25
  242.7 1.5 collective-permute-start.27
  244.2 3.0 %collective-permute-done.25 = f32[16,768]{1,0:T(8,128)S(1)} collective-permute-done((f32[16,768]{1,0:T(8,128)S(1)}, f32[16,768]{1,0:T(8,128)S(1)}, u32[]{:S(2)}, u32[]{:S(2)}) %collective-permute-start.25) | collective-permute-done | bytes 49184 | tf_op jit(solution)/shard_map/ppermute | solution.py:23
  247.2 1.3 collective-permute-done.26
  248.8 1.5 reduce-scatter.8.cloned.1.call-done
  250.4 1.0 collective-permute-start.31
  251.9 2.9 %collective-permute-start.29 = (bf16[96,640]{1,0:T(8,128)(2,1)S(1)}, bf16[96,640]{1,0:T(8,128)(2,1)S(1)}, u32[]{:S(2)}, u32[]{:S(2)}) collective-permute-start(bf16[96,640]{1,0:T(8,128)(2,1)S(1)} %get-tuple-element.297), channel_id=1, source_target_pairs={{0,2},{1,3},{2,0},{3,1},{4,6},{5,7},{6,4},{7,5},{8,10},{9,11},{10,... | collective-permute-start | bytes 368648 | tf_op jit(solution)/shard_map/ppermute | solution.py:23
  255.7 1.5 collective-permute-start.32
  257.2 2.0 collective-permute-start.33
  260.9 6.3 %collective-permute-done.32 = f32[16,768]{1,0:T(8,128)S(1)} collective-permute-done((f32[16,768]{1,0:T(8,128)S(1)}, f32[16,768]{1,0:T(8,128)S(1)}, u32[]{:S(2)}, u32[]{:S(2)}) %collective-permute-start.32) | collective-permute-done | bytes 49184 | tf_op jit(solution)/shard_map/ppermute | solution.py:23
  (165 shorter events, 23.7 us)
Async XLA Ops:
  7.2 23.0 %copy-start.11 = (bf16[96,576]{1,0:T(8,128)(2,1)S(1)}, bf16[96,576]{1,0:T(8,128)(2,1)}, u32[]{:S(2)}) copy-start(bf16[96,576]{1,0:T(8,128)(2,1)} %param.20) | copy-start | bytes 331780
  7.2 23.0 %copy-start.14 = (bf16[96,192]{1,0:T(8,128)(2,1)S(1)}, bf16[96,192]{1,0:T(8,128)(2,1)}, u32[]{:S(2)}) copy-start(bf16[96,192]{1,0:T(8,128)(2,1)} %param.21) | copy-start | bytes 110596
  7.2 95.0 %all-gather.5.cloned.1.call-start = ((), (), s32[]{:S(2)}) async-start(), calls=%async_computation.6 | async-start | bytes 5308416 | tf_op jit(solution)/shard_map/all_gather | solution.py:925
  10.4 9.9 %collective-permute-start = (bf16[112,768]{1,0:T(8,128)(2,1)S(1)}, bf16[112,768]{1,0:T(8,128)(2,1)S(1)}, u32[]{:S(2)}, u32[]{:S(2)}) collective-permute-start(bf16[112,768]{1,0:T(8,128)(2,1)S(1)} %fusion.6), channel_id=1, source_target_pairs={{0,3},{1,0},{2,1},{3,2},{4,7},{5,4},{6,5},{7,6},{8,11},{9,8},{10,9... | collective-permute-start | bytes 516104 | tf_op jit(solution)/shard_map/ppermute | solution.py:23
  15.6 14.6 %collective-permute-start.1 = (bf16[112,768]{1,0:T(8,128)(2,1)S(1)}, bf16[112,768]{1,0:T(8,128)(2,1)S(1)}, u32[]{:S(2)}, u32[]{:S(2)}) collective-permute-start(bf16[112,768]{1,0:T(8,128)(2,1)S(1)} %fusion.6), channel_id=1, source_target_pairs={{0,2},{1,3},{2,0},{3,1},{4,6},{5,7},{6,4},{7,5},{8,10},{9,11},{10,... | collective-permute-start | bytes 516104 | tf_op jit(solution)/shard_map/ppermute | solution.py:23
  15.6 14.6 %collective-permute-start.2 = (bf16[112,768]{1,0:T(8,128)(2,1)S(1)}, bf16[112,768]{1,0:T(8,128)(2,1)S(1)}, u32[]{:S(2)}, u32[]{:S(2)}) collective-permute-start(bf16[112,768]{1,0:T(8,128)(2,1)S(1)} %fusion.6), channel_id=1, source_target_pairs={{0,1},{1,2},{2,3},{3,0},{4,5},{5,6},{6,7},{7,4},{8,9},{9,10},{10,1... | collective-permute-start | bytes 516104 | tf_op jit(solution)/shard_map/ppermute | solution.py:23
  31.3 18.2 %copy-start.8 = (bf16[400,768]{1,0:T(8,128)(2,1)}, bf16[400,768]{1,0:T(8,128)(2,1)S(1)}, u32[]{:S(2)}) copy-start(bf16[400,768]{1,0:T(8,128)(2,1)S(1)} %constant_dynamic-update-slice_fusion) | copy-start | bytes 1843204
  31.3 16.3 %collective-permute-start.3 = (bf16[1,400,768]{2,1,0:T(8,128)(2,1)S(1)}, bf16[1,400,768]{2,1,0:T(8,128)(2,1)S(1)}, u32[]{:S(2)}, u32[]{:S(2)}) collective-permute-start(bf16[1,400,768]{2,1,0:T(8,128)(2,1)S(1)} %bitcast.191), channel_id=1, source_target_pairs={{0,8},{4,12},{8,0},{12,4},{16,24},{20,28},{24,16},{28,20},{1,9},{5... | collective-permute-start | bytes 1843208 | tf_op jit(solution)/shard_map/ppermute | solution.py:23
  32.8 15.2 %collective-permute-start.4 = (bf16[1,400,768]{2,1,0:T(8,128)(2,1)S(1)}, bf16[1,400,768]{2,1,0:T(8,128)(2,1)S(1)}, u32[]{:S(2)}, u32[]{:S(2)}) collective-permute-start(bf16[1,400,768]{2,1,0:T(8,128)(2,1)S(1)} %bitcast.192), channel_id=1, source_target_pairs={{0,16},{4,20},{8,24},{12,28},{16,0},{20,4},{24,8},{28,12},{1,17},{... | collective-permute-start | bytes 1843208 | tf_op jit(solution)/shard_map/ppermute | solution.py:23
  34.3 8.6 %collective-permute-start.5 = (bf16[96,768]{1,0:T(8,128)(2,1)S(1)}, bf16[96,768]{1,0:T(8,128)(2,1)S(1)}, u32[]{:S(2)}, u32[]{:S(2)}) collective-permute-start(bf16[96,768]{1,0:T(8,128)(2,1)S(1)} %copy-done.13), channel_id=1, source_target_pairs={{0,1},{1,2},{2,3},{3,0},{4,5},{5,6},{6,7},{7,4},{8,9},{9,10},{10,1... | collective-permute-start | bytes 442376 | tf_op jit(solution)/shard_map/ppermute | solution.py:23
  35.2 12.3 %collective-permute-start.6 = (bf16[96,768]{1,0:T(8,128)(2,1)S(1)}, bf16[96,768]{1,0:T(8,128)(2,1)S(1)}, u32[]{:S(2)}, u32[]{:S(2)}) collective-permute-start(bf16[96,768]{1,0:T(8,128)(2,1)S(1)} %copy-done.13), channel_id=1, source_target_pairs={{0,2},{1,3},{2,0},{3,1},{4,6},{5,7},{6,4},{7,5},{8,10},{9,11},{10,... | collective-permute-start | bytes 442376 | tf_op jit(solution)/shard_map/ppermute | solution.py:23
  37.1 10.4 %collective-permute-start.7 = (bf16[96,768]{1,0:T(8,128)(2,1)S(1)}, bf16[96,768]{1,0:T(8,128)(2,1)S(1)}, u32[]{:S(2)}, u32[]{:S(2)}) collective-permute-start(bf16[96,768]{1,0:T(8,128)(2,1)S(1)} %copy-done.13), channel_id=1, source_target_pairs={{0,3},{1,0},{2,1},{3,2},{4,7},{5,4},{6,5},{7,6},{8,11},{9,8},{10,9... | collective-permute-start | bytes 442376 | tf_op jit(solution)/shard_map/ppermute | solution.py:23
  49.7 11.1 %copy-start.15 = (bf16[384,192]{0,1:T(8,128)(2,1)S(1)}, bf16[384,192]{0,1:T(8,128)(2,1)}, u32[]{:S(2)}) copy-start(bf16[384,192]{0,1:T(8,128)(2,1)} %param.23) | copy-start | bytes 442372
  50.6 80.5 %all-gather.7.cloned.1.call-start = ((), (), s32[]{:S(2)}) async-start(), calls=%async_computation.7 | async-start | bytes 5308416 | tf_op jit(solution)/shard_map/all_gather | solution.py:941
  50.6 10.0 %collective-permute-start.10 = (bf16[3,400,768]{2,1,0:T(8,128)(2,1)}, bf16[3,400,768]{2,1,0:T(8,128)(2,1)S(1)}, u32[]{:S(2)}, u32[]{:S(2)}) collective-permute-start(bf16[3,400,768]{2,1,0:T(8,128)(2,1)} %pad_maximum_fusion), channel_id=1, source_target_pairs={{0,4},{4,0},{8,12},{12,8},{16,20},{20,16},{24,28},{28,24},{1,5},{5... | collective-permute-start | bytes 5529608 | tf_op jit(solution)/shard_map/ppermute | solution.py:23
  50.7 10.0 %collective-permute-start.9 = (bf16[1,208,768]{2,1,0:T(8,128)(2,1)S(1)}, bf16[1,208,768]{2,1,0:T(8,128)(2,1)S(1)}, u32[]{:S(2)}, u32[]{:S(2)}) collective-permute-start(bf16[1,208,768]{2,1,0:T(8,128)(2,1)S(1)} %slice.270), channel_id=1, source_target_pairs={{0,8},{4,12},{8,0},{12,4},{16,24},{20,28},{24,16},{28,20},{1,9},{5... | collective-permute-start | bytes 958472 | tf_op jit(solution)/shard_map/ppermute | solution.py:23
  51.3 9.1 %collective-permute-start.8 = (bf16[1,192,768]{2,1,0:T(8,128)(2,1)S(1)}, bf16[1,192,768]{2,1,0:T(8,128)(2,1)S(1)}, u32[]{:S(2)}, u32[]{:S(2)}) collective-permute-start(bf16[1,192,768]{2,1,0:T(8,128)(2,1)S(1)} %slice.269), channel_id=1, source_target_pairs={{0,16},{4,20},{8,24},{12,28},{16,0},{20,4},{24,8},{28,12},{1,17},{... | collective-permute-start | bytes 884744 | tf_op jit(solution)/shard_map/ppermute | solution.py:23
  60.6 7.6 %copy-start.9 = (bf16[3,400,768]{2,1,0:T(8,128)(2,1)}, bf16[3,400,768]{2,1,0:T(8,128)(2,1)S(1)}, u32[]{:S(2)}) copy-start(bf16[3,400,768]{2,1,0:T(8,128)(2,1)S(1)} %collective-permute-done.10.refs_4_) | copy-start | bytes 5529604
  60.7 6.8 %collective-permute-start.11 = (bf16[1,400,768]{2,1,0:T(8,128)(2,1)S(1)}, bf16[1,400,768]{2,1,0:T(8,128)(2,1)S(1)}, u32[]{:S(2)}, u32[]{:S(2)}) collective-permute-start(bf16[1,400,768]{2,1,0:T(8,128)(2,1)S(1)} %constant_dynamic-update-slice_fusion.1.refs_3_), channel_id=1, source_target_pairs={{0,4},{4,0},{8,12},{12,8},{16,20},{20,16},{24,28},{28,24},{1,5},{5... | collective-permute-start | bytes 1843208 | tf_op jit(solution)/shard_map/ppermute | solution.py:23
  61.4 17.1 %collective-permute-start.12 = (bf16[96,768]{1,0:T(8,128)(2,1)S(1)}, bf16[96,768]{1,0:T(8,128)(2,1)S(1)}, u32[]{:S(2)}, u32[]{:S(2)}) collective-permute-start(bf16[96,768]{1,0:T(8,128)(2,1)S(1)} %pad_maximum_fusion.5), channel_id=1, source_target_pairs={{0,1},{1,2},{2,3},{3,0},{4,5},{5,6},{6,7},{7,4},{8,9},{9,10},{10,1... | collective-permute-start | bytes 442376 | tf_op jit(solution)/shard_map/ppermute | solution.py:23
  65.1 13.4 %collective-permute-start.13 = (bf16[96,768]{1,0:T(8,128)(2,1)S(1)}, bf16[96,768]{1,0:T(8,128)(2,1)S(1)}, u32[]{:S(2)}, u32[]{:S(2)}) collective-permute-start(bf16[96,768]{1,0:T(8,128)(2,1)S(1)} %pad_maximum_fusion.5), channel_id=1, source_target_pairs={{0,2},{1,3},{2,0},{3,1},{4,6},{5,7},{6,4},{7,5},{8,10},{9,11},{10,... | collective-permute-start | bytes 442376 | tf_op jit(solution)/shard_map/ppermute | solution.py:23
  67.1 11.5 %collective-permute-start.14 = (bf16[96,768]{1,0:T(8,128)(2,1)S(1)}, bf16[96,768]{1,0:T(8,128)(2,1)S(1)}, u32[]{:S(2)}, u32[]{:S(2)}) collective-permute-start(bf16[96,768]{1,0:T(8,128)(2,1)S(1)} %pad_maximum_fusion.5), channel_id=1, source_target_pairs={{0,3},{1,0},{2,1},{3,2},{4,7},{5,4},{6,5},{7,6},{8,11},{9,8},{10,9... | collective-permute-start | bytes 442376 | tf_op jit(solution)/shard_map/ppermute | solution.py:23
  80.1 107.6 %reduce-scatter.4.cloned.1.call-start = ((), (), s32[]{:S(2)}) async-start(), calls=%async_computation.3 | async-start | bytes 5308416 | tf_op jit(solution)/shard_map/reduce_scatter | solution.py:955
  130.8 89.1 %reduce-scatter.6.cloned.1.call-start = ((), (), s32[]{:S(2)}) async-start(), calls=%async_computation.4 | async-start | bytes 737280 | tf_op jit(solution)/shard_map/reduce_scatter | solution.py:976
  173.4 8.6 %collective-permute-start.15 = (bf16[4,480,768]{2,1,0:T(8,128)(2,1)}, bf16[4,480,768]{2,1,0:T(8,128)(2,1)}, u32[]{:S(2)}, u32[]{:S(2)}) collective-permute-start(bf16[4,480,768]{2,1,0:T(8,128)(2,1)} %bitcast.222), channel_id=1, source_target_pairs={{0,4},{4,0},{8,12},{12,8},{16,20},{20,16},{24,28},{28,24},{1,5},{5... | collective-permute-start | bytes 8847368 | tf_op jit(solution)/shard_map/ppermute | solution.py:23
  173.4 8.6 %copy-start = (bf16[4,5,96,768]{3,2,1,0:T(8,128)(2,1)S(1)}, bf16[4,5,96,768]{3,2,1,0:T(8,128)(2,1)}, u32[]{:S(2)}) copy-start(bf16[4,5,96,768]{3,2,1,0:T(8,128)(2,1)} %get-tuple-element.222) | copy-start | bytes 8847364
  187.7 19.2 %collective-permute-start.16 = (bf16[1,2,240,768]{3,2,1,0:T(8,128)(2,1)}, bf16[1,2,240,768]{3,2,1,0:T(8,128)(2,1)S(1)}, u32[]{:S(2)}, u32[]{:S(2)}) collective-permute-start(bf16[1,2,240,768]{3,2,1,0:T(8,128)(2,1)} %bitcast.188), channel_id=1, source_target_pairs={{0,8},{4,12},{8,0},{12,4},{16,24},{20,28},{24,16},{28,20},{1,9},{5... | collective-permute-start | bytes 2211848 | tf_op jit(solution)/shard_map/ppermute | solution.py:23
  189.1 18.2 %collective-permute-start.17 = (bf16[1,2,240,768]{3,2,1,0:T(8,128)(2,1)}, bf16[1,2,240,768]{3,2,1,0:T(8,128)(2,1)S(1)}, u32[]{:S(2)}, u32[]{:S(2)}) collective-permute-start(bf16[1,2,240,768]{3,2,1,0:T(8,128)(2,1)} %bitcast.187), channel_id=1, source_target_pairs={{0,16},{4,20},{8,24},{12,28},{16,0},{20,4},{24,8},{28,12},{1,17},{... | collective-permute-start | bytes 2211848 | tf_op jit(solution)/shard_map/ppermute | solution.py:23
  189.8 60.6 %reduce-scatter.8.cloned.1.call-start = ((), (), s32[]{:S(2)}) async-start(), calls=%async_computation.5 | async-start | bytes 983040 | tf_op jit(solution)/shard_map/reduce_scatter | solution.py:992
  195.4 11.9 %copy-start.3 = (bf16[1,240,768]{2,1,0:T(8,128)(2,1)S(1)}, bf16[1,240,768]{2,1,0:T(8,128)(2,1)}, u32[]{:S(2)}) copy-start(bf16[1,240,768]{2,1,0:T(8,128)(2,1)} %copy-done.2) | copy-start | bytes 1105924
  207.5 10.8 %collective-permute-start.18 = (bf16[1,240,768]{2,1,0:T(8,128)(2,1)S(1)}, bf16[1,240,768]{2,1,0:T(8,128)(2,1)S(1)}, u32[]{:S(2)}, u32[]{:S(2)}) collective-permute-start(bf16[1,240,768]{2,1,0:T(8,128)(2,1)S(1)} %get-tuple-element.251), channel_id=1, source_target_pairs={{0,8},{4,12},{8,0},{12,4},{16,24},{20,28},{24,16},{28,20},{1,9},{5... | collective-permute-start | bytes 1105928 | tf_op jit(solution)/shard_map/ppermute | solution.py:23
  208.6 9.7 %collective-permute-start.19 = (bf16[1,240,768]{2,1,0:T(8,128)(2,1)S(1)}, bf16[1,240,768]{2,1,0:T(8,128)(2,1)S(1)}, u32[]{:S(2)}, u32[]{:S(2)}) collective-permute-start(bf16[1,240,768]{2,1,0:T(8,128)(2,1)S(1)} %get-tuple-element.252), channel_id=1, source_target_pairs={{0,16},{4,20},{8,24},{12,28},{16,0},{20,4},{24,8},{28,12},{1,17},{... | collective-permute-start | bytes 1105928 | tf_op jit(solution)/shard_map/ppermute | solution.py:23
  219.9 3.9 %collective-permute-start.20 = (bf16[4,288,768]{2,1,0:T(8,128)(2,1)}, bf16[4,288,768]{2,1,0:T(8,128)(2,1)S(1)}, u32[]{:S(2)}, u32[]{:S(2)}) collective-permute-start(bf16[4,288,768]{2,1,0:T(8,128)(2,1)} %bitcast.223), channel_id=1, source_target_pairs={{0,4},{4,0},{8,12},{12,8},{16,20},{20,16},{24,28},{28,24},{1,5},{5... | collective-permute-start | bytes 5308424 | tf_op jit(solution)/shard_map/ppermute | solution.py:23
  224.9 13.5 %collective-permute-start.21 = (bf16[1,2,144,768]{3,2,1,0:T(8,128)(2,1)S(1)}, bf16[1,2,144,768]{3,2,1,0:T(8,128)(2,1)S(1)}, u32[]{:S(2)}, u32[]{:S(2)}) collective-permute-start(bf16[1,2,144,768]{3,2,1,0:T(8,128)(2,1)S(1)} %bitcast.190), channel_id=1, source_target_pairs={{0,8},{4,12},{8,0},{12,4},{16,24},{20,28},{24,16},{28,20},{1,9},{5... | collective-permute-start | bytes 1327112 | tf_op jit(solution)/shard_map/ppermute | solution.py:23
  226.0 12.4 %collective-permute-start.22 = (bf16[1,2,144,768]{3,2,1,0:T(8,128)(2,1)S(1)}, bf16[1,2,144,768]{3,2,1,0:T(8,128)(2,1)S(1)}, u32[]{:S(2)}, u32[]{:S(2)}) collective-permute-start(bf16[1,2,144,768]{3,2,1,0:T(8,128)(2,1)S(1)} %bitcast.189), channel_id=1, source_target_pairs={{0,16},{4,20},{8,24},{12,28},{16,0},{20,4},{24,8},{28,12},{1,17},{... | collective-permute-start | bytes 1327112 | tf_op jit(solution)/shard_map/ppermute | solution.py:23
  238.5 9.9 %collective-permute-start.23 = (bf16[1,144,768]{2,1,0:T(8,128)(2,1)S(1)}, bf16[1,144,768]{2,1,0:T(8,128)(2,1)S(1)}, u32[]{:S(2)}, u32[]{:S(2)}) collective-permute-start(bf16[1,144,768]{2,1,0:T(8,128)(2,1)S(1)} %fusion.3), channel_id=1, source_target_pairs={{0,8},{4,12},{8,0},{12,4},{16,24},{20,28},{24,16},{28,20},{1,9},{5... | collective-permute-start | bytes 663560 | tf_op jit(solution)/shard_map/ppermute | solution.py:23
  239.8 8.7 %collective-permute-start.24 = (bf16[1,144,768]{2,1,0:T(8,128)(2,1)S(1)}, bf16[1,144,768]{2,1,0:T(8,128)(2,1)S(1)}, u32[]{:S(2)}, u32[]{:S(2)}) collective-permute-start(bf16[1,144,768]{2,1,0:T(8,128)(2,1)S(1)} %fusion.2), channel_id=1, source_target_pairs={{0,16},{4,20},{8,24},{12,28},{16,0},{20,4},{24,8},{28,12},{1,17},{... | collective-permute-start | bytes 663560 | tf_op jit(solution)/shard_map/ppermute | solution.py:23
  240.7 6.5 %collective-permute-start.25 = (f32[16,768]{1,0:T(8,128)S(1)}, f32[16,768]{1,0:T(8,128)S(1)}, u32[]{:S(2)}, u32[]{:S(2)}) collective-permute-start(f32[16,768]{1,0:T(8,128)S(1)} %copy-done.17), channel_id=1, source_target_pairs={{0,8},{4,12},{8,0},{12,4},{16,24},{20,28},{24,16},{28,20},{1,9},{5... | collective-permute-start | bytes 147464 | tf_op jit(solution)/shard_map/ppermute | solution.py:23
  241.8 6.7 %collective-permute-start.26 = (f32[16,768]{1,0:T(8,128)S(1)}, f32[16,768]{1,0:T(8,128)S(1)}, u32[]{:S(2)}, u32[]{:S(2)}) collective-permute-start(f32[16,768]{1,0:T(8,128)S(1)} %copy-done.17), channel_id=1, source_target_pairs={{0,16},{4,20},{8,24},{12,28},{16,0},{20,4},{24,8},{28,12},{1,17},{... | collective-permute-start | bytes 147464 | tf_op jit(solution)/shard_map/ppermute | solution.py:23
  242.7 5.8 %collective-permute-start.27 = (f32[16,768]{1,0:T(8,128)S(1)}, f32[16,768]{1,0:T(8,128)S(1)}, u32[]{:S(2)}, u32[]{:S(2)}) collective-permute-start(f32[16,768]{1,0:T(8,128)S(1)} %copy-done.17), channel_id=1, source_target_pairs={{0,24},{4,28},{8,16},{12,20},{16,8},{20,12},{24,0},{28,4},{1,25},{... | collective-permute-start | bytes 147464 | tf_op jit(solution)/shard_map/ppermute | solution.py:23
  248.7 10.5 %copy-start.16 = (bf16[1,192,384]{2,1,0:T(8,128)(2,1)S(1)}, bf16[1,192,384]{2,1,0:T(8,128)(2,1)}, u32[]{:S(2)}) copy-start(bf16[1,192,384]{2,1,0:T(8,128)(2,1)} %reduce-scatter.6.cloned.1.call-done) | copy-start | bytes 442372
  250.4 6.8 %collective-permute-start.31 = (f32[16,768]{1,0:T(8,128)S(1)}, f32[16,768]{1,0:T(8,128)S(1)}, u32[]{:S(2)}, u32[]{:S(2)}) collective-permute-start(f32[16,768]{1,0:T(8,128)S(1)} %add_add_fusion.1), channel_id=1, source_target_pairs={{0,1},{1,2},{2,3},{3,0},{4,5},{5,6},{6,7},{7,4},{8,9},{9,10},{10,1... | collective-permute-start | bytes 147464 | tf_op jit(solution)/shard_map/ppermute | solution.py:23
  251.4 15.8 %collective-permute-start.28 = (bf16[96,640]{1,0:T(8,128)(2,1)S(1)}, bf16[96,640]{1,0:T(8,128)(2,1)S(1)}, u32[]{:S(2)}, u32[]{:S(2)}) collective-permute-start(bf16[96,640]{1,0:T(8,128)(2,1)S(1)} %get-tuple-element.296), channel_id=1, source_target_pairs={{0,1},{1,2},{2,3},{3,0},{4,5},{5,6},{6,7},{7,4},{8,9},{9,10},{10,1... | collective-permute-start | bytes 368648 | tf_op jit(solution)/shard_map/ppermute | solution.py:23
  251.9 15.3 %collective-permute-start.29 = (bf16[96,640]{1,0:T(8,128)(2,1)S(1)}, bf16[96,640]{1,0:T(8,128)(2,1)S(1)}, u32[]{:S(2)}, u32[]{:S(2)}) collective-permute-start(bf16[96,640]{1,0:T(8,128)(2,1)S(1)} %get-tuple-element.297), channel_id=1, source_target_pairs={{0,2},{1,3},{2,0},{3,1},{4,6},{5,7},{6,4},{7,5},{8,10},{9,11},{10,... | collective-permute-start | bytes 368648 | tf_op jit(solution)/shard_map/ppermute | solution.py:23
  254.8 12.4 %collective-permute-start.30 = (bf16[96,640]{1,0:T(8,128)(2,1)S(1)}, bf16[96,640]{1,0:T(8,128)(2,1)S(1)}, u32[]{:S(2)}, u32[]{:S(2)}) collective-permute-start(bf16[96,640]{1,0:T(8,128)(2,1)S(1)} %get-tuple-element.298), channel_id=1, source_target_pairs={{0,3},{1,0},{2,1},{3,2},{4,7},{5,4},{6,5},{7,6},{8,11},{9,8},{10,9... | collective-permute-start | bytes 368648 | tf_op jit(solution)/shard_map/ppermute | solution.py:23
  255.7 11.4 %collective-permute-start.32 = (f32[16,768]{1,0:T(8,128)S(1)}, f32[16,768]{1,0:T(8,128)S(1)}, u32[]{:S(2)}, u32[]{:S(2)}) collective-permute-start(f32[16,768]{1,0:T(8,128)S(1)} %add_add_fusion.1), channel_id=1, source_target_pairs={{0,2},{1,3},{2,0},{3,1},{4,6},{5,7},{6,4},{7,5},{8,10},{9,11},{10,... | collective-permute-start | bytes 147464 | tf_op jit(solution)/shard_map/ppermute | solution.py:23
  257.2 9.9 %collective-permute-start.33 = (f32[16,768]{1,0:T(8,128)S(1)}, f32[16,768]{1,0:T(8,128)S(1)}, u32[]{:S(2)}, u32[]{:S(2)}) collective-permute-start(f32[16,768]{1,0:T(8,128)S(1)} %add_add_fusion.1), channel_id=1, source_target_pairs={{0,3},{1,0},{2,1},{3,2},{4,7},{5,4},{6,5},{7,6},{8,11},{9,8},{10,9... | collective-permute-start | bytes 147464 | tf_op jit(solution)/shard_map/ppermute | solution.py:23
  267.2 2.4 collective-permute-start.34
  (10 other events, 25.6 us)
Sparse Core Ops, SparseCore 0:
  50.7 38.8 all-gather.4
  91.4 38.9 all-gather.6
  133.8 53.8 reduce-scatter.3
  190.0 21.9 reduce-scatter.5
  227.1 23.2 reduce-scatter.7
